TPU v7x, 256 devices: a whole 4x4x8 slice. The times are simulated.
256 devices in a mesh: dp: 8 (over y, core), ctx: 8 (over z), mp: 4 (over x).
Axes of the slice: x: 4, y: 4, z: 8, core: 2. Of those that a mesh axis runs over, the one named last changes fastest.
Arguments:
- text_rows: bfloat16 [32768, 4096], P(('dp', 'ctx'), 'mp'), may hold values from -210 to 210
- visual_rows: bfloat16 [4096, 4096], P(('dp', 'ctx'), 'mp'), may hold values from -210 to 210, as said below
- image_counts: int32 [8], replicated, may hold values from 1 to 8, as said below
- image_starts: int32 [8, 8], replicated, may hold values from -1 to 4032, as said below
- norm_gain: float32 [4096], replicated, may hold values from 0.5 to 8
- w_query: bfloat16 [4096, 4096], P(None, 'mp'), may hold values from -0.09375 to 0.09375
- w_key: bfloat16 [4096, 512], P(None, 'mp'), may hold values from -0.09375 to 0.09375
- w_value: bfloat16 [4096, 512], P(None, 'mp'), may hold values from -0.09375 to 0.09375
Outputs:
- attn_mix: bfloat16 [32768, 4096], P(('dp', 'ctx'), 'mp')
Inputs may be any that keep to these rules, and one draw needn't show every extreme that they name: `image_counts`: every draw has a sample with 8 images. `image_starts`: for k below image_counts[s], image k of sample s starts at this position, a multiple of 64, rising with k, images never intersecting; the other entries are -1. Every sample with 8 images has one in its last 64 positions. `visual_rows`: visual rows; rows of slots past the last image are not read.
All inputs are finite; a program needn't handle non-finite values.
Results may differ from a plain program's by a relative error of at most 0.0075.
The roundings to bfloat16 on the way count: a program that leaves them out, or rounds other values in their place, can miss the bound.
Values may be sent and summed in bfloat16 or wider, within the bound.
No kernel may reach another device: no remote copies, remote signals or barrier semaphores. Data moves between devices by JAX's collectives and lax.ppermute only.
A program may use at most 192 MiB of HBM per device.

v0:
```python
import math

import jax
import jax.numpy as jnp
from jax import lax
from jax.sharding import PartitionSpec as P

HD = 128
IMG_TOK = 64
MAX_IMG = 8


rope_base = 500000.0
eps = 1e-05


def rotary(vectors, positions):
    half_size = vectors.shape[-1] // 2
    exponent = jnp.arange(half_size, dtype=jnp.float32) * (2.0 / vectors.shape[-1])
    frequency = jnp.exp(-exponent * math.log(rope_base))
    angles = positions.astype(jnp.float32)[:, None] * frequency[None, :]
    cosine = jnp.cos(angles)[:, None, :]
    sine = jnp.sin(angles)[:, None, :]
    first = vectors[..., :half_size]
    second = vectors[..., half_size:]
    return jnp.concatenate(
        [first * cosine - second * sine, second * cosine + first * sine], axis=-1
    )


def on_device(
    text_rows, visual_rows, image_counts, image_starts, norm_gain, w_query, w_key, w_value
):
    ctx_index = lax.axis_index("ctx")
    dp_index = lax.axis_index("dp")
    tok_rows = text_rows.shape[0]
    image_index = jnp.arange(MAX_IMG, dtype=jnp.int32)
    offsets = jnp.cumsum(image_counts) - image_counts
    my_count = lax.dynamic_index_in_dim(image_counts, dp_index, 0, keepdims=False)
    my_offset = lax.dynamic_index_in_dim(offsets, dp_index, 0, keepdims=False)
    my_starts = lax.dynamic_index_in_dim(image_starts, dp_index, 0, keepdims=False)
    positions = ctx_index * tok_rows + jnp.arange(tok_rows, dtype=jnp.int32)
    inside = (
        (image_index[None, :] < my_count)
        & (positions[:, None] >= my_starts[None, :])
        & (positions[:, None] < my_starts[None, :] + IMG_TOK)
    )
    is_visual = jnp.any(inside, axis=1)
    which_image = jnp.sum(jnp.where(inside, image_index[None, :], 0), axis=1)
    image_start = jnp.sum(jnp.where(inside, my_starts[None, :], 0), axis=1)
    within = positions - image_start
    packed = my_offset + which_image
    received = lax.all_gather(visual_rows, ("dp", "ctx"), axis=0, tiled=True)
    source_row = packed * IMG_TOK + within
    picked = jnp.take(received, jnp.where(is_visual, source_row, 0), axis=0)
    context = jnp.where(is_visual[:, None], picked, text_rows)
    whole = lax.all_gather(context, "mp", axis=1, tiled=True)
    widened = whole.astype(jnp.float32)
    mean_square = jnp.mean(widened * widened, axis=1, keepdims=True)
    normed = (widened * lax.rsqrt(mean_square + eps) * norm_gain[None, :]).astype(jnp.bfloat16)
    q_dev = w_query.shape[1] // HD
    kv_dev = w_key.shape[1] // HD
    group_size = q_dev // kv_dev
    query_lin = jnp.dot(normed, w_query, preferred_element_type=jnp.float32)
    key_lin = jnp.dot(normed, w_key, preferred_element_type=jnp.float32)
    value_lin = jnp.dot(normed, w_value, preferred_element_type=jnp.float32)
    queries = rotary(query_lin.reshape(tok_rows, q_dev, HD), positions).astype(jnp.bfloat16)
    keys_now = rotary(key_lin.reshape(tok_rows, kv_dev, HD), positions).astype(jnp.bfloat16)
    values_now = value_lin.reshape(tok_rows, kv_dev, HD).astype(jnp.bfloat16)
    grouped = queries.reshape(tok_rows, kv_dev, group_size, HD)
    score_scale = 1.0 / math.sqrt(HD)
    last_row = ctx_index * tok_rows + tok_rows - 1
    initial = (
        jnp.full((kv_dev, group_size, tok_rows), -1e30, jnp.float32),
        jnp.zeros((kv_dev, group_size, tok_rows), jnp.float32),
        jnp.zeros((kv_dev, group_size, tok_rows, HD), jnp.float32),
    )
    block_pair = (
        lax.all_gather(keys_now, "ctx", axis=0, tiled=True),
        lax.all_gather(values_now, "ctx", axis=0, tiled=True),
    )

    def update(running):
        run_max, run_total, run_acc = running
        keys_block, values_block = block_pair
        block_len = keys_block.shape[0]
        scores = (
            jnp.einsum("tagd,sad->agts", grouped, keys_block, preferred_element_type=jnp.float32)
            * score_scale
        )
        key_pos = jnp.arange(block_len, dtype=jnp.int32)
        visible = (key_pos[None, :] <= positions[:, None])[None, None]
        masked = jnp.where(visible, scores, -1e30)
        new_max = jnp.maximum(run_max, jnp.max(masked, axis=3))
        weights = jnp.where(visible, jnp.exp(masked - new_max[..., None]), 0.0)
        new_total = jnp.sum(weights, axis=3)
        new_acc = jnp.einsum(
            "agts,sad->agtd",
            weights.astype(jnp.bfloat16),
            values_block,
            preferred_element_type=jnp.float32,
        )
        return (new_max, new_total, new_acc)

    def unchanged(running):
        return running

    run_max, run_total, run_acc = lax.cond(jnp.int32(0) <= last_row, update, unchanged, initial)
    mixed_out = run_acc / run_total[..., None]
    return jnp.transpose(mixed_out, (2, 0, 1, 3)).reshape(tok_rows, q_dev * HD).astype(jnp.bfloat16)


def solution(mesh):
    in_specs = (
        P(("dp", "ctx"), "mp"),
        P(("dp", "ctx"), "mp"),
        P(),
        P(),
        P(),
        P(None, "mp"),
        P(None, "mp"),
        P(None, "mp"),
    )
    out_specs = P(("dp", "ctx"), "mp")
    return jax.shard_map(
        on_device, mesh=mesh, in_specs=in_specs, out_specs=out_specs, check_vma=False
    )
```

profile of v0, /device:TPU:224, one launch (start us, length us, event | category | flops | bytes accessed | tf_op | source)
XLA Modules:
  0.0 321.7 jit_solution(8295931253771307505)
XLA Ops:
  6.5 0.0 copy-start
  6.5 0.0 copy-start.1
  6.5 0.0 all-gather.6.cloned.1.call-start
  6.5 0.7 all-gather.6.cloned.1.call-update
  7.3 0.0 all-gather.8.cloned.1.call-start
  7.3 1.2 dynamic_slice.11
  8.6 0.8 reduce-window.9
  9.4 0.7 bitcast_subtract_fusion
  10.0 0.6 dynamic_slice.13
  10.7 0.6 iota_compare_fusion.1
  11.3 0.7 fusion.32
  12.0 0.1 fusion.33
  12.1 0.1 select_reduce_fusion
  12.2 0.6 compare_and_fusion.1
  12.9 0.0 copy-start.3
  12.9 79.8 %all-gather.6.cloned.1.call-done = bf16[4096,1024]{1,0:T(8,128)(2,1)} async-done(((bf16[64,1024]{1,0:T(8,128)(2,1)}), bf16[4096,1024]{1,0:T(8,128)(2,1)}) %all-gather.6.cloned.1.call-update) | async-done | bytes 8388624 | tf_op jit(solution)/shard_map/all_gather | solution.py:53
  92.7 7.2 %gather_fusion = bf16[512,1024]{1,0:T(8,128)(2,1)S(1)} fusion(bf16[4096,1024]{1,0:T(8,128)(2,1)} %all-gather.6.cloned.1.call-done, s32[1024]{0:T(1024)S(1)} %pad_clamp_fusion), kind=kCustom, calls=%fused_computation | custom fusion | bytes 2099200 | tf_op jit(solution)/shard_map/jit(_take)/gather | solution.py:55
  99.9 0.0 copy-done.1
  99.9 1.2 select_select_fusion
  101.1 0.0 copy-start.2
  101.1 0.0 all-gather.8.cloned.1.call-update
  101.2 0.0 all-gather.12.cloned.1.call-start
  101.2 48.9 %all-gather.8.cloned.1.call-done = bf16[512,4096]{1,0:T(8,128)(2,1)} async-done(((bf16[512,1024]{1,0:T(8,128)(2,1)}), bf16[512,4096]{1,0:T(8,128)(2,1)}) %all-gather.8.cloned.1.call-update) | async-done | bytes 4194320 | tf_op jit(solution)/shard_map/all_gather | solution.py:57
  150.1 3.1 fusion.17
  153.2 0.0 copy-done
  153.2 0.0 copy-done.3
  153.2 4.1 %convolution_convert_fusion = bf16[512,128]{1,0:T(8,128)(2,1)} fusion(bf16[4096,128]{1,0:T(8,128)(2,1)S(1)} %copy-done, bf16[512,4096]{1,0:T(8,128)(2,1)} %all-gather.8.cloned.1.call-done, f32[4096]{0:T(1024)S(1)} %copy-done.3, f32[512]{0:T(512)S(1)} %add_rsqrt_fusion), kind=kOutput, calls=%fused_computation.29 | convolution fusion | flops 545325056 | bytes 5392384 | tf_op jit(solution)/shard_map/dot_general | solution.py:66
  157.3 0.0 all-gather.12.cloned.1.call-update
  157.3 0.0 all-gather.10.cloned.1.call-start
  157.4 1.0 multiply_cosine_fusion
  158.4 0.0 copy-done.2
  158.4 3.8 %convolution_bitcast_fusion.1 = f32[512,1,128]{0,2,1:T(8,128)S(1)} fusion(bf16[4096,128]{1,0:T(8,128)(2,1)S(1)} %copy-done.2, bf16[512,4096]{1,0:T(8,128)(2,1)} %all-gather.8.cloned.1.call-done, f32[4096]{0:T(1024)S(1)} %copy-done.3, f32[512]{0:T(512)S(1)} %add_rsqrt_fusion), kind=kOutput, calls=%fused_computation.28 | convolution fusion | flops 545259520 | bytes 5523456 | tf_op jit(solution)/shard_map/dot_general | solution.py:65
  162.2 0.6 fusion.28
  162.8 0.7 pad_maximum_fusion.1
  163.5 0.0 all-gather.10.cloned.1.call-update
  163.5 8.4 %convolution_bitcast_fusion = f32[64,8,8,128]{3,1,2,0:T(8,128)S(1)} fusion(bf16[4096,1024]{1,0:T(8,128)(2,1)} %param.15, bf16[512,4096]{1,0:T(8,128)(2,1)} %all-gather.8.cloned.1.call-done, f32[4096]{0:T(1024)S(1)} %copy-done.3, f32[512]{0:T(512)S(1)} %add_rsqrt_fusion), kind=kOutput, calls=%fused_computation.27 | convolution fusion | flops 4303355904 | bytes 14698496 | tf_op jit(solution)/shard_map/dot_general | solution.py:64
  171.9 0.5 copy.27
  172.4 0.7 fusion.37
  173.1 0.8 fusion.20
  173.9 1.5 pad_maximum_fusion
  175.4 19.5 %all-gather.12.cloned.1.call-done = bf16[4096,128]{1,0:T(8,128)(2,1)} async-done(((bf16[512,128]{1,0:T(8,128)(2,1)}), bf16[4096,128]{1,0:T(8,128)(2,1)}) %all-gather.12.cloned.1.call-update) | async-done | bytes 1048592 | tf_op jit(solution)/shard_map/all_gather | solution.py:80
  195.0 38.7 %all-gather.10.cloned.1.call-done = bf16[4096,1,128]{0,2,1:T(8,128)(2,1)} async-done(((bf16[512,1,128]{0,2,1:T(8,128)(2,1)}), bf16[4096,1,128]{0,2,1:T(8,128)(2,1)}) %all-gather.10.cloned.1.call-update) | async-done | bytes 1048592 | tf_op jit(solution)/shard_map/all_gather | solution.py:79
  233.6 77.6 %conditional.1 = (f32[1,8,512]{2,1,0:T(8,128)S(1)}, f32[1,8,512,128]{3,2,1,0:T(8,128)}) conditional(s32[]{:T(128)} %convert_element_type.52, () %tuple.13, (s32[512]{0:T(512)S(1)}, bf16[4096,1,128]{0,2,1:T(8,128)(2,1)}, bf16[512,1,8,128]{3,0,2,1:T(8,128)(2,1)}, bf16[4096,1,128]{2,0,1:T(8,128)(2,1)}) %tuple.36), branch_computations={%region_5.6_spmd, %region_6.9_spmd} | conditional | flops 8810131456 | bytes 215058448 | solution.py:108
  233.6 1.7 iota_compare_fusion
  235.4 26.6 %fusion = (f32[8,512]{1,0:T(8,128)S(1)}, f32[4096,512,8]{1,0,2:T(8,128)}) fusion(pred[512,4096]{0,1:T(8,128)(4,1)S(1)} %iota_compare_fusion, bf16[512,1,8,128]{3,0,2,1:T(8,128)(2,1)} %get-tuple-element.15, bf16[4096,1,128]{0,2,1:T(8,128)(2,1)} %get-tuple-element.30), kind=kOutput, calls=%fused_computation.3 | convolution fusion | flops 4345294848 | bytes 71319552 | tf_op jit(solution)/shard_map/cond/branch_1_fun/tagd,sad->agts/dot_general | solution.py:88
  262.0 21.7 %fusion.2 = f32[8,512]{1,0:T(8,128)S(1)} fusion(f32[4096,512,8]{1,0,2:T(8,128)} %get-tuple-element.38, f32[8,512]{1,0:T(8,128)S(1)} %broadcast_maximum_fusion, pred[512,4096]{0,1:T(8,128)(4,1)S(1)} %iota_compare_fusion), kind=kLoop, calls=%fused_computation.5 | loop fusion | flops 83881984 | bytes 69238784 | tf_op jit(solution)/shard_map/cond/branch_1_fun/reduce_sum | solution.py:96
  283.7 27.6 %fusion.7 = f32[1,8,512,128]{3,2,1,0:T(8,128)} fusion(f32[4096,512,8]{1,0,2:T(8,128)} %get-tuple-element.38, f32[8,512]{1,0:T(8,128)S(1)} %broadcast_maximum_fusion, pred[512,4096]{0,1:T(8,128)(4,1)S(1)} %iota_compare_fusion, bf16[4096,1,128]{2,0,1:T(8,128)(2,1)} %get-tuple-element.16), kind=kOutput, calls=%fused_computation.10 | convolution fusion | flops 4378853376 | bytes 72368128 | tf_op jit(solution)/shard_map/cond/branch_1_fun/agts,sad->agtd/dot_general | solution.py:97
  311.3 2.0 fusion.22
  313.2 0.7 copy.23
  313.9 1.2 copy.42
  (7 shorter events, 0.0 us)
Async XLA Ops:
  6.5 146.6 %copy-start = (bf16[4096,128]{1,0:T(8,128)(2,1)S(1)}, bf16[4096,128]{1,0:T(8,128)(2,1)}, u32[]{:S(2)}) copy-start(bf16[4096,128]{1,0:T(8,128)(2,1)} %param.17) | copy-start | bytes 3145732
  6.5 93.4 %copy-start.1 = (bf16[512,1024]{1,0:T(8,128)(2,1)S(1)}, bf16[512,1024]{1,0:T(8,128)(2,1)}, u32[]{:S(2)}) copy-start(bf16[512,1024]{1,0:T(8,128)(2,1)} %param.10) | copy-start | bytes 3145732
  6.5 86.2 %all-gather.6.cloned.1.call-start = ((), (), s32[]{:S(2)}) async-start(), calls=%async_computation | async-start | bytes 8519680 | tf_op jit(solution)/shard_map/all_gather | solution.py:53
  7.3 142.8 %all-gather.8.cloned.1.call-start = ((), (), s32[]{:S(2)}) async-start(), calls=%async_computation.1 | async-start | bytes 5242880 | tf_op jit(solution)/shard_map/all_gather | solution.py:57
  12.9 140.3 %copy-start.3 = (f32[4096]{0:T(1024)S(1)}, f32[4096]{0:T(1024)}, u32[]{:S(2)}) copy-start(f32[4096]{0:T(1024)} %param.14) | copy-start | bytes 49156
  101.1 57.3 %copy-start.2 = (bf16[4096,128]{1,0:T(8,128)(2,1)S(1)}, bf16[4096,128]{1,0:T(8,128)(2,1)}, u32[]{:S(2)}) copy-start(bf16[4096,128]{1,0:T(8,128)(2,1)} %param.16) | copy-start | bytes 3145732
  101.2 93.8 %all-gather.12.cloned.1.call-start = ((), (), s32[]{:S(2)}) async-start(), calls=%async_computation.3 | async-start | bytes 1179648 | tf_op jit(solution)/shard_map/all_gather | solution.py:80
  157.3 76.3 %all-gather.10.cloned.1.call-start = ((), (), s32[]{:S(2)}) async-start(), calls=%async_computation.2 | async-start | bytes 1179648 | tf_op jit(solution)/shard_map/all_gather | solution.py:79
Sparse Core Ops, SparseCore 0:
  10.1 82.5 all-gather.5
  101.3 48.7 all-gather.7
  157.5 37.4 all-gather.11
  196.6 36.9 all-gather.9
where the time goes:
time: 326 us; the launch traced here: 322 us
  waiting for transfers between devices  188 us (58%)
  matrix products  70.6 us (22%)
  other arithmetic  37.9 us (12%)
  between operations  13.3 us (4%)
  local copies, waits for them, and re-layouts  12.1 us (4%)
    all_gather x1, waiting for transfers between devices, on_device(): received = lax.all_gather(visual_rows, ('dp', 'ctx'), axis=0, tiled=True)  79.8 us
    all_gather x1, waiting for transfers between devices, on_device(): whole = lax.all_gather(context, 'mp', axis=1, tiled=True)  48.9 us
    all_gather x1, waiting for transfers between devices, on_device(): lax.all_gather(keys_now, 'ctx', axis=0, tiled=True)  38.7 us
    dot_general x1, matrix products, update(): jnp.einsum('agts,sad->agtd', weights.astype(jnp.bfloat16), values_block,...  27.6 us
    dot_general x1, matrix products, update(): jnp.einsum('tagd,sad->agts', grouped, keys_block, preferred_element_type=...  26.6 us
    reduce_sum x1, other arithmetic, update(): new_total = jnp.sum(weights, axis=3)  21.7 us
    all_gather x1, waiting for transfers between devices, on_device(): lax.all_gather(values_now, 'ctx', axis=0, tiled=True)  19.5 us
    dot_general x1, matrix products, on_device(): query_lin = jnp.dot(normed, w_query, preferred_element_type=jnp.float32)  8.43 us
  transfers between devices with their start and end apart: 4, of which 4 were waited for; matrix products, arithmetic and copies ran while one was open for 7% of the time, Pallas kernels for 0%

commit v1 on v0

v1 whole, which is shorter than its diff:
```python
import functools
import math

import jax
import jax.numpy as jnp
from jax import lax
from jax.experimental import pallas as pl
from jax.experimental.pallas import tpu as pltpu
from jax.sharding import PartitionSpec as P

HD = 128
IMG_TOK = 64
MAX_IMG = 8
D = 4096
SHARDS = 8
rope_base = 500000.0
eps = 1e-05
BF16 = jnp.bfloat16
F32 = jnp.float32
VMEM = pltpu.VMEM
SMEM = pltpu.SMEM


def rotary_tables(positions):
    half_size = HD // 2
    exponent = jnp.arange(half_size, dtype=F32) * (2.0 / HD)
    frequency = jnp.exp(-exponent * math.log(rope_base))
    angles = positions.astype(F32)[:, None] * frequency[None, :]
    cosine, sine = jnp.cos(angles), jnp.sin(angles)
    return jnp.concatenate([cosine, cosine], axis=1), jnp.concatenate([-sine, sine], axis=1)


def rotate(u, cosine, sine):
    return u * cosine + pltpu.roll(u, HD // 2, 1) * sine


def exchange(x, mask):
    return lax.ppermute(x, "mp", [(i, i ^ mask) for i in range(4)])


def first_hop(x):
    return exchange(x, 1), exchange(x, 3)


def second_hop(a, b):
    half = a.shape[0] // 2
    return exchange(a[:half], 3), exchange(b[half:], 1)


def key_value_kernel(row_counts, mp_ref, *refs):
    groups = len(row_counts)
    gain_ref, w_ref, cos_ref, sin_ref = refs[5 * groups : 5 * groups + 4]
    normed_ref, kv_ref = refs[5 * groups + 4 :]
    mp = mp_ref[0]
    base = 0
    for g, rows in enumerate(row_counts):
        own, one, three, two_lo, two_hi = refs[5 * g : 5 * g + 5]
        half = rows // 2
        for part, two in ((0, two_lo), (1, two_hi)):
            span = pl.ds(part * half, half)
            pieces = [(0, own[span, :]), (1, one[span, :]), (3, three[span, :]), (2, two[...])]
            total = jnp.zeros((half, 1), F32)
            for _, piece in pieces:
                wide = piece.astype(F32)
                total = total + jnp.sum(wide * wide, axis=1, keepdims=True)
            scale = lax.rsqrt(total * (1.0 / D) + eps)
            for mask, piece in pieces:
                columns = pl.ds(pl.multiple_of((mp ^ mask) * 1024, 1024), 1024)
                value = piece.astype(F32) * scale * gain_ref[:, columns]
                normed_ref[pl.ds(base + part * half, half), columns] = value.astype(BF16)
        base += rows
    product = jnp.dot(normed_ref[...], w_ref[...], preferred_element_type=F32)
    kv_ref[:, :HD] = rotate(product[:, :HD], cos_ref[...], sin_ref[...]).astype(BF16)
    kv_ref[:, HD:] = product[:, HD:].astype(BF16)


def key_value(mp, groups, gain, w_kv, cosine, sine):
    row_counts = tuple(g[0].shape[0] for g in groups)
    rows = sum(row_counts)
    arrays = [a for g in groups for a in g]
    return pl.pallas_call(
        functools.partial(key_value_kernel, row_counts),
        out_shape=(
            jax.ShapeDtypeStruct((rows, D), BF16),
            jax.ShapeDtypeStruct((rows, 2 * HD), BF16),
        ),
        in_specs=[pl.BlockSpec(memory_space=SMEM)]
        + [pl.BlockSpec(memory_space=VMEM)] * (len(arrays) + 4),
        out_specs=[pl.BlockSpec(memory_space=VMEM)] * 2,
        compiler_params=pltpu.CompilerParams(vmem_limit_bytes=40 * 2**20),
        cost_estimate=pl.CostEstimate(
            flops=2 * rows * D * 2 * HD, bytes_accessed=rows * D * 4 + D * 512, transcendentals=0
        ),
        name="key_value",
    )(mp, *arrays, gain, w_kv, cosine, sine)


def query_kernel(x_ref, w_ref, cos_ref, sin_ref, q_ref):
    product = jnp.dot(x_ref[...], w_ref[...], preferred_element_type=F32)
    for h in range(2):
        span = slice(h * HD, (h + 1) * HD)
        q_ref[:, span] = rotate(product[:, span], cos_ref[...], sin_ref[...]).astype(BF16)


def query(normed, w_query, cosine, sine):
    rows, columns = normed.shape[0], w_query.shape[1]
    tile = 2 * HD
    return pl.pallas_call(
        query_kernel,
        out_shape=jax.ShapeDtypeStruct((rows, columns), BF16),
        grid=(columns // tile,),
        in_specs=[
            pl.BlockSpec((rows, D), lambda n: (0, 0)),
            pl.BlockSpec((D, tile), lambda n: (0, n)),
            pl.BlockSpec((rows, HD), lambda n: (0, 0)),
            pl.BlockSpec((rows, HD), lambda n: (0, 0)),
        ],
        out_specs=pl.BlockSpec((rows, tile), lambda n: (0, n)),
        compiler_params=pltpu.CompilerParams(vmem_limit_bytes=40 * 2**20),
        cost_estimate=pl.CostEstimate(
            flops=2 * rows * D * columns, bytes_accessed=D * columns * 2 + rows * D * 2, transcendentals=0
        ),
        name="query",
    )(normed, w_query, cosine, sine)


def attention_kernel(
    tok, heads, info_ref, *refs
):
    q_refs = refs[:2]
    own_refs = refs[2:4]
    far_refs = refs[4 : 4 + SHARDS - 1]
    img_ref = refs[4 + SHARDS - 1]
    out_ref = refs[5 + SHARDS - 1]
    q_buf, kt_buf, v_buf, s_buf, max_buf, sum_buf, acc_buf = refs[6 + SHARDS - 1 :]
    step = pl.program_id(0)
    ctx = info_ref[0]
    factor = math.log2(math.e) / math.sqrt(HD)
    half = tok // 2

    @pl.when(step == 0)
    def _():
        for part in range(2):
            q_buf[pl.ds(part * half, half), :] = q_refs[part][...]
            rows = pl.ds(pl.multiple_of(ctx * tok + part * half, half), half)
            v_buf[rows, :] = own_refs[part][...]
        for d in range(1, SHARDS):
            @pl.when(ctx >= d)
            def _():
                rows = pl.ds(pl.multiple_of((ctx - d) * tok, tok), tok)
                v_buf[rows, :] = far_refs[d - 1][...]
        for c in range(MAX_IMG):
            start = info_ref[1 + c]

            @pl.when(start >= 0)
            def _():
                v_buf[pl.ds(pl.multiple_of(start, IMG_TOK), IMG_TOK), :] = img_ref[c, :, heads * HD :]

            @pl.when((start >= ctx * tok) & (start < ctx * tok + tok))
            def _():
                rows = pl.ds(pl.multiple_of(start - ctx * tok, IMG_TOK), IMG_TOK)
                q_buf[rows, :] = img_ref[c, :, : heads * HD]

        @pl.loop(0, ctx + 1)
        def _(j):
            rows = pl.ds(pl.multiple_of(j * tok, tok), tok)
            kt_buf[j] = v_buf[rows, :HD].astype(F32).T.astype(BF16)

    def score(j, slot, q_head, masked):
        s = jnp.dot(q_head, kt_buf[j], preferred_element_type=F32)
        if masked:
            row = lax.broadcasted_iota(jnp.int32, (tok, tok), 0)
            column = lax.broadcasted_iota(jnp.int32, (tok, tok), 1)
            s = jnp.where(column <= row, s, -1e30)
        s_buf[slot, j] = s
        top = s[:, :HD]
        for g in range(1, tok // HD):
            top = jnp.maximum(top, s[:, g * HD : (g + 1) * HD])
        return top

    def mix(j, slot):
        top = max_buf[slot]
        weights = []
        total = None
        for g in range(tok // HD):
            w = jnp.exp2(s_buf[slot, j, :, g * HD : (g + 1) * HD] * factor - top)
            total = w if total is None else total + w
            weights.append(w.astype(BF16))
        rows = pl.ds(pl.multiple_of(j * tok, tok), tok)
        acc = jnp.dot(
            jnp.concatenate(weights, axis=1), v_buf[rows, HD:], preferred_element_type=F32
        )
        return total, acc

    def phase(do_score, do_mix):
        slot = lax.rem(step, 2)
        other = 1 - slot
        if do_score:
            columns = pl.ds(pl.multiple_of(step * HD, HD), HD)
            q_head = q_buf[:, columns]
            top = score(ctx, slot, q_head, True)
            max_buf[slot] = top
        if do_mix:
            total, acc = mix(ctx, other)
            sum_buf[...] = total
            acc_buf[...] = acc

        @pl.loop(0, ctx)
        def _(j):
            if do_score:
                max_buf[slot] = jnp.maximum(max_buf[slot], score(j, slot, q_head, False))
            if do_mix:
                total, acc = mix(j, other)
                sum_buf[...] += total
                acc_buf[...] += acc

        if do_score:
            top = jnp.max(max_buf[slot], axis=1, keepdims=True) * factor
            max_buf[slot] = jnp.broadcast_to(top, (tok, HD))
        if do_mix:
            total = jnp.sum(sum_buf[...], axis=1, keepdims=True)
            out_ref[...] = (acc_buf[...] / total).astype(BF16)

    pl.when(step == 0)(lambda: phase(True, False))
    pl.when((step > 0) & (step < heads))(lambda: phase(True, True))
    pl.when(step == heads)(lambda: phase(False, True))


def attention(info, q_parts, own_parts, far_parts, img_all, tok, heads):
    whole = pl.BlockSpec(memory_space=VMEM)
    count = len(q_parts) + len(own_parts) + len(far_parts) + 1
    return pl.pallas_call(
        functools.partial(attention_kernel, tok, heads),
        out_shape=jax.ShapeDtypeStruct((tok, heads * HD), BF16),
        grid=(heads + 1,),
        in_specs=[pl.BlockSpec(memory_space=SMEM)] + [whole] * count,
        out_specs=pl.BlockSpec((tok, HD), lambda t: (0, jnp.maximum(t - 1, 0))),
        scratch_shapes=[
            pltpu.VMEM((tok, heads * HD), BF16),
            pltpu.VMEM((SHARDS, HD, tok), BF16),
            pltpu.VMEM((SHARDS * tok, 2 * HD), BF16),
            pltpu.VMEM((2, SHARDS, tok, tok), F32),
            pltpu.VMEM((2, tok, HD), F32),
            pltpu.VMEM((tok, HD), F32),
            pltpu.VMEM((tok, HD), F32),
        ],
        compiler_params=pltpu.CompilerParams(vmem_limit_bytes=52 * 2**20),
        cost_estimate=pl.CostEstimate(
            flops=4 * tok * heads * SHARDS * tok * HD,
            bytes_accessed=8 * 2**20,
            transcendentals=tok * heads * SHARDS * tok,
        ),
        name="attention",
    )(info, *q_parts, *own_parts, *far_parts, img_all)


def on_device(
    text_rows, visual_rows, image_counts, image_starts, norm_gain, w_query, w_key, w_value
):
    ctx = lax.axis_index("ctx")
    sample = lax.axis_index("dp")
    mp = lax.axis_index("mp")
    tok = text_rows.shape[0]
    half = tok // 2
    heads = w_query.shape[1] // HD

    before = jnp.sum(jnp.where(jnp.arange(SHARDS) < sample, image_counts, 0))
    count = lax.dynamic_index_in_dim(image_counts, sample, 0, keepdims=False)
    starts = lax.dynamic_index_in_dim(image_starts, sample, 0, keepdims=False)
    residue = jnp.arange(SHARDS, dtype=jnp.int32)
    slot = (residue - before) & (MAX_IMG - 1)
    start_of = jnp.where(slot < count, jnp.take(starts, slot), -1)
    my_slot = (ctx - before) & (MAX_IMG - 1)
    source = jnp.minimum((before + my_slot) // SHARDS, SHARDS - 1)
    my_start = lax.dynamic_index_in_dim(start_of, ctx, 0, keepdims=False)

    gathered = lax.all_gather(visual_rows, "dp", axis=0)
    low, high = text_rows[:half], text_rows[half:]
    a_low, b_low = first_hop(low)
    a_high, b_high = first_hop(high)
    c_low, d_low = second_hop(a_low, b_low)
    c_high, d_high = second_hop(a_high, b_high)
    image = lax.dynamic_index_in_dim(gathered, source, 0, keepdims=False)
    a_img, b_img = first_hop(image)
    c_img, d_img = second_hop(a_img, b_img)

    w_kv = jnp.concatenate([w_key, w_value], axis=1)
    gain = norm_gain[None, :]
    cos_text, sin_text = rotary_tables(ctx * tok + jnp.arange(tok, dtype=jnp.int32))
    cos_img, sin_img = rotary_tables(my_start + jnp.arange(IMG_TOK, dtype=jnp.int32))
    mp_arr = mp.astype(jnp.int32)[None]

    def project(groups, cosine, sine):
        normed, kv = key_value(mp_arr, groups, gain, w_kv, cosine, sine)
        return query(normed, w_query, cosine, sine), kv

    q_low, kv_low = project([(low, a_low, b_low, c_low, d_low)], cos_text[:half], sin_text[:half])
    q_high, kv_high = project(
        [(high, a_high, b_high, c_high, d_high)], cos_text[half:], sin_text[half:]
    )
    q_img, kv_img = project([(image, a_img, b_img, c_img, d_img)], cos_img, sin_img)

    kv = jnp.concatenate([kv_low, kv_high], axis=0)
    far = [
        lax.ppermute(kv, "ctx", [(i, i + d) for i in range(SHARDS) if i + d < SHARDS])
        for d in range(1, SHARDS)
    ]
    img_all = lax.all_gather(jnp.concatenate([q_img, kv_img], axis=1), "ctx", axis=0)
    info = jnp.concatenate([ctx.astype(jnp.int32)[None], start_of.astype(jnp.int32)])
    return attention(info, [q_low, q_high], [kv_low, kv_high], far, img_all, tok, heads)


def solution(mesh):
    in_specs = (
        P(("dp", "ctx"), "mp"),
        P(("dp", "ctx"), "mp"),
        P(),
        P(),
        P(),
        P(None, "mp"),
        P(None, "mp"),
        P(None, "mp"),
    )
    out_specs = P(("dp", "ctx"), "mp")
    return jax.shard_map(
        on_device, mesh=mesh, in_specs=in_specs, out_specs=out_specs, check_vma=False
    )
```

time: 326 us -> 211 us (0.65); the launches traced: 322 us -> 210 us
  waiting for transfers between devices: 188 us -> 74.4 us
  matrix products: 70.6 us -> 0 us
  Pallas kernels: 0 us -> 63.7 us
  other arithmetic: 37.9 us -> 6.06 us
  starting transfers between devices: 0.13 us -> 24.1 us
  local copies, waits for them, and re-layouts: 12.1 us -> 26.9 us
    all_gather x4 -> x2, waiting for transfers between devices: 187 us -> 19 us  [the longest x1 19 us: on_device(): gathered = lax.all_gather(visual_rows, 'dp', axis=0)]
    dot_general x5 -> x0, matrix products: 70.6 us -> none  [the longest x1 27.6 us: update(): jnp.einsum('agts,sad->agtd', weights.astype(jnp.bfloat16), values_block,...]
    pallas_call x0 -> x7, Pallas kernels: none -> 63.7 us  [the longest x1 44.4 us: attention(): pl.pallas_call(functools.partial(attention_kernel, tok, heads), out_shape...]
    ppermute x0 -> x19, waiting for transfers between devices: none -> 54.7 us  [the longest x7 29.2 us: on_device(): lax.ppermute(kv, 'ctx', [(i, i + d) for i in range(SHARDS) if i + d < SHA...]
    ppermute x0 -> x19, starting transfers between devices: none -> 24.1 us  [the longest x12 15.1 us: exchange(): return lax.ppermute(x, 'mp', [(i, i ^ mask) for i in range(4)])]
    reduce_sum x3 -> x1, other arithmetic: 24.9 us -> 1.29 us  [on_device(): before = jnp.sum(jnp.where(jnp.arange(SHARDS) < sample, image_counts, 0))]
    unnamed x10 -> x42, local copies, waits for them, and re-layouts: 1.73 us -> 18.1 us
    gather x1, local copies, waits for them, and re-layouts: 7.19 us -> 0.64 us  [on_device(): start_of = jnp.where(slot < count, jnp.take(starts, slot), -1)]
  transfers between devices with their start and end apart: 4 -> 21, of which waited for: 4 -> 10; matrix products, arithmetic and copies ran while one was open for 7% -> 7% of each run, Pallas kernels for 0% -> 7%
where the time goes in v1:
time: 211 us; the launch traced here: 210 us
  waiting for transfers between devices  74.4 us (35%)
  Pallas kernels  63.7 us (30%)
  local copies, waits for them, and re-layouts  26.9 us (13%)
  starting transfers between devices  24.1 us (11%)
  between operations  15.1 us (7%)
  other arithmetic  6.06 us (3%)
    pallas_call x1, Pallas kernels, attention(): pl.pallas_call(functools.partial(attention_kernel, tok, heads), out_shape...  44.4 us
    ppermute x7, waiting for transfers between devices, on_device(): lax.ppermute(kv, 'ctx', [(i, i + d) for i in range(SHARDS) if i + d < SHA...  29.2 us
    ppermute x12, waiting for transfers between devices, exchange(): return lax.ppermute(x, 'mp', [(i, i ^ mask) for i in range(4)])  25.5 us
    all_gather x1, waiting for transfers between devices, on_device(): gathered = lax.all_gather(visual_rows, 'dp', axis=0)  19 us
    unnamed x42, local copies, waits for them, and re-layouts  18.1 us
    ppermute x12, starting transfers between devices, exchange(): return lax.ppermute(x, 'mp', [(i, i ^ mask) for i in range(4)])  15.1 us
    pallas_call x3, Pallas kernels, query(): pl.pallas_call(query_kernel, out_shape=jax.ShapeDtypeStruct((rows, column...  12.2 us
    ppermute x7, starting transfers between devices, on_device(): lax.ppermute(kv, 'ctx', [(i, i + d) for i in range(SHARDS) if i + d < SHA...  9.01 us
  transfers between devices with their start and end apart: 21, of which 10 were waited for; matrix products, arithmetic and copies ran while one was open for 7% of the time, Pallas kernels for 7%

profile of v1, /device:TPU:224, one launch (start us, length us, event | category | flops | bytes accessed | tf_op | source)
XLA Modules:
  0.0 210.3 jit_solution(4461645081300633533)
XLA Ops:
  6.5 0.7 all-gather.5.cloned.1.call-update
  7.3 1.3 fusion.4
  9.9 1.2 dynamic_slice.15
  11.1 0.7 fusion.5
  11.8 0.6 gather_fusion
  12.5 1.2 compare_select_fusion.2
  13.7 0.6 dynamic_slice.18
  14.3 0.7 add_convert_fusion.1
  15.0 1.4 constant_dynamic-update-slice_fusion.1
  16.6 19.0 %all-gather.5.cloned.1.call-done = bf16[512,1024]{1,0:T(8,128)(2,1)} async-done(((bf16[64,1024]{1,0:T(8,128)(2,1)}), bf16[512,1024]{1,0:T(8,128)(2,1)}) %all-gather.5.cloned.1.call-update) | async-done | bytes 1048592 | tf_op jit(solution)/shard_map/all_gather | solution.py:277
  35.6 0.9 dynamic-slice_bitcast_fusion.refs_0_
  36.5 1.6 collective-permute-start.15
  38.1 2.1 collective-permute-start.16
  40.4 1.9 collective-permute-done.15.refs_1_
  42.3 2.7 %collective-permute-start.17 = (bf16[32,1024]{1,0:T(8,128)(2,1)S(1)}, bf16[32,1024]{1,0:T(8,128)(2,1)S(1)}, u32[]{:S(2)}, u32[]{:S(2)}) collective-permute-start(bf16[32,1024]{1,0:T(8,128)(2,1)S(1)} %slice.58), channel_id=1, source_target_pairs={{0,3},{1,2},{2,1},{3,0},{4,7},{5,6},{6,5},{7,4},{8,11},{9,10},{10,... | collective-permute-start | bytes 196616 | tf_op jit(solution)/shard_map/ppermute | solution.py:38
  45.0 0.3 collective-permute-start.18
  45.4 2.4 %collective-permute-done.17.refs_3_ = bf16[32,1024]{1,0:T(8,128)(2,1)S(1)} collective-permute-done((bf16[32,1024]{1,0:T(8,128)(2,1)S(1)}, bf16[32,1024]{1,0:T(8,128)(2,1)S(1)}, u32[]{:S(2)}, u32[]{:S(2)}) %collective-permute-start.17) | collective-permute-done | bytes 65568 | tf_op jit(solution)/shard_map/ppermute | solution.py:38
  47.8 1.6 collective-permute-done.18.refs_4_
  49.3 0.8 key_value.5
  50.2 3.4 %copy-done.1 = bf16[4096,1024]{1,0:T(8,128)(2,1)S(1)} copy-done((bf16[4096,1024]{1,0:T(8,128)(2,1)S(1)}, bf16[4096,1024]{1,0:T(8,128)(2,1)}, u32[]{:S(2)}) %copy-start.1) | copy-done | bytes 8388632
  53.5 3.4 %query.5 = bf16[64,1024]{1,0:T(8,128)(2,1)S(1)} custom-call(bf16[64,4096]{1,0:T(8,128)(2,1)S(1)} %get-tuple-element.15.x_ref, bf16[4096,1024]{1,0:T(8,128)(2,1)S(1)} %copy-done.1, f32[64,128]{1,0:T(8,128)S(1)} %get-tuple-element.31.refs_7_.cos_ref, f32[64,128]{1,0:T(8,128)S(1)} %get-tuple-element.32.refs_8_.sin_ref), custom_call_target="tpu_custom_call" | custom-call | flops 536870912 | bytes 8912896 | tf_op jit(solution)/shard_map/query/pallas_call | solution.py:108
  57.0 0.7 pad_maximum_fusion
  57.7 1.3 fusion.6
  59.0 0.3 collective-permute-start
  59.3 1.5 collective-permute-start.1
  60.9 1.3 collective-permute-start.4
  62.2 1.5 collective-permute-start.5
  63.7 10.3 %collective-permute-done.refs_1_ = bf16[256,1024]{1,0:T(8,128)(2,1)} collective-permute-done((bf16[256,1024]{1,0:T(8,128)(2,1)S(1)}, bf16[256,1024]{1,0:T(8,128)(2,1)}, u32[]{:S(2)}, u32[]{:S(2)}) %collective-permute-start) | collective-permute-done | bytes 524320 | tf_op jit(solution)/shard_map/ppermute | solution.py:38
  74.0 1.0 slice.50
  75.0 1.8 collective-permute-start.2
  76.8 1.0 slice.51
  77.9 7.4 %collective-permute-done.4.refs_1_ = bf16[256,1024]{1,0:T(8,128)(2,1)} collective-permute-done((bf16[256,1024]{1,0:T(8,128)(2,1)S(1)}, bf16[256,1024]{1,0:T(8,128)(2,1)}, u32[]{:S(2)}, u32[]{:S(2)}) %collective-permute-start.4) | collective-permute-done | bytes 524320 | tf_op jit(solution)/shard_map/ppermute | solution.py:38
  85.3 1.0 slice.56
  86.2 1.5 collective-permute-start.6
  87.8 1.0 slice.57
  89.0 1.0 multiply_sine_fusion
  90.2 2.0 collective-permute-done.2.refs_3_
  92.2 3.1 %key_value.3 = (bf16[256,4096]{1,0:T(8,128)(2,1)S(1)}, bf16[256,256]{1,0:T(8,128)(2,1)S(1)}) custom-call(s32[1]{0:T(128)} %bitcast.4.mp_ref, bf16[256,1024]{1,0:T(8,128)(2,1)S(1)} %get-tuple-element.18.refs_0_, bf16[256,1024]{1,0:T(8,128)(2,1)} %collective-permute-done.refs_1_, bf16[256,1024]{1,0:T(8,128)(2,1)} %collective-permute-done.1.refs_2_, ...), custom_call_target="tpu_custom_call" | custom-call | flops 536870912 | bytes 6291456 | tf_op jit(solution)/shard_map/key_value/pallas_call | solution.py:81
  95.3 1.3 copy-done.3
  96.7 3.1 %key_value.4 = (bf16[256,4096]{1,0:T(8,128)(2,1)S(1)}, bf16[256,256]{1,0:T(8,128)(2,1)S(1)}) custom-call(s32[1]{0:T(128)} %bitcast.4.mp_ref, bf16[256,1024]{1,0:T(8,128)(2,1)S(1)} %get-tuple-element.17.refs_0_, bf16[256,1024]{1,0:T(8,128)(2,1)} %collective-permute-done.4.refs_1_, bf16[256,1024]{1,0:T(8,128)(2,1)} %collective-permute-done.5.refs_2_, ...), custom_call_target="tpu_custom_call" | custom-call | flops 536870912 | bytes 6291456 | tf_op jit(solution)/shard_map/key_value/pallas_call | solution.py:81
  99.8 1.3 copy-done.5
  101.2 1.3 collective-permute-start.8
  102.5 1.3 collective-permute-start.9
  103.9 1.3 collective-permute-start.10
  105.2 1.3 collective-permute-start.11
  106.5 1.3 collective-permute-start.12
  107.8 2.8 %collective-permute-done.8.refs_4_ = bf16[512,256]{1,0:T(8,128)(2,1)S(1)} collective-permute-done((bf16[512,256]{1,0:T(8,128)(2,1)S(1)}, bf16[512,256]{1,0:T(8,128)(2,1)S(1)}, u32[]{:S(2)}, u32[]{:S(2)}) %collective-permute-start.8) | collective-permute-done | bytes 262176 | tf_op jit(solution)/shard_map/ppermute | solution.py:305
  110.5 1.3 collective-permute-start.13
  111.8 11.0 %collective-permute-done.9.refs_5_ = bf16[512,256]{1,0:T(8,128)(2,1)S(1)} collective-permute-done((bf16[512,256]{1,0:T(8,128)(2,1)S(1)}, bf16[512,256]{1,0:T(8,128)(2,1)S(1)}, u32[]{:S(2)}, u32[]{:S(2)}) %collective-permute-start.9) | collective-permute-done | bytes 262176 | tf_op jit(solution)/shard_map/ppermute | solution.py:305
  122.8 1.3 collective-permute-start.14
  124.1 3.4 %copy-done.2 = bf16[4096,1024]{1,0:T(8,128)(2,1)S(1)} copy-done((bf16[4096,1024]{1,0:T(8,128)(2,1)S(1)}, bf16[4096,1024]{1,0:T(8,128)(2,1)}, u32[]{:S(2)}) %copy-start.2) | copy-done | bytes 8388632
  127.5 4.4 %query.3.refs_0_ = bf16[256,1024]{1,0:T(8,128)(2,1)S(1)} custom-call(bf16[256,4096]{1,0:T(8,128)(2,1)S(1)} %copy-done.4, bf16[4096,1024]{1,0:T(8,128)(2,1)S(1)} %copy-done.2, f32[256,128]{1,0:T(8,128)S(1)} %get-tuple-element.29.refs_7_.cos_ref, f32[256,128]{1,0:T(8,128)S(1)} %get-tuple-element.20.refs_8_.sin_ref), custom_call_target="tpu_custom_call" | custom-call | flops 2147483648 | bytes 10485760 | tf_op jit(solution)/shard_map/query/pallas_call | solution.py:108
  131.9 0.8 copy-done.7
  132.7 4.4 %query.4.refs_1_ = bf16[256,1024]{1,0:T(8,128)(2,1)S(1)} custom-call(bf16[256,4096]{1,0:T(8,128)(2,1)S(1)} %copy-done.6, bf16[4096,1024]{1,0:T(8,128)(2,1)S(1)} %bitcast.14, f32[256,128]{1,0:T(8,128)S(1)} %get-tuple-element.30.refs_7_.cos_ref, f32[256,128]{1,0:T(8,128)S(1)} %get-tuple-element.19.refs_8_.sin_ref), custom_call_target="tpu_custom_call" | custom-call | flops 2147483648 | bytes 10485760 | tf_op jit(solution)/shard_map/query/pallas_call | solution.py:108
  137.1 0.8 copy-done.8
  137.9 0.7 copy-done.10
  138.7 0.7 copy-done.12
  139.4 0.7 copy-done.14
  140.1 15.5 %collective-permute-done.14.refs_10_ = bf16[512,256]{1,0:T(8,128)(2,1)S(1)} collective-permute-done((bf16[512,256]{1,0:T(8,128)(2,1)S(1)}, bf16[512,256]{1,0:T(8,128)(2,1)S(1)}, u32[]{:S(2)}, u32[]{:S(2)}) %collective-permute-start.14) | collective-permute-done | bytes 262176 | tf_op jit(solution)/shard_map/ppermute | solution.py:305
  155.5 0.7 copy-done.17
  156.2 0.9 copy-done.11
  157.2 0.9 copy-done.13
  158.1 0.9 copy-done.15
  159.1 44.4 %attention.1 = bf16[512,1024]{1,0:T(8,128)(2,1)} custom-call(s32[9]{0:T(128)S(1)} %pad_add_fusion.info_ref, bf16[256,1024]{1,0:T(8,128)(2,1)} %copy-done.7, bf16[256,1024]{1,0:T(8,128)(2,1)} %copy-done.8, bf16[256,256]{1,0:T(8,128)(2,1)S(1)} %get-tuple-element.13.refs_2_, bf16[256,256]{1,0:T(8,128)(2,1)S(1)} %get-tuple-element.14.refs_3_, ...), custom_call_target="tpu_custom_call" | custom-call | flops 8589934592 | bytes 8388608 | tf_op jit(solution)/shard_map/attention/pallas_call | solution.py:232
  (57 shorter events, 1.4 us)
Async XLA Ops:
  6.5 5.3 %copy-start = (s32[8,8]{1,0:T(8,128)S(1)}, s32[8,8]{1,0:T(8,128)}, u32[]{:S(2)}) copy-start(s32[8,8]{1,0:T(8,128)} %param.11) | copy-start | bytes 772
  6.5 9.8 %copy-start.16 = (bf16[4096,128]{1,0:T(8,128)(2,1)S(1)}, bf16[4096,128]{1,0:T(8,128)(2,1)}, u32[]{:S(2)}) copy-start(bf16[4096,128]{1,0:T(8,128)(2,1)} %param.15) | copy-start | bytes 3145732
  6.5 29.1 %all-gather.5.cloned.1.call-start = ((), (), s32[]{:S(2)}) async-start(), calls=%async_computation | async-start | bytes 1179648 | tf_op jit(solution)/shard_map/all_gather | solution.py:277
  7.3 148.3 %all-gather.7.cloned.1.call-start = ((), (), s32[]{:S(2)}) async-start(), calls=%async_computation.1 | async-start | bytes 1474560 | tf_op jit(solution)/shard_map/all_gather | solution.py:308
  15.0 34.4 %copy-start.9 = (f32[4096]{0:T(1024)S(1)}, f32[4096]{0:T(1024)}, u32[]{:S(2)}) copy-start(f32[4096]{0:T(1024)} %param.12) | copy-start | bytes 49156
  36.5 5.8 %collective-permute-start.15 = (bf16[64,1024]{1,0:T(8,128)(2,1)S(1)}, bf16[64,1024]{1,0:T(8,128)(2,1)S(1)}, u32[]{:S(2)}, u32[]{:S(2)}) collective-permute-start(bf16[64,1024]{1,0:T(8,128)(2,1)S(1)} %dynamic-slice_bitcast_fusion.refs_0_), channel_id=1, source_target_pairs={{0,1},{1,0},{2,3},{3,2},{4,5},{5,4},{6,7},{7,6},{8,9},{9,8},{10,11... | collective-permute-start | bytes 393224 | tf_op jit(solution)/shard_map/ppermute | solution.py:38
  38.1 6.9 %collective-permute-start.16 = (bf16[64,1024]{1,0:T(8,128)(2,1)S(1)}, bf16[64,1024]{1,0:T(8,128)(2,1)S(1)}, u32[]{:S(2)}, u32[]{:S(2)}) collective-permute-start(bf16[64,1024]{1,0:T(8,128)(2,1)S(1)} %dynamic-slice_bitcast_fusion.refs_0_), channel_id=1, source_target_pairs={{0,3},{1,2},{2,1},{3,0},{4,7},{5,6},{6,5},{7,4},{8,11},{9,10},{10,... | collective-permute-start | bytes 393224 | tf_op jit(solution)/shard_map/ppermute | solution.py:38
  42.3 5.5 %collective-permute-start.17 = (bf16[32,1024]{1,0:T(8,128)(2,1)S(1)}, bf16[32,1024]{1,0:T(8,128)(2,1)S(1)}, u32[]{:S(2)}, u32[]{:S(2)}) collective-permute-start(bf16[32,1024]{1,0:T(8,128)(2,1)S(1)} %slice.58), channel_id=1, source_target_pairs={{0,3},{1,2},{2,1},{3,0},{4,7},{5,6},{6,5},{7,4},{8,11},{9,10},{10,... | collective-permute-start | bytes 196616 | tf_op jit(solution)/shard_map/ppermute | solution.py:38
  45.0 4.4 %collective-permute-start.18 = (bf16[32,1024]{1,0:T(8,128)(2,1)S(1)}, bf16[32,1024]{1,0:T(8,128)(2,1)S(1)}, u32[]{:S(2)}, u32[]{:S(2)}) collective-permute-start(bf16[32,1024]{1,0:T(8,128)(2,1)S(1)} %slice.59), channel_id=1, source_target_pairs={{0,1},{1,0},{2,3},{3,2},{4,5},{5,4},{6,7},{7,6},{8,9},{9,8},{10,11... | collective-permute-start | bytes 196616 | tf_op jit(solution)/shard_map/ppermute | solution.py:38
  50.2 3.4 %copy-start.1 = (bf16[4096,1024]{1,0:T(8,128)(2,1)S(1)}, bf16[4096,1024]{1,0:T(8,128)(2,1)}, u32[]{:S(2)}) copy-start(bf16[4096,1024]{1,0:T(8,128)(2,1)} %w_ref.5) | copy-start | bytes 25165828
  59.0 15.1 %collective-permute-start = (bf16[256,1024]{1,0:T(8,128)(2,1)S(1)}, bf16[256,1024]{1,0:T(8,128)(2,1)}, u32[]{:S(2)}, u32[]{:S(2)}) collective-permute-start(bf16[256,1024]{1,0:T(8,128)(2,1)S(1)} %get-tuple-element.18.refs_0_), channel_id=1, source_target_pairs={{0,1},{1,0},{2,3},{3,2},{4,5},{5,4},{6,7},{7,6},{8,9},{9,8},{10,11... | collective-permute-start | bytes 1572872 | tf_op jit(solution)/shard_map/ppermute | solution.py:38
  59.3 17.5 %collective-permute-start.1 = (bf16[256,1024]{1,0:T(8,128)(2,1)S(1)}, bf16[256,1024]{1,0:T(8,128)(2,1)}, u32[]{:S(2)}, u32[]{:S(2)}) collective-permute-start(bf16[256,1024]{1,0:T(8,128)(2,1)S(1)} %get-tuple-element.18.refs_0_), channel_id=1, source_target_pairs={{0,3},{1,2},{2,1},{3,0},{4,7},{5,6},{6,5},{7,4},{8,11},{9,10},{10,... | collective-permute-start | bytes 1572872 | tf_op jit(solution)/shard_map/ppermute | solution.py:38
  60.9 24.4 %collective-permute-start.4 = (bf16[256,1024]{1,0:T(8,128)(2,1)S(1)}, bf16[256,1024]{1,0:T(8,128)(2,1)}, u32[]{:S(2)}, u32[]{:S(2)}) collective-permute-start(bf16[256,1024]{1,0:T(8,128)(2,1)S(1)} %get-tuple-element.17.refs_0_), channel_id=1, source_target_pairs={{0,1},{1,0},{2,3},{3,2},{4,5},{5,4},{6,7},{7,6},{8,9},{9,8},{10,11... | collective-permute-start | bytes 1572872 | tf_op jit(solution)/shard_map/ppermute | solution.py:38
  62.2 25.6 %collective-permute-start.5 = (bf16[256,1024]{1,0:T(8,128)(2,1)S(1)}, bf16[256,1024]{1,0:T(8,128)(2,1)}, u32[]{:S(2)}, u32[]{:S(2)}) collective-permute-start(bf16[256,1024]{1,0:T(8,128)(2,1)S(1)} %get-tuple-element.17.refs_0_), channel_id=1, source_target_pairs={{0,3},{1,2},{2,1},{3,0},{4,7},{5,6},{6,5},{7,4},{8,11},{9,10},{10,... | collective-permute-start | bytes 1572872 | tf_op jit(solution)/shard_map/ppermute | solution.py:38
  75.0 17.2 %collective-permute-start.2 = (bf16[128,1024]{1,0:T(8,128)(2,1)S(1)}, bf16[128,1024]{1,0:T(8,128)(2,1)S(1)}, u32[]{:S(2)}, u32[]{:S(2)}) collective-permute-start(bf16[128,1024]{1,0:T(8,128)(2,1)S(1)} %slice.50), channel_id=1, source_target_pairs={{0,3},{1,2},{2,1},{3,0},{4,7},{5,6},{6,5},{7,4},{8,11},{9,10},{10,... | collective-permute-start | bytes 786440 | tf_op jit(solution)/shard_map/ppermute | solution.py:38
  77.8 14.4 %collective-permute-start.3 = (bf16[128,1024]{1,0:T(8,128)(2,1)S(1)}, bf16[128,1024]{1,0:T(8,128)(2,1)S(1)}, u32[]{:S(2)}, u32[]{:S(2)}) collective-permute-start(bf16[128,1024]{1,0:T(8,128)(2,1)S(1)} %slice.51), channel_id=1, source_target_pairs={{0,1},{1,0},{2,3},{3,2},{4,5},{5,4},{6,7},{7,6},{8,9},{9,8},{10,11... | collective-permute-start | bytes 786440 | tf_op jit(solution)/shard_map/ppermute | solution.py:38
  86.2 10.4 %collective-permute-start.6 = (bf16[128,1024]{1,0:T(8,128)(2,1)S(1)}, bf16[128,1024]{1,0:T(8,128)(2,1)S(1)}, u32[]{:S(2)}, u32[]{:S(2)}) collective-permute-start(bf16[128,1024]{1,0:T(8,128)(2,1)S(1)} %slice.56), channel_id=1, source_target_pairs={{0,3},{1,2},{2,1},{3,0},{4,7},{5,6},{6,5},{7,4},{8,11},{9,10},{10,... | collective-permute-start | bytes 786440 | tf_op jit(solution)/shard_map/ppermute | solution.py:38
  88.7 7.9 %collective-permute-start.7 = (bf16[128,1024]{1,0:T(8,128)(2,1)S(1)}, bf16[128,1024]{1,0:T(8,128)(2,1)S(1)}, u32[]{:S(2)}, u32[]{:S(2)}) collective-permute-start(bf16[128,1024]{1,0:T(8,128)(2,1)S(1)} %slice.57), channel_id=1, source_target_pairs={{0,1},{1,0},{2,3},{3,2},{4,5},{5,4},{6,7},{7,6},{8,9},{9,8},{10,11... | collective-permute-start | bytes 786440 | tf_op jit(solution)/shard_map/ppermute | solution.py:38
  92.2 40.5 %slice-start = ((s8[8388608]{0:T(1024)(128)(4,1)}), s8[4194304]{0:T(1024)(128)(4,1)S(1)}, s32[]{:S(2)}) async-start(s8[8388608]{0:T(1024)(128)(4,1)} %bitcast.13), calls=%async_computation.2 | async-start | bytes 8388608
  95.3 1.3 copy-start.3
  96.7 27.4 %copy-start.4 = (bf16[256,4096]{1,0:T(8,128)(2,1)S(1)}, bf16[256,4096]{1,0:T(8,128)(2,1)}, u32[]{:S(2)}) copy-start(bf16[256,4096]{1,0:T(8,128)(2,1)} %copy-done.3) | copy-start | bytes 6291460
  99.8 1.3 copy-start.5
  101.2 9.3 %collective-permute-start.8 = (bf16[512,256]{1,0:T(8,128)(2,1)S(1)}, bf16[512,256]{1,0:T(8,128)(2,1)S(1)}, u32[]{:S(2)}, u32[]{:S(2)}) collective-permute-start(bf16[512,256]{1,0:T(8,128)(2,1)S(1)} %constant_dynamic-update-slice_fusion.2), channel_id=1, source_target_pairs={{0,4},{4,8},{8,12},{12,16},{16,20},{20,24},{24,28},{1,5},{5,9},{9,... | collective-permute-start | bytes 786440 | tf_op jit(solution)/shard_map/ppermute | solution.py:305
  102.5 20.3 %collective-permute-start.9 = (bf16[512,256]{1,0:T(8,128)(2,1)S(1)}, bf16[512,256]{1,0:T(8,128)(2,1)S(1)}, u32[]{:S(2)}, u32[]{:S(2)}) collective-permute-start(bf16[512,256]{1,0:T(8,128)(2,1)S(1)} %constant_dynamic-update-slice_fusion.2), channel_id=1, source_target_pairs={{0,8},{4,12},{8,16},{12,20},{16,24},{20,28},{1,9},{5,13},{9,17},{1... | collective-permute-start | bytes 786440 | tf_op jit(solution)/shard_map/ppermute | solution.py:305
  103.9 34.1 %collective-permute-start.10 = (bf16[512,256]{1,0:T(8,128)(2,1)S(1)}, bf16[512,256]{1,0:T(8,128)(2,1)S(1)}, u32[]{:S(2)}, u32[]{:S(2)}) collective-permute-start(bf16[512,256]{1,0:T(8,128)(2,1)S(1)} %constant_dynamic-update-slice_fusion.2), channel_id=1, source_target_pairs={{0,12},{4,16},{8,20},{12,24},{16,28},{1,13},{5,17},{9,21},{13,25},... | collective-permute-start | bytes 786440 | tf_op jit(solution)/shard_map/ppermute | solution.py:305
  105.2 32.8 %collective-permute-start.11 = (bf16[512,256]{1,0:T(8,128)(2,1)S(1)}, bf16[512,256]{1,0:T(8,128)(2,1)S(1)}, u32[]{:S(2)}, u32[]{:S(2)}) collective-permute-start(bf16[512,256]{1,0:T(8,128)(2,1)S(1)} %constant_dynamic-update-slice_fusion.2), channel_id=1, source_target_pairs={{0,16},{4,20},{8,24},{12,28},{1,17},{5,21},{9,25},{13,29},{2,18},{... | collective-permute-start | bytes 786440 | tf_op jit(solution)/shard_map/ppermute | solution.py:305
  106.5 32.2 %collective-permute-start.12 = (bf16[512,256]{1,0:T(8,128)(2,1)S(1)}, bf16[512,256]{1,0:T(8,128)(2,1)S(1)}, u32[]{:S(2)}, u32[]{:S(2)}) collective-permute-start(bf16[512,256]{1,0:T(8,128)(2,1)S(1)} %constant_dynamic-update-slice_fusion.2), channel_id=1, source_target_pairs={{0,20},{4,24},{8,28},{1,21},{5,25},{9,29},{2,22},{6,26},{10,30},{3... | collective-permute-start | bytes 786440 | tf_op jit(solution)/shard_map/ppermute | solution.py:305
  110.5 28.8 %collective-permute-start.13 = (bf16[512,256]{1,0:T(8,128)(2,1)S(1)}, bf16[512,256]{1,0:T(8,128)(2,1)S(1)}, u32[]{:S(2)}, u32[]{:S(2)}) collective-permute-start(bf16[512,256]{1,0:T(8,128)(2,1)S(1)} %constant_dynamic-update-slice_fusion.2), channel_id=1, source_target_pairs={{0,24},{4,28},{1,25},{5,29},{2,26},{6,30},{3,27},{7,31},{32,56},{3... | collective-permute-start | bytes 786440 | tf_op jit(solution)/shard_map/ppermute | solution.py:305
  122.8 32.7 %collective-permute-start.14 = (bf16[512,256]{1,0:T(8,128)(2,1)S(1)}, bf16[512,256]{1,0:T(8,128)(2,1)S(1)}, u32[]{:S(2)}, u32[]{:S(2)}) collective-permute-start(bf16[512,256]{1,0:T(8,128)(2,1)S(1)} %constant_dynamic-update-slice_fusion.2), channel_id=1, source_target_pairs={{0,28},{1,29},{2,30},{3,31},{32,60},{33,61},{34,62},{35,63},{64,92... | collective-permute-start | bytes 786440 | tf_op jit(solution)/shard_map/ppermute | solution.py:305
  124.1 3.4 %copy-start.2 = (bf16[4096,1024]{1,0:T(8,128)(2,1)S(1)}, bf16[4096,1024]{1,0:T(8,128)(2,1)}, u32[]{:S(2)}) copy-start(bf16[4096,1024]{1,0:T(8,128)(2,1)} %w_ref.5) | copy-start | bytes 25165828
  127.5 5.2 %slice-start.1 = ((s8[8388608]{0:T(1024)(128)(4,1)}), s8[4194304]{0:T(1024)(128)(4,1)S(1)}, s32[]{:S(2)}) async-start(s8[8388608]{0:T(1024)(128)(4,1)} %bitcast.13), calls=%async_computation.3 | async-start | bytes 8388608
  127.5 5.2 %copy-start.6 = (bf16[256,4096]{1,0:T(8,128)(2,1)S(1)}, bf16[256,4096]{1,0:T(8,128)(2,1)}, u32[]{:S(2)}) copy-start(bf16[256,4096]{1,0:T(8,128)(2,1)} %copy-done.5) | copy-start | bytes 6291460
  131.9 0.8 copy-start.7
  137.1 0.8 copy-start.8
  137.9 0.7 copy-start.10
  138.6 0.7 copy-start.12
  139.4 0.7 copy-start.14
  155.5 0.7 copy-start.17
  156.2 0.9 copy-start.11
  157.2 0.9 copy-start.13
  158.1 0.9 copy-start.15
Sparse Core Ops, SparseCore 0:
  9.2 26.3 all-gather.4
  57.8 36.3 all-gather.6

commit v2 on v1

v2 whole, which is shorter than its diff:
```python
import functools
import math

import jax
import jax.numpy as jnp
from jax import lax
from jax.experimental import pallas as pl
from jax.experimental.pallas import tpu as pltpu
from jax.sharding import PartitionSpec as P

HD = 128
IMG_TOK = 64
MAX_IMG = 8
D = 4096
SHARDS = 8
BLOCK = 2048
rope_base = 500000.0
eps = 1e-05
BF16 = jnp.bfloat16
F32 = jnp.float32
VMEM = pltpu.VMEM
SMEM = pltpu.SMEM


def rotary_tables(positions):
    half_size = HD // 2
    exponent = jnp.arange(half_size, dtype=F32) * (2.0 / HD)
    frequency = jnp.exp(-exponent * math.log(rope_base))
    angles = positions.astype(F32)[:, None] * frequency[None, :]
    return jnp.cos(angles), jnp.sin(angles)


def rotate(u, cosine, sine):
    cosine = jnp.concatenate([cosine, cosine], axis=1)
    sine = jnp.concatenate([-sine, sine], axis=1)
    return u * cosine + pltpu.roll(u, HD // 2, 1) * sine


def shift(x, axis, d, wrap):
    pairs = [(i, (i + d) % SHARDS) for i in range(SHARDS) if wrap or 0 <= i + d < SHARDS]
    return lax.ppermute(x, axis, pairs)


def exchange(x, mask):
    return lax.ppermute(x, "mp", [(i, i ^ mask) for i in range(4)])


def first_hop(x):
    return exchange(x, 1), exchange(x, 3)


def second_hop(a, b):
    half = a.shape[0] // 2
    return exchange(a[:half], 3), exchange(b[half:], 1)


def key_value_kernel(shapes, mp_ref, *refs):
    arrays = sum(count for _, count in shapes)
    gain_ref, w_ref, cos_ref, sin_ref = refs[arrays : arrays + 4]
    normed_ref, kv_ref = refs[-2:]
    mp = mp_ref[0]
    base = taken = 0
    for rows, count in shapes:
        own, one, three, *two = refs[taken : taken + count]
        part = rows // len(two)
        for n, two_part in enumerate(two):
            span = pl.ds(n * part, part)
            pieces = [(0, own[span, :]), (1, one[span, :]), (3, three[span, :]), (2, two_part[...])]
            total = jnp.zeros((part, 1), F32)
            for _, piece in pieces:
                wide = piece.astype(F32)
                total = total + jnp.sum(wide * wide, axis=1, keepdims=True)
            scale = lax.rsqrt(total * (1.0 / D) + eps)
            for mask, piece in pieces:
                columns = pl.ds(pl.multiple_of((mp ^ mask) * 1024, 1024), 1024)
                value = piece.astype(F32) * scale * gain_ref[:, columns]
                normed_ref[pl.ds(base + n * part, part), columns] = value.astype(BF16)
        base += rows
        taken += count
    product = jnp.dot(normed_ref[...], w_ref[...], preferred_element_type=F32)
    kv_ref[:, :HD] = rotate(product[:, :HD], cos_ref[...], sin_ref[...]).astype(BF16)
    kv_ref[:, HD:] = product[:, HD:].astype(BF16)


def key_value(mp, groups, gain, w_kv, cosine, sine, after=()):
    shapes = tuple((g[0].shape[0], len(g)) for g in groups)
    rows = sum(size for size, _ in shapes)
    arrays = [a for g in groups for a in g]
    return pl.pallas_call(
        functools.partial(key_value_kernel, shapes),
        out_shape=(
            jax.ShapeDtypeStruct((rows, D), BF16),
            jax.ShapeDtypeStruct((rows, 2 * HD), BF16),
        ),
        in_specs=[pl.BlockSpec(memory_space=SMEM)]
        + [pl.BlockSpec(memory_space=VMEM)] * (len(arrays) + 4)
        + [pl.BlockSpec(memory_space=pl.ANY)] * len(after),
        out_specs=[pl.BlockSpec(memory_space=VMEM)] * 2,
        compiler_params=pltpu.CompilerParams(vmem_limit_bytes=58 * 2**20),
        cost_estimate=pl.CostEstimate(
            flops=0, bytes_accessed=0, transcendentals=0
        ),
        name="key_value",
    )(mp, *arrays, gain, w_kv, cosine, sine, *after)


def images_before(counts_ref, sample):
    total = jnp.int32(0)
    for i in range(SHARDS):
        total = total + jnp.where(i < sample, counts_ref[i], 0)
    return total


def query_kernel(text, x_ref, w_ref, cos_ref, sin_ref, q_ref, *img_ref):
    product = jnp.dot(x_ref[...], w_ref[...], preferred_element_type=F32)
    for h in range(2):
        span = slice(h * HD, (h + 1) * HD)
        turned = rotate(product[:, span], cos_ref[...], sin_ref[...]).astype(BF16)
        q_ref[:, span] = turned[:text]
        if img_ref:
            img_ref[0][:, span] = turned[text:]


def query(normed, w_query, cosine, sine, text):
    rows, columns = normed.shape[0], w_query.shape[1]
    tile = 2 * HD
    img = rows - text
    out_shape = [jax.ShapeDtypeStruct((text, columns), BF16)]
    out_specs = [pl.BlockSpec((text, tile), lambda n: (0, n))]
    if img:
        out_shape.append(jax.ShapeDtypeStruct((img * (columns // tile), tile), BF16))
        out_specs.append(pl.BlockSpec((img, tile), lambda n: (n, 0)))
    return pl.pallas_call(
        functools.partial(query_kernel, text),
        out_shape=out_shape,
        grid=(columns // tile,),
        in_specs=[
            pl.BlockSpec((rows, D), lambda n: (0, 0)),
            pl.BlockSpec((D, tile), lambda n: (0, n)),
            pl.BlockSpec((rows, HD // 2), lambda n: (0, 0)),
            pl.BlockSpec((rows, HD // 2), lambda n: (0, 0)),
        ],
        out_specs=out_specs,
        compiler_params=pltpu.CompilerParams(vmem_limit_bytes=58 * 2**20),
        cost_estimate=pl.CostEstimate(flops=0, bytes_accessed=0, transcendentals=0),
        name="query",
    )(normed, w_query, cosine, sine)


def image_start(counts_ref, starts_ref, sample, residue):
    slot = (residue - images_before(counts_ref, sample)) & (MAX_IMG - 1)
    return jnp.where(slot < counts_ref[sample], starts_ref[sample, slot], -1)


def attention_kernel(tok, heads, ids_ref, counts_ref, starts_ref, *refs):
    half = tok // 2
    img_rows = IMG_TOK * (1 + heads // 2)
    q_low, q_high, early, own, f1, f2, f3, b1, b2, b3, f4, b4, out_ref = refs[:13]
    q_buf, kv_buf, img_buf, s_buf, max_buf, sum_buf, acc_buf, sems = refs[13:]
    step = pl.program_id(0)
    ctx, sample = ids_ref[1], ids_ref[2]
    factor = math.log2(math.e) / math.sqrt(HD)

    @pl.when(step == 0)
    def _():
        copies = [
            pltpu.make_async_copy(q_low, q_buf.at[pl.ds(0, half), :], sems.at[0]),
            pltpu.make_async_copy(q_high, q_buf.at[pl.ds(half, half), :], sems.at[1]),
        ]
        for c in range(SHARDS):
            copies.append(
                pltpu.make_async_copy(
                    early.at[c, pl.ds(0, half), :],
                    kv_buf.at[pl.ds(c * tok, half), :],
                    sems.at[2 + 2 * c],
                )
            )
            copies.append(
                pltpu.make_async_copy(
                    early.at[c, pl.ds(half, img_rows), :], img_buf.at[c], sems.at[3 + 2 * c]
                )
            )
        used = 2 + 2 * SHARDS
        cut = f4.shape[0]
        pieces = [(0, own, 0), (1, f1, 0), (2, f2, 0), (3, f3, 0), (5, b3, 0), (6, b2, 0), (7, b1, 0)]
        for n, (d, piece, offset) in enumerate(pieces + [(4, f4, 0), (4, b4, cut)]):
            shard = (ctx - d) & (SHARDS - 1)
            place = pl.multiple_of(shard * tok + half + offset, cut)
            copies.append(
                pltpu.make_async_copy(
                    piece, kv_buf.at[pl.ds(place, piece.shape[0]), :], sems.at[used + n]
                )
            )
        for copy in copies:
            copy.start()
        for copy in copies:
            copy.wait()
        before = images_before(counts_ref, sample)
        for c in range(SHARDS):
            slot = (c - before) & (MAX_IMG - 1)
            start = jnp.where(slot < counts_ref[sample], starts_ref[sample, slot], -1)

            @pl.when(start >= 0)
            def _():
                rows = pl.ds(pl.multiple_of(start, IMG_TOK), IMG_TOK)
                kv_buf[rows, :] = img_buf[c, :IMG_TOK, :]

            @pl.when((start >= ctx * tok) & (start < ctx * tok + tok))
            def _():
                rows = pl.ds(pl.multiple_of(start - ctx * tok, IMG_TOK), IMG_TOK)
                for n in range(heads // 2):
                    q_buf[rows, n * 2 * HD : (n + 1) * 2 * HD] = img_buf[
                        c, IMG_TOK * (n + 1) : IMG_TOK * (n + 2), :
                    ]

    def phase(do_score, do_mix):
        slot = lax.rem(step, 2)
        other = 1 - slot

        def block(j):
            keys = pl.ds(pl.multiple_of(j * BLOCK, BLOCK), BLOCK)
            if do_score:
                columns = pl.ds(pl.multiple_of(step * HD, HD), HD)
                s = lax.dot_general(
                    q_buf[:, columns],
                    kv_buf[keys, :HD],
                    (((1,), (1,)), ((), ())),
                    preferred_element_type=F32,
                )
                row = lax.broadcasted_iota(jnp.int32, (tok, HD), 0) + (ctx * tok - j * BLOCK)
                column = lax.broadcasted_iota(jnp.int32, (tok, HD), 1)
                top = max_buf[slot]
                for g in range(BLOCK // HD):
                    seen = s[:, g * HD : (g + 1) * HD]
                    seen = jnp.where(column + g * HD <= row, seen, -1e30)
                    s_buf[slot, j, :, g * HD : (g + 1) * HD] = seen
                    top = jnp.maximum(top, seen)
                max_buf[slot] = top
            if do_mix:
                shared = max_buf[other]
                total = sum_buf[...]
                weights = []
                for g in range(BLOCK // HD):
                    w = jnp.exp2(s_buf[other, j, :, g * HD : (g + 1) * HD] * factor - shared)
                    total = total + w
                    weights.append(w.astype(BF16))
                sum_buf[...] = total
                acc_buf[...] += jnp.dot(
                    jnp.concatenate(weights, axis=1), kv_buf[keys, HD:], preferred_element_type=F32
                )

        if do_score:
            max_buf[slot] = jnp.full((tok, HD), -1e30, F32)
        if do_mix:
            sum_buf[...] = jnp.zeros((tok, HD), F32)
            acc_buf[...] = jnp.zeros((tok, HD), F32)
        pl.loop(0, (ctx * tok + tok + BLOCK - 1) // BLOCK)(block)
        if do_score:
            top = jnp.max(max_buf[slot], axis=1, keepdims=True) * factor
            max_buf[slot] = jnp.broadcast_to(top, (tok, HD))
        if do_mix:
            total = jnp.sum(sum_buf[...], axis=1, keepdims=True)
            out_ref[...] = (acc_buf[...] / total).astype(BF16)

    pl.when(step == 0)(lambda: phase(True, False))
    pl.when((step > 0) & (step < heads))(lambda: phase(True, True))
    pl.when(step == heads)(lambda: phase(False, True))


def attention(tok, heads, scalars, arrays):
    img_rows = IMG_TOK * (1 + heads // 2)
    return pl.pallas_call(
        functools.partial(attention_kernel, tok, heads),
        out_shape=jax.ShapeDtypeStruct((tok, heads * HD), BF16),
        grid=(heads + 1,),
        in_specs=[pl.BlockSpec(memory_space=SMEM)] * 3
        + [pl.BlockSpec(memory_space=pl.ANY)] * len(arrays),
        out_specs=pl.BlockSpec((tok, HD), lambda t: (0, jnp.maximum(t - 1, 0))),
        scratch_shapes=[
            pltpu.VMEM((tok, heads * HD), BF16),
            pltpu.VMEM((SHARDS * tok, 2 * HD), BF16),
            pltpu.VMEM((SHARDS, img_rows, 2 * HD), BF16),
            pltpu.VMEM((2, SHARDS * tok // BLOCK, tok, BLOCK), F32),
            pltpu.VMEM((2, tok, HD), F32),
            pltpu.VMEM((tok, HD), F32),
            pltpu.VMEM((tok, HD), F32),
            pltpu.SemaphoreType.DMA((2 + 2 * SHARDS + 9,)),
        ],
        compiler_params=pltpu.CompilerParams(vmem_limit_bytes=52 * 2**20),
        cost_estimate=pl.CostEstimate(
            flops=4 * tok * heads * SHARDS * tok * HD,
            bytes_accessed=8 * 2**20,
            transcendentals=tok * heads * SHARDS * tok,
        ),
        name="attention",
    )(*scalars, *arrays)


def on_device(
    text_rows, visual_rows, image_counts, image_starts, norm_gain, w_query, w_key, w_value
):
    ctx = lax.axis_index("ctx").astype(jnp.int32)
    sample = lax.axis_index("dp").astype(jnp.int32)
    mp = lax.axis_index("mp").astype(jnp.int32)
    tok = text_rows.shape[0]
    half = tok // 2
    heads = w_query.shape[1] // HD
    ids = jnp.stack([mp, ctx, sample])

    w_kv = jnp.concatenate([w_key, w_value], axis=1)
    gain = norm_gain[None, :]
    every = jnp.arange(SHARDS, dtype=jnp.int32)

    def source(who):
        before = jnp.sum(jnp.where(every < who, image_counts, 0))
        slot = (ctx - before) & (MAX_IMG - 1)
        owner = jnp.minimum((before + slot) >> 3, SHARDS - 1)
        return slot, (owner ^ who) & 1, jnp.clip((who >> 1) - (owner >> 1), 0, 3)

    def choose(which, choices):
        chosen = choices[0]
        for n, choice in enumerate(choices[1:], 1):
            chosen = jnp.where(which == n, choice, chosen)
        return chosen

    my_slot, my_across, my_distance = source(sample)
    _, _, its_distance = source(sample ^ 1)
    low, high = text_rows[:half], text_rows[half:]
    routed = [visual_rows] + [shift(visual_rows, "dp", 2 * d, False) for d in (1, 2, 3)]
    a_low, b_low = first_hop(low)
    for_other = choose(its_distance, routed)
    from_other = lax.ppermute(for_other, "dp", [(i, i ^ 1) for i in range(SHARDS)])
    image = choose(jnp.where(my_across == 1, 4, my_distance), routed + [from_other])
    a_img, b_img, c_img = (exchange(image, mask) for mask in (1, 3, 2))
    a_high, b_high = first_hop(high)
    c_low, d_low = second_hop(a_low, b_low)
    c_high, d_high = second_hop(a_high, b_high)

    mine = (every[:, None] == sample) & (every[None, :] == my_slot)
    my_start = jnp.sum(jnp.where(mine, image_starts, 0))
    rows = jnp.arange(tok + IMG_TOK, dtype=jnp.int32)
    positions = jnp.where(
        rows < half,
        ctx * tok + rows,
        jnp.where(rows < half + IMG_TOK, my_start + rows - half, ctx * tok + rows - IMG_TOK),
    )
    cosine, sine = rotary_tables(positions)
    first = half + IMG_TOK
    mp_arr = ids[:1]

    normed, kv = key_value(
        mp_arr,
        [(low, a_low, b_low, c_low, d_low), (image, a_img, b_img, c_img)],
        gain, w_kv, cosine[:first], sine[:first], (a_high, b_high),
    )
    q_low, q_img = query(normed, w_query, cosine[:first], sine[:first], half)
    early = lax.all_gather(jnp.concatenate([kv, q_img], axis=0), "ctx", axis=0)
    normed_high, own = key_value(
        mp_arr, [(high, a_high, b_high, c_high, d_high)], gain, w_kv, cosine[first:], sine[first:],
        (q_img,),
    )
    cut = half // 2
    f1, b1 = shift(own, "ctx", 1, True), shift(own, "ctx", -1, True)
    f2, b2 = shift(f1, "ctx", 1, True), shift(b1, "ctx", -1, True)
    f3, b3 = shift(f2, "ctx", 1, True), shift(b2, "ctx", -1, True)
    f4, b4 = shift(f3[:cut], "ctx", 1, True), shift(b3[cut:], "ctx", -1, True)
    (q_high,) = query(normed_high, w_query, cosine[first:], sine[first:], half)
    return attention(
        tok, heads, (ids, image_counts, image_starts),
        [q_low, q_high, early, own, f1, f2, f3, b1, b2, b3, f4, b4],
    )


def solution(mesh):
    in_specs = (
        P(("dp", "ctx"), "mp"),
        P(("dp", "ctx"), "mp"),
        P(),
        P(),
        P(),
        P(None, "mp"),
        P(None, "mp"),
        P(None, "mp"),
    )
    out_specs = P(("dp", "ctx"), "mp")
    return jax.shard_map(
        on_device, mesh=mesh, in_specs=in_specs, out_specs=out_specs, check_vma=False
    )
```

time: 211 us -> 161 us (0.76)
  the two profiles are of different devices: /device:TPU:224 before, /device:TPU:128 now
where the time goes in v2:
time: 161 us; the launch traced here: 160 us
  Pallas kernels  57.3 us (36%)
  starting transfers between devices  36 us (22%)
  waiting for transfers between devices  30.7 us (19%)
  between operations  16 us (10%)
  local copies, waits for them, and re-layouts  14.4 us (9%)
  other arithmetic  5.5 us (3%)
    pallas_call x1, Pallas kernels, attention(): pl.pallas_call(functools.partial(attention_kernel, tok, heads), out_shape...  32.3 us
    ppermute x11, starting transfers between devices, shift(): return lax.ppermute(x, axis, pairs)  22.8 us
    ppermute x11, waiting for transfers between devices, shift(): return lax.ppermute(x, axis, pairs)  18 us
    pallas_call x2, Pallas kernels, query(): pl.pallas_call(functools.partial(query_kernel, text), out_shape=out_shape...  14.9 us
    ppermute x11, starting transfers between devices, exchange(): return lax.ppermute(x, 'mp', [(i, i ^ mask) for i in range(4)])  13.2 us
    ppermute x11, waiting for transfers between devices, exchange(): return lax.ppermute(x, 'mp', [(i, i ^ mask) for i in range(4)])  12.6 us
    pallas_call x2, Pallas kernels, key_value(): pl.pallas_call(functools.partial(key_value_kernel, shapes), out_shape=(ja...  10 us
    slice x4, local copies, waits for them, and re-layouts, second_hop(): return (exchange(a[:half], 3), exchange(b[half:], 1))  3.39 us
  transfers between devices with their start and end apart: 24, of which 7 were waited for; matrix products, arithmetic and copies ran while one was open for 8% of the time, Pallas kernels for 7%

profile of v2, /device:TPU:128, one launch (start us, length us, event | category | flops | bytes accessed | tf_op | source)
XLA Modules:
  0.0 160.0 jit_solution(17790361087264663478)
XLA Ops:
  6.5 2.4 %fusion.2 = (bf16[256,1024]{1,0:T(8,128)(2,1)}, bf16[256,1024]{1,0:T(8,128)(2,1)}) fusion(bf16[512,1024]{1,0:T(8,128)(2,1)} %param.8), kind=kLoop, calls=%fused_computation.19 | loop fusion | bytes 2097152 | tf_op jit(solution)/shard_map/slice | solution.py:328
  8.9 1.5 collective-permute-start
  10.4 2.1 %collective-permute-start.1 = (bf16[256,1024]{1,0:T(8,128)(2,1)}, bf16[256,1024]{1,0:T(8,128)(2,1)}, u32[]{:S(2)}, u32[]{:S(2)}) collective-permute-start(bf16[256,1024]{1,0:T(8,128)(2,1)} %get-tuple-element.20.refs_0_), channel_id=1, source_target_pairs={{0,3},{1,2},{2,1},{3,0},{4,7},{5,6},{6,5},{7,4},{8,11},{9,10},{10,... | collective-permute-start | bytes 1572872 | tf_op jit(solution)/shard_map/ppermute | solution.py:45
  12.5 4.9 %collective-permute-start.4 = (bf16[64,1024]{1,0:T(8,128)(2,1)S(1)}, bf16[64,1024]{1,0:T(8,128)(2,1)S(1)}, u32[]{:S(2)}, u32[]{:S(2)}) collective-permute-start(bf16[64,1024]{1,0:T(8,128)(2,1)S(1)} %copy-done.13), channel_id=1, source_target_pairs={{0,192},{32,224},{1,193},{33,225},{2,194},{34,226},{3,195},{35,227... | collective-permute-start | bytes 393224 | tf_op jit(solution)/shard_map/ppermute | solution.py:41
  17.4 1.3 collective-permute-start.5
  18.7 3.4 %collective-permute-start.6 = (bf16[64,1024]{1,0:T(8,128)(2,1)S(1)}, bf16[64,1024]{1,0:T(8,128)(2,1)}, u32[]{:S(2)}, u32[]{:S(2)}) collective-permute-start(bf16[64,1024]{1,0:T(8,128)(2,1)S(1)} %copy-done.13), channel_id=1, source_target_pairs={{0,64},{32,96},{64,128},{96,160},{128,192},{160,224},{1,65},{33,97... | collective-permute-start | bytes 393224 | tf_op jit(solution)/shard_map/ppermute | solution.py:41
  22.1 0.2 constant_dynamic-update-slice_fusion.1
  22.3 0.0 copy-start
  22.4 0.6 fusion
  24.1 0.0 collective-permute-done.4
  24.1 0.7 collective-permute-start.11
  24.8 0.7 collective-permute-start.12
  25.5 0.0 collective-permute-done.6
  25.5 0.7 select_select_fusion.1
  26.2 1.5 constant_dynamic-update-slice_fusion.refs_10_.refs_6_
  28.9 0.0 collective-permute-done.7
  28.9 0.1 select_select_fusion.refs_5_
  29.0 1.4 collective-permute-start.8
  30.4 0.7 select_reduce_fusion
  31.1 2.1 %collective-permute-start.9 = (bf16[64,1024]{1,0:T(8,128)(2,1)S(1)}, bf16[64,1024]{1,0:T(8,128)(2,1)S(1)}, u32[]{:S(2)}, u32[]{:S(2)}) collective-permute-start(bf16[64,1024]{1,0:T(8,128)(2,1)S(1)} %select_select_fusion.refs_5_), channel_id=1, source_target_pairs={{0,3},{1,2},{2,1},{3,0},{4,7},{5,6},{6,5},{7,4},{8,11},{9,10},{10,... | collective-permute-start | bytes 393224 | tf_op jit(solution)/shard_map/ppermute | solution.py:45
  33.2 0.6 select_convert_fusion
  33.8 1.7 %slice.52 = bf16[128,1024]{1,0:T(8,128)(2,1)} slice(bf16[256,1024]{1,0:T(8,128)(2,1)} %collective-permute-done.refs_1_), slice={[0:128], [0:1024]} | slice | bytes 524288 | tf_op jit(solution)/shard_map/slice | solution.py:54
  35.4 1.1 collective-permute-start.2
  36.6 1.7 %slice.53 = bf16[128,1024]{1,0:T(8,128)(2,1)} slice(bf16[256,1024]{1,0:T(8,128)(2,1)} %collective-permute-done.1.refs_2_), slice={[128:256], [0:1024]} | slice | bytes 524288 | tf_op jit(solution)/shard_map/slice | solution.py:54
  38.2 1.5 collective-permute-done.8.refs_6_
  39.8 0.6 collective-permute-start.3
  40.4 1.9 %collective-permute-done.9.refs_7_ = bf16[64,1024]{1,0:T(8,128)(2,1)S(1)} collective-permute-done((bf16[64,1024]{1,0:T(8,128)(2,1)S(1)}, bf16[64,1024]{1,0:T(8,128)(2,1)S(1)}, u32[]{:S(2)}, u32[]{:S(2)}) %collective-permute-start.9) | collective-permute-done | bytes 131104 | tf_op jit(solution)/shard_map/ppermute | solution.py:45
  42.3 1.6 collective-permute-start.10
  43.8 1.1 multiply_sine_fusion
  45.0 0.7 slice.54.refs_11_.cos_ref
  45.7 0.7 slice.55.refs_12_.sin_ref
  46.4 5.2 %collective-permute-done.10.refs_8_ = bf16[64,1024]{1,0:T(8,128)(2,1)S(1)} collective-permute-done((bf16[64,1024]{1,0:T(8,128)(2,1)S(1)}, bf16[64,1024]{1,0:T(8,128)(2,1)S(1)}, u32[]{:S(2)}, u32[]{:S(2)}) %collective-permute-start.10) | collective-permute-done | bytes 131104 | tf_op jit(solution)/shard_map/ppermute | solution.py:45
  51.6 0.0 collective-permute-done.11.refs_13_.refs_1_
  51.6 0.0 collective-permute-done.2.refs_3_
  51.7 0.5 copy-done.20
  52.2 0.2 copy-done.5
  52.4 0.2 copy-done.7
  52.6 5.3 %key_value.2 = (bf16[320,4096]{1,0:T(8,128)(2,1)}, bf16[320,256]{1,0:T(8,128)(2,1)}) custom-call(s32[1]{0:T(128)} %bitcast.mp_ref, bf16[256,1024]{1,0:T(8,128)(2,1)} %get-tuple-element.20.refs_0_, bf16[256,1024]{1,0:T(8,128)(2,1)} %collective-permute-done.refs_1_, bf16[256,1024]{1,0:T(8,128)(2,1)} %collective-permute-done.1.refs_2_, ...), custom_call_target="tpu_custom_call" | custom-call | tf_op jit(solution)/shard_map/key_value/pallas_call | solution.py:89
  57.9 7.8 %query.2 = (bf16[256,1024]{1,0:T(8,128)(2,1)}, bf16[256,256]{1,0:T(8,128)(2,1)}) custom-call(bf16[320,4096]{1,0:T(8,128)(2,1)} %get-tuple-element.11.x_ref, bf16[4096,1024]{1,0:T(8,128)(2,1)} %w_ref.3, f32[320,64]{1,0:T(8,128)} %slice.54.refs_11_.cos_ref, f32[320,64]{1,0:T(8,128)} %slice.55.refs_12_.sin_ref), custom_call_target="tpu_custom_call" | custom-call | tf_op jit(solution)/shard_map/query/pallas_call | solution.py:133
  65.7 1.6 %pad_maximum_fusion = bf16[576,256]{1,0:T(8,128)(2,1)} fusion(bf16[256,256]{1,0:T(8,128)(2,1)} %get-tuple-element.13.refs_9_, bf16[320,256]{1,0:T(8,128)(2,1)S(1)} %copy-done.17), kind=kLoop, calls=%fused_computation.2 | loop fusion | flops 589824 | bytes 589824 | tf_op jit(solution)/shard_map/concatenate | solution.py:357
  67.3 0.0 all-gather.3.cloned.1.call-update
  67.4 1.2 collective-permute-start.13
  68.7 0.3 collective-permute-start.14
  68.9 1.6 slice.58.refs_7_.cos_ref
  70.5 1.6 slice.59.refs_8_.sin_ref
  72.1 4.0 %collective-permute-done.13.refs_3_ = bf16[128,1024]{1,0:T(8,128)(2,1)S(1)} collective-permute-done((bf16[128,1024]{1,0:T(8,128)(2,1)S(1)}, bf16[128,1024]{1,0:T(8,128)(2,1)S(1)}, u32[]{:S(2)}, u32[]{:S(2)}) %collective-permute-start.13) | collective-permute-done | bytes 262176 | tf_op jit(solution)/shard_map/ppermute | solution.py:45
  76.0 0.0 collective-permute-done.14.refs_4_
  76.0 0.7 copy-done.15
  76.8 0.7 copy-done.16
  77.5 4.7 %key_value.3 = (bf16[256,4096]{1,0:T(8,128)(2,1)}, bf16[256,256]{1,0:T(8,128)(2,1)}) custom-call(s32[1]{0:T(128)} %bitcast.mp_ref, bf16[256,1024]{1,0:T(8,128)(2,1)} %get-tuple-element.19.refs_0_, bf16[256,1024]{1,0:T(8,128)(2,1)} %copy-done.5, bf16[256,1024]{1,0:T(8,128)(2,1)} %copy-done.7, bf16[128,1024]{1,0:T(8,128)(2,1)} %copy-done.15, ...), custom_call_target="tpu_custom_call" | custom-call | tf_op jit(solution)/shard_map/key_value/pallas_call | solution.py:89
  82.2 1.0 collective-permute-start.15
  83.2 2.2 %collective-permute-start.18 = (bf16[256,256]{1,0:T(8,128)(2,1)}, bf16[256,256]{1,0:T(8,128)(2,1)S(1)}, u32[]{:S(2)}, u32[]{:S(2)}) collective-permute-start(bf16[256,256]{1,0:T(8,128)(2,1)} %get-tuple-element.16.refs_3_), channel_id=1, source_target_pairs={{0,28},{4,0},{8,4},{12,8},{16,12},{20,16},{24,20},{28,24},{1,29},{... | collective-permute-start | bytes 393224 | tf_op jit(solution)/shard_map/ppermute | solution.py:41
  85.5 6.3 %collective-permute-done.15.refs_4_ = bf16[256,256]{1,0:T(8,128)(2,1)S(1)} collective-permute-done((bf16[256,256]{1,0:T(8,128)(2,1)}, bf16[256,256]{1,0:T(8,128)(2,1)S(1)}, u32[]{:S(2)}, u32[]{:S(2)}) %collective-permute-start.15) | collective-permute-done | bytes 131104 | tf_op jit(solution)/shard_map/ppermute | solution.py:41
  91.7 0.0 collective-permute-start.16
  91.7 0.0 collective-permute-done.18.refs_7_
  91.7 3.2 %collective-permute-start.19 = (bf16[256,256]{1,0:T(8,128)(2,1)S(1)}, bf16[256,256]{1,0:T(8,128)(2,1)S(1)}, u32[]{:S(2)}, u32[]{:S(2)}) collective-permute-start(bf16[256,256]{1,0:T(8,128)(2,1)S(1)} %collective-permute-done.18.refs_7_), channel_id=1, source_target_pairs={{0,28},{4,0},{8,4},{12,8},{16,12},{20,16},{24,20},{28,24},{1,29},{... | collective-permute-start | bytes 393224 | tf_op jit(solution)/shard_map/ppermute | solution.py:41
  95.0 5.8 %collective-permute-done.16.refs_5_ = bf16[256,256]{1,0:T(8,128)(2,1)S(1)} collective-permute-done((bf16[256,256]{1,0:T(8,128)(2,1)S(1)}, bf16[256,256]{1,0:T(8,128)(2,1)S(1)}, u32[]{:S(2)}, u32[]{:S(2)}) %collective-permute-start.16) | collective-permute-done | bytes 131104 | tf_op jit(solution)/shard_map/ppermute | solution.py:41
  100.8 3.2 %collective-permute-start.20 = (bf16[256,256]{1,0:T(8,128)(2,1)S(1)}, bf16[256,256]{1,0:T(8,128)(2,1)S(1)}, u32[]{:S(2)}, u32[]{:S(2)}) collective-permute-start(bf16[256,256]{1,0:T(8,128)(2,1)S(1)} %collective-permute-done.19.refs_8_), channel_id=1, source_target_pairs={{0,28},{4,0},{8,4},{12,8},{16,12},{20,16},{24,20},{28,24},{1,29},{... | collective-permute-start | bytes 393224 | tf_op jit(solution)/shard_map/ppermute | solution.py:41
  104.0 5.9 %collective-permute-done.17.refs_6_ = bf16[256,256]{1,0:T(8,128)(2,1)S(1)} collective-permute-done((bf16[256,256]{1,0:T(8,128)(2,1)S(1)}, bf16[256,256]{1,0:T(8,128)(2,1)S(1)}, u32[]{:S(2)}, u32[]{:S(2)}) %collective-permute-start.17) | collective-permute-done | bytes 131104 | tf_op jit(solution)/shard_map/ppermute | solution.py:41
  110.0 3.5 %collective-permute-start.22 = (bf16[128,256]{1,0:T(8,128)(2,1)S(1)}, bf16[128,256]{1,0:T(8,128)(2,1)S(1)}, u32[]{:S(2)}, u32[]{:S(2)}) collective-permute-start(bf16[128,256]{1,0:T(8,128)(2,1)S(1)} %slice.61), channel_id=1, source_target_pairs={{0,28},{4,0},{8,4},{12,8},{16,12},{20,16},{24,20},{28,24},{1,29},{... | collective-permute-start | bytes 196616 | tf_op jit(solution)/shard_map/ppermute | solution.py:41
  113.5 0.1 pad_add_fusion.ids_ref
  113.6 7.2 %query.3.refs_1_ = bf16[256,1024]{1,0:T(8,128)(2,1)} custom-call(bf16[256,4096]{1,0:T(8,128)(2,1)} %get-tuple-element.14.x_ref, bf16[4096,1024]{1,0:T(8,128)(2,1)} %w_ref.3, f32[256,64]{1,0:T(8,128)} %slice.58.refs_7_.cos_ref, f32[256,64]{1,0:T(8,128)} %slice.59.refs_8_.sin_ref), custom_call_target="tpu_custom_call" | custom-call | tf_op jit(solution)/shard_map/query/pallas_call | solution.py:133
  120.8 0.0 all-gather.3.cloned.1.call-done
  120.8 32.3 %attention.1 = bf16[512,1024]{1,0:T(8,128)(2,1)} custom-call(s32[3]{0:T(128)S(1)} %pad_add_fusion.ids_ref, s32[8]{0:T(128)S(1)} %copy-done.1, s32[8,8]{1,0:T(8,128)S(1)} %copy-done, bf16[256,1024]{1,0:T(8,128)(2,1)S(1)} %copy-done.2, bf16[256,1024]{1,0:T(8,128)(2,1)} %query.3.refs_1_, bf16[8,576,256]{2,1,0:T(8,128)(2,1)} %bitcast.7, ...), custom_call_target="tpu_custom_call" | custom-call | flops 8589934592 | bytes 8388608 | tf_op jit(solution)/shard_map/attention/pallas_call | solution.py:272
  (55 shorter events, 0.2 us)
Async XLA Ops:
  6.5 6.0 %copy-start.13 = (bf16[64,1024]{1,0:T(8,128)(2,1)S(1)}, bf16[64,1024]{1,0:T(8,128)(2,1)}, u32[]{:S(2)}) copy-start(bf16[64,1024]{1,0:T(8,128)(2,1)} %param.9) | copy-start | bytes 393220
  6.5 15.6 %copy-start.11 = (bf16[4096,128]{1,0:T(8,128)(2,1)S(1)}, bf16[4096,128]{1,0:T(8,128)(2,1)}, u32[]{:S(2)}) copy-start(bf16[4096,128]{1,0:T(8,128)(2,1)} %param.14) | copy-start | bytes 3145732
  6.5 15.8 %copy-start.1 = (s32[8]{0:T(128)S(1)}, s32[8]{0:T(128)}, u32[]{:S(2)}) copy-start(s32[8]{0:T(128)} %counts_ref.1) | copy-start | bytes 100
  6.5 114.2 %all-gather.3.cloned.1.call-start = ((), (), s32[]{:S(2)}) async-start(), calls=%async_computation | async-start | bytes 2654208 | tf_op jit(solution)/shard_map/all_gather | solution.py:357
  8.9 22.2 %collective-permute-start = (bf16[256,1024]{1,0:T(8,128)(2,1)}, bf16[256,1024]{1,0:T(8,128)(2,1)}, u32[]{:S(2)}, u32[]{:S(2)}) collective-permute-start(bf16[256,1024]{1,0:T(8,128)(2,1)} %get-tuple-element.20.refs_0_), channel_id=1, source_target_pairs={{0,1},{1,0},{2,3},{3,2},{4,5},{5,4},{6,7},{7,6},{8,9},{9,8},{10,11... | collective-permute-start | bytes 1572872 | tf_op jit(solution)/shard_map/ppermute | solution.py:45
  10.4 25.0 %collective-permute-start.1 = (bf16[256,1024]{1,0:T(8,128)(2,1)}, bf16[256,1024]{1,0:T(8,128)(2,1)}, u32[]{:S(2)}, u32[]{:S(2)}) collective-permute-start(bf16[256,1024]{1,0:T(8,128)(2,1)} %get-tuple-element.20.refs_0_), channel_id=1, source_target_pairs={{0,3},{1,2},{2,1},{3,0},{4,7},{5,6},{6,5},{7,4},{8,11},{9,10},{10,... | collective-permute-start | bytes 1572872 | tf_op jit(solution)/shard_map/ppermute | solution.py:45
  12.5 11.6 %collective-permute-start.4 = (bf16[64,1024]{1,0:T(8,128)(2,1)S(1)}, bf16[64,1024]{1,0:T(8,128)(2,1)S(1)}, u32[]{:S(2)}, u32[]{:S(2)}) collective-permute-start(bf16[64,1024]{1,0:T(8,128)(2,1)S(1)} %copy-done.13), channel_id=1, source_target_pairs={{0,192},{32,224},{1,193},{33,225},{2,194},{34,226},{3,195},{35,227... | collective-permute-start | bytes 393224 | tf_op jit(solution)/shard_map/ppermute | solution.py:41
  17.4 7.4 %collective-permute-start.5 = (bf16[64,1024]{1,0:T(8,128)(2,1)S(1)}, bf16[64,1024]{1,0:T(8,128)(2,1)S(1)}, u32[]{:S(2)}, u32[]{:S(2)}) collective-permute-start(bf16[64,1024]{1,0:T(8,128)(2,1)S(1)} %copy-done.13), channel_id=1, source_target_pairs={{0,128},{32,160},{64,192},{96,224},{1,129},{33,161},{65,193},{97,2... | collective-permute-start | bytes 393224 | tf_op jit(solution)/shard_map/ppermute | solution.py:41
  18.7 6.8 %collective-permute-start.6 = (bf16[64,1024]{1,0:T(8,128)(2,1)S(1)}, bf16[64,1024]{1,0:T(8,128)(2,1)}, u32[]{:S(2)}, u32[]{:S(2)}) collective-permute-start(bf16[64,1024]{1,0:T(8,128)(2,1)S(1)} %copy-done.13), channel_id=1, source_target_pairs={{0,64},{32,96},{64,128},{96,160},{128,192},{160,224},{1,65},{33,97... | collective-permute-start | bytes 393224 | tf_op jit(solution)/shard_map/ppermute | solution.py:41
  22.3 8.0 %copy-start = (s32[8,8]{1,0:T(8,128)S(1)}, s32[8,8]{1,0:T(8,128)}, u32[]{:S(2)}) copy-start(s32[8,8]{1,0:T(8,128)} %starts_ref.1) | copy-start | bytes 772
  24.1 27.4 %collective-permute-start.11 = (bf16[256,1024]{1,0:T(8,128)(2,1)}, bf16[256,1024]{1,0:T(8,128)(2,1)S(1)}, u32[]{:S(2)}, u32[]{:S(2)}) collective-permute-start(bf16[256,1024]{1,0:T(8,128)(2,1)} %get-tuple-element.19.refs_0_), channel_id=1, source_target_pairs={{0,1},{1,0},{2,3},{3,2},{4,5},{5,4},{6,7},{7,6},{8,9},{9,8},{10,11... | collective-permute-start | bytes 1572872 | tf_op jit(solution)/shard_map/ppermute | solution.py:45
  24.8 4.0 %copy-start.14 = (bf16[64,1024]{1,0:T(8,128)(2,1)}, bf16[64,1024]{1,0:T(8,128)(2,1)S(1)}, u32[]{:S(2)}) copy-start(bf16[64,1024]{1,0:T(8,128)(2,1)S(1)} %collective-permute-done.5) | copy-start | bytes 393220
  24.8 26.8 %collective-permute-start.12 = (bf16[256,1024]{1,0:T(8,128)(2,1)}, bf16[256,1024]{1,0:T(8,128)(2,1)S(1)}, u32[]{:S(2)}, u32[]{:S(2)}) collective-permute-start(bf16[256,1024]{1,0:T(8,128)(2,1)} %get-tuple-element.19.refs_0_), channel_id=1, source_target_pairs={{0,3},{1,2},{2,1},{3,0},{4,7},{5,6},{6,5},{7,4},{8,11},{9,10},{10,... | collective-permute-start | bytes 1572872 | tf_op jit(solution)/shard_map/ppermute | solution.py:45
  26.2 2.7 %collective-permute-start.7 = (bf16[64,1024]{1,0:T(8,128)(2,1)}, bf16[64,1024]{1,0:T(8,128)(2,1)}, u32[]{:S(2)}, u32[]{:S(2)}) collective-permute-start(bf16[64,1024]{1,0:T(8,128)(2,1)} %select_select_fusion.1), channel_id=1, source_target_pairs={{0,32},{32,0},{64,96},{96,64},{128,160},{160,128},{192,224},{224,1... | collective-permute-start | bytes 393224 | tf_op jit(solution)/shard_map/ppermute | solution.py:332
  27.7 24.0 %copy-start.4 = (bf16[4096,256]{1,0:T(8,128)(2,1)}, bf16[4096,256]{1,0:T(8,128)(2,1)S(1)}, u32[]{:S(2)}) copy-start(bf16[4096,256]{1,0:T(8,128)(2,1)S(1)} %constant_dynamic-update-slice_fusion.refs_10_.refs_6_) | copy-start | bytes 6291460
  29.0 22.7 %copy-start.12 = (bf16[64,1024]{1,0:T(8,128)(2,1)}, bf16[64,1024]{1,0:T(8,128)(2,1)S(1)}, u32[]{:S(2)}) copy-start(bf16[64,1024]{1,0:T(8,128)(2,1)S(1)} %select_select_fusion.refs_5_) | copy-start | bytes 393220
  29.0 10.8 %collective-permute-start.8 = (bf16[64,1024]{1,0:T(8,128)(2,1)S(1)}, bf16[64,1024]{1,0:T(8,128)(2,1)S(1)}, u32[]{:S(2)}, u32[]{:S(2)}) collective-permute-start(bf16[64,1024]{1,0:T(8,128)(2,1)S(1)} %select_select_fusion.refs_5_), channel_id=1, source_target_pairs={{0,1},{1,0},{2,3},{3,2},{4,5},{5,4},{6,7},{7,6},{8,9},{9,8},{10,11... | collective-permute-start | bytes 393224 | tf_op jit(solution)/shard_map/ppermute | solution.py:45
  31.1 11.2 %collective-permute-start.9 = (bf16[64,1024]{1,0:T(8,128)(2,1)S(1)}, bf16[64,1024]{1,0:T(8,128)(2,1)S(1)}, u32[]{:S(2)}, u32[]{:S(2)}) collective-permute-start(bf16[64,1024]{1,0:T(8,128)(2,1)S(1)} %select_select_fusion.refs_5_), channel_id=1, source_target_pairs={{0,3},{1,2},{2,1},{3,0},{4,7},{5,6},{6,5},{7,4},{8,11},{9,10},{10,... | collective-permute-start | bytes 393224 | tf_op jit(solution)/shard_map/ppermute | solution.py:45
  35.4 16.2 %collective-permute-start.2 = (bf16[128,1024]{1,0:T(8,128)(2,1)}, bf16[128,1024]{1,0:T(8,128)(2,1)}, u32[]{:S(2)}, u32[]{:S(2)}) collective-permute-start(bf16[128,1024]{1,0:T(8,128)(2,1)} %slice.52), channel_id=1, source_target_pairs={{0,3},{1,2},{2,1},{3,0},{4,7},{5,6},{6,5},{7,4},{8,11},{9,10},{10,... | collective-permute-start | bytes 786440 | tf_op jit(solution)/shard_map/ppermute | solution.py:45
  39.8 11.9 %copy-start.18 = (bf16[64,1024]{1,0:T(8,128)(2,1)}, bf16[64,1024]{1,0:T(8,128)(2,1)S(1)}, u32[]{:S(2)}) copy-start(bf16[64,1024]{1,0:T(8,128)(2,1)S(1)} %collective-permute-done.8.refs_6_) | copy-start | bytes 393220
  39.8 11.8 %collective-permute-start.3 = (bf16[128,1024]{1,0:T(8,128)(2,1)}, bf16[128,1024]{1,0:T(8,128)(2,1)}, u32[]{:S(2)}, u32[]{:S(2)}) collective-permute-start(bf16[128,1024]{1,0:T(8,128)(2,1)} %slice.53), channel_id=1, source_target_pairs={{0,1},{1,0},{2,3},{3,2},{4,5},{5,4},{6,7},{7,6},{8,9},{9,8},{10,11... | collective-permute-start | bytes 786440 | tf_op jit(solution)/shard_map/ppermute | solution.py:45
  42.3 9.4 %copy-start.19 = (bf16[64,1024]{1,0:T(8,128)(2,1)}, bf16[64,1024]{1,0:T(8,128)(2,1)S(1)}, u32[]{:S(2)}) copy-start(bf16[64,1024]{1,0:T(8,128)(2,1)S(1)} %collective-permute-done.9.refs_7_) | copy-start | bytes 393220
  42.3 9.3 %collective-permute-start.10 = (bf16[64,1024]{1,0:T(8,128)(2,1)S(1)}, bf16[64,1024]{1,0:T(8,128)(2,1)S(1)}, u32[]{:S(2)}, u32[]{:S(2)}) collective-permute-start(bf16[64,1024]{1,0:T(8,128)(2,1)S(1)} %select_select_fusion.refs_5_), channel_id=1, source_target_pairs={{0,2},{1,3},{2,0},{3,1},{4,6},{5,7},{6,4},{7,5},{8,10},{9,11},{10,... | collective-permute-start | bytes 393224 | tf_op jit(solution)/shard_map/ppermute | solution.py:45
  44.9 6.6 %copy-start.9 = (f32[576,64]{1,0:T(8,128)}, f32[576,64]{1,0:T(8,128)S(1)}, u32[]{:S(2)}) copy-start(f32[576,64]{1,0:T(8,128)S(1)} %get-tuple-element.21) | copy-start | bytes 442372
  44.9 6.7 %copy-start.10 = (f32[576,64]{1,0:T(8,128)}, f32[576,64]{1,0:T(8,128)S(1)}, u32[]{:S(2)}) copy-start(f32[576,64]{1,0:T(8,128)S(1)} %get-tuple-element.22) | copy-start | bytes 442372
  51.6 0.7 copy-start.20
  51.6 0.8 copy-start.5
  51.6 1.0 copy-start.7
  57.9 7.8 %copy-start.17 = (bf16[320,256]{1,0:T(8,128)(2,1)S(1)}, bf16[320,256]{1,0:T(8,128)(2,1)}, u32[]{:S(2)}) copy-start(bf16[320,256]{1,0:T(8,128)(2,1)} %get-tuple-element.15) | copy-start | bytes 491524
  57.9 9.4 %copy-start.6 = (bf16[256,1024]{1,0:T(8,128)(2,1)S(1)}, bf16[256,1024]{1,0:T(8,128)(2,1)}, u32[]{:S(2)}) copy-start(bf16[256,1024]{1,0:T(8,128)(2,1)} %copy-done.5) | copy-start | bytes 1572868
  57.9 10.7 %copy-start.8 = (bf16[256,1024]{1,0:T(8,128)(2,1)S(1)}, bf16[256,1024]{1,0:T(8,128)(2,1)}, u32[]{:S(2)}) copy-start(bf16[256,1024]{1,0:T(8,128)(2,1)} %copy-done.7) | copy-start | bytes 1572868
  67.4 8.6 %collective-permute-start.13 = (bf16[128,1024]{1,0:T(8,128)(2,1)S(1)}, bf16[128,1024]{1,0:T(8,128)(2,1)S(1)}, u32[]{:S(2)}, u32[]{:S(2)}) collective-permute-start(bf16[128,1024]{1,0:T(8,128)(2,1)S(1)} %slice.56), channel_id=1, source_target_pairs={{0,3},{1,2},{2,1},{3,0},{4,7},{5,6},{6,5},{7,4},{8,11},{9,10},{10,... | collective-permute-start | bytes 786440 | tf_op jit(solution)/shard_map/ppermute | solution.py:45
  68.7 7.4 %collective-permute-start.14 = (bf16[128,1024]{1,0:T(8,128)(2,1)S(1)}, bf16[128,1024]{1,0:T(8,128)(2,1)S(1)}, u32[]{:S(2)}, u32[]{:S(2)}) collective-permute-start(bf16[128,1024]{1,0:T(8,128)(2,1)S(1)} %slice.57), channel_id=1, source_target_pairs={{0,1},{1,0},{2,3},{3,2},{4,5},{5,4},{6,7},{7,6},{8,9},{9,8},{10,11... | collective-permute-start | bytes 786440 | tf_op jit(solution)/shard_map/ppermute | solution.py:45
  76.0 0.7 copy-start.15
  76.8 0.7 copy-start.16
  82.2 9.5 %collective-permute-start.15 = (bf16[256,256]{1,0:T(8,128)(2,1)}, bf16[256,256]{1,0:T(8,128)(2,1)S(1)}, u32[]{:S(2)}, u32[]{:S(2)}) collective-permute-start(bf16[256,256]{1,0:T(8,128)(2,1)} %get-tuple-element.16.refs_3_), channel_id=1, source_target_pairs={{0,4},{4,8},{8,12},{12,16},{16,20},{20,24},{24,28},{28,0},{1,5},{5... | collective-permute-start | bytes 393224 | tf_op jit(solution)/shard_map/ppermute | solution.py:41
  83.2 8.5 %collective-permute-start.18 = (bf16[256,256]{1,0:T(8,128)(2,1)}, bf16[256,256]{1,0:T(8,128)(2,1)S(1)}, u32[]{:S(2)}, u32[]{:S(2)}) collective-permute-start(bf16[256,256]{1,0:T(8,128)(2,1)} %get-tuple-element.16.refs_3_), channel_id=1, source_target_pairs={{0,28},{4,0},{8,4},{12,8},{16,12},{20,16},{24,20},{28,24},{1,29},{... | collective-permute-start | bytes 393224 | tf_op jit(solution)/shard_map/ppermute | solution.py:41
  91.7 9.1 %collective-permute-start.16 = (bf16[256,256]{1,0:T(8,128)(2,1)S(1)}, bf16[256,256]{1,0:T(8,128)(2,1)S(1)}, u32[]{:S(2)}, u32[]{:S(2)}) collective-permute-start(bf16[256,256]{1,0:T(8,128)(2,1)S(1)} %collective-permute-done.15.refs_4_), channel_id=1, source_target_pairs={{0,4},{4,8},{8,12},{12,16},{16,20},{20,24},{24,28},{28,0},{1,5},{5... | collective-permute-start | bytes 393224 | tf_op jit(solution)/shard_map/ppermute | solution.py:41
  91.7 9.1 %collective-permute-start.19 = (bf16[256,256]{1,0:T(8,128)(2,1)S(1)}, bf16[256,256]{1,0:T(8,128)(2,1)S(1)}, u32[]{:S(2)}, u32[]{:S(2)}) collective-permute-start(bf16[256,256]{1,0:T(8,128)(2,1)S(1)} %collective-permute-done.18.refs_7_), channel_id=1, source_target_pairs={{0,28},{4,0},{8,4},{12,8},{16,12},{20,16},{24,20},{28,24},{1,29},{... | collective-permute-start | bytes 393224 | tf_op jit(solution)/shard_map/ppermute | solution.py:41
  100.8 9.2 %collective-permute-start.17 = (bf16[256,256]{1,0:T(8,128)(2,1)S(1)}, bf16[256,256]{1,0:T(8,128)(2,1)S(1)}, u32[]{:S(2)}, u32[]{:S(2)}) collective-permute-start(bf16[256,256]{1,0:T(8,128)(2,1)S(1)} %collective-permute-done.16.refs_5_), channel_id=1, source_target_pairs={{0,4},{4,8},{8,12},{12,16},{16,20},{20,24},{24,28},{28,0},{1,5},{5... | collective-permute-start | bytes 393224 | tf_op jit(solution)/shard_map/ppermute | solution.py:41
  100.8 9.2 %collective-permute-start.20 = (bf16[256,256]{1,0:T(8,128)(2,1)S(1)}, bf16[256,256]{1,0:T(8,128)(2,1)S(1)}, u32[]{:S(2)}, u32[]{:S(2)}) collective-permute-start(bf16[256,256]{1,0:T(8,128)(2,1)S(1)} %collective-permute-done.19.refs_8_), channel_id=1, source_target_pairs={{0,28},{4,0},{8,4},{12,8},{16,12},{20,16},{24,20},{28,24},{1,29},{... | collective-permute-start | bytes 393224 | tf_op jit(solution)/shard_map/ppermute | solution.py:41
  109.9 10.8 %collective-permute-start.21 = (bf16[128,256]{1,0:T(8,128)(2,1)S(1)}, bf16[128,256]{1,0:T(8,128)(2,1)S(1)}, u32[]{:S(2)}, u32[]{:S(2)}) collective-permute-start(bf16[128,256]{1,0:T(8,128)(2,1)S(1)} %slice.60), channel_id=1, source_target_pairs={{0,4},{4,8},{8,12},{12,16},{16,20},{20,24},{24,28},{28,0},{1,5},{5... | collective-permute-start | bytes 196616 | tf_op jit(solution)/shard_map/ppermute | solution.py:41
  110.0 10.8 %collective-permute-start.22 = (bf16[128,256]{1,0:T(8,128)(2,1)S(1)}, bf16[128,256]{1,0:T(8,128)(2,1)S(1)}, u32[]{:S(2)}, u32[]{:S(2)}) collective-permute-start(bf16[128,256]{1,0:T(8,128)(2,1)S(1)} %slice.61), channel_id=1, source_target_pairs={{0,28},{4,0},{8,4},{12,8},{16,12},{20,16},{24,20},{28,24},{1,29},{... | collective-permute-start | bytes 196616 | tf_op jit(solution)/shard_map/ppermute | solution.py:41
  113.6 7.2 %copy-start.2 = (bf16[256,1024]{1,0:T(8,128)(2,1)S(1)}, bf16[256,1024]{1,0:T(8,128)(2,1)}, u32[]{:S(2)}) copy-start(bf16[256,1024]{1,0:T(8,128)(2,1)} %get-tuple-element.12.refs_0_) | copy-start | bytes 1572868
  113.6 7.2 %copy-start.3 = (bf16[256,256]{1,0:T(8,128)(2,1)S(1)}, bf16[256,256]{1,0:T(8,128)(2,1)}, u32[]{:S(2)}) copy-start(bf16[256,256]{1,0:T(8,128)(2,1)} %get-tuple-element.16.refs_3_) | copy-start | bytes 393220
Sparse Core Ops, SparseCore 0:
  67.5 43.9 all-gather.2

commit v3 on v2

--- a/solution.py
+++ b/solution.py
@@ -54,54 +54,132 @@
     return exchange(a[:half], 3), exchange(b[half:], 1)
 
 
-def key_value_kernel(shapes, mp_ref, *refs):
-    arrays = sum(count for _, count in shapes)
-    gain_ref, w_ref, cos_ref, sin_ref = refs[arrays : arrays + 4]
-    normed_ref, kv_ref = refs[-2:]
-    mp = mp_ref[0]
-    base = taken = 0
-    for rows, count in shapes:
-        own, one, three, *two = refs[taken : taken + count]
-        part = rows // len(two)
-        for n, two_part in enumerate(two):
+def normalise(mp, gain_ref, pieces, out_ref, rows):
+    total = 0.0
+    for piece in pieces:
+        wide = piece.astype(F32)
+        total = total + jnp.sum(wide * wide, axis=1, keepdims=True)
+    scale = lax.rsqrt(total * (1.0 / D) + eps)
+    for mask, piece in zip((0, 1, 3, 2), pieces):
+        columns = pl.ds(pl.multiple_of((mp ^ mask) * 1024, 1024), 1024)
+        value = piece.astype(F32) * scale * gain_ref[:, columns]
+        out_ref[rows, columns] = value.astype(BF16)
+
+
+def write_key_value(x, w_ref, cos, sin, out_ref, rows):
+    product = jnp.dot(x, w_ref[...], preferred_element_type=F32)
+    out_ref[rows, :HD] = rotate(product[:, :HD], cos, sin).astype(BF16)
+    out_ref[rows, HD:] = product[:, HD:].astype(BF16)
+
+
+def early_kernel(ids_ref, own, one, three, x3, x1, img, img_two, gain, w_kv, w_q, cos, sin, *refs):
+    normed_ref, out_ref, img_normed = refs[-3:]
+    text, img_rows = own.shape[0], img.shape[0]
+    part = text // 2
+    step = pl.program_id(0)
+    mp = ids_ref[0]
+
+    @pl.when(step == 0)
+    def _():
+        for n, two in enumerate((x3, x1)):
             span = pl.ds(n * part, part)
-            pieces = [(0, own[span, :]), (1, one[span, :]), (3, three[span, :]), (2, two_part[...])]
-            total = jnp.zeros((part, 1), F32)
-            for _, piece in pieces:
-                wide = piece.astype(F32)
-                total = total + jnp.sum(wide * wide, axis=1, keepdims=True)
-            scale = lax.rsqrt(total * (1.0 / D) + eps)
-            for mask, piece in pieces:
-                columns = pl.ds(pl.multiple_of((mp ^ mask) * 1024, 1024), 1024)
-                value = piece.astype(F32) * scale * gain_ref[:, columns]
-                normed_ref[pl.ds(base + n * part, part), columns] = value.astype(BF16)
-        base += rows
-        taken += count
-    product = jnp.dot(normed_ref[...], w_ref[...], preferred_element_type=F32)
-    kv_ref[:, :HD] = rotate(product[:, :HD], cos_ref[...], sin_ref[...]).astype(BF16)
-    kv_ref[:, HD:] = product[:, HD:].astype(BF16)
-
-
-def key_value(mp, groups, gain, w_kv, cosine, sine, after=()):
-    shapes = tuple((g[0].shape[0], len(g)) for g in groups)
-    rows = sum(size for size, _ in shapes)
-    arrays = [a for g in groups for a in g]
+            pieces = [own[span, :], one[span, :], three[span, :], two[:part, :]]
+            normalise(mp, gain, pieces, normed_ref, span)
+        pieces = [img[...], x1[part:, :], x3[part:, :], img_two[...]]
+        normalise(mp, gain, pieces, img_normed, slice(0, img_rows))
+        rows = slice(0, text)
+        write_key_value(normed_ref[...], w_kv, cos[rows, :], sin[rows, :], out_ref, rows)
+        rows = slice(text, text + img_rows)
+        write_key_value(img_normed[...], w_kv, cos[rows, :], sin[rows, :], out_ref, rows)
+
+    product = jnp.dot(img_normed[...], w_q[...], preferred_element_type=F32)
+    start = text + img_rows + step * img_rows
+    rows = pl.ds(pl.multiple_of(start, IMG_TOK), img_rows)
+    for h in range(2):
+        span = slice(h * HD, (h + 1) * HD)
+        turned = rotate(product[:, span], cos[text:, :], sin[text:, :])
+        out_ref[rows, span] = turned.astype(BF16)
+
+
+def early(ids, arrays, gain, w_kv, w_query, cosine, sine, after):
+    text, img_rows, tile = arrays[0].shape[0], arrays[5].shape[0], 2 * HD
+    steps = w_query.shape[1] // tile
+    whole = pl.BlockSpec(memory_space=VMEM)
     return pl.pallas_call(
-        functools.partial(key_value_kernel, shapes),
-        out_shape=(
+        early_kernel,
+        out_shape=[
+            jax.ShapeDtypeStruct((text, D), BF16),
+            jax.ShapeDtypeStruct((text + (1 + steps) * img_rows, tile), BF16),
+        ],
+        grid=(steps,),
+        in_specs=[pl.BlockSpec(memory_space=SMEM)]
+        + [whole] * (len(arrays) + 2)
+        + [pl.BlockSpec((D, tile), lambda n: (0, n))]
+        + [whole] * 2
+        + [pl.BlockSpec(memory_space=pl.ANY)] * len(after),
+        out_specs=[
+            pl.BlockSpec((text, D), lambda n: (0, 0)),
+            pl.BlockSpec((text + (1 + steps) * img_rows, tile), lambda n: (0, 0)),
+        ],
+        scratch_shapes=[pltpu.VMEM((img_rows, D), BF16)],
+        compiler_params=pltpu.CompilerParams(vmem_limit_bytes=58 * 2**20),
+        cost_estimate=pl.CostEstimate(flops=0, bytes_accessed=0, transcendentals=0),
+        name="early",
+    )(ids, *arrays, gain, w_kv, w_query, cosine, sine, *after)
+
+
+def late_kernel(ids_ref, own, one, three, two_lo, two_hi, gain, w_kv, cos, sin, normed_ref, out_ref):
+    part = own.shape[0] // 2
+    for n, two in enumerate((two_lo, two_hi)):
+        span = pl.ds(n * part, part)
+        pieces = [own[span, :], one[span, :], three[span, :], two[...]]
+        normalise(ids_ref[0], gain, pieces, normed_ref, span)
+    write_key_value(
+        normed_ref[...], w_kv, cos[...], sin[...], out_ref, slice(0, own.shape[0])
+    )
+
+
+def late(ids, arrays, gain, w_kv, cosine, sine):
+    rows = arrays[0].shape[0]
+    return pl.pallas_call(
+        late_kernel,
+        out_shape=[
             jax.ShapeDtypeStruct((rows, D), BF16),
             jax.ShapeDtypeStruct((rows, 2 * HD), BF16),
-        ),
+        ],
         in_specs=[pl.BlockSpec(memory_space=SMEM)]
-        + [pl.BlockSpec(memory_space=VMEM)] * (len(arrays) + 4)
-        + [pl.BlockSpec(memory_space=pl.ANY)] * len(after),
+        + [pl.BlockSpec(memory_space=VMEM)] * (len(arrays) + 4),
         out_specs=[pl.BlockSpec(memory_space=VMEM)] * 2,
         compiler_params=pltpu.CompilerParams(vmem_limit_bytes=58 * 2**20),
-        cost_estimate=pl.CostEstimate(
-            flops=0, bytes_accessed=0, transcendentals=0
-        ),
-        name="key_value",
-    )(mp, *arrays, gain, w_kv, cosine, sine, *after)
+        cost_estimate=pl.CostEstimate(flops=0, bytes_accessed=0, transcendentals=0),
+        name="late",
+    )(ids, *arrays, gain, w_kv, cosine, sine)
+
+
+def query_kernel(low_ref, high_ref, w_ref, cos_low, sin_low, cos_high, sin_high, q_ref):
+    half = low_ref.shape[0]
+    parts = ((low_ref, cos_low, sin_low), (high_ref, cos_high, sin_high))
+    for n, (x_ref, cos, sin) in enumerate(parts):
+        product = jnp.dot(x_ref[...], w_ref[...], preferred_element_type=F32)
+        for h in range(2):
+            span = slice(h * HD, (h + 1) * HD)
+            turned = rotate(product[:, span], cos[:half, :], sin[:half, :])
+            q_ref[n * half : (n + 1) * half, span] = turned.astype(BF16)
+
+
+def query(low, high, w_query, tables):
+    half, columns, tile = low.shape[0], w_query.shape[1], 2 * HD
+    whole = pl.BlockSpec(memory_space=VMEM)
+    return pl.pallas_call(
+        query_kernel,
+        out_shape=jax.ShapeDtypeStruct((2 * half, columns), BF16),
+        grid=(columns // tile,),
+        in_specs=[whole] * 2 + [pl.BlockSpec((D, tile), lambda n: (0, n))] + [whole] * 4,
+        out_specs=pl.BlockSpec((2 * half, tile), lambda n: (0, n)),
+        compiler_params=pltpu.CompilerParams(vmem_limit_bytes=58 * 2**20),
+        cost_estimate=pl.CostEstimate(flops=0, bytes_accessed=0, transcendentals=0),
+        name="query",
+    )(low, high, w_query, *tables)
 
 
 def images_before(counts_ref, sample):
@@ -111,86 +189,61 @@
     return total
 
 
-def query_kernel(text, x_ref, w_ref, cos_ref, sin_ref, q_ref, *img_ref):
-    product = jnp.dot(x_ref[...], w_ref[...], preferred_element_type=F32)
-    for h in range(2):
-        span = slice(h * HD, (h + 1) * HD)
-        turned = rotate(product[:, span], cos_ref[...], sin_ref[...]).astype(BF16)
-        q_ref[:, span] = turned[:text]
-        if img_ref:
-            img_ref[0][:, span] = turned[text:]
-
-
-def query(normed, w_query, cosine, sine, text):
-    rows, columns = normed.shape[0], w_query.shape[1]
-    tile = 2 * HD
-    img = rows - text
-    out_shape = [jax.ShapeDtypeStruct((text, columns), BF16)]
-    out_specs = [pl.BlockSpec((text, tile), lambda n: (0, n))]
-    if img:
-        out_shape.append(jax.ShapeDtypeStruct((img * (columns // tile), tile), BF16))
-        out_specs.append(pl.BlockSpec((img, tile), lambda n: (n, 0)))
-    return pl.pallas_call(
-        functools.partial(query_kernel, text),
-        out_shape=out_shape,
-        grid=(columns // tile,),
-        in_specs=[
-            pl.BlockSpec((rows, D), lambda n: (0, 0)),
-            pl.BlockSpec((D, tile), lambda n: (0, n)),
-            pl.BlockSpec((rows, HD // 2), lambda n: (0, 0)),
-            pl.BlockSpec((rows, HD // 2), lambda n: (0, 0)),
-        ],
-        out_specs=out_specs,
-        compiler_params=pltpu.CompilerParams(vmem_limit_bytes=58 * 2**20),
-        cost_estimate=pl.CostEstimate(flops=0, bytes_accessed=0, transcendentals=0),
-        name="query",
-    )(normed, w_query, cosine, sine)
-
-
-def image_start(counts_ref, starts_ref, sample, residue):
-    slot = (residue - images_before(counts_ref, sample)) & (MAX_IMG - 1)
-    return jnp.where(slot < counts_ref[sample], starts_ref[sample, slot], -1)
-
-
 def attention_kernel(tok, heads, ids_ref, counts_ref, starts_ref, *refs):
     half = tok // 2
     img_rows = IMG_TOK * (1 + heads // 2)
-    q_low, q_high, early, own, f1, f2, f3, b1, b2, b3, f4, b4, out_ref = refs[:13]
-    q_buf, kv_buf, img_buf, s_buf, max_buf, sum_buf, acc_buf, sems = refs[13:]
+    q_ref, own_e, own_l, f1, f2, f3, f4, f5, b1, b2, b3, b4, b5, out_ref = refs[:14]
+    q_buf, kv_buf, img_buf, s_buf, max_buf, sum_buf, acc_buf, sems = refs[14:]
     step = pl.program_id(0)
     ctx, sample = ids_ref[1], ids_ref[2]
     factor = math.log2(math.e) / math.sqrt(HD)
 
     @pl.when(step == 0)
     def _():
+        rows_e = own_e.shape[0]
+        cut = rows_e // 2
+        quarter = half // 2
+        early_parts = [
+            (0, own_e, 0, 0, rows_e),
+            (1, f1, 0, 0, rows_e),
+            (2, f2, 0, 0, rows_e),
+            (3, f3, 0, 0, rows_e),
+            (4, b4, half, 0, cut),
+            (4, f4, 0, cut, cut),
+            (5, b3, half, 0, rows_e),
+            (6, b2, half, 0, rows_e),
+            (7, b1, 0, 0, rows_e),
+        ]
+        late_parts = [
+            (0, own_l, 0, 0, half),
+            (1, f2, rows_e, 0, half),
+            (2, f3, rows_e, 0, half),
+            (3, f4, cut, 0, half),
+            (4, f5, 0, 0, quarter),
+            (4, b5, 0, quarter, quarter),
+            (5, b4, 0, 0, half),
+            (6, b3, 0, 0, half),
+            (7, b2, 0, 0, half),
+        ]
+        moves = [(q_ref, q_buf)]
+        for d, array, base, first, count in early_parts:
+            shard = (ctx - d) & (SHARDS - 1)
+            if first < half:
+                place = pl.ds(pl.multiple_of(shard * tok, tok), half)
+                moves.append((array.at[pl.ds(base, half), :], kv_buf.at[place, :]))
+            skip = max(half - first, 0)
+            place = pl.ds(first + skip - half, count - skip)
+            moves.append(
+                (array.at[pl.ds(base + skip, count - skip), :], img_buf.at[shard, place, :])
+            )
+        for d, array, base, first, count in late_parts:
+            shard = (ctx - d) & (SHARDS - 1)
+            place = pl.ds(pl.multiple_of(shard * tok + half + first, quarter), count)
+            moves.append((array.at[pl.ds(base, count), :], kv_buf.at[place, :]))
         copies = [
-            pltpu.make_async_copy(q_low, q_buf.at[pl.ds(0, half), :], sems.at[0]),
-            pltpu.make_async_copy(q_high, q_buf.at[pl.ds(half, half), :], sems.at[1]),
+            pltpu.make_async_copy(source, target, sems.at[n])
+            for n, (source, target) in enumerate(moves)
         ]
-        for c in range(SHARDS):
-            copies.append(
-                pltpu.make_async_copy(
-                    early.at[c, pl.ds(0, half), :],
-                    kv_buf.at[pl.ds(c * tok, half), :],
-                    sems.at[2 + 2 * c],
-                )
-            )
-            copies.append(
-                pltpu.make_async_copy(
-                    early.at[c, pl.ds(half, img_rows), :], img_buf.at[c], sems.at[3 + 2 * c]
-                )
-            )
-        used = 2 + 2 * SHARDS
-        cut = f4.shape[0]
-        pieces = [(0, own, 0), (1, f1, 0), (2, f2, 0), (3, f3, 0), (5, b3, 0), (6, b2, 0), (7, b1, 0)]
-        for n, (d, piece, offset) in enumerate(pieces + [(4, f4, 0), (4, b4, cut)]):
-            shard = (ctx - d) & (SHARDS - 1)
-            place = pl.multiple_of(shard * tok + half + offset, cut)
-            copies.append(
-                pltpu.make_async_copy(
-                    piece, kv_buf.at[pl.ds(place, piece.shape[0]), :], sems.at[used + n]
-                )
-            )
         for copy in copies:
             copy.start()
         for copy in copies:
@@ -284,7 +337,7 @@
             pltpu.VMEM((2, tok, HD), F32),
             pltpu.VMEM((tok, HD), F32),
             pltpu.VMEM((tok, HD), F32),
-            pltpu.SemaphoreType.DMA((2 + 2 * SHARDS + 9,)),
+            pltpu.SemaphoreType.DMA((32,)),
         ],
         compiler_params=pltpu.CompilerParams(vmem_limit_bytes=52 * 2**20),
         cost_estimate=pl.CostEstimate(
@@ -328,12 +381,13 @@
     low, high = text_rows[:half], text_rows[half:]
     routed = [visual_rows] + [shift(visual_rows, "dp", 2 * d, False) for d in (1, 2, 3)]
     a_low, b_low = first_hop(low)
+    a_high, b_high = first_hop(high)
     for_other = choose(its_distance, routed)
     from_other = lax.ppermute(for_other, "dp", [(i, i ^ 1) for i in range(SHARDS)])
     image = choose(jnp.where(my_across == 1, 4, my_distance), routed + [from_other])
-    a_img, b_img, c_img = (exchange(image, mask) for mask in (1, 3, 2))
-    a_high, b_high = first_hop(high)
-    c_low, d_low = second_hop(a_low, b_low)
+    x3 = exchange(jnp.concatenate([a_low[: half // 2], image], axis=0), 3)
+    x1 = exchange(jnp.concatenate([b_low[half // 2 :], image], axis=0), 1)
+    img_two = exchange(image, 2)
     c_high, d_high = second_hop(a_high, b_high)
 
     mine = (every[:, None] == sample) & (every[None, :] == my_slot)
@@ -346,28 +400,29 @@
     )
     cosine, sine = rotary_tables(positions)
     first = half + IMG_TOK
-    mp_arr = ids[:1]
-
-    normed, kv = key_value(
-        mp_arr,
-        [(low, a_low, b_low, c_low, d_low), (image, a_img, b_img, c_img)],
-        gain, w_kv, cosine[:first], sine[:first], (a_high, b_high),
-    )
-    q_low, q_img = query(normed, w_query, cosine[:first], sine[:first], half)
-    early = lax.all_gather(jnp.concatenate([kv, q_img], axis=0), "ctx", axis=0)
-    normed_high, own = key_value(
-        mp_arr, [(high, a_high, b_high, c_high, d_high)], gain, w_kv, cosine[first:], sine[first:],
-        (q_img,),
-    )
-    cut = half // 2
-    f1, b1 = shift(own, "ctx", 1, True), shift(own, "ctx", -1, True)
-    f2, b2 = shift(f1, "ctx", 1, True), shift(b1, "ctx", -1, True)
+    tables_e = (cosine[:first], sine[:first])
+    tables_l = (cosine[first:], sine[first:])
+    normed_low, own_e = early(
+        ids, [low, a_low, b_low, x3, x1, image, img_two], gain, w_kv, w_query, *tables_e,
+        (a_high, b_high),
+    )
+    normed_high, own_l = late(
+        ids, [high, a_high, b_high, c_high, d_high], gain, w_kv, *tables_l
+    )
+    q_all = query(normed_low, normed_high, w_query, tables_e + tables_l)
+
+    cut = own_e.shape[0] // 2
+    quarter = half // 2
+    f1, b1 = shift(own_e, "ctx", 1, True), shift(own_e, "ctx", -1, True)
+    f2 = shift(jnp.concatenate([f1, own_l], axis=0), "ctx", 1, True)
+    b2 = shift(jnp.concatenate([own_l, b1], axis=0), "ctx", -1, True)
     f3, b3 = shift(f2, "ctx", 1, True), shift(b2, "ctx", -1, True)
-    f4, b4 = shift(f3[:cut], "ctx", 1, True), shift(b3[cut:], "ctx", -1, True)
-    (q_high,) = query(normed_high, w_query, cosine[first:], sine[first:], half)
+    f4, b4 = shift(f3[cut:], "ctx", 1, True), shift(b3[: half + cut], "ctx", -1, True)
+    f5 = shift(f4[cut : cut + quarter], "ctx", 1, True)
+    b5 = shift(b4[quarter:half], "ctx", -1, True)
     return attention(
         tok, heads, (ids, image_counts, image_starts),
-        [q_low, q_high, early, own, f1, f2, f3, b1, b2, b3, f4, b4],
+        [q_all, own_e, own_l, f1, f2, f3, f4, f5, b1, b2, b3, b4, b5],
     )
 
 

time: 161 us -> 156 us (0.969)
  the two profiles are of different devices: /device:TPU:128 before, /device:TPU:224 now
where the time goes in v3:
time: 156 us; the launch traced here: 153 us
  Pallas kernels  58.7 us (38%)
  starting transfers between devices  37 us (24%)
  waiting for transfers between devices  32 us (21%)
  local copies, waits for them, and re-layouts  15.1 us (10%)
  other arithmetic  7.59 us (5%)
  between operations  3.03 us (2%)
    pallas_call x1, Pallas kernels, attention(): pl.pallas_call(functools.partial(attention_kernel, tok, heads), out_shape...  34 us
    ppermute x13, starting transfers between devices, shift(): return lax.ppermute(x, axis, pairs)  24.6 us
    ppermute x13, waiting for transfers between devices, shift(): return lax.ppermute(x, axis, pairs)  19.6 us
    ppermute x9, waiting for transfers between devices, exchange(): return lax.ppermute(x, 'mp', [(i, i ^ mask) for i in range(4)])  12.4 us
    ppermute x9, starting transfers between devices, exchange(): return lax.ppermute(x, 'mp', [(i, i ^ mask) for i in range(4)])  12.4 us
    pallas_call x1, Pallas kernels, early(): pl.pallas_call(early_kernel, out_shape=[jax.ShapeDtypeStruct((text, D), B...  10.2 us
    pallas_call x1, Pallas kernels, query(): pl.pallas_call(query_kernel, out_shape=jax.ShapeDtypeStruct((2 * half, co...  9.76 us
    pallas_call x1, Pallas kernels, late(): pl.pallas_call(late_kernel, out_shape=[jax.ShapeDtypeStruct((rows, D), BF...  4.79 us
  transfers between devices with their start and end apart: 23, of which 8 were waited for; matrix products, arithmetic and copies ran while one was open for 12% of the time, Pallas kernels for 9%

profile of v3, /device:TPU:224, one launch (start us, length us, event | category | flops | bytes accessed | tf_op | source)
XLA Modules:
  0.0 153.4 jit_solution(16442588944119433570)
XLA Ops:
  0.0 2.3 %fusion.2 = (bf16[256,1024]{1,0:T(8,128)(2,1)}, bf16[256,1024]{1,0:T(8,128)(2,1)}) fusion(bf16[512,1024]{1,0:T(8,128)(2,1)} %param.8), kind=kLoop, calls=%fused_computation.22 | loop fusion | bytes 2097152 | tf_op jit(solution)/shard_map/slice | solution.py:381
  2.3 1.5 collective-permute-start
  3.8 2.1 %collective-permute-start.1 = (bf16[256,1024]{1,0:T(8,128)(2,1)}, bf16[256,1024]{1,0:T(8,128)(2,1)}, u32[]{:S(2)}, u32[]{:S(2)}) collective-permute-start(bf16[256,1024]{1,0:T(8,128)(2,1)} %get-tuple-element.16.own), channel_id=1, source_target_pairs={{0,3},{1,2},{2,1},{3,0},{4,7},{5,6},{6,5},{7,4},{8,11},{9,10},{10,... | collective-permute-start | bytes 1572872 | tf_op jit(solution)/shard_map/ppermute | solution.py:45
  5.9 4.9 %collective-permute-start.2 = (bf16[64,1024]{1,0:T(8,128)(2,1)S(1)}, bf16[64,1024]{1,0:T(8,128)(2,1)S(1)}, u32[]{:S(2)}, u32[]{:S(2)}) collective-permute-start(bf16[64,1024]{1,0:T(8,128)(2,1)S(1)} %copy-done.10), channel_id=1, source_target_pairs={{0,192},{32,224},{1,193},{33,225},{2,194},{34,226},{3,195},{35,227... | collective-permute-start | bytes 393224 | tf_op jit(solution)/shard_map/ppermute | solution.py:41
  10.9 1.3 collective-permute-start.3
  12.2 3.4 %collective-permute-start.4 = (bf16[64,1024]{1,0:T(8,128)(2,1)S(1)}, bf16[64,1024]{1,0:T(8,128)(2,1)}, u32[]{:S(2)}, u32[]{:S(2)}) collective-permute-start(bf16[64,1024]{1,0:T(8,128)(2,1)S(1)} %copy-done.10), channel_id=1, source_target_pairs={{0,64},{32,96},{64,128},{96,160},{128,192},{160,224},{1,65},{33,97... | collective-permute-start | bytes 393224 | tf_op jit(solution)/shard_map/ppermute | solution.py:41
  15.6 0.2 constant_dynamic-update-slice_fusion.1
  15.8 1.5 constant_dynamic-update-slice_fusion.w_kv
  17.3 0.9 fusion
  20.0 0.0 collective-permute-done.2
  20.0 0.7 collective-permute-start.9
  20.7 0.0 collective-permute-done.3
  20.7 0.7 collective-permute-start.10
  21.4 0.0 collective-permute-done.4
  21.4 0.7 select_select_fusion.1
  22.1 0.0 collective-permute-start.5
  22.1 0.7 select_reduce_fusion
  23.4 0.6 select_convert_fusion
  24.0 0.0 collective-permute-done.5
  24.0 0.1 select_select_fusion.img
  24.1 1.0 slice.57
  25.2 0.0 collective-permute-done.one
  25.2 1.0 slice.56
  26.1 1.0 pad_maximum_fusion
  27.1 2.6 %collective-permute-start.6 = (bf16[192,1024]{1,0:T(8,128)(2,1)}, bf16[192,1024]{1,0:T(8,128)(2,1)}, u32[]{:S(2)}, u32[]{:S(2)}) collective-permute-start(bf16[192,1024]{1,0:T(8,128)(2,1)} %get-tuple-element.20), channel_id=1, source_target_pairs={{0,3},{1,2},{2,1},{3,0},{4,7},{5,6},{6,5},{7,4},{8,11},{9,10},{10,... | collective-permute-start | bytes 1179656 | tf_op jit(solution)/shard_map/ppermute | solution.py:45
  29.7 0.2 collective-permute-start.7
  29.9 1.9 %collective-permute-start.8 = (bf16[64,1024]{1,0:T(8,128)(2,1)S(1)}, bf16[64,1024]{1,0:T(8,128)(2,1)S(1)}, u32[]{:S(2)}, u32[]{:S(2)}) collective-permute-start(bf16[64,1024]{1,0:T(8,128)(2,1)S(1)} %select_select_fusion.img), channel_id=1, source_target_pairs={{0,2},{1,3},{2,0},{3,1},{4,6},{5,7},{6,4},{7,5},{8,10},{9,11},{10,... | collective-permute-start | bytes 393224 | tf_op jit(solution)/shard_map/ppermute | solution.py:45
  31.8 2.0 %multiply_sine_fusion = (f32[576,64]{1,0:T(8,128)}, f32[576,64]{1,0:T(8,128)}) fusion(f32[64]{0:T(128)S(1)} %multiply_exponential_fusion, f32[576]{0:T(1024)S(1)} %select_convert_fusion), kind=kLoop, calls=%fused_computation.4 | loop fusion | flops 36864 | bytes 297472 | tf_op jit(solution)/shard_map/sin | solution.py:30
  33.8 1.6 %slice.58.cos.cos_low = f32[320,64]{1,0:T(8,128)} slice(f32[576,64]{1,0:T(8,128)} %get-tuple-element.22), slice={[0:320], [0:64]} | slice | bytes 163840 | tf_op jit(solution)/shard_map/slice | solution.py:403
  35.4 1.6 %slice.59.sin.sin_low = f32[320,64]{1,0:T(8,128)} slice(f32[576,64]{1,0:T(8,128)} %get-tuple-element.21), slice={[0:320], [0:64]} | slice | bytes 163840 | tf_op jit(solution)/shard_map/slice | solution.py:403
  37.0 0.7 pad_add_fusion.ids_ref
  37.7 7.1 %collective-permute-done.8.img_two = bf16[64,1024]{1,0:T(8,128)(2,1)S(1)} collective-permute-done((bf16[64,1024]{1,0:T(8,128)(2,1)S(1)}, bf16[64,1024]{1,0:T(8,128)(2,1)S(1)}, u32[]{:S(2)}, u32[]{:S(2)}) %collective-permute-start.8) | collective-permute-done | bytes 131104 | tf_op jit(solution)/shard_map/ppermute | solution.py:45
  44.8 0.0 collective-permute-done.9.refs_0_.one
  44.8 0.0 collective-permute-done.10.refs_1_.three
  44.8 1.0 collective-permute-done.6.x3
  45.8 0.0 collective-permute-done.7.x1
  45.8 10.2 %early.1 = (bf16[256,4096]{1,0:T(8,128)(2,1)}, bf16[576,256]{1,0:T(8,128)(2,1)}) custom-call(s32[3]{0:T(128)} %pad_add_fusion.ids_ref, bf16[256,1024]{1,0:T(8,128)(2,1)} %get-tuple-element.16.own, bf16[256,1024]{1,0:T(8,128)(2,1)} %collective-permute-done.one, bf16[256,1024]{1,0:T(8,128)(2,1)} %collective-permute-done.1.three, ...), custom_call_target="tpu_custom_call" | custom-call | tf_op jit(solution)/shard_map/early/pallas_call | solution.py:108
  56.0 0.0 collective-permute-start.13
  56.0 2.0 %collective-permute-start.18 = (bf16[576,256]{1,0:T(8,128)(2,1)}, bf16[576,256]{1,0:T(8,128)(2,1)S(1)}, u32[]{:S(2)}, u32[]{:S(2)}) collective-permute-start(bf16[576,256]{1,0:T(8,128)(2,1)} %get-tuple-element.11.refs_1_), channel_id=1, source_target_pairs={{0,28},{4,0},{8,4},{12,8},{16,12},{20,16},{24,20},{28,24},{1,29},{... | collective-permute-start | bytes 884744 | tf_op jit(solution)/shard_map/ppermute | solution.py:41
  58.0 1.0 slice.60
  59.0 2.5 %collective-permute-start.11 = (bf16[128,1024]{1,0:T(8,128)(2,1)S(1)}, bf16[128,1024]{1,0:T(8,128)(2,1)S(1)}, u32[]{:S(2)}, u32[]{:S(2)}) collective-permute-start(bf16[128,1024]{1,0:T(8,128)(2,1)S(1)} %slice.60), channel_id=1, source_target_pairs={{0,3},{1,2},{2,1},{3,0},{4,7},{5,6},{6,5},{7,4},{8,11},{9,10},{10,... | collective-permute-start | bytes 786440 | tf_op jit(solution)/shard_map/ppermute | solution.py:45
  61.5 1.0 slice.61
  62.5 0.3 collective-permute-start.12
  62.8 1.6 %slice.62.cos.cos_high = f32[256,64]{1,0:T(8,128)} slice(f32[576,64]{1,0:T(8,128)} %get-tuple-element.22), slice={[320:576], [0:64]} | slice | bytes 131072 | tf_op jit(solution)/shard_map/slice | solution.py:404
  64.4 1.6 %slice.63.sin.sin_high = f32[256,64]{1,0:T(8,128)} slice(f32[576,64]{1,0:T(8,128)} %get-tuple-element.21), slice={[320:576], [0:64]} | slice | bytes 131072 | tf_op jit(solution)/shard_map/slice | solution.py:404
  65.9 2.1 %collective-permute-done.11.two_lo = bf16[128,1024]{1,0:T(8,128)(2,1)S(1)} collective-permute-done((bf16[128,1024]{1,0:T(8,128)(2,1)S(1)}, bf16[128,1024]{1,0:T(8,128)(2,1)S(1)}, u32[]{:S(2)}, u32[]{:S(2)}) %collective-permute-start.11) | collective-permute-done | bytes 262176 | tf_op jit(solution)/shard_map/ppermute | solution.py:45
  68.0 2.3 %collective-permute-done.12.two_hi = bf16[128,1024]{1,0:T(8,128)(2,1)S(1)} collective-permute-done((bf16[128,1024]{1,0:T(8,128)(2,1)S(1)}, bf16[128,1024]{1,0:T(8,128)(2,1)S(1)}, u32[]{:S(2)}, u32[]{:S(2)}) %collective-permute-start.12) | collective-permute-done | bytes 262176 | tf_op jit(solution)/shard_map/ppermute | solution.py:45
  70.3 0.7 copy-done.13
  71.0 4.8 %late.1 = (bf16[256,4096]{1,0:T(8,128)(2,1)}, bf16[256,256]{1,0:T(8,128)(2,1)}) custom-call(s32[3]{0:T(128)} %pad_add_fusion.ids_ref, bf16[256,1024]{1,0:T(8,128)(2,1)} %get-tuple-element.15.own, bf16[256,1024]{1,0:T(8,128)(2,1)} %copy-done.6, bf16[256,1024]{1,0:T(8,128)(2,1)} %copy-done.7, bf16[128,1024]{1,0:T(8,128)(2,1)} %copy-done.12, ...), custom_call_target="tpu_custom_call" | custom-call | tf_op jit(solution)/shard_map/late/pallas_call | solution.py:144
  75.8 1.1 pad_maximum_fusion.3
  76.8 1.6 %collective-permute-start.14 = (bf16[832,256]{1,0:T(8,128)(2,1)S(1)}, bf16[832,256]{1,0:T(8,128)(2,1)S(1)}, u32[]{:S(2)}, u32[]{:S(2)}) collective-permute-start(bf16[832,256]{1,0:T(8,128)(2,1)S(1)} %get-tuple-element.18), channel_id=1, source_target_pairs={{0,4},{4,8},{8,12},{12,16},{16,20},{20,24},{24,28},{28,0},{1,5},{5... | collective-permute-start | bytes 1277960 | tf_op jit(solution)/shard_map/ppermute | solution.py:41
  78.5 0.5 collective-permute-start.19
  78.9 8.0 %collective-permute-done.14.refs_4_ = bf16[832,256]{1,0:T(8,128)(2,1)S(1)} collective-permute-done((bf16[832,256]{1,0:T(8,128)(2,1)S(1)}, bf16[832,256]{1,0:T(8,128)(2,1)S(1)}, u32[]{:S(2)}, u32[]{:S(2)}) %collective-permute-start.14) | collective-permute-done | bytes 426016 | tf_op jit(solution)/shard_map/ppermute | solution.py:41
  87.0 3.1 %collective-permute-start.15 = (bf16[832,256]{1,0:T(8,128)(2,1)S(1)}, bf16[832,256]{1,0:T(8,128)(2,1)S(1)}, u32[]{:S(2)}, u32[]{:S(2)}) collective-permute-start(bf16[832,256]{1,0:T(8,128)(2,1)S(1)} %collective-permute-done.14.refs_4_), channel_id=1, source_target_pairs={{0,4},{4,8},{8,12},{12,16},{16,20},{20,24},{24,28},{28,0},{1,5},{5... | collective-permute-start | bytes 1277960 | tf_op jit(solution)/shard_map/ppermute | solution.py:41
  90.1 0.0 collective-permute-done.19.refs_9_
  90.1 7.0 %collective-permute-done.15.refs_5_ = bf16[832,256]{1,0:T(8,128)(2,1)S(1)} collective-permute-done((bf16[832,256]{1,0:T(8,128)(2,1)S(1)}, bf16[832,256]{1,0:T(8,128)(2,1)S(1)}, u32[]{:S(2)}, u32[]{:S(2)}) %collective-permute-start.15) | collective-permute-done | bytes 426016 | tf_op jit(solution)/shard_map/ppermute | solution.py:41
  97.1 3.8 %collective-permute-start.16 = (bf16[544,256]{1,0:T(8,128)(2,1)S(1)}, bf16[544,256]{1,0:T(8,128)(2,1)S(1)}, u32[]{:S(2)}, u32[]{:S(2)}) collective-permute-start(bf16[544,256]{1,0:T(8,128)(2,1)S(1)} %slice.64), channel_id=1, source_target_pairs={{0,4},{4,8},{8,12},{12,16},{16,20},{20,24},{24,28},{28,0},{1,5},{5... | collective-permute-start | bytes 835592 | tf_op jit(solution)/shard_map/ppermute | solution.py:41
  100.9 0.1 collective-permute-start.21
  100.9 4.4 %collective-permute-done.16.refs_6_ = bf16[544,256]{1,0:T(8,128)(2,1)S(1)} collective-permute-done((bf16[544,256]{1,0:T(8,128)(2,1)S(1)}, bf16[544,256]{1,0:T(8,128)(2,1)S(1)}, u32[]{:S(2)}, u32[]{:S(2)}) %collective-permute-start.16) | collective-permute-done | bytes 278560 | tf_op jit(solution)/shard_map/ppermute | solution.py:41
  105.4 3.7 %collective-permute-start.17 = (bf16[128,256]{1,0:T(8,128)(2,1)S(1)}, bf16[128,256]{1,0:T(8,128)(2,1)S(1)}, u32[]{:S(2)}, u32[]{:S(2)}) collective-permute-start(bf16[128,256]{1,0:T(8,128)(2,1)S(1)} %slice.65), channel_id=1, source_target_pairs={{0,4},{4,8},{8,12},{12,16},{16,20},{20,24},{24,28},{28,0},{1,5},{5... | collective-permute-start | bytes 196616 | tf_op jit(solution)/shard_map/ppermute | solution.py:41
  109.1 0.2 collective-permute-done.21.refs_11_
  109.2 0.2 collective-permute-start.22
  109.4 9.8 %query.1.refs_0_ = bf16[512,1024]{1,0:T(8,128)(2,1)} custom-call(bf16[256,4096]{1,0:T(8,128)(2,1)} %get-tuple-element.9.low_ref, bf16[256,4096]{1,0:T(8,128)(2,1)} %get-tuple-element.10.high_ref, bf16[4096,1024]{1,0:T(8,128)(2,1)} %w_ref.1, f32[320,64]{1,0:T(8,128)} %slice.58.cos.cos_low, f32[320,64]{1,0:T(8,128)} %slice.59.sin.sin_low, ...), custom_call_target="tpu_custom_call" | custom-call | tf_op jit(solution)/shard_map/query/pallas_call | solution.py:173
  119.3 34.0 %attention.1 = bf16[512,1024]{1,0:T(8,128)(2,1)} custom-call(s32[3]{0:T(128)S(1)} %copy-done.1, s32[8]{0:T(128)S(1)} %copy-done.3, s32[8,8]{1,0:T(8,128)S(1)} %copy-done.2, bf16[512,1024]{1,0:T(8,128)(2,1)} %query.1.refs_0_, bf16[576,256]{1,0:T(8,128)(2,1)S(1)} %copy-done.4, bf16[256,256]{1,0:T(8,128)(2,1)S(1)} %copy-done, ...), custom_call_target="tpu_custom_call" | custom-call | flops 8589934592 | bytes 8388608 | tf_op jit(solution)/shard_map/attention/pallas_call | solution.py:325
  (50 shorter events, 0.2 us)
Async XLA Ops:
  0.0 5.9 %copy-start.10 = (bf16[64,1024]{1,0:T(8,128)(2,1)S(1)}, bf16[64,1024]{1,0:T(8,128)(2,1)}, u32[]{:S(2)}) copy-start(bf16[64,1024]{1,0:T(8,128)(2,1)} %param.9) | copy-start | bytes 393220
  0.0 15.6 %copy-start.9 = (bf16[4096,128]{1,0:T(8,128)(2,1)S(1)}, bf16[4096,128]{1,0:T(8,128)(2,1)}, u32[]{:S(2)}) copy-start(bf16[4096,128]{1,0:T(8,128)(2,1)} %param.14) | copy-start | bytes 3145732
  2.3 22.8 %collective-permute-start = (bf16[256,1024]{1,0:T(8,128)(2,1)}, bf16[256,1024]{1,0:T(8,128)(2,1)}, u32[]{:S(2)}, u32[]{:S(2)}) collective-permute-start(bf16[256,1024]{1,0:T(8,128)(2,1)} %get-tuple-element.16.own), channel_id=1, source_target_pairs={{0,1},{1,0},{2,3},{3,2},{4,5},{5,4},{6,7},{7,6},{8,9},{9,8},{10,11... | collective-permute-start | bytes 1572872 | tf_op jit(solution)/shard_map/ppermute | solution.py:45
  3.8 20.3 %collective-permute-start.1 = (bf16[256,1024]{1,0:T(8,128)(2,1)}, bf16[256,1024]{1,0:T(8,128)(2,1)}, u32[]{:S(2)}, u32[]{:S(2)}) collective-permute-start(bf16[256,1024]{1,0:T(8,128)(2,1)} %get-tuple-element.16.own), channel_id=1, source_target_pairs={{0,3},{1,2},{2,1},{3,0},{4,7},{5,6},{6,5},{7,4},{8,11},{9,10},{10,... | collective-permute-start | bytes 1572872 | tf_op jit(solution)/shard_map/ppermute | solution.py:45
  5.9 14.1 %collective-permute-start.2 = (bf16[64,1024]{1,0:T(8,128)(2,1)S(1)}, bf16[64,1024]{1,0:T(8,128)(2,1)S(1)}, u32[]{:S(2)}, u32[]{:S(2)}) collective-permute-start(bf16[64,1024]{1,0:T(8,128)(2,1)S(1)} %copy-done.10), channel_id=1, source_target_pairs={{0,192},{32,224},{1,193},{33,225},{2,194},{34,226},{3,195},{35,227... | collective-permute-start | bytes 393224 | tf_op jit(solution)/shard_map/ppermute | solution.py:41
  10.9 9.9 %collective-permute-start.3 = (bf16[64,1024]{1,0:T(8,128)(2,1)S(1)}, bf16[64,1024]{1,0:T(8,128)(2,1)S(1)}, u32[]{:S(2)}, u32[]{:S(2)}) collective-permute-start(bf16[64,1024]{1,0:T(8,128)(2,1)S(1)} %copy-done.10), channel_id=1, source_target_pairs={{0,128},{32,160},{64,192},{96,224},{1,129},{33,161},{65,193},{97,2... | collective-permute-start | bytes 393224 | tf_op jit(solution)/shard_map/ppermute | solution.py:41
  12.2 9.2 %collective-permute-start.4 = (bf16[64,1024]{1,0:T(8,128)(2,1)S(1)}, bf16[64,1024]{1,0:T(8,128)(2,1)}, u32[]{:S(2)}, u32[]{:S(2)}) collective-permute-start(bf16[64,1024]{1,0:T(8,128)(2,1)S(1)} %copy-done.10), channel_id=1, source_target_pairs={{0,64},{32,96},{64,128},{96,160},{128,192},{160,224},{1,65},{33,97... | collective-permute-start | bytes 393224 | tf_op jit(solution)/shard_map/ppermute | solution.py:41
  15.6 1.7 %copy-start.3 = (s32[8]{0:T(128)S(1)}, s32[8]{0:T(128)}, u32[]{:S(2)}) copy-start(s32[8]{0:T(128)} %counts_ref.1) | copy-start | bytes 100
  15.6 6.5 %copy-start.2 = (s32[8,8]{1,0:T(8,128)S(1)}, s32[8,8]{1,0:T(8,128)}, u32[]{:S(2)}) copy-start(s32[8,8]{1,0:T(8,128)} %starts_ref.1) | copy-start | bytes 772
  17.3 16.5 %copy-start.5 = (bf16[4096,256]{1,0:T(8,128)(2,1)}, bf16[4096,256]{1,0:T(8,128)(2,1)S(1)}, u32[]{:S(2)}) copy-start(bf16[4096,256]{1,0:T(8,128)(2,1)S(1)} %constant_dynamic-update-slice_fusion.w_kv) | copy-start | bytes 6291460
  20.0 24.7 %collective-permute-start.9 = (bf16[256,1024]{1,0:T(8,128)(2,1)}, bf16[256,1024]{1,0:T(8,128)(2,1)S(1)}, u32[]{:S(2)}, u32[]{:S(2)}) collective-permute-start(bf16[256,1024]{1,0:T(8,128)(2,1)} %get-tuple-element.15.own), channel_id=1, source_target_pairs={{0,1},{1,0},{2,3},{3,2},{4,5},{5,4},{6,7},{7,6},{8,9},{9,8},{10,11... | collective-permute-start | bytes 1572872 | tf_op jit(solution)/shard_map/ppermute | solution.py:45
  20.7 3.3 %copy-start.11 = (bf16[64,1024]{1,0:T(8,128)(2,1)}, bf16[64,1024]{1,0:T(8,128)(2,1)S(1)}, u32[]{:S(2)}) copy-start(bf16[64,1024]{1,0:T(8,128)(2,1)S(1)} %collective-permute-done.3) | copy-start | bytes 393220
  20.7 24.0 %collective-permute-start.10 = (bf16[256,1024]{1,0:T(8,128)(2,1)}, bf16[256,1024]{1,0:T(8,128)(2,1)S(1)}, u32[]{:S(2)}, u32[]{:S(2)}) collective-permute-start(bf16[256,1024]{1,0:T(8,128)(2,1)} %get-tuple-element.15.own), channel_id=1, source_target_pairs={{0,3},{1,2},{2,1},{3,0},{4,7},{5,6},{6,5},{7,4},{8,11},{9,10},{10,... | collective-permute-start | bytes 1572872 | tf_op jit(solution)/shard_map/ppermute | solution.py:45
  22.1 1.9 %collective-permute-start.5 = (bf16[64,1024]{1,0:T(8,128)(2,1)}, bf16[64,1024]{1,0:T(8,128)(2,1)}, u32[]{:S(2)}, u32[]{:S(2)}) collective-permute-start(bf16[64,1024]{1,0:T(8,128)(2,1)} %select_select_fusion.1), channel_id=1, source_target_pairs={{0,32},{32,0},{64,96},{96,64},{128,160},{160,128},{192,224},{224,1... | collective-permute-start | bytes 393224 | tf_op jit(solution)/shard_map/ppermute | solution.py:386
  24.1 21.6 %copy-start.8 = (bf16[64,1024]{1,0:T(8,128)(2,1)}, bf16[64,1024]{1,0:T(8,128)(2,1)S(1)}, u32[]{:S(2)}) copy-start(bf16[64,1024]{1,0:T(8,128)(2,1)S(1)} %select_select_fusion.img) | copy-start | bytes 393220
  27.1 18.6 %collective-permute-start.6 = (bf16[192,1024]{1,0:T(8,128)(2,1)}, bf16[192,1024]{1,0:T(8,128)(2,1)}, u32[]{:S(2)}, u32[]{:S(2)}) collective-permute-start(bf16[192,1024]{1,0:T(8,128)(2,1)} %get-tuple-element.20), channel_id=1, source_target_pairs={{0,3},{1,2},{2,1},{3,0},{4,7},{5,6},{6,5},{7,4},{8,11},{9,10},{10,... | collective-permute-start | bytes 1179656 | tf_op jit(solution)/shard_map/ppermute | solution.py:45
  29.7 16.1 %collective-permute-start.7 = (bf16[192,1024]{1,0:T(8,128)(2,1)}, bf16[192,1024]{1,0:T(8,128)(2,1)}, u32[]{:S(2)}, u32[]{:S(2)}) collective-permute-start(bf16[192,1024]{1,0:T(8,128)(2,1)} %get-tuple-element.19), channel_id=1, source_target_pairs={{0,1},{1,0},{2,3},{3,2},{4,5},{5,4},{6,7},{7,6},{8,9},{9,8},{10,11... | collective-permute-start | bytes 1179656 | tf_op jit(solution)/shard_map/ppermute | solution.py:45
  29.9 14.8 %collective-permute-start.8 = (bf16[64,1024]{1,0:T(8,128)(2,1)S(1)}, bf16[64,1024]{1,0:T(8,128)(2,1)S(1)}, u32[]{:S(2)}, u32[]{:S(2)}) collective-permute-start(bf16[64,1024]{1,0:T(8,128)(2,1)S(1)} %select_select_fusion.img), channel_id=1, source_target_pairs={{0,2},{1,3},{2,0},{3,1},{4,6},{5,7},{6,4},{7,5},{8,10},{9,11},{10,... | collective-permute-start | bytes 393224 | tf_op jit(solution)/shard_map/ppermute | solution.py:45
  44.8 1.0 copy-start.16
  44.8 1.0 copy-start.6
  44.8 1.0 copy-start.7
  56.0 19.7 %collective-permute-start.13 = (bf16[576,256]{1,0:T(8,128)(2,1)}, bf16[576,256]{1,0:T(8,128)(2,1)S(1)}, u32[]{:S(2)}, u32[]{:S(2)}) collective-permute-start(bf16[576,256]{1,0:T(8,128)(2,1)} %get-tuple-element.11.refs_1_), channel_id=1, source_target_pairs={{0,4},{4,8},{8,12},{12,16},{16,20},{20,24},{24,28},{28,0},{1,5},{5... | collective-permute-start | bytes 884744 | tf_op jit(solution)/shard_map/ppermute | solution.py:41
  56.0 19.7 %collective-permute-start.18 = (bf16[576,256]{1,0:T(8,128)(2,1)}, bf16[576,256]{1,0:T(8,128)(2,1)S(1)}, u32[]{:S(2)}, u32[]{:S(2)}) collective-permute-start(bf16[576,256]{1,0:T(8,128)(2,1)} %get-tuple-element.11.refs_1_), channel_id=1, source_target_pairs={{0,28},{4,0},{8,4},{12,8},{16,12},{20,16},{24,20},{28,24},{1,29},{... | collective-permute-start | bytes 884744 | tf_op jit(solution)/shard_map/ppermute | solution.py:41
  59.0 9.0 %collective-permute-start.11 = (bf16[128,1024]{1,0:T(8,128)(2,1)S(1)}, bf16[128,1024]{1,0:T(8,128)(2,1)S(1)}, u32[]{:S(2)}, u32[]{:S(2)}) collective-permute-start(bf16[128,1024]{1,0:T(8,128)(2,1)S(1)} %slice.60), channel_id=1, source_target_pairs={{0,3},{1,2},{2,1},{3,0},{4,7},{5,6},{6,5},{7,4},{8,11},{9,10},{10,... | collective-permute-start | bytes 786440 | tf_op jit(solution)/shard_map/ppermute | solution.py:45
  62.5 7.8 %collective-permute-start.12 = (bf16[128,1024]{1,0:T(8,128)(2,1)S(1)}, bf16[128,1024]{1,0:T(8,128)(2,1)S(1)}, u32[]{:S(2)}, u32[]{:S(2)}) collective-permute-start(bf16[128,1024]{1,0:T(8,128)(2,1)S(1)} %slice.61), channel_id=1, source_target_pairs={{0,1},{1,0},{2,3},{3,2},{4,5},{5,4},{6,7},{7,6},{8,9},{9,8},{10,11... | collective-permute-start | bytes 786440 | tf_op jit(solution)/shard_map/ppermute | solution.py:45
  68.0 2.3 %copy-start.12 = (bf16[128,1024]{1,0:T(8,128)(2,1)}, bf16[128,1024]{1,0:T(8,128)(2,1)S(1)}, u32[]{:S(2)}) copy-start(bf16[128,1024]{1,0:T(8,128)(2,1)S(1)} %collective-permute-done.11.two_lo) | copy-start | bytes 786436
  70.3 0.7 copy-start.13
  76.8 10.1 %collective-permute-start.14 = (bf16[832,256]{1,0:T(8,128)(2,1)S(1)}, bf16[832,256]{1,0:T(8,128)(2,1)S(1)}, u32[]{:S(2)}, u32[]{:S(2)}) collective-permute-start(bf16[832,256]{1,0:T(8,128)(2,1)S(1)} %get-tuple-element.18), channel_id=1, source_target_pairs={{0,4},{4,8},{8,12},{12,16},{16,20},{20,24},{24,28},{28,0},{1,5},{5... | collective-permute-start | bytes 1277960 | tf_op jit(solution)/shard_map/ppermute | solution.py:41
  78.5 11.6 %collective-permute-start.19 = (bf16[832,256]{1,0:T(8,128)(2,1)S(1)}, bf16[832,256]{1,0:T(8,128)(2,1)S(1)}, u32[]{:S(2)}, u32[]{:S(2)}) collective-permute-start(bf16[832,256]{1,0:T(8,128)(2,1)S(1)} %get-tuple-element.17), channel_id=1, source_target_pairs={{0,28},{4,0},{8,4},{12,8},{16,12},{20,16},{24,20},{28,24},{1,29},{... | collective-permute-start | bytes 1277960 | tf_op jit(solution)/shard_map/ppermute | solution.py:41
  87.0 32.2 %copy-start.17 = (bf16[832,256]{1,0:T(8,128)(2,1)}, bf16[832,256]{1,0:T(8,128)(2,1)S(1)}, u32[]{:S(2)}) copy-start(bf16[832,256]{1,0:T(8,128)(2,1)S(1)} %collective-permute-done.14.refs_4_) | copy-start | bytes 1277956
  87.0 10.0 %collective-permute-start.15 = (bf16[832,256]{1,0:T(8,128)(2,1)S(1)}, bf16[832,256]{1,0:T(8,128)(2,1)S(1)}, u32[]{:S(2)}, u32[]{:S(2)}) collective-permute-start(bf16[832,256]{1,0:T(8,128)(2,1)S(1)} %collective-permute-done.14.refs_4_), channel_id=1, source_target_pairs={{0,4},{4,8},{8,12},{12,16},{16,20},{20,24},{24,28},{28,0},{1,5},{5... | collective-permute-start | bytes 1277960 | tf_op jit(solution)/shard_map/ppermute | solution.py:41
  90.1 29.1 %copy-start.18 = (bf16[832,256]{1,0:T(8,128)(2,1)}, bf16[832,256]{1,0:T(8,128)(2,1)S(1)}, u32[]{:S(2)}) copy-start(bf16[832,256]{1,0:T(8,128)(2,1)S(1)} %collective-permute-done.19.refs_9_) | copy-start | bytes 1277956
  90.1 10.8 %collective-permute-start.20 = (bf16[832,256]{1,0:T(8,128)(2,1)S(1)}, bf16[832,256]{1,0:T(8,128)(2,1)S(1)}, u32[]{:S(2)}, u32[]{:S(2)}) collective-permute-start(bf16[832,256]{1,0:T(8,128)(2,1)S(1)} %collective-permute-done.19.refs_9_), channel_id=1, source_target_pairs={{0,28},{4,0},{8,4},{12,8},{16,12},{20,16},{24,20},{28,24},{1,29},{... | collective-permute-start | bytes 1277960 | tf_op jit(solution)/shard_map/ppermute | solution.py:41
  97.0 22.2 %copy-start.14 = (bf16[832,256]{1,0:T(8,128)(2,1)}, bf16[832,256]{1,0:T(8,128)(2,1)S(1)}, u32[]{:S(2)}) copy-start(bf16[832,256]{1,0:T(8,128)(2,1)S(1)} %collective-permute-done.15.refs_5_) | copy-start | bytes 1277956
  97.1 8.3 %collective-permute-start.16 = (bf16[544,256]{1,0:T(8,128)(2,1)S(1)}, bf16[544,256]{1,0:T(8,128)(2,1)S(1)}, u32[]{:S(2)}, u32[]{:S(2)}) collective-permute-start(bf16[544,256]{1,0:T(8,128)(2,1)S(1)} %slice.64), channel_id=1, source_target_pairs={{0,4},{4,8},{8,12},{12,16},{16,20},{20,24},{24,28},{28,0},{1,5},{5... | collective-permute-start | bytes 835592 | tf_op jit(solution)/shard_map/ppermute | solution.py:41
  100.8 18.4 %copy-start.15 = (bf16[832,256]{1,0:T(8,128)(2,1)}, bf16[832,256]{1,0:T(8,128)(2,1)S(1)}, u32[]{:S(2)}) copy-start(bf16[832,256]{1,0:T(8,128)(2,1)S(1)} %collective-permute-done.20.refs_10_) | copy-start | bytes 1277956
  100.9 8.4 %collective-permute-start.21 = (bf16[544,256]{1,0:T(8,128)(2,1)S(1)}, bf16[544,256]{1,0:T(8,128)(2,1)S(1)}, u32[]{:S(2)}, u32[]{:S(2)}) collective-permute-start(bf16[544,256]{1,0:T(8,128)(2,1)S(1)} %slice.66), channel_id=1, source_target_pairs={{0,28},{4,0},{8,4},{12,8},{16,12},{20,16},{24,20},{28,24},{1,29},{... | collective-permute-start | bytes 835592 | tf_op jit(solution)/shard_map/ppermute | solution.py:41
  105.4 13.9 %collective-permute-start.17 = (bf16[128,256]{1,0:T(8,128)(2,1)S(1)}, bf16[128,256]{1,0:T(8,128)(2,1)S(1)}, u32[]{:S(2)}, u32[]{:S(2)}) collective-permute-start(bf16[128,256]{1,0:T(8,128)(2,1)S(1)} %slice.65), channel_id=1, source_target_pairs={{0,4},{4,8},{8,12},{12,16},{16,20},{20,24},{24,28},{28,0},{1,5},{5... | collective-permute-start | bytes 196616 | tf_op jit(solution)/shard_map/ppermute | solution.py:41
  109.2 10.0 %collective-permute-start.22 = (bf16[128,256]{1,0:T(8,128)(2,1)S(1)}, bf16[128,256]{1,0:T(8,128)(2,1)S(1)}, u32[]{:S(2)}, u32[]{:S(2)}) collective-permute-start(bf16[128,256]{1,0:T(8,128)(2,1)S(1)} %slice.67), channel_id=1, source_target_pairs={{0,28},{4,0},{8,4},{12,8},{16,12},{20,16},{24,20},{28,24},{1,29},{... | collective-permute-start | bytes 196616 | tf_op jit(solution)/shard_map/ppermute | solution.py:41
  109.4 9.8 %copy-start = (bf16[256,256]{1,0:T(8,128)(2,1)S(1)}, bf16[256,256]{1,0:T(8,128)(2,1)}, u32[]{:S(2)}) copy-start(bf16[256,256]{1,0:T(8,128)(2,1)} %get-tuple-element.12.refs_2_) | copy-start | bytes 393220
  109.4 9.8 %copy-start.1 = (s32[3]{0:T(128)S(1)}, s32[3]{0:T(128)}, u32[]{:S(2)}) copy-start(s32[3]{0:T(128)} %pad_add_fusion.ids_ref) | copy-start | bytes 40
  109.4 9.8 %copy-start.4 = (bf16[576,256]{1,0:T(8,128)(2,1)S(1)}, bf16[576,256]{1,0:T(8,128)(2,1)}, u32[]{:S(2)}) copy-start(bf16[576,256]{1,0:T(8,128)(2,1)} %get-tuple-element.11.refs_1_) | copy-start | bytes 884740

commit v4 on v3

--- a/solution.py
+++ b/solution.py
@@ -72,114 +72,107 @@
     out_ref[rows, HD:] = product[:, HD:].astype(BF16)
 
 
-def early_kernel(ids_ref, own, one, three, x3, x1, img, img_two, gain, w_kv, w_q, cos, sin, *refs):
-    normed_ref, out_ref, img_normed = refs[-3:]
-    text, img_rows = own.shape[0], img.shape[0]
-    part = text // 2
+def image_kernel(ids_ref, own, one, three, two, gain, w_kv, w_q, cos, sin, *refs):
+    out_ref, normed = refs[-2:]
+    rows = own.shape[0]
     step = pl.program_id(0)
-    mp = ids_ref[0]
 
     @pl.when(step == 0)
     def _():
-        for n, two in enumerate((x3, x1)):
-            span = pl.ds(n * part, part)
-            pieces = [own[span, :], one[span, :], three[span, :], two[:part, :]]
-            normalise(mp, gain, pieces, normed_ref, span)
-        pieces = [img[...], x1[part:, :], x3[part:, :], img_two[...]]
-        normalise(mp, gain, pieces, img_normed, slice(0, img_rows))
-        rows = slice(0, text)
-        write_key_value(normed_ref[...], w_kv, cos[rows, :], sin[rows, :], out_ref, rows)
-        rows = slice(text, text + img_rows)
-        write_key_value(img_normed[...], w_kv, cos[rows, :], sin[rows, :], out_ref, rows)
-
-    product = jnp.dot(img_normed[...], w_q[...], preferred_element_type=F32)
-    start = text + img_rows + step * img_rows
-    rows = pl.ds(pl.multiple_of(start, IMG_TOK), img_rows)
+        pieces = [own[...], one[...], three[...], two[...]]
+        normalise(ids_ref[0], gain, pieces, normed, slice(0, rows))
+        write_key_value(normed[...], w_kv, cos[...], sin[...], out_ref, slice(0, rows))
+
+    product = jnp.dot(normed[...], w_q[...], preferred_element_type=F32)
+    span = pl.ds(pl.multiple_of((step + 1) * rows, IMG_TOK), rows)
     for h in range(2):
-        span = slice(h * HD, (h + 1) * HD)
-        turned = rotate(product[:, span], cos[text:, :], sin[text:, :])
-        out_ref[rows, span] = turned.astype(BF16)
-
-
-def early(ids, arrays, gain, w_kv, w_query, cosine, sine, after):
-    text, img_rows, tile = arrays[0].shape[0], arrays[5].shape[0], 2 * HD
+        columns = slice(h * HD, (h + 1) * HD)
+        out_ref[span, columns] = rotate(product[:, columns], cos[...], sin[...]).astype(BF16)
+
+
+def project_image(ids, arrays, gain, w_kv, w_query, tables, after):
+    rows, tile = arrays[0].shape[0], 2 * HD
     steps = w_query.shape[1] // tile
     whole = pl.BlockSpec(memory_space=VMEM)
     return pl.pallas_call(
-        early_kernel,
-        out_shape=[
-            jax.ShapeDtypeStruct((text, D), BF16),
-            jax.ShapeDtypeStruct((text + (1 + steps) * img_rows, tile), BF16),
-        ],
+        image_kernel,
+        out_shape=jax.ShapeDtypeStruct(((1 + steps) * rows, tile), BF16),
         grid=(steps,),
         in_specs=[pl.BlockSpec(memory_space=SMEM)]
         + [whole] * (len(arrays) + 2)
         + [pl.BlockSpec((D, tile), lambda n: (0, n))]
         + [whole] * 2
         + [pl.BlockSpec(memory_space=pl.ANY)] * len(after),
-        out_specs=[
-            pl.BlockSpec((text, D), lambda n: (0, 0)),
-            pl.BlockSpec((text + (1 + steps) * img_rows, tile), lambda n: (0, 0)),
-        ],
-        scratch_shapes=[pltpu.VMEM((img_rows, D), BF16)],
+        out_specs=pl.BlockSpec(((1 + steps) * rows, tile), lambda n: (0, 0)),
+        scratch_shapes=[pltpu.VMEM((rows, D), BF16)],
         compiler_params=pltpu.CompilerParams(vmem_limit_bytes=58 * 2**20),
-        cost_estimate=pl.CostEstimate(flops=0, bytes_accessed=0, transcendentals=0),
-        name="early",
-    )(ids, *arrays, gain, w_kv, w_query, cosine, sine, *after)
-
-
-def late_kernel(ids_ref, own, one, three, two_lo, two_hi, gain, w_kv, cos, sin, normed_ref, out_ref):
-    part = own.shape[0] // 2
-    for n, two in enumerate((two_lo, two_hi)):
-        span = pl.ds(n * part, part)
-        pieces = [own[span, :], one[span, :], three[span, :], two[...]]
-        normalise(ids_ref[0], gain, pieces, normed_ref, span)
-    write_key_value(
-        normed_ref[...], w_kv, cos[...], sin[...], out_ref, slice(0, own.shape[0])
-    )
-
-
-def late(ids, arrays, gain, w_kv, cosine, sine):
-    rows = arrays[0].shape[0]
+        cost_estimate=pl.CostEstimate(flops=8 * 10**9, bytes_accessed=10 * 2**20, transcendentals=0),
+        name="project_image",
+    )(ids, *arrays, gain, w_kv, w_query, *tables, *after)
+
+
+def text_kernel(ids_ref, own, one, three, two_lo, two_hi, gain, w_kv, cos, sin, *refs):
+    normed_ref, out_ref = refs[-2:]
+    rows = own.shape[0]
+    low = pl.program_id(0) < pl.num_programs(0) // 2
+    two = jnp.where(low, two_lo[...], two_hi[...])
+    pieces = [own[...], one[...], three[...], two]
+    normalise(ids_ref[0], gain, pieces, normed_ref, slice(0, rows))
+    write_key_value(normed_ref[...], w_kv, cos[...], sin[...], out_ref, slice(0, rows))
+
+
+def project_text(ids, arrays, gain, w_kv, tables, after):
+    rows, tile = arrays[0].shape[0], 128
+    steps = rows // tile
+    whole = pl.BlockSpec(memory_space=VMEM)
+    block = pl.BlockSpec((tile, D // 4), lambda r: (r, 0))
+    table = pl.BlockSpec((tile, HD // 2), lambda r: (r, 0))
     return pl.pallas_call(
-        late_kernel,
+        text_kernel,
         out_shape=[
             jax.ShapeDtypeStruct((rows, D), BF16),
             jax.ShapeDtypeStruct((rows, 2 * HD), BF16),
         ],
+        grid=(steps,),
         in_specs=[pl.BlockSpec(memory_space=SMEM)]
-        + [pl.BlockSpec(memory_space=VMEM)] * (len(arrays) + 4),
-        out_specs=[pl.BlockSpec(memory_space=VMEM)] * 2,
+        + [block] * 3
+        + [
+            pl.BlockSpec((tile, D // 4), lambda r: (jnp.minimum(r, steps // 2 - 1), 0)),
+            pl.BlockSpec((tile, D // 4), lambda r: (jnp.maximum(r - steps // 2, 0), 0)),
+        ]
+        + [whole] * 2
+        + [table] * 2
+        + [pl.BlockSpec(memory_space=pl.ANY)] * len(after),
+        out_specs=[
+            pl.BlockSpec((tile, D), lambda r: (r, 0)),
+            pl.BlockSpec((tile, 2 * HD), lambda r: (r, 0)),
+        ],
         compiler_params=pltpu.CompilerParams(vmem_limit_bytes=58 * 2**20),
         cost_estimate=pl.CostEstimate(flops=0, bytes_accessed=0, transcendentals=0),
-        name="late",
-    )(ids, *arrays, gain, w_kv, cosine, sine)
-
-
-def query_kernel(low_ref, high_ref, w_ref, cos_low, sin_low, cos_high, sin_high, q_ref):
-    half = low_ref.shape[0]
-    parts = ((low_ref, cos_low, sin_low), (high_ref, cos_high, sin_high))
-    for n, (x_ref, cos, sin) in enumerate(parts):
-        product = jnp.dot(x_ref[...], w_ref[...], preferred_element_type=F32)
-        for h in range(2):
-            span = slice(h * HD, (h + 1) * HD)
-            turned = rotate(product[:, span], cos[:half, :], sin[:half, :])
-            q_ref[n * half : (n + 1) * half, span] = turned.astype(BF16)
-
-
-def query(low, high, w_query, tables):
-    half, columns, tile = low.shape[0], w_query.shape[1], 2 * HD
+        name="project_text",
+    )(ids, *arrays, gain, w_kv, *tables, *after)
+
+
+def query_kernel(x_ref, w_ref, cos, sin, q_ref):
+    product = jnp.dot(x_ref[...], w_ref[...], preferred_element_type=F32)
+    for h in range(w_ref.shape[1] // HD):
+        span = slice(h * HD, (h + 1) * HD)
+        q_ref[:, span] = rotate(product[:, span], cos[...], sin[...]).astype(BF16)
+
+
+def query(normed, w_query, tables):
+    rows, columns, tile = normed.shape[0], w_query.shape[1], 2 * HD
     whole = pl.BlockSpec(memory_space=VMEM)
     return pl.pallas_call(
         query_kernel,
-        out_shape=jax.ShapeDtypeStruct((2 * half, columns), BF16),
+        out_shape=jax.ShapeDtypeStruct((rows, columns), BF16),
         grid=(columns // tile,),
-        in_specs=[whole] * 2 + [pl.BlockSpec((D, tile), lambda n: (0, n))] + [whole] * 4,
-        out_specs=pl.BlockSpec((2 * half, tile), lambda n: (0, n)),
+        in_specs=[whole, pl.BlockSpec((D, tile), lambda n: (0, n))] + [whole] * 2,
+        out_specs=pl.BlockSpec((rows, tile), lambda n: (0, n)),
         compiler_params=pltpu.CompilerParams(vmem_limit_bytes=58 * 2**20),
-        cost_estimate=pl.CostEstimate(flops=0, bytes_accessed=0, transcendentals=0),
+        cost_estimate=pl.CostEstimate(flops=8 * 10**9, bytes_accessed=10 * 2**20, transcendentals=0),
         name="query",
-    )(low, high, w_query, *tables)
+    )(normed, w_query, *tables)
 
 
 def images_before(counts_ref, sample):
@@ -190,8 +183,6 @@
 
 
 def attention_kernel(tok, heads, ids_ref, counts_ref, starts_ref, *refs):
-    half = tok // 2
-    img_rows = IMG_TOK * (1 + heads // 2)
     q_ref, own_e, own_l, f1, f2, f3, f4, f5, b1, b2, b3, b4, b5, out_ref = refs[:14]
     q_buf, kv_buf, img_buf, s_buf, max_buf, sum_buf, acc_buf, sems = refs[14:]
     step = pl.program_id(0)
@@ -200,45 +191,37 @@
 
     @pl.when(step == 0)
     def _():
-        rows_e = own_e.shape[0]
-        cut = rows_e // 2
-        quarter = half // 2
-        early_parts = [
+        rows_e, rows_l = own_e.shape[0], own_l.shape[0]
+        cut, part = rows_e // 2, rows_l // 2
+        moves = [(q_ref, q_buf)]
+        for d, array, base, first, count in (
             (0, own_e, 0, 0, rows_e),
             (1, f1, 0, 0, rows_e),
             (2, f2, 0, 0, rows_e),
             (3, f3, 0, 0, rows_e),
-            (4, b4, half, 0, cut),
             (4, f4, 0, cut, cut),
-            (5, b3, half, 0, rows_e),
-            (6, b2, half, 0, rows_e),
+            (4, b4, rows_l, 0, cut),
+            (5, b3, rows_l, 0, rows_e),
+            (6, b2, rows_l, 0, rows_e),
             (7, b1, 0, 0, rows_e),
-        ]
-        late_parts = [
-            (0, own_l, 0, 0, half),
-            (1, f2, rows_e, 0, half),
-            (2, f3, rows_e, 0, half),
-            (3, f4, cut, 0, half),
-            (4, f5, 0, 0, quarter),
-            (4, b5, 0, quarter, quarter),
-            (5, b4, 0, 0, half),
-            (6, b3, 0, 0, half),
-            (7, b2, 0, 0, half),
-        ]
-        moves = [(q_ref, q_buf)]
-        for d, array, base, first, count in early_parts:
+        ):
             shard = (ctx - d) & (SHARDS - 1)
-            if first < half:
-                place = pl.ds(pl.multiple_of(shard * tok, tok), half)
-                moves.append((array.at[pl.ds(base, half), :], kv_buf.at[place, :]))
-            skip = max(half - first, 0)
-            place = pl.ds(first + skip - half, count - skip)
             moves.append(
-                (array.at[pl.ds(base + skip, count - skip), :], img_buf.at[shard, place, :])
+                (array.at[pl.ds(base, count), :], img_buf.at[shard, pl.ds(first, count), :])
             )
-        for d, array, base, first, count in late_parts:
+        for d, array, base, first, count in (
+            (0, own_l, 0, 0, rows_l),
+            (1, f2, rows_e, 0, rows_l),
+            (2, f3, rows_e, 0, rows_l),
+            (3, f4, cut, 0, rows_l),
+            (4, f5, 0, 0, part),
+            (4, b5, 0, part, part),
+            (5, b4, 0, 0, rows_l),
+            (6, b3, 0, 0, rows_l),
+            (7, b2, 0, 0, rows_l),
+        ):
             shard = (ctx - d) & (SHARDS - 1)
-            place = pl.ds(pl.multiple_of(shard * tok + half + first, quarter), count)
+            place = pl.ds(pl.multiple_of(shard * tok + first, part), count)
             moves.append((array.at[pl.ds(base, count), :], kv_buf.at[place, :]))
         copies = [
             pltpu.make_async_copy(source, target, sems.at[n])
@@ -356,7 +339,6 @@
     sample = lax.axis_index("dp").astype(jnp.int32)
     mp = lax.axis_index("mp").astype(jnp.int32)
     tok = text_rows.shape[0]
-    half = tok // 2
     heads = w_query.shape[1] // HD
     ids = jnp.stack([mp, ctx, sample])
 
@@ -378,48 +360,32 @@
 
     my_slot, my_across, my_distance = source(sample)
     _, _, its_distance = source(sample ^ 1)
-    low, high = text_rows[:half], text_rows[half:]
+    one, three = first_hop(text_rows)
     routed = [visual_rows] + [shift(visual_rows, "dp", 2 * d, False) for d in (1, 2, 3)]
-    a_low, b_low = first_hop(low)
-    a_high, b_high = first_hop(high)
     for_other = choose(its_distance, routed)
     from_other = lax.ppermute(for_other, "dp", [(i, i ^ 1) for i in range(SHARDS)])
     image = choose(jnp.where(my_across == 1, 4, my_distance), routed + [from_other])
-    x3 = exchange(jnp.concatenate([a_low[: half // 2], image], axis=0), 3)
-    x1 = exchange(jnp.concatenate([b_low[half // 2 :], image], axis=0), 1)
-    img_two = exchange(image, 2)
-    c_high, d_high = second_hop(a_high, b_high)
+    image_parts = [image] + [exchange(image, mask) for mask in (1, 3, 2)]
+    two_lo, two_hi = second_hop(one, three)
 
     mine = (every[:, None] == sample) & (every[None, :] == my_slot)
     my_start = jnp.sum(jnp.where(mine, image_starts, 0))
-    rows = jnp.arange(tok + IMG_TOK, dtype=jnp.int32)
-    positions = jnp.where(
-        rows < half,
-        ctx * tok + rows,
-        jnp.where(rows < half + IMG_TOK, my_start + rows - half, ctx * tok + rows - IMG_TOK),
+    text_tables = rotary_tables(ctx * tok + jnp.arange(tok, dtype=jnp.int32))
+    image_tables = rotary_tables(my_start + jnp.arange(IMG_TOK, dtype=jnp.int32))
+    own_e = project_image(ids, image_parts, gain, w_kv, w_query, image_tables, (one, three))
+    normed, own_l = project_text(
+        ids, [text_rows, one, three, two_lo, two_hi], gain, w_kv, text_tables, (own_e,)
     )
-    cosine, sine = rotary_tables(positions)
-    first = half + IMG_TOK
-    tables_e = (cosine[:first], sine[:first])
-    tables_l = (cosine[first:], sine[first:])
-    normed_low, own_e = early(
-        ids, [low, a_low, b_low, x3, x1, image, img_two], gain, w_kv, w_query, *tables_e,
-        (a_high, b_high),
-    )
-    normed_high, own_l = late(
-        ids, [high, a_high, b_high, c_high, d_high], gain, w_kv, *tables_l
-    )
-    q_all = query(normed_low, normed_high, w_query, tables_e + tables_l)
-
-    cut = own_e.shape[0] // 2
-    quarter = half // 2
+    q_all = query(normed, w_query, text_tables)
+
+    cut, part = own_e.shape[0] // 2, tok // 2
     f1, b1 = shift(own_e, "ctx", 1, True), shift(own_e, "ctx", -1, True)
     f2 = shift(jnp.concatenate([f1, own_l], axis=0), "ctx", 1, True)
     b2 = shift(jnp.concatenate([own_l, b1], axis=0), "ctx", -1, True)
     f3, b3 = shift(f2, "ctx", 1, True), shift(b2, "ctx", -1, True)
-    f4, b4 = shift(f3[cut:], "ctx", 1, True), shift(b3[: half + cut], "ctx", -1, True)
-    f5 = shift(f4[cut : cut + quarter], "ctx", 1, True)
-    b5 = shift(b4[quarter:half], "ctx", -1, True)
+    f4, b4 = shift(f3[cut:], "ctx", 1, True), shift(b3[: tok + cut], "ctx", -1, True)
+    f5 = shift(f4[cut : cut + part], "ctx", 1, True)
+    b5 = shift(b4[part:tok], "ctx", -1, True)
     return attention(
         tok, heads, (ids, image_counts, image_starts),
         [q_all, own_e, own_l, f1, f2, f3, f4, f5, b1, b2, b3, b4, b5],

time: 156 us -> 149 us (0.955); the launches traced: 153 us -> 148 us
  local copies, waits for them, and re-layouts: 15.1 us -> 4.77 us
  waiting for transfers between devices: 32 us -> 36.8 us
    slice x10 -> x3, local copies, waits for them, and re-layouts: 10.7 us -> 0.04 us  [the longest x1 0.02 us: on_device(): b3[:tok + cut]]
    ppermute x13, waiting for transfers between devices: 19.6 us -> 23.2 us  [shift(): return lax.ppermute(x, axis, pairs)]
    ppermute x13, starting transfers between devices: 24.6 us -> 27.6 us  [shift(): return lax.ppermute(x, axis, pairs)]
    ppermute x9 -> x7, starting transfers between devices: 12.4 us -> 10 us  [exchange(): return lax.ppermute(x, 'mp', [(i, i ^ mask) for i in range(4)])]
    unnamed x39 -> x37, local copies, waits for them, and re-layouts: 0.96 us -> 3.34 us
    ppermute x9 -> x7, waiting for transfers between devices: 12.4 us -> 13.1 us  [exchange(): return lax.ppermute(x, 'mp', [(i, i ^ mask) for i in range(4)])]
  transfers between devices with their start and end apart: 23 -> 21, of which waited for: 8 -> 7; matrix products, arithmetic and copies ran while one was open for 12% -> 7% of each run, Pallas kernels for 9% -> 17%
where the time goes in v4:
time: 149 us; the launch traced here: 148 us
  Pallas kernels  57.6 us (39%)
  starting transfers between devices  37.7 us (25%)
  waiting for transfers between devices  36.8 us (25%)
  other arithmetic  8.15 us (5%)
  local copies, waits for them, and re-layouts  4.77 us (3%)
  between operations  3.22 us (2%)
    pallas_call x1, Pallas kernels, attention(): pl.pallas_call(functools.partial(attention_kernel, tok, heads), out_shape...  32.9 us
    ppermute x13, starting transfers between devices, shift(): return lax.ppermute(x, axis, pairs)  27.6 us
    ppermute x13, waiting for transfers between devices, shift(): return lax.ppermute(x, axis, pairs)  23.2 us
    ppermute x7, waiting for transfers between devices, exchange(): return lax.ppermute(x, 'mp', [(i, i ^ mask) for i in range(4)])  13.1 us
    ppermute x7, starting transfers between devices, exchange(): return lax.ppermute(x, 'mp', [(i, i ^ mask) for i in range(4)])  10 us
    pallas_call x1, Pallas kernels, query(): pl.pallas_call(query_kernel, out_shape=jax.ShapeDtypeStruct((rows, column...  9.48 us
    pallas_call x1, Pallas kernels, project_text(): pl.pallas_call(text_kernel, out_shape=[jax.ShapeDtypeStruct((rows, D), BF...  7.72 us
    pallas_call x1, Pallas kernels, project_image(): pl.pallas_call(image_kernel, out_shape=jax.ShapeDtypeStruct(((1 + steps)...  7.48 us
  transfers between devices with their start and end apart: 21, of which 7 were waited for; matrix products, arithmetic and copies ran while one was open for 7% of the time, Pallas kernels for 17%

profile of v4, /device:TPU:224, one launch (start us, length us, event | category | flops | bytes accessed | tf_op | source)
XLA Modules:
  0.0 148.2 jit_solution(16255675628234941145)
XLA Ops:
  0.0 3.5 %collective-permute-start.6 = (bf16[64,1024]{1,0:T(8,128)(2,1)}, bf16[64,1024]{1,0:T(8,128)(2,1)S(1)}, u32[]{:S(2)}, u32[]{:S(2)}) collective-permute-start(bf16[64,1024]{1,0:T(8,128)(2,1)} %param.9), channel_id=1, source_target_pairs={{0,64},{32,96},{64,128},{96,160},{128,192},{160,224},{1,65},{33,97... | collective-permute-start | bytes 393224 | tf_op jit(solution)/shard_map/ppermute | solution.py:41
  3.5 4.8 %collective-permute-start.5 = (bf16[64,1024]{1,0:T(8,128)(2,1)}, bf16[64,1024]{1,0:T(8,128)(2,1)S(1)}, u32[]{:S(2)}, u32[]{:S(2)}) collective-permute-start(bf16[64,1024]{1,0:T(8,128)(2,1)} %param.9), channel_id=1, source_target_pairs={{0,128},{32,160},{64,192},{96,224},{1,129},{33,161},{65,193},{97,2... | collective-permute-start | bytes 393224 | tf_op jit(solution)/shard_map/ppermute | solution.py:41
  8.3 1.9 %collective-permute-start.4 = (bf16[64,1024]{1,0:T(8,128)(2,1)}, bf16[64,1024]{1,0:T(8,128)(2,1)}, u32[]{:S(2)}, u32[]{:S(2)}) collective-permute-start(bf16[64,1024]{1,0:T(8,128)(2,1)} %param.9), channel_id=1, source_target_pairs={{0,192},{32,224},{1,193},{33,225},{2,194},{34,226},{3,195},{35,227... | collective-permute-start | bytes 393224 | tf_op jit(solution)/shard_map/ppermute | solution.py:41
  10.3 1.5 %collective-permute-start = (bf16[512,1024]{1,0:T(8,128)(2,1)}, bf16[512,1024]{1,0:T(8,128)(2,1)S(1)}, u32[]{:S(2)}, u32[]{:S(2)}) collective-permute-start(bf16[512,1024]{1,0:T(8,128)(2,1)} %own.1), channel_id=1, source_target_pairs={{0,1},{1,0},{2,3},{3,2},{4,5},{5,4},{6,7},{7,6},{8,9},{9,8},{10,11... | collective-permute-start | bytes 3145736 | tf_op jit(solution)/shard_map/ppermute | solution.py:45
  11.7 2.1 %collective-permute-start.1 = (bf16[512,1024]{1,0:T(8,128)(2,1)}, bf16[512,1024]{1,0:T(8,128)(2,1)}, u32[]{:S(2)}, u32[]{:S(2)}) collective-permute-start(bf16[512,1024]{1,0:T(8,128)(2,1)} %own.1), channel_id=1, source_target_pairs={{0,3},{1,2},{2,1},{3,0},{4,7},{5,6},{6,5},{7,4},{8,11},{9,10},{10,... | collective-permute-start | bytes 3145736 | tf_op jit(solution)/shard_map/ppermute | solution.py:45
  13.8 1.4 fusion
  15.9 0.0 copy-start.7
  15.9 0.0 copy-start.2
  15.9 0.0 copy-start.8
  15.9 1.5 %constant_dynamic-update-slice_fusion.1 = bf16[4096,256]{1,0:T(8,128)(2,1)S(1)} fusion(bf16[4096,128]{1,0:T(8,128)(2,1)} %param.14), kind=kLoop, calls=%fused_computation.9 | loop fusion | bytes 2097152
  17.4 0.2 constant_dynamic-update-slice_fusion.w_kv
  17.7 1.0 select_reduce_fusion
  20.7 0.6 add_convert_fusion.1
  21.4 0.0 collective-permute-done.6
  21.4 0.0 collective-permute-done.5
  21.4 0.0 collective-permute-done.4
  21.4 0.1 select_select_fusion.1
  21.5 0.1 collective-permute-start.7
  21.6 0.8 multiply_sine_fusion.1
  22.4 0.5 collective-permute-done.7
  22.9 0.7 select_select_fusion.own
  23.6 0.6 collective-permute-start.10
  24.2 2.6 %collective-permute-start.9 = (bf16[64,1024]{1,0:T(8,128)(2,1)}, bf16[64,1024]{1,0:T(8,128)(2,1)S(1)}, u32[]{:S(2)}, u32[]{:S(2)}) collective-permute-start(bf16[64,1024]{1,0:T(8,128)(2,1)} %select_select_fusion.own), channel_id=1, source_target_pairs={{0,3},{1,2},{2,1},{3,0},{4,7},{5,6},{6,5},{7,4},{8,11},{9,10},{10,... | collective-permute-start | bytes 393224 | tf_op jit(solution)/shard_map/ppermute | solution.py:45
  26.9 0.2 collective-permute-start.8
  27.1 0.6 pad_add_fusion.ids_ref
  27.7 8.8 %collective-permute-done.refs_0_.one = bf16[512,1024]{1,0:T(8,128)(2,1)S(1)} collective-permute-done((bf16[512,1024]{1,0:T(8,128)(2,1)}, bf16[512,1024]{1,0:T(8,128)(2,1)S(1)}, u32[]{:S(2)}, u32[]{:S(2)}) %collective-permute-start) | collective-permute-done | bytes 1048608 | tf_op jit(solution)/shard_map/ppermute | solution.py:45
  36.6 2.8 %collective-permute-start.2 = (bf16[256,1024]{1,0:T(8,128)(2,1)S(1)}, bf16[256,1024]{1,0:T(8,128)(2,1)S(1)}, u32[]{:S(2)}, u32[]{:S(2)}) collective-permute-start(bf16[256,1024]{1,0:T(8,128)(2,1)S(1)} %slice.24), channel_id=1, source_target_pairs={{0,3},{1,2},{2,1},{3,0},{4,7},{5,6},{6,5},{7,4},{8,11},{9,10},{10,... | collective-permute-start | bytes 1572872 | tf_op jit(solution)/shard_map/ppermute | solution.py:45
  39.5 2.7 %collective-permute-done.1.refs_1_.three = bf16[512,1024]{1,0:T(8,128)(2,1)} collective-permute-done((bf16[512,1024]{1,0:T(8,128)(2,1)}, bf16[512,1024]{1,0:T(8,128)(2,1)}, u32[]{:S(2)}, u32[]{:S(2)}) %collective-permute-start.1) | collective-permute-done | bytes 1048608 | tf_op jit(solution)/shard_map/ppermute | solution.py:45
  42.2 1.1 slice.25
  43.3 0.1 collective-permute-start.3
  43.4 0.0 collective-permute-done.10.two
  43.4 1.5 %collective-permute-done.9.three = bf16[64,1024]{1,0:T(8,128)(2,1)S(1)} collective-permute-done((bf16[64,1024]{1,0:T(8,128)(2,1)}, bf16[64,1024]{1,0:T(8,128)(2,1)S(1)}, u32[]{:S(2)}, u32[]{:S(2)}) %collective-permute-start.9) | collective-permute-done | bytes 131104 | tf_op jit(solution)/shard_map/ppermute | solution.py:45
  44.9 0.0 collective-permute-done.8.one
  44.9 0.6 copy-done.16
  45.6 0.1 copy-done.17
  45.6 7.5 %project_image.1.refs_0_.refs_1_ = bf16[320,256]{1,0:T(8,128)(2,1)} custom-call(s32[3]{0:T(128)} %pad_add_fusion.ids_ref, bf16[64,1024]{1,0:T(8,128)(2,1)} %select_select_fusion.own, bf16[64,1024]{1,0:T(8,128)(2,1)} %copy-done.17, bf16[64,1024]{1,0:T(8,128)(2,1)} %copy-done.16, bf16[64,1024]{1,0:T(8,128)(2,1)} %copy-done.15, f32[1,4096]{1,0:T(1,128)} %bitcast.4, ...), custom_call_target="tpu_custom_call" | custom-call | flops 8000000000 | bytes 10485760 | tf_op jit(solution)/shard_map/project_image/pallas_call | solution.py:97
  53.1 1.0 collective-permute-start.16
  54.1 2.2 %collective-permute-start.11 = (bf16[320,256]{1,0:T(8,128)(2,1)}, bf16[320,256]{1,0:T(8,128)(2,1)S(1)}, u32[]{:S(2)}, u32[]{:S(2)}) collective-permute-start(bf16[320,256]{1,0:T(8,128)(2,1)} %project_image.1.refs_0_.refs_1_), channel_id=1, source_target_pairs={{0,4},{4,8},{8,12},{12,16},{16,20},{20,24},{24,28},{28,0},{1,5},{5... | collective-permute-start | bytes 491528 | tf_op jit(solution)/shard_map/ppermute | solution.py:41
  56.3 1.8 %multiply_sine_fusion = (f32[512,64]{1,0:T(8,128)}, f32[512,64]{1,0:T(8,128)}) fusion(f32[64]{0:T(128)S(1)} %multiply_exponential_fusion, f32[512]{0:T(512)S(1)} %add_convert_fusion), kind=kLoop, calls=%fused_computation.2 | loop fusion | flops 32768 | bytes 264448 | tf_op jit(solution)/shard_map/sin | solution.py:30
  58.1 0.0 collective-permute-done.2.two_lo
  58.1 0.0 collective-permute-done.3.two_hi
  58.2 0.8 copy-done.9
  59.0 0.3 copy-done.10
  59.2 7.7 %project_text.1 = (bf16[512,4096]{1,0:T(8,128)(2,1)}, bf16[512,256]{1,0:T(8,128)(2,1)}) custom-call(s32[3]{0:T(128)} %pad_add_fusion.ids_ref, bf16[512,1024]{1,0:T(8,128)(2,1)} %own.1, bf16[512,1024]{1,0:T(8,128)(2,1)} %copy-done.6, bf16[512,1024]{1,0:T(8,128)(2,1)} %collective-permute-done.1.refs_1_.three, bf16[256,1024]{1,0:T(8,128)(2,1)} %copy-done.9, ...), custom_call_target="tpu_custom_call" | custom-call | tf_op jit(solution)/shard_map/project_text/pallas_call | solution.py:130
  67.0 0.0 collective-permute-done.16.refs_8_
  67.0 0.0 collective-permute-done.11.refs_3_
  67.0 1.1 pad_maximum_fusion.1
  68.1 0.1 collective-permute-start.17
  68.2 3.2 %collective-permute-start.12 = (bf16[832,256]{1,0:T(8,128)(2,1)S(1)}, bf16[832,256]{1,0:T(8,128)(2,1)S(1)}, u32[]{:S(2)}, u32[]{:S(2)}) collective-permute-start(bf16[832,256]{1,0:T(8,128)(2,1)S(1)} %get-tuple-element.12), channel_id=1, source_target_pairs={{0,4},{4,8},{8,12},{12,16},{16,20},{20,24},{24,28},{28,0},{1,5},{5... | collective-permute-start | bytes 1277960 | tf_op jit(solution)/shard_map/ppermute | solution.py:41
  71.4 8.6 %collective-permute-done.17.refs_9_ = bf16[832,256]{1,0:T(8,128)(2,1)S(1)} collective-permute-done((bf16[832,256]{1,0:T(8,128)(2,1)S(1)}, bf16[832,256]{1,0:T(8,128)(2,1)S(1)}, u32[]{:S(2)}, u32[]{:S(2)}) %collective-permute-start.17) | collective-permute-done | bytes 426016 | tf_op jit(solution)/shard_map/ppermute | solution.py:41
  80.0 0.0 collective-permute-start.18
  80.0 0.0 collective-permute-done.12.refs_4_
  80.0 3.5 %collective-permute-start.13 = (bf16[832,256]{1,0:T(8,128)(2,1)S(1)}, bf16[832,256]{1,0:T(8,128)(2,1)S(1)}, u32[]{:S(2)}, u32[]{:S(2)}) collective-permute-start(bf16[832,256]{1,0:T(8,128)(2,1)S(1)} %collective-permute-done.12.refs_4_), channel_id=1, source_target_pairs={{0,4},{4,8},{8,12},{12,16},{16,20},{20,24},{24,28},{28,0},{1,5},{5... | collective-permute-start | bytes 1277960 | tf_op jit(solution)/shard_map/ppermute | solution.py:41
  83.5 9.3 %collective-permute-done.18.refs_10_ = bf16[832,256]{1,0:T(8,128)(2,1)S(1)} collective-permute-done((bf16[832,256]{1,0:T(8,128)(2,1)S(1)}, bf16[832,256]{1,0:T(8,128)(2,1)S(1)}, u32[]{:S(2)}, u32[]{:S(2)}) %collective-permute-start.18) | collective-permute-done | bytes 426016 | tf_op jit(solution)/shard_map/ppermute | solution.py:41
  92.8 0.1 collective-permute-start.19
  92.9 0.0 collective-permute-done.13.refs_5_
  93.0 3.6 %collective-permute-start.14 = (bf16[672,256]{1,0:T(8,128)(2,1)S(1)}, bf16[672,256]{1,0:T(8,128)(2,1)S(1)}, u32[]{:S(2)}, u32[]{:S(2)}) collective-permute-start(bf16[672,256]{1,0:T(8,128)(2,1)S(1)} %slice.26), channel_id=1, source_target_pairs={{0,4},{4,8},{8,12},{12,16},{16,20},{20,24},{24,28},{28,0},{1,5},{5... | collective-permute-start | bytes 1032200 | tf_op jit(solution)/shard_map/ppermute | solution.py:41
  96.6 5.3 %collective-permute-done.19.refs_11_ = bf16[672,256]{1,0:T(8,128)(2,1)S(1)} collective-permute-done((bf16[672,256]{1,0:T(8,128)(2,1)S(1)}, bf16[672,256]{1,0:T(8,128)(2,1)S(1)}, u32[]{:S(2)}, u32[]{:S(2)}) %collective-permute-start.19) | collective-permute-done | bytes 344096 | tf_op jit(solution)/shard_map/ppermute | solution.py:41
  101.9 0.1 collective-permute-start.20
  102.0 0.0 collective-permute-done.14.refs_6_
  102.0 3.5 %collective-permute-start.15 = (bf16[256,256]{1,0:T(8,128)(2,1)S(1)}, bf16[256,256]{1,0:T(8,128)(2,1)S(1)}, u32[]{:S(2)}, u32[]{:S(2)}) collective-permute-start(bf16[256,256]{1,0:T(8,128)(2,1)S(1)} %slice.27), channel_id=1, source_target_pairs={{0,4},{4,8},{8,12},{12,16},{16,20},{20,24},{24,28},{28,0},{1,5},{5... | collective-permute-start | bytes 393224 | tf_op jit(solution)/shard_map/ppermute | solution.py:41
  105.6 9.5 %query.1.refs_0_ = bf16[512,1024]{1,0:T(8,128)(2,1)} custom-call(bf16[512,4096]{1,0:T(8,128)(2,1)} %get-tuple-element.7.x_ref, bf16[4096,1024]{1,0:T(8,128)(2,1)} %w_ref.1, f32[512,64]{1,0:T(8,128)} %get-tuple-element.14.cos, f32[512,64]{1,0:T(8,128)} %get-tuple-element.13.sin), custom_call_target="tpu_custom_call" | custom-call | flops 8000000000 | bytes 10485760 | tf_op jit(solution)/shard_map/query/pallas_call | solution.py:166
  115.1 0.0 collective-permute-done.20.refs_12_
  115.1 32.9 %attention.1 = bf16[512,1024]{1,0:T(8,128)(2,1)} custom-call(s32[3]{0:T(128)S(1)} %copy-done.3, s32[8]{0:T(128)S(1)} %copy-done.4, s32[8,8]{1,0:T(8,128)S(1)} %copy-done.2, bf16[512,1024]{1,0:T(8,128)(2,1)} %query.1.refs_0_, bf16[320,256]{1,0:T(8,128)(2,1)S(1)} %copy-done.1, bf16[512,256]{1,0:T(8,128)(2,1)S(1)} %copy-done, ...), custom_call_target="tpu_custom_call" | custom-call | flops 8589934592 | bytes 8388608 | tf_op jit(solution)/shard_map/attention/pallas_call | solution.py:308
  (38 shorter events, 0.2 us)
Async XLA Ops:
  0.0 21.4 %collective-permute-start.6 = (bf16[64,1024]{1,0:T(8,128)(2,1)}, bf16[64,1024]{1,0:T(8,128)(2,1)S(1)}, u32[]{:S(2)}, u32[]{:S(2)}) collective-permute-start(bf16[64,1024]{1,0:T(8,128)(2,1)} %param.9), channel_id=1, source_target_pairs={{0,64},{32,96},{64,128},{96,160},{128,192},{160,224},{1,65},{33,97... | collective-permute-start | bytes 393224 | tf_op jit(solution)/shard_map/ppermute | solution.py:41
  3.5 17.9 %collective-permute-start.5 = (bf16[64,1024]{1,0:T(8,128)(2,1)}, bf16[64,1024]{1,0:T(8,128)(2,1)S(1)}, u32[]{:S(2)}, u32[]{:S(2)}) collective-permute-start(bf16[64,1024]{1,0:T(8,128)(2,1)} %param.9), channel_id=1, source_target_pairs={{0,128},{32,160},{64,192},{96,224},{1,129},{33,161},{65,193},{97,2... | collective-permute-start | bytes 393224 | tf_op jit(solution)/shard_map/ppermute | solution.py:41
  8.3 13.1 %collective-permute-start.4 = (bf16[64,1024]{1,0:T(8,128)(2,1)}, bf16[64,1024]{1,0:T(8,128)(2,1)}, u32[]{:S(2)}, u32[]{:S(2)}) collective-permute-start(bf16[64,1024]{1,0:T(8,128)(2,1)} %param.9), channel_id=1, source_target_pairs={{0,192},{32,224},{1,193},{33,225},{2,194},{34,226},{3,195},{35,227... | collective-permute-start | bytes 393224 | tf_op jit(solution)/shard_map/ppermute | solution.py:41
  10.3 26.3 %collective-permute-start = (bf16[512,1024]{1,0:T(8,128)(2,1)}, bf16[512,1024]{1,0:T(8,128)(2,1)S(1)}, u32[]{:S(2)}, u32[]{:S(2)}) collective-permute-start(bf16[512,1024]{1,0:T(8,128)(2,1)} %own.1), channel_id=1, source_target_pairs={{0,1},{1,0},{2,3},{3,2},{4,5},{5,4},{6,7},{7,6},{8,9},{9,8},{10,11... | collective-permute-start | bytes 3145736 | tf_op jit(solution)/shard_map/ppermute | solution.py:45
  11.7 30.4 %collective-permute-start.1 = (bf16[512,1024]{1,0:T(8,128)(2,1)}, bf16[512,1024]{1,0:T(8,128)(2,1)}, u32[]{:S(2)}, u32[]{:S(2)}) collective-permute-start(bf16[512,1024]{1,0:T(8,128)(2,1)} %own.1), channel_id=1, source_target_pairs={{0,3},{1,2},{2,1},{3,0},{4,7},{5,6},{6,5},{7,4},{8,11},{9,10},{10,... | collective-permute-start | bytes 3145736 | tf_op jit(solution)/shard_map/ppermute | solution.py:45
  15.9 1.5 %copy-start.7 = (bf16[4096,128]{1,0:T(8,128)(2,1)S(1)}, bf16[4096,128]{1,0:T(8,128)(2,1)}, u32[]{:S(2)}) copy-start(bf16[4096,128]{1,0:T(8,128)(2,1)} %param.15) | copy-start | bytes 3145732
  15.9 1.8 %copy-start.2 = (s32[8,8]{1,0:T(8,128)S(1)}, s32[8,8]{1,0:T(8,128)}, u32[]{:S(2)}) copy-start(s32[8,8]{1,0:T(8,128)} %starts_ref.1) | copy-start | bytes 772
  15.9 5.5 %copy-start.8 = (bf16[64,1024]{1,0:T(8,128)(2,1)S(1)}, bf16[64,1024]{1,0:T(8,128)(2,1)}, u32[]{:S(2)}) copy-start(bf16[64,1024]{1,0:T(8,128)(2,1)} %param.9) | copy-start | bytes 393220
  17.7 27.2 %copy-start.5 = (bf16[4096,256]{1,0:T(8,128)(2,1)}, bf16[4096,256]{1,0:T(8,128)(2,1)S(1)}, u32[]{:S(2)}) copy-start(bf16[4096,256]{1,0:T(8,128)(2,1)S(1)} %constant_dynamic-update-slice_fusion.w_kv) | copy-start | bytes 6291460
  21.5 1.4 collective-permute-start.7
  23.6 19.8 %collective-permute-start.10 = (bf16[64,1024]{1,0:T(8,128)(2,1)}, bf16[64,1024]{1,0:T(8,128)(2,1)S(1)}, u32[]{:S(2)}, u32[]{:S(2)}) collective-permute-start(bf16[64,1024]{1,0:T(8,128)(2,1)} %select_select_fusion.own), channel_id=1, source_target_pairs={{0,2},{1,3},{2,0},{3,1},{4,6},{5,7},{6,4},{7,5},{8,10},{9,11},{10,... | collective-permute-start | bytes 393224 | tf_op jit(solution)/shard_map/ppermute | solution.py:45
  24.2 20.6 %collective-permute-start.9 = (bf16[64,1024]{1,0:T(8,128)(2,1)}, bf16[64,1024]{1,0:T(8,128)(2,1)S(1)}, u32[]{:S(2)}, u32[]{:S(2)}) collective-permute-start(bf16[64,1024]{1,0:T(8,128)(2,1)} %select_select_fusion.own), channel_id=1, source_target_pairs={{0,3},{1,2},{2,1},{3,0},{4,7},{5,6},{6,5},{7,4},{8,11},{9,10},{10,... | collective-permute-start | bytes 393224 | tf_op jit(solution)/shard_map/ppermute | solution.py:45
  26.9 18.0 %collective-permute-start.8 = (bf16[64,1024]{1,0:T(8,128)(2,1)}, bf16[64,1024]{1,0:T(8,128)(2,1)S(1)}, u32[]{:S(2)}, u32[]{:S(2)}) collective-permute-start(bf16[64,1024]{1,0:T(8,128)(2,1)} %select_select_fusion.own), channel_id=1, source_target_pairs={{0,1},{1,0},{2,3},{3,2},{4,5},{5,4},{6,7},{7,6},{8,9},{9,8},{10,11... | collective-permute-start | bytes 393224 | tf_op jit(solution)/shard_map/ppermute | solution.py:45
  36.6 8.3 %copy-start.6 = (bf16[512,1024]{1,0:T(8,128)(2,1)}, bf16[512,1024]{1,0:T(8,128)(2,1)S(1)}, u32[]{:S(2)}) copy-start(bf16[512,1024]{1,0:T(8,128)(2,1)S(1)} %collective-permute-done.refs_0_.one) | copy-start | bytes 3145732
  36.6 21.5 %collective-permute-start.2 = (bf16[256,1024]{1,0:T(8,128)(2,1)S(1)}, bf16[256,1024]{1,0:T(8,128)(2,1)S(1)}, u32[]{:S(2)}, u32[]{:S(2)}) collective-permute-start(bf16[256,1024]{1,0:T(8,128)(2,1)S(1)} %slice.24), channel_id=1, source_target_pairs={{0,3},{1,2},{2,1},{3,0},{4,7},{5,6},{6,5},{7,4},{8,11},{9,10},{10,... | collective-permute-start | bytes 1572872 | tf_op jit(solution)/shard_map/ppermute | solution.py:45
  43.3 14.9 %collective-permute-start.3 = (bf16[256,1024]{1,0:T(8,128)(2,1)S(1)}, bf16[256,1024]{1,0:T(8,128)(2,1)S(1)}, u32[]{:S(2)}, u32[]{:S(2)}) collective-permute-start(bf16[256,1024]{1,0:T(8,128)(2,1)S(1)} %slice.25), channel_id=1, source_target_pairs={{0,1},{1,0},{2,3},{3,2},{4,5},{5,4},{6,7},{7,6},{8,9},{9,8},{10,11... | collective-permute-start | bytes 1572872 | tf_op jit(solution)/shard_map/ppermute | solution.py:45
  43.4 1.5 %copy-start.15 = (bf16[64,1024]{1,0:T(8,128)(2,1)}, bf16[64,1024]{1,0:T(8,128)(2,1)S(1)}, u32[]{:S(2)}) copy-start(bf16[64,1024]{1,0:T(8,128)(2,1)S(1)} %collective-permute-done.10.two) | copy-start | bytes 393220
  44.9 0.7 copy-start.16
  44.9 0.7 copy-start.17
  53.1 13.9 %collective-permute-start.16 = (bf16[320,256]{1,0:T(8,128)(2,1)}, bf16[320,256]{1,0:T(8,128)(2,1)S(1)}, u32[]{:S(2)}, u32[]{:S(2)}) collective-permute-start(bf16[320,256]{1,0:T(8,128)(2,1)} %project_image.1.refs_0_.refs_1_), channel_id=1, source_target_pairs={{0,28},{4,0},{8,4},{12,8},{16,12},{20,16},{24,20},{28,24},{1,29},{... | collective-permute-start | bytes 491528 | tf_op jit(solution)/shard_map/ppermute | solution.py:41
  54.1 12.9 %collective-permute-start.11 = (bf16[320,256]{1,0:T(8,128)(2,1)}, bf16[320,256]{1,0:T(8,128)(2,1)S(1)}, u32[]{:S(2)}, u32[]{:S(2)}) collective-permute-start(bf16[320,256]{1,0:T(8,128)(2,1)} %project_image.1.refs_0_.refs_1_), channel_id=1, source_target_pairs={{0,4},{4,8},{8,12},{12,16},{16,20},{20,24},{24,28},{28,0},{1,5},{5... | collective-permute-start | bytes 491528 | tf_op jit(solution)/shard_map/ppermute | solution.py:41
  58.1 0.8 copy-start.9
  58.2 1.1 copy-start.10
  68.1 11.9 %collective-permute-start.17 = (bf16[832,256]{1,0:T(8,128)(2,1)S(1)}, bf16[832,256]{1,0:T(8,128)(2,1)S(1)}, u32[]{:S(2)}, u32[]{:S(2)}) collective-permute-start(bf16[832,256]{1,0:T(8,128)(2,1)S(1)} %get-tuple-element.11), channel_id=1, source_target_pairs={{0,28},{4,0},{8,4},{12,8},{16,12},{20,16},{24,20},{28,24},{1,29},{... | collective-permute-start | bytes 1277960 | tf_op jit(solution)/shard_map/ppermute | solution.py:41
  68.2 11.8 %collective-permute-start.12 = (bf16[832,256]{1,0:T(8,128)(2,1)S(1)}, bf16[832,256]{1,0:T(8,128)(2,1)S(1)}, u32[]{:S(2)}, u32[]{:S(2)}) collective-permute-start(bf16[832,256]{1,0:T(8,128)(2,1)S(1)} %get-tuple-element.12), channel_id=1, source_target_pairs={{0,4},{4,8},{8,12},{12,16},{16,20},{20,24},{24,28},{28,0},{1,5},{5... | collective-permute-start | bytes 1277960 | tf_op jit(solution)/shard_map/ppermute | solution.py:41
  80.0 35.1 %copy-start.13 = (bf16[832,256]{1,0:T(8,128)(2,1)}, bf16[832,256]{1,0:T(8,128)(2,1)S(1)}, u32[]{:S(2)}) copy-start(bf16[832,256]{1,0:T(8,128)(2,1)S(1)} %collective-permute-done.17.refs_9_) | copy-start | bytes 1277956
  80.0 12.8 %collective-permute-start.18 = (bf16[832,256]{1,0:T(8,128)(2,1)S(1)}, bf16[832,256]{1,0:T(8,128)(2,1)S(1)}, u32[]{:S(2)}, u32[]{:S(2)}) collective-permute-start(bf16[832,256]{1,0:T(8,128)(2,1)S(1)} %collective-permute-done.17.refs_9_), channel_id=1, source_target_pairs={{0,28},{4,0},{8,4},{12,8},{16,12},{20,16},{24,20},{28,24},{1,29},{... | collective-permute-start | bytes 1277960 | tf_op jit(solution)/shard_map/ppermute | solution.py:41
  80.0 35.1 %copy-start.14 = (bf16[832,256]{1,0:T(8,128)(2,1)}, bf16[832,256]{1,0:T(8,128)(2,1)S(1)}, u32[]{:S(2)}) copy-start(bf16[832,256]{1,0:T(8,128)(2,1)S(1)} %collective-permute-done.12.refs_4_) | copy-start | bytes 1277956
  80.0 12.9 %collective-permute-start.13 = (bf16[832,256]{1,0:T(8,128)(2,1)S(1)}, bf16[832,256]{1,0:T(8,128)(2,1)S(1)}, u32[]{:S(2)}, u32[]{:S(2)}) collective-permute-start(bf16[832,256]{1,0:T(8,128)(2,1)S(1)} %collective-permute-done.12.refs_4_), channel_id=1, source_target_pairs={{0,4},{4,8},{8,12},{12,16},{16,20},{20,24},{24,28},{28,0},{1,5},{5... | collective-permute-start | bytes 1277960 | tf_op jit(solution)/shard_map/ppermute | solution.py:41
  92.8 22.3 %copy-start.11 = (bf16[832,256]{1,0:T(8,128)(2,1)}, bf16[832,256]{1,0:T(8,128)(2,1)S(1)}, u32[]{:S(2)}) copy-start(bf16[832,256]{1,0:T(8,128)(2,1)S(1)} %collective-permute-done.18.refs_10_) | copy-start | bytes 1277956
  92.8 9.1 %collective-permute-start.19 = (bf16[672,256]{1,0:T(8,128)(2,1)S(1)}, bf16[672,256]{1,0:T(8,128)(2,1)S(1)}, u32[]{:S(2)}, u32[]{:S(2)}) collective-permute-start(bf16[672,256]{1,0:T(8,128)(2,1)S(1)} %slice.28), channel_id=1, source_target_pairs={{0,28},{4,0},{8,4},{12,8},{16,12},{20,16},{24,20},{28,24},{1,29},{... | collective-permute-start | bytes 1032200 | tf_op jit(solution)/shard_map/ppermute | solution.py:41
  92.9 22.1 %copy-start.12 = (bf16[832,256]{1,0:T(8,128)(2,1)}, bf16[832,256]{1,0:T(8,128)(2,1)S(1)}, u32[]{:S(2)}) copy-start(bf16[832,256]{1,0:T(8,128)(2,1)S(1)} %collective-permute-done.13.refs_5_) | copy-start | bytes 1277956
  93.0 9.0 %collective-permute-start.14 = (bf16[672,256]{1,0:T(8,128)(2,1)S(1)}, bf16[672,256]{1,0:T(8,128)(2,1)S(1)}, u32[]{:S(2)}, u32[]{:S(2)}) collective-permute-start(bf16[672,256]{1,0:T(8,128)(2,1)S(1)} %slice.26), channel_id=1, source_target_pairs={{0,4},{4,8},{8,12},{12,16},{16,20},{20,24},{24,28},{28,0},{1,5},{5... | collective-permute-start | bytes 1032200 | tf_op jit(solution)/shard_map/ppermute | solution.py:41
  101.9 13.2 %collective-permute-start.20 = (bf16[256,256]{1,0:T(8,128)(2,1)S(1)}, bf16[256,256]{1,0:T(8,128)(2,1)S(1)}, u32[]{:S(2)}, u32[]{:S(2)}) collective-permute-start(bf16[256,256]{1,0:T(8,128)(2,1)S(1)} %slice.29), channel_id=1, source_target_pairs={{0,28},{4,0},{8,4},{12,8},{16,12},{20,16},{24,20},{28,24},{1,29},{... | collective-permute-start | bytes 393224 | tf_op jit(solution)/shard_map/ppermute | solution.py:41
  102.0 13.1 %collective-permute-start.15 = (bf16[256,256]{1,0:T(8,128)(2,1)S(1)}, bf16[256,256]{1,0:T(8,128)(2,1)S(1)}, u32[]{:S(2)}, u32[]{:S(2)}) collective-permute-start(bf16[256,256]{1,0:T(8,128)(2,1)S(1)} %slice.27), channel_id=1, source_target_pairs={{0,4},{4,8},{8,12},{12,16},{16,20},{20,24},{24,28},{28,0},{1,5},{5... | collective-permute-start | bytes 393224 | tf_op jit(solution)/shard_map/ppermute | solution.py:41
  105.6 9.5 %copy-start = (bf16[512,256]{1,0:T(8,128)(2,1)S(1)}, bf16[512,256]{1,0:T(8,128)(2,1)}, u32[]{:S(2)}) copy-start(bf16[512,256]{1,0:T(8,128)(2,1)} %get-tuple-element.8.refs_2_) | copy-start | bytes 786436
  105.6 9.5 %copy-start.1 = (bf16[320,256]{1,0:T(8,128)(2,1)S(1)}, bf16[320,256]{1,0:T(8,128)(2,1)}, u32[]{:S(2)}) copy-start(bf16[320,256]{1,0:T(8,128)(2,1)} %project_image.1.refs_0_.refs_1_) | copy-start | bytes 491524
  105.6 9.6 %copy-start.3 = (s32[3]{0:T(128)S(1)}, s32[3]{0:T(128)}, u32[]{:S(2)}) copy-start(s32[3]{0:T(128)} %pad_add_fusion.ids_ref) | copy-start | bytes 40
  105.6 9.6 %copy-start.4 = (s32[8]{0:T(128)S(1)}, s32[8]{0:T(128)}, u32[]{:S(2)}) copy-start(s32[8]{0:T(128)} %counts_ref.1) | copy-start | bytes 100

commit v5 on v4

--- a/solution.py
+++ b/solution.py
@@ -111,21 +111,28 @@
     )(ids, *arrays, gain, w_kv, w_query, *tables, *after)
 
 
-def text_kernel(ids_ref, own, one, three, two_lo, two_hi, gain, w_kv, cos, sin, *refs):
+def text_kernel(ids_ref, own, one_lo, one_hi, three_lo, three_hi, *refs):
+    twos = refs[:4]
+    gain, w_kv, cos, sin = refs[4:8]
     normed_ref, out_ref = refs[-2:]
     rows = own.shape[0]
-    low = pl.program_id(0) < pl.num_programs(0) // 2
-    two = jnp.where(low, two_lo[...], two_hi[...])
-    pieces = [own[...], one[...], three[...], two]
-    normalise(ids_ref[0], gain, pieces, normed_ref, slice(0, rows))
+    for n in range(4):
+        @pl.when(pl.program_id(0) == n)
+        def _():
+            one, three = ((one_lo, three_lo), (one_hi, three_hi))[n // 2]
+            pieces = [own[...], one[...], three[...], twos[n][...]]
+            normalise(ids_ref[0], gain, pieces, normed_ref, slice(0, rows))
+
     write_key_value(normed_ref[...], w_kv, cos[...], sin[...], out_ref, slice(0, rows))
 
 
 def project_text(ids, arrays, gain, w_kv, tables, after):
-    rows, tile = arrays[0].shape[0], 128
-    steps = rows // tile
+    rows = arrays[0].shape[0]
+    steps = 4
+    tile = rows // steps
     whole = pl.BlockSpec(memory_space=VMEM)
-    block = pl.BlockSpec((tile, D // 4), lambda r: (r, 0))
+    low = pl.BlockSpec((tile, D // 4), lambda r: (jnp.minimum(r, 1), 0))
+    high = pl.BlockSpec((tile, D // 4), lambda r: (jnp.maximum(r - 2, 0), 0))
     table = pl.BlockSpec((tile, HD // 2), lambda r: (r, 0))
     return pl.pallas_call(
         text_kernel,
@@ -135,12 +142,8 @@
         ],
         grid=(steps,),
         in_specs=[pl.BlockSpec(memory_space=SMEM)]
-        + [block] * 3
-        + [
-            pl.BlockSpec((tile, D // 4), lambda r: (jnp.minimum(r, steps // 2 - 1), 0)),
-            pl.BlockSpec((tile, D // 4), lambda r: (jnp.maximum(r - steps // 2, 0), 0)),
-        ]
-        + [whole] * 2
+        + [pl.BlockSpec((tile, D // 4), lambda r: (r, 0)), low, high, low, high]
+        + [whole] * 6
         + [table] * 2
         + [pl.BlockSpec(memory_space=pl.ANY)] * len(after),
         out_specs=[
@@ -151,6 +154,23 @@
         cost_estimate=pl.CostEstimate(flops=0, bytes_accessed=0, transcendentals=0),
         name="project_text",
     )(ids, *arrays, gain, w_kv, *tables, *after)
+
+
+def cut_kernel(starts, a_ref, b_ref, _, a_out, b_out):
+    for start, ref, out in zip(starts, (a_ref, b_ref), (a_out, b_out)):
+        out[...] = ref[start : start + out.shape[0], :]
+
+
+def cut_payloads(a, b, starts, rows, after):
+    whole = pl.BlockSpec(memory_space=VMEM)
+    return pl.pallas_call(
+        functools.partial(cut_kernel, starts),
+        out_shape=[jax.ShapeDtypeStruct((rows, a.shape[1]), a.dtype)] * 2,
+        in_specs=[whole] * 2 + [pl.BlockSpec(memory_space=pl.ANY)],
+        out_specs=[whole] * 2,
+        cost_estimate=pl.CostEstimate(flops=0, bytes_accessed=0, transcendentals=0),
+        name="cut_payloads",
+    )(a, b, after)
 
 
 def query_kernel(x_ref, w_ref, cos, sin, q_ref):
@@ -185,71 +205,68 @@
 def attention_kernel(tok, heads, ids_ref, counts_ref, starts_ref, *refs):
     q_ref, own_e, own_l, f1, f2, f3, f4, f5, b1, b2, b3, b4, b5, out_ref = refs[:14]
     q_buf, kv_buf, img_buf, s_buf, max_buf, sum_buf, acc_buf, sems = refs[14:]
-    step = pl.program_id(0)
     ctx, sample = ids_ref[1], ids_ref[2]
     factor = math.log2(math.e) / math.sqrt(HD)
 
-    @pl.when(step == 0)
-    def _():
-        rows_e, rows_l = own_e.shape[0], own_l.shape[0]
-        cut, part = rows_e // 2, rows_l // 2
-        moves = [(q_ref, q_buf)]
-        for d, array, base, first, count in (
-            (0, own_e, 0, 0, rows_e),
-            (1, f1, 0, 0, rows_e),
-            (2, f2, 0, 0, rows_e),
-            (3, f3, 0, 0, rows_e),
-            (4, f4, 0, cut, cut),
-            (4, b4, rows_l, 0, cut),
-            (5, b3, rows_l, 0, rows_e),
-            (6, b2, rows_l, 0, rows_e),
-            (7, b1, 0, 0, rows_e),
-        ):
-            shard = (ctx - d) & (SHARDS - 1)
-            moves.append(
-                (array.at[pl.ds(base, count), :], img_buf.at[shard, pl.ds(first, count), :])
-            )
-        for d, array, base, first, count in (
-            (0, own_l, 0, 0, rows_l),
-            (1, f2, rows_e, 0, rows_l),
-            (2, f3, rows_e, 0, rows_l),
-            (3, f4, cut, 0, rows_l),
-            (4, f5, 0, 0, part),
-            (4, b5, 0, part, part),
-            (5, b4, 0, 0, rows_l),
-            (6, b3, 0, 0, rows_l),
-            (7, b2, 0, 0, rows_l),
-        ):
-            shard = (ctx - d) & (SHARDS - 1)
-            place = pl.ds(pl.multiple_of(shard * tok + first, part), count)
-            moves.append((array.at[pl.ds(base, count), :], kv_buf.at[place, :]))
-        copies = [
-            pltpu.make_async_copy(source, target, sems.at[n])
-            for n, (source, target) in enumerate(moves)
-        ]
-        for copy in copies:
-            copy.start()
-        for copy in copies:
-            copy.wait()
-        before = images_before(counts_ref, sample)
-        for c in range(SHARDS):
-            slot = (c - before) & (MAX_IMG - 1)
-            start = jnp.where(slot < counts_ref[sample], starts_ref[sample, slot], -1)
-
-            @pl.when(start >= 0)
-            def _():
-                rows = pl.ds(pl.multiple_of(start, IMG_TOK), IMG_TOK)
-                kv_buf[rows, :] = img_buf[c, :IMG_TOK, :]
-
-            @pl.when((start >= ctx * tok) & (start < ctx * tok + tok))
-            def _():
-                rows = pl.ds(pl.multiple_of(start - ctx * tok, IMG_TOK), IMG_TOK)
-                for n in range(heads // 2):
-                    q_buf[rows, n * 2 * HD : (n + 1) * 2 * HD] = img_buf[
-                        c, IMG_TOK * (n + 1) : IMG_TOK * (n + 2), :
-                    ]
-
-    def phase(do_score, do_mix):
+    rows_e, rows_l = own_e.shape[0], own_l.shape[0]
+    cut, part = rows_e // 2, rows_l // 2
+    moves = [(q_ref, q_buf)]
+    for d, array, base, first, count in (
+        (0, own_e, 0, 0, rows_e),
+        (1, f1, 0, 0, rows_e),
+        (2, f2, 0, 0, rows_e),
+        (3, f3, 0, 0, rows_e),
+        (4, f4, 0, cut, cut),
+        (4, b4, rows_l, 0, cut),
+        (5, b3, rows_l, 0, rows_e),
+        (6, b2, rows_l, 0, rows_e),
+        (7, b1, 0, 0, rows_e),
+    ):
+        shard = (ctx - d) & (SHARDS - 1)
+        moves.append(
+            (array.at[pl.ds(base, count), :], img_buf.at[shard, pl.ds(first, count), :])
+        )
+    for d, array, base, first, count in (
+        (0, own_l, 0, 0, rows_l),
+        (1, f2, rows_e, 0, rows_l),
+        (2, f3, rows_e, 0, rows_l),
+        (3, f4, cut, 0, rows_l),
+        (4, f5, 0, 0, part),
+        (4, b5, 0, part, part),
+        (5, b4, 0, 0, rows_l),
+        (6, b3, 0, 0, rows_l),
+        (7, b2, 0, 0, rows_l),
+    ):
+        shard = (ctx - d) & (SHARDS - 1)
+        place = pl.ds(pl.multiple_of(shard * tok + first, part), count)
+        moves.append((array.at[pl.ds(base, count), :], kv_buf.at[place, :]))
+    copies = [
+        pltpu.make_async_copy(source, target, sems.at[n])
+        for n, (source, target) in enumerate(moves)
+    ]
+    for copy in copies:
+        copy.start()
+    for copy in copies:
+        copy.wait()
+    before = images_before(counts_ref, sample)
+    for c in range(SHARDS):
+        slot = (c - before) & (MAX_IMG - 1)
+        start = jnp.where(slot < counts_ref[sample], starts_ref[sample, slot], -1)
+
+        @pl.when(start >= 0)
+        def _():
+            rows = pl.ds(pl.multiple_of(start, IMG_TOK), IMG_TOK)
+            kv_buf[rows, :] = img_buf[c, :IMG_TOK, :]
+
+        @pl.when((start >= ctx * tok) & (start < ctx * tok + tok))
+        def _():
+            rows = pl.ds(pl.multiple_of(start - ctx * tok, IMG_TOK), IMG_TOK)
+            for n in range(heads // 2):
+                q_buf[rows, n * 2 * HD : (n + 1) * 2 * HD] = img_buf[
+                    c, IMG_TOK * (n + 1) : IMG_TOK * (n + 2), :
+                ]
+
+    def phase(step, do_score, do_mix):
         slot = lax.rem(step, 2)
         other = 1 - slot
 
@@ -296,11 +313,12 @@
             max_buf[slot] = jnp.broadcast_to(top, (tok, HD))
         if do_mix:
             total = jnp.sum(sum_buf[...], axis=1, keepdims=True)
-            out_ref[...] = (acc_buf[...] / total).astype(BF16)
-
-    pl.when(step == 0)(lambda: phase(True, False))
-    pl.when((step > 0) & (step < heads))(lambda: phase(True, True))
-    pl.when(step == heads)(lambda: phase(False, True))
+            columns = pl.ds(pl.multiple_of((step - 1) * HD, HD), HD)
+            out_ref[:, columns] = (acc_buf[...] / total).astype(BF16)
+
+    phase(jnp.int32(0), True, False)
+    pl.loop(1, heads)(lambda step: phase(step, True, True))
+    phase(jnp.int32(heads), False, True)
 
 
 def attention(tok, heads, scalars, arrays):
@@ -308,10 +326,9 @@
     return pl.pallas_call(
         functools.partial(attention_kernel, tok, heads),
         out_shape=jax.ShapeDtypeStruct((tok, heads * HD), BF16),
-        grid=(heads + 1,),
         in_specs=[pl.BlockSpec(memory_space=SMEM)] * 3
         + [pl.BlockSpec(memory_space=pl.ANY)] * len(arrays),
-        out_specs=pl.BlockSpec((tok, HD), lambda t: (0, jnp.maximum(t - 1, 0))),
+        out_specs=pl.BlockSpec(memory_space=VMEM),
         scratch_shapes=[
             pltpu.VMEM((tok, heads * HD), BF16),
             pltpu.VMEM((SHARDS * tok, 2 * HD), BF16),
@@ -360,21 +377,28 @@
 
     my_slot, my_across, my_distance = source(sample)
     _, _, its_distance = source(sample ^ 1)
-    one, three = first_hop(text_rows)
+    half = tok // 2
+    low, high = text_rows[:half], text_rows[half:]
+    one_lo, three_lo = first_hop(low)
     routed = [visual_rows] + [shift(visual_rows, "dp", 2 * d, False) for d in (1, 2, 3)]
+    one_hi, three_hi = first_hop(high)
     for_other = choose(its_distance, routed)
     from_other = lax.ppermute(for_other, "dp", [(i, i ^ 1) for i in range(SHARDS)])
     image = choose(jnp.where(my_across == 1, 4, my_distance), routed + [from_other])
+    twos_lo = second_hop(one_lo, three_lo)
     image_parts = [image] + [exchange(image, mask) for mask in (1, 3, 2)]
-    two_lo, two_hi = second_hop(one, three)
+    twos_hi = second_hop(one_hi, three_hi)
 
     mine = (every[:, None] == sample) & (every[None, :] == my_slot)
     my_start = jnp.sum(jnp.where(mine, image_starts, 0))
     text_tables = rotary_tables(ctx * tok + jnp.arange(tok, dtype=jnp.int32))
     image_tables = rotary_tables(my_start + jnp.arange(IMG_TOK, dtype=jnp.int32))
-    own_e = project_image(ids, image_parts, gain, w_kv, w_query, image_tables, (one, three))
+    own_e = project_image(
+        ids, image_parts, gain, w_kv, w_query, image_tables, (one_hi, three_hi)
+    )
     normed, own_l = project_text(
-        ids, [text_rows, one, three, two_lo, two_hi], gain, w_kv, text_tables, (own_e,)
+        ids, [text_rows, one_lo, one_hi, three_lo, three_hi, *twos_lo, *twos_hi],
+        gain, w_kv, text_tables, (own_e,)
     )
     q_all = query(normed, w_query, text_tables)
 
@@ -383,7 +407,8 @@
     f2 = shift(jnp.concatenate([f1, own_l], axis=0), "ctx", 1, True)
     b2 = shift(jnp.concatenate([own_l, b1], axis=0), "ctx", -1, True)
     f3, b3 = shift(f2, "ctx", 1, True), shift(b2, "ctx", -1, True)
-    f4, b4 = shift(f3[cut:], "ctx", 1, True), shift(b3[: tok + cut], "ctx", -1, True)
+    onward = cut_payloads(f3, b3, (cut, 0), tok + cut, q_all)
+    f4, b4 = shift(onward[0], "ctx", 1, True), shift(onward[1], "ctx", -1, True)
     f5 = shift(f4[cut : cut + part], "ctx", 1, True)
     b5 = shift(b4[part:tok], "ctx", -1, True)
     return attention(

time: 149 us -> 150 us (level)
  waiting for transfers between devices: 36.8 us -> 28.7 us
  local copies, waits for them, and re-layouts: 4.77 us -> 9.01 us
  Pallas kernels: 57.6 us -> 59.7 us
  starting transfers between devices: 37.7 us -> 39.4 us
    ppermute x7 -> x11, starting transfers between devices: 10 us -> 14.8 us  [exchange(): return lax.ppermute(x, 'mp', [(i, i ^ mask) for i in range(4)])]
    ppermute x7 -> x11, waiting for transfers between devices: 13.1 us -> 8.83 us  [exchange(): return lax.ppermute(x, 'mp', [(i, i ^ mask) for i in range(4)])]
    ppermute x13, waiting for transfers between devices: 23.2 us -> 19.6 us  [shift(): return lax.ppermute(x, axis, pairs)]
    ppermute x13, starting transfers between devices: 27.6 us -> 24.6 us  [shift(): return lax.ppermute(x, axis, pairs)]
    slice x2 -> x1, local copies, waits for them, and re-layouts: 0.05 us -> 2.23 us  [on_device(): low, high = (text_rows[:half], text_rows[half:])]
    pallas_call x0 -> x1, Pallas kernels: none -> 2 us  [cut_payloads(): pl.pallas_call(functools.partial(cut_kernel, starts), out_shape=[jax.Shap...]
    unnamed x37 -> x43, local copies, waits for them, and re-layouts: 3.34 us -> 4.55 us
  transfers between devices with their start and end apart: 21 -> 25, of which waited for: 7 -> 6; matrix products, arithmetic and copies ran while one was open for 7% -> 9% of each run, Pallas kernels for 17% -> 17%
where the time goes in v5:
time: 150 us; the launch traced here: 148 us
  Pallas kernels  59.7 us (40%)
  starting transfers between devices  39.4 us (26%)
  waiting for transfers between devices  28.7 us (19%)
  local copies, waits for them, and re-layouts  9.01 us (6%)
  other arithmetic  8.26 us (6%)
  between operations  3.07 us (2%)
    pallas_call x1, Pallas kernels, attention(): pl.pallas_call(functools.partial(attention_kernel, tok, heads), out_shape...  33.1 us
    ppermute x13, starting transfers between devices, shift(): return lax.ppermute(x, axis, pairs)  24.6 us
    ppermute x13, waiting for transfers between devices, shift(): return lax.ppermute(x, axis, pairs)  19.6 us
    ppermute x11, starting transfers between devices, exchange(): return lax.ppermute(x, 'mp', [(i, i ^ mask) for i in range(4)])  14.8 us
    pallas_call x1, Pallas kernels, query(): pl.pallas_call(query_kernel, out_shape=jax.ShapeDtypeStruct((rows, column...  9.42 us
    ppermute x11, waiting for transfers between devices, exchange(): return lax.ppermute(x, 'mp', [(i, i ^ mask) for i in range(4)])  8.83 us
    pallas_call x1, Pallas kernels, project_text(): pl.pallas_call(text_kernel, out_shape=[jax.ShapeDtypeStruct((rows, D), BF...  7.87 us
    pallas_call x1, Pallas kernels, project_image(): pl.pallas_call(image_kernel, out_shape=jax.ShapeDtypeStruct(((1 + steps)...  7.35 us
  transfers between devices with their start and end apart: 25, of which 6 were waited for; matrix products, arithmetic and copies ran while one was open for 9% of the time, Pallas kernels for 17%

profile of v5, /device:TPU:224, one launch (start us, length us, event | category | flops | bytes accessed | tf_op | source)
XLA Modules:
  0.0 148.2 jit_solution(14826390740925041804)
XLA Ops:
  0.0 3.6 %collective-permute-start.10 = (bf16[64,1024]{1,0:T(8,128)(2,1)}, bf16[64,1024]{1,0:T(8,128)(2,1)S(1)}, u32[]{:S(2)}, u32[]{:S(2)}) collective-permute-start(bf16[64,1024]{1,0:T(8,128)(2,1)} %param.9), channel_id=1, source_target_pairs={{0,64},{32,96},{64,128},{96,160},{128,192},{160,224},{1,65},{33,97... | collective-permute-start | bytes 393224 | tf_op jit(solution)/shard_map/ppermute | solution.py:41
  3.6 4.8 %collective-permute-start.9 = (bf16[64,1024]{1,0:T(8,128)(2,1)}, bf16[64,1024]{1,0:T(8,128)(2,1)S(1)}, u32[]{:S(2)}, u32[]{:S(2)}) collective-permute-start(bf16[64,1024]{1,0:T(8,128)(2,1)} %param.9), channel_id=1, source_target_pairs={{0,128},{32,160},{64,192},{96,224},{1,129},{33,161},{65,193},{97,2... | collective-permute-start | bytes 393224 | tf_op jit(solution)/shard_map/ppermute | solution.py:41
  8.4 1.9 %collective-permute-start.8 = (bf16[64,1024]{1,0:T(8,128)(2,1)}, bf16[64,1024]{1,0:T(8,128)(2,1)}, u32[]{:S(2)}, u32[]{:S(2)}) collective-permute-start(bf16[64,1024]{1,0:T(8,128)(2,1)} %param.9), channel_id=1, source_target_pairs={{0,192},{32,224},{1,193},{33,225},{2,194},{34,226},{3,195},{35,227... | collective-permute-start | bytes 393224 | tf_op jit(solution)/shard_map/ppermute | solution.py:41
  10.4 2.2 %fusion.2 = (bf16[256,1024]{1,0:T(8,128)(2,1)}, bf16[256,1024]{1,0:T(8,128)(2,1)}) fusion(bf16[512,1024]{1,0:T(8,128)(2,1)} %own.1), kind=kLoop, calls=%fused_computation.21 | loop fusion | bytes 2097152 | tf_op jit(solution)/shard_map/slice | solution.py:381
  12.6 2.8 %collective-permute-start.3 = (bf16[256,1024]{1,0:T(8,128)(2,1)}, bf16[256,1024]{1,0:T(8,128)(2,1)S(1)}, u32[]{:S(2)}, u32[]{:S(2)}) collective-permute-start(bf16[256,1024]{1,0:T(8,128)(2,1)} %get-tuple-element.15), channel_id=1, source_target_pairs={{0,3},{1,2},{2,1},{3,0},{4,7},{5,6},{6,5},{7,4},{8,11},{9,10},{10,... | collective-permute-start | bytes 1572872 | tf_op jit(solution)/shard_map/ppermute | solution.py:45
  15.4 0.2 collective-permute-start.1
  15.6 0.7 fusion
  16.9 0.0 copy-start.8
  17.0 0.0 copy-start.2
  17.0 0.0 copy-start.9
  17.0 1.5 %constant_dynamic-update-slice_fusion.1 = bf16[4096,256]{1,0:T(8,128)(2,1)S(1)} fusion(bf16[4096,128]{1,0:T(8,128)(2,1)} %param.14), kind=kLoop, calls=%fused_computation.9 | loop fusion | bytes 2097152
  18.5 0.2 constant_dynamic-update-slice_fusion.w_kv.refs_5_
  18.8 0.9 select_reduce_fusion
  21.0 0.7 add_convert_fusion.1
  21.7 1.2 collective-permute-start.2
  22.9 0.8 collective-permute-start
  23.7 0.0 collective-permute-done.8
  23.7 0.7 select_select_fusion.1
  24.4 0.8 multiply_sine_fusion.1
  25.9 0.2 collective-permute-done.11
  26.1 0.7 select_select_fusion.own
  26.8 2.8 %collective-permute-start.14 = (bf16[64,1024]{1,0:T(8,128)(2,1)}, bf16[64,1024]{1,0:T(8,128)(2,1)S(1)}, u32[]{:S(2)}, u32[]{:S(2)}) collective-permute-start(bf16[64,1024]{1,0:T(8,128)(2,1)} %select_select_fusion.own), channel_id=1, source_target_pairs={{0,2},{1,3},{2,0},{3,1},{4,6},{5,7},{6,4},{7,5},{8,10},{9,11},{10,... | collective-permute-start | bytes 393224 | tf_op jit(solution)/shard_map/ppermute | solution.py:45
  29.6 0.0 collective-permute-done.3.refs_1_.three_hi
  29.6 2.1 %collective-permute-start.13 = (bf16[64,1024]{1,0:T(8,128)(2,1)}, bf16[64,1024]{1,0:T(8,128)(2,1)S(1)}, u32[]{:S(2)}, u32[]{:S(2)}) collective-permute-start(bf16[64,1024]{1,0:T(8,128)(2,1)} %select_select_fusion.own), channel_id=1, source_target_pairs={{0,3},{1,2},{2,1},{3,0},{4,7},{5,6},{6,5},{7,4},{8,11},{9,10},{10,... | collective-permute-start | bytes 393224 | tf_op jit(solution)/shard_map/ppermute | solution.py:45
  31.7 0.8 pad_add_fusion.ids_ref
  32.5 8.8 %collective-permute-done.2.three_lo = bf16[256,1024]{1,0:T(8,128)(2,1)} collective-permute-done((bf16[256,1024]{1,0:T(8,128)(2,1)}, bf16[256,1024]{1,0:T(8,128)(2,1)}, u32[]{:S(2)}, u32[]{:S(2)}) %collective-permute-start.2) | collective-permute-done | bytes 524320 | tf_op jit(solution)/shard_map/ppermute | solution.py:45
  41.3 0.3 collective-permute-start.7
  41.6 1.0 slice.33
  42.6 2.6 %collective-permute-start.6 = (bf16[128,1024]{1,0:T(8,128)(2,1)S(1)}, bf16[128,1024]{1,0:T(8,128)(2,1)S(1)}, u32[]{:S(2)}, u32[]{:S(2)}) collective-permute-start(bf16[128,1024]{1,0:T(8,128)(2,1)S(1)} %slice.34), channel_id=1, source_target_pairs={{0,3},{1,2},{2,1},{3,0},{4,7},{5,6},{6,5},{7,4},{8,11},{9,10},{10,... | collective-permute-start | bytes 786440 | tf_op jit(solution)/shard_map/ppermute | solution.py:45
  45.1 1.0 slice.32
  46.1 0.0 collective-permute-done.14.two
  46.1 1.5 %collective-permute-start.5 = (bf16[128,1024]{1,0:T(8,128)(2,1)S(1)}, bf16[128,1024]{1,0:T(8,128)(2,1)S(1)}, u32[]{:S(2)}, u32[]{:S(2)}) collective-permute-start(bf16[128,1024]{1,0:T(8,128)(2,1)S(1)} %slice.33), channel_id=1, source_target_pairs={{0,1},{1,0},{2,3},{3,2},{4,5},{5,4},{6,7},{7,6},{8,9},{9,8},{10,11... | collective-permute-start | bytes 786440 | tf_op jit(solution)/shard_map/ppermute | solution.py:45
  47.6 0.6 collective-permute-start.4
  48.2 0.0 collective-permute-done.12.one
  48.3 0.6 copy-done.20
  48.9 7.4 %project_image.1.refs_8_.refs_1_ = bf16[320,256]{1,0:T(8,128)(2,1)} custom-call(s32[3]{0:T(128)} %pad_add_fusion.ids_ref, bf16[64,1024]{1,0:T(8,128)(2,1)} %select_select_fusion.own, bf16[64,1024]{1,0:T(8,128)(2,1)} %copy-done.20, bf16[64,1024]{1,0:T(8,128)(2,1)} %copy-done.19, bf16[64,1024]{1,0:T(8,128)(2,1)} %copy-done.18, f32[1,4096]{1,0:T(1,128)} %bitcast.4, ...), custom_call_target="tpu_custom_call" | custom-call | flops 8000000000 | bytes 10485760 | tf_op jit(solution)/shard_map/project_image/pallas_call | solution.py:97
  56.3 1.0 collective-permute-start.18
  57.3 0.0 collective-permute-done.7.refs_3_
  57.3 2.2 %collective-permute-start.15 = (bf16[320,256]{1,0:T(8,128)(2,1)}, bf16[320,256]{1,0:T(8,128)(2,1)S(1)}, u32[]{:S(2)}, u32[]{:S(2)}) collective-permute-start(bf16[320,256]{1,0:T(8,128)(2,1)} %project_image.1.refs_8_.refs_1_), channel_id=1, source_target_pairs={{0,4},{4,8},{8,12},{12,16},{16,20},{20,24},{24,28},{28,0},{1,5},{5... | collective-permute-start | bytes 491528 | tf_op jit(solution)/shard_map/ppermute | solution.py:41
  59.5 1.8 %multiply_sine_fusion = (f32[512,64]{1,0:T(8,128)}, f32[512,64]{1,0:T(8,128)}) fusion(f32[64]{0:T(128)S(1)} %multiply_exponential_fusion, f32[512]{0:T(512)S(1)} %add_convert_fusion), kind=kLoop, calls=%fused_computation.2 | loop fusion | flops 32768 | bytes 264448 | tf_op jit(solution)/shard_map/sin | solution.py:30
  61.3 0.0 collective-permute-done.6.refs_2_
  61.3 0.0 collective-permute-done.5.refs_1_
  61.4 0.7 copy-done.13
  62.0 0.1 copy-done.14
  62.1 0.1 copy-done.15
  62.2 7.9 %project_text.1 = (bf16[512,4096]{1,0:T(8,128)(2,1)}, bf16[512,256]{1,0:T(8,128)(2,1)}) custom-call(s32[3]{0:T(128)} %pad_add_fusion.ids_ref, bf16[512,1024]{1,0:T(8,128)(2,1)} %own.1, bf16[256,1024]{1,0:T(8,128)(2,1)} %collective-permute-done.one_lo, bf16[256,1024]{1,0:T(8,128)(2,1)} %copy-done.7, bf16[256,1024]{1,0:T(8,128)(2,1)} %collective-permute-done.2.three_lo, ...), custom_call_target="tpu_custom_call" | custom-call | tf_op jit(solution)/shard_map/project_text/pallas_call | solution.py:137
  70.1 0.0 collective-permute-done.18.refs_8_
  70.1 1.1 pad_maximum_fusion.1
  71.2 0.1 collective-permute-start.19
  71.3 3.2 %collective-permute-start.16 = (bf16[832,256]{1,0:T(8,128)(2,1)S(1)}, bf16[832,256]{1,0:T(8,128)(2,1)S(1)}, u32[]{:S(2)}, u32[]{:S(2)}) collective-permute-start(bf16[832,256]{1,0:T(8,128)(2,1)S(1)} %get-tuple-element.18), channel_id=1, source_target_pairs={{0,4},{4,8},{8,12},{12,16},{16,20},{20,24},{24,28},{28,0},{1,5},{5... | collective-permute-start | bytes 1277960 | tf_op jit(solution)/shard_map/ppermute | solution.py:41
  74.6 8.7 %collective-permute-done.19.refs_9_ = bf16[832,256]{1,0:T(8,128)(2,1)S(1)} collective-permute-done((bf16[832,256]{1,0:T(8,128)(2,1)S(1)}, bf16[832,256]{1,0:T(8,128)(2,1)S(1)}, u32[]{:S(2)}, u32[]{:S(2)}) %collective-permute-start.19) | collective-permute-done | bytes 426016 | tf_op jit(solution)/shard_map/ppermute | solution.py:41
  83.2 3.5 %collective-permute-start.17 = (bf16[832,256]{1,0:T(8,128)(2,1)S(1)}, bf16[832,256]{1,0:T(8,128)(2,1)S(1)}, u32[]{:S(2)}, u32[]{:S(2)}) collective-permute-start(bf16[832,256]{1,0:T(8,128)(2,1)S(1)} %collective-permute-done.16.refs_4_), channel_id=1, source_target_pairs={{0,4},{4,8},{8,12},{12,16},{16,20},{20,24},{24,28},{28,0},{1,5},{5... | collective-permute-start | bytes 1277960 | tf_op jit(solution)/shard_map/ppermute | solution.py:41
  86.7 9.4 %query.1._.refs_0_ = bf16[512,1024]{1,0:T(8,128)(2,1)} custom-call(bf16[512,4096]{1,0:T(8,128)(2,1)} %get-tuple-element.9.x_ref, bf16[4096,1024]{1,0:T(8,128)(2,1)} %w_ref.1, f32[512,64]{1,0:T(8,128)} %get-tuple-element.20.refs_6_.cos, f32[512,64]{1,0:T(8,128)} %get-tuple-element.19.refs_7_.sin), custom_call_target="tpu_custom_call" | custom-call | flops 8000000000 | bytes 10485760 | tf_op jit(solution)/shard_map/query/pallas_call | solution.py:186
  96.2 0.8 copy-done.10
  97.0 0.8 copy-done.11
  97.7 2.0 %cut_payloads.1 = (bf16[672,256]{1,0:T(8,128)(2,1)}, bf16[672,256]{1,0:T(8,128)(2,1)}) custom-call(bf16[832,256]{1,0:T(8,128)(2,1)} %copy-done.11, bf16[832,256]{1,0:T(8,128)(2,1)} %copy-done.10, bf16[512,1024]{1,0:T(8,128)(2,1)} %query.1._.refs_0_), custom_call_target="tpu_custom_call" | custom-call | tf_op jit(solution)/shard_map/cut_payloads/pallas_call | solution.py:166
  99.7 0.2 collective-permute-start.21
  99.9 1.9 %collective-permute-start.23 = (bf16[672,256]{1,0:T(8,128)(2,1)}, bf16[672,256]{1,0:T(8,128)(2,1)S(1)}, u32[]{:S(2)}, u32[]{:S(2)}) collective-permute-start(bf16[672,256]{1,0:T(8,128)(2,1)} %get-tuple-element.12), channel_id=1, source_target_pairs={{0,28},{4,0},{8,4},{12,8},{16,12},{20,16},{24,20},{28,24},{1,29},{... | collective-permute-start | bytes 1032200 | tf_op jit(solution)/shard_map/ppermute | solution.py:41
  101.7 5.4 %collective-permute-done.21.refs_6_ = bf16[672,256]{1,0:T(8,128)(2,1)S(1)} collective-permute-done((bf16[672,256]{1,0:T(8,128)(2,1)}, bf16[672,256]{1,0:T(8,128)(2,1)S(1)}, u32[]{:S(2)}, u32[]{:S(2)}) %collective-permute-start.21) | collective-permute-done | bytes 344096 | tf_op jit(solution)/shard_map/ppermute | solution.py:41
  107.2 1.5 collective-permute-start.22
  108.7 0.7 collective-permute-start.24
  109.4 2.8 %collective-permute-done.22.refs_7_ = bf16[256,256]{1,0:T(8,128)(2,1)S(1)} collective-permute-done((bf16[256,256]{1,0:T(8,128)(2,1)S(1)}, bf16[256,256]{1,0:T(8,128)(2,1)S(1)}, u32[]{:S(2)}, u32[]{:S(2)}) %collective-permute-start.22) | collective-permute-done | bytes 131104 | tf_op jit(solution)/shard_map/ppermute | solution.py:41
  112.2 2.7 %collective-permute-done.24.refs_12_ = bf16[256,256]{1,0:T(8,128)(2,1)S(1)} collective-permute-done((bf16[256,256]{1,0:T(8,128)(2,1)S(1)}, bf16[256,256]{1,0:T(8,128)(2,1)S(1)}, u32[]{:S(2)}, u32[]{:S(2)}) %collective-permute-start.24) | collective-permute-done | bytes 131104 | tf_op jit(solution)/shard_map/ppermute | solution.py:41
  114.9 33.1 %attention.1 = bf16[512,1024]{1,0:T(8,128)(2,1)} custom-call(s32[3]{0:T(128)S(1)} %copy-done.3, s32[8]{0:T(128)S(1)} %copy-done.4, s32[8,8]{1,0:T(8,128)S(1)} %copy-done.2, bf16[512,1024]{1,0:T(8,128)(2,1)} %query.1._.refs_0_, bf16[320,256]{1,0:T(8,128)(2,1)S(1)} %copy-done.1, bf16[512,256]{1,0:T(8,128)(2,1)S(1)} %copy-done, ...), custom_call_target="tpu_custom_call" | custom-call | flops 8589934592 | bytes 8388608 | tf_op jit(solution)/shard_map/attention/pallas_call | solution.py:326
  (54 shorter events, 0.2 us)
Async XLA Ops:
  0.0 15.6 %copy-start.4 = (s32[8]{0:T(128)S(1)}, s32[8]{0:T(128)}, u32[]{:S(2)}) copy-start(s32[8]{0:T(128)} %counts_ref.1) | copy-start | bytes 100
  0.0 21.7 %collective-permute-start.10 = (bf16[64,1024]{1,0:T(8,128)(2,1)}, bf16[64,1024]{1,0:T(8,128)(2,1)S(1)}, u32[]{:S(2)}, u32[]{:S(2)}) collective-permute-start(bf16[64,1024]{1,0:T(8,128)(2,1)} %param.9), channel_id=1, source_target_pairs={{0,64},{32,96},{64,128},{96,160},{128,192},{160,224},{1,65},{33,97... | collective-permute-start | bytes 393224 | tf_op jit(solution)/shard_map/ppermute | solution.py:41
  3.6 19.3 %collective-permute-start.9 = (bf16[64,1024]{1,0:T(8,128)(2,1)}, bf16[64,1024]{1,0:T(8,128)(2,1)S(1)}, u32[]{:S(2)}, u32[]{:S(2)}) collective-permute-start(bf16[64,1024]{1,0:T(8,128)(2,1)} %param.9), channel_id=1, source_target_pairs={{0,128},{32,160},{64,192},{96,224},{1,129},{33,161},{65,193},{97,2... | collective-permute-start | bytes 393224 | tf_op jit(solution)/shard_map/ppermute | solution.py:41
  8.4 15.2 %collective-permute-start.8 = (bf16[64,1024]{1,0:T(8,128)(2,1)}, bf16[64,1024]{1,0:T(8,128)(2,1)}, u32[]{:S(2)}, u32[]{:S(2)}) collective-permute-start(bf16[64,1024]{1,0:T(8,128)(2,1)} %param.9), channel_id=1, source_target_pairs={{0,192},{32,224},{1,193},{33,225},{2,194},{34,226},{3,195},{35,227... | collective-permute-start | bytes 393224 | tf_op jit(solution)/shard_map/ppermute | solution.py:41
  12.6 17.0 %collective-permute-start.3 = (bf16[256,1024]{1,0:T(8,128)(2,1)}, bf16[256,1024]{1,0:T(8,128)(2,1)S(1)}, u32[]{:S(2)}, u32[]{:S(2)}) collective-permute-start(bf16[256,1024]{1,0:T(8,128)(2,1)} %get-tuple-element.15), channel_id=1, source_target_pairs={{0,3},{1,2},{2,1},{3,0},{4,7},{5,6},{6,5},{7,4},{8,11},{9,10},{10,... | collective-permute-start | bytes 1572872 | tf_op jit(solution)/shard_map/ppermute | solution.py:45
  15.4 16.3 %collective-permute-start.1 = (bf16[256,1024]{1,0:T(8,128)(2,1)}, bf16[256,1024]{1,0:T(8,128)(2,1)S(1)}, u32[]{:S(2)}, u32[]{:S(2)}) collective-permute-start(bf16[256,1024]{1,0:T(8,128)(2,1)} %get-tuple-element.15), channel_id=1, source_target_pairs={{0,1},{1,0},{2,3},{3,2},{4,5},{5,4},{6,7},{7,6},{8,9},{9,8},{10,11... | collective-permute-start | bytes 1572872 | tf_op jit(solution)/shard_map/ppermute | solution.py:45
  16.9 1.5 %copy-start.8 = (bf16[4096,128]{1,0:T(8,128)(2,1)S(1)}, bf16[4096,128]{1,0:T(8,128)(2,1)}, u32[]{:S(2)}) copy-start(bf16[4096,128]{1,0:T(8,128)(2,1)} %param.15) | copy-start | bytes 3145732
  17.0 1.8 %copy-start.2 = (s32[8,8]{1,0:T(8,128)S(1)}, s32[8,8]{1,0:T(8,128)}, u32[]{:S(2)}) copy-start(s32[8,8]{1,0:T(8,128)} %starts_ref.1) | copy-start | bytes 772
  17.0 6.7 %copy-start.9 = (bf16[64,1024]{1,0:T(8,128)(2,1)S(1)}, bf16[64,1024]{1,0:T(8,128)(2,1)}, u32[]{:S(2)}) copy-start(bf16[64,1024]{1,0:T(8,128)(2,1)} %param.9) | copy-start | bytes 393220
  18.7 29.5 %copy-start.5 = (bf16[4096,256]{1,0:T(8,128)(2,1)}, bf16[4096,256]{1,0:T(8,128)(2,1)S(1)}, u32[]{:S(2)}) copy-start(bf16[4096,256]{1,0:T(8,128)(2,1)S(1)} %constant_dynamic-update-slice_fusion.w_kv.refs_5_) | copy-start | bytes 6291460
  21.7 19.6 %collective-permute-start.2 = (bf16[256,1024]{1,0:T(8,128)(2,1)}, bf16[256,1024]{1,0:T(8,128)(2,1)}, u32[]{:S(2)}, u32[]{:S(2)}) collective-permute-start(bf16[256,1024]{1,0:T(8,128)(2,1)} %get-tuple-element.16), channel_id=1, source_target_pairs={{0,3},{1,2},{2,1},{3,0},{4,7},{5,6},{6,5},{7,4},{8,11},{9,10},{10,... | collective-permute-start | bytes 1572872 | tf_op jit(solution)/shard_map/ppermute | solution.py:45
  22.9 19.6 %collective-permute-start = (bf16[256,1024]{1,0:T(8,128)(2,1)}, bf16[256,1024]{1,0:T(8,128)(2,1)}, u32[]{:S(2)}, u32[]{:S(2)}) collective-permute-start(bf16[256,1024]{1,0:T(8,128)(2,1)} %get-tuple-element.16), channel_id=1, source_target_pairs={{0,1},{1,0},{2,3},{3,2},{4,5},{5,4},{6,7},{7,6},{8,9},{9,8},{10,11... | collective-permute-start | bytes 1572872 | tf_op jit(solution)/shard_map/ppermute | solution.py:45
  24.4 1.7 %collective-permute-start.11 = (bf16[64,1024]{1,0:T(8,128)(2,1)}, bf16[64,1024]{1,0:T(8,128)(2,1)}, u32[]{:S(2)}, u32[]{:S(2)}) collective-permute-start(bf16[64,1024]{1,0:T(8,128)(2,1)} %select_select_fusion.1), channel_id=1, source_target_pairs={{0,32},{32,0},{64,96},{96,64},{128,160},{160,128},{192,224},{224,1... | collective-permute-start | bytes 393224 | tf_op jit(solution)/shard_map/ppermute | solution.py:386
  26.8 19.3 %collective-permute-start.14 = (bf16[64,1024]{1,0:T(8,128)(2,1)}, bf16[64,1024]{1,0:T(8,128)(2,1)S(1)}, u32[]{:S(2)}, u32[]{:S(2)}) collective-permute-start(bf16[64,1024]{1,0:T(8,128)(2,1)} %select_select_fusion.own), channel_id=1, source_target_pairs={{0,2},{1,3},{2,0},{3,1},{4,6},{5,7},{6,4},{7,5},{8,10},{9,11},{10,... | collective-permute-start | bytes 393224 | tf_op jit(solution)/shard_map/ppermute | solution.py:45
  29.6 18.7 %copy-start.6 = (bf16[256,1024]{1,0:T(8,128)(2,1)}, bf16[256,1024]{1,0:T(8,128)(2,1)S(1)}, u32[]{:S(2)}) copy-start(bf16[256,1024]{1,0:T(8,128)(2,1)S(1)} %collective-permute-done.3.refs_1_.three_hi) | copy-start | bytes 1572868
  29.6 18.0 %collective-permute-start.13 = (bf16[64,1024]{1,0:T(8,128)(2,1)}, bf16[64,1024]{1,0:T(8,128)(2,1)S(1)}, u32[]{:S(2)}, u32[]{:S(2)}) collective-permute-start(bf16[64,1024]{1,0:T(8,128)(2,1)} %select_select_fusion.own), channel_id=1, source_target_pairs={{0,3},{1,2},{2,1},{3,0},{4,7},{5,6},{6,5},{7,4},{8,11},{9,10},{10,... | collective-permute-start | bytes 393224 | tf_op jit(solution)/shard_map/ppermute | solution.py:45
  31.7 16.6 %copy-start.7 = (bf16[256,1024]{1,0:T(8,128)(2,1)}, bf16[256,1024]{1,0:T(8,128)(2,1)S(1)}, u32[]{:S(2)}) copy-start(bf16[256,1024]{1,0:T(8,128)(2,1)S(1)} %collective-permute-done.1.refs_0_.one_hi) | copy-start | bytes 1572868
  31.7 16.6 %collective-permute-start.12 = (bf16[64,1024]{1,0:T(8,128)(2,1)}, bf16[64,1024]{1,0:T(8,128)(2,1)S(1)}, u32[]{:S(2)}, u32[]{:S(2)}) collective-permute-start(bf16[64,1024]{1,0:T(8,128)(2,1)} %select_select_fusion.own), channel_id=1, source_target_pairs={{0,1},{1,0},{2,3},{3,2},{4,5},{5,4},{6,7},{7,6},{8,9},{9,8},{10,11... | collective-permute-start | bytes 393224 | tf_op jit(solution)/shard_map/ppermute | solution.py:45
  41.3 16.0 %collective-permute-start.7 = (bf16[128,1024]{1,0:T(8,128)(2,1)S(1)}, bf16[128,1024]{1,0:T(8,128)(2,1)S(1)}, u32[]{:S(2)}, u32[]{:S(2)}) collective-permute-start(bf16[128,1024]{1,0:T(8,128)(2,1)S(1)} %slice.35), channel_id=1, source_target_pairs={{0,1},{1,0},{2,3},{3,2},{4,5},{5,4},{6,7},{7,6},{8,9},{9,8},{10,11... | collective-permute-start | bytes 786440 | tf_op jit(solution)/shard_map/ppermute | solution.py:45
  42.6 18.8 %collective-permute-start.6 = (bf16[128,1024]{1,0:T(8,128)(2,1)S(1)}, bf16[128,1024]{1,0:T(8,128)(2,1)S(1)}, u32[]{:S(2)}, u32[]{:S(2)}) collective-permute-start(bf16[128,1024]{1,0:T(8,128)(2,1)S(1)} %slice.34), channel_id=1, source_target_pairs={{0,3},{1,2},{2,1},{3,0},{4,7},{5,6},{6,5},{7,4},{8,11},{9,10},{10,... | collective-permute-start | bytes 786440 | tf_op jit(solution)/shard_map/ppermute | solution.py:45
  46.1 2.2 %copy-start.18 = (bf16[64,1024]{1,0:T(8,128)(2,1)}, bf16[64,1024]{1,0:T(8,128)(2,1)S(1)}, u32[]{:S(2)}) copy-start(bf16[64,1024]{1,0:T(8,128)(2,1)S(1)} %collective-permute-done.14.two) | copy-start | bytes 393220
  46.1 15.2 %collective-permute-start.5 = (bf16[128,1024]{1,0:T(8,128)(2,1)S(1)}, bf16[128,1024]{1,0:T(8,128)(2,1)S(1)}, u32[]{:S(2)}, u32[]{:S(2)}) collective-permute-start(bf16[128,1024]{1,0:T(8,128)(2,1)S(1)} %slice.33), channel_id=1, source_target_pairs={{0,1},{1,0},{2,3},{3,2},{4,5},{5,4},{6,7},{7,6},{8,9},{9,8},{10,11... | collective-permute-start | bytes 786440 | tf_op jit(solution)/shard_map/ppermute | solution.py:45
  47.6 0.7 copy-start.19
  47.6 13.7 %collective-permute-start.4 = (bf16[128,1024]{1,0:T(8,128)(2,1)S(1)}, bf16[128,1024]{1,0:T(8,128)(2,1)S(1)}, u32[]{:S(2)}, u32[]{:S(2)}) collective-permute-start(bf16[128,1024]{1,0:T(8,128)(2,1)S(1)} %slice.32), channel_id=1, source_target_pairs={{0,3},{1,2},{2,1},{3,0},{4,7},{5,6},{6,5},{7,4},{8,11},{9,10},{10,... | collective-permute-start | bytes 786440 | tf_op jit(solution)/shard_map/ppermute | solution.py:45
  48.2 0.7 copy-start.20
  56.3 13.8 %collective-permute-start.18 = (bf16[320,256]{1,0:T(8,128)(2,1)}, bf16[320,256]{1,0:T(8,128)(2,1)S(1)}, u32[]{:S(2)}, u32[]{:S(2)}) collective-permute-start(bf16[320,256]{1,0:T(8,128)(2,1)} %project_image.1.refs_8_.refs_1_), channel_id=1, source_target_pairs={{0,28},{4,0},{8,4},{12,8},{16,12},{20,16},{24,20},{28,24},{1,29},{... | collective-permute-start | bytes 491528 | tf_op jit(solution)/shard_map/ppermute | solution.py:41
  57.3 4.1 %copy-start.12 = (bf16[128,1024]{1,0:T(8,128)(2,1)}, bf16[128,1024]{1,0:T(8,128)(2,1)S(1)}, u32[]{:S(2)}) copy-start(bf16[128,1024]{1,0:T(8,128)(2,1)S(1)} %collective-permute-done.7.refs_3_) | copy-start | bytes 786436
  57.3 12.8 %collective-permute-start.15 = (bf16[320,256]{1,0:T(8,128)(2,1)}, bf16[320,256]{1,0:T(8,128)(2,1)S(1)}, u32[]{:S(2)}, u32[]{:S(2)}) collective-permute-start(bf16[320,256]{1,0:T(8,128)(2,1)} %project_image.1.refs_8_.refs_1_), channel_id=1, source_target_pairs={{0,4},{4,8},{8,12},{12,16},{16,20},{20,24},{24,28},{28,0},{1,5},{5... | collective-permute-start | bytes 491528 | tf_op jit(solution)/shard_map/ppermute | solution.py:41
  61.3 0.7 copy-start.13
  61.3 0.8 copy-start.14
  61.3 0.9 copy-start.15
  71.2 12.0 %collective-permute-start.19 = (bf16[832,256]{1,0:T(8,128)(2,1)S(1)}, bf16[832,256]{1,0:T(8,128)(2,1)S(1)}, u32[]{:S(2)}, u32[]{:S(2)}) collective-permute-start(bf16[832,256]{1,0:T(8,128)(2,1)S(1)} %get-tuple-element.17), channel_id=1, source_target_pairs={{0,28},{4,0},{8,4},{12,8},{16,12},{20,16},{24,20},{28,24},{1,29},{... | collective-permute-start | bytes 1277960 | tf_op jit(solution)/shard_map/ppermute | solution.py:41
  71.3 11.9 %collective-permute-start.16 = (bf16[832,256]{1,0:T(8,128)(2,1)S(1)}, bf16[832,256]{1,0:T(8,128)(2,1)S(1)}, u32[]{:S(2)}, u32[]{:S(2)}) collective-permute-start(bf16[832,256]{1,0:T(8,128)(2,1)S(1)} %get-tuple-element.18), channel_id=1, source_target_pairs={{0,4},{4,8},{8,12},{12,16},{16,20},{20,24},{24,28},{28,0},{1,5},{5... | collective-permute-start | bytes 1277960 | tf_op jit(solution)/shard_map/ppermute | solution.py:41
  83.2 12.9 %copy-start.16 = (bf16[832,256]{1,0:T(8,128)(2,1)}, bf16[832,256]{1,0:T(8,128)(2,1)S(1)}, u32[]{:S(2)}) copy-start(bf16[832,256]{1,0:T(8,128)(2,1)S(1)} %collective-permute-done.19.refs_9_) | copy-start | bytes 1277956
  83.2 13.0 %collective-permute-start.20 = (bf16[832,256]{1,0:T(8,128)(2,1)S(1)}, bf16[832,256]{1,0:T(8,128)(2,1)S(1)}, u32[]{:S(2)}, u32[]{:S(2)}) collective-permute-start(bf16[832,256]{1,0:T(8,128)(2,1)S(1)} %collective-permute-done.19.refs_9_), channel_id=1, source_target_pairs={{0,28},{4,0},{8,4},{12,8},{16,12},{20,16},{24,20},{28,24},{1,29},{... | collective-permute-start | bytes 1277960 | tf_op jit(solution)/shard_map/ppermute | solution.py:41
  83.2 12.9 %copy-start.17 = (bf16[832,256]{1,0:T(8,128)(2,1)}, bf16[832,256]{1,0:T(8,128)(2,1)S(1)}, u32[]{:S(2)}) copy-start(bf16[832,256]{1,0:T(8,128)(2,1)S(1)} %collective-permute-done.16.refs_4_) | copy-start | bytes 1277956
  83.2 13.0 %collective-permute-start.17 = (bf16[832,256]{1,0:T(8,128)(2,1)S(1)}, bf16[832,256]{1,0:T(8,128)(2,1)S(1)}, u32[]{:S(2)}, u32[]{:S(2)}) collective-permute-start(bf16[832,256]{1,0:T(8,128)(2,1)S(1)} %collective-permute-done.16.refs_4_), channel_id=1, source_target_pairs={{0,4},{4,8},{8,12},{12,16},{16,20},{20,24},{24,28},{28,0},{1,5},{5... | collective-permute-start | bytes 1277960 | tf_op jit(solution)/shard_map/ppermute | solution.py:41
  96.1 18.8 %copy-start = (bf16[512,256]{1,0:T(8,128)(2,1)S(1)}, bf16[512,256]{1,0:T(8,128)(2,1)}, u32[]{:S(2)}) copy-start(bf16[512,256]{1,0:T(8,128)(2,1)} %get-tuple-element.10.refs_2_) | copy-start | bytes 786436
  96.2 18.8 %copy-start.1 = (bf16[320,256]{1,0:T(8,128)(2,1)S(1)}, bf16[320,256]{1,0:T(8,128)(2,1)}, u32[]{:S(2)}) copy-start(bf16[320,256]{1,0:T(8,128)(2,1)} %project_image.1.refs_8_.refs_1_) | copy-start | bytes 491524
  96.2 18.8 %copy-start.3 = (s32[3]{0:T(128)S(1)}, s32[3]{0:T(128)}, u32[]{:S(2)}) copy-start(s32[3]{0:T(128)} %pad_add_fusion.ids_ref) | copy-start | bytes 40
  96.2 0.8 copy-start.10
  97.0 0.8 copy-start.11
  99.7 7.5 %collective-permute-start.21 = (bf16[672,256]{1,0:T(8,128)(2,1)}, bf16[672,256]{1,0:T(8,128)(2,1)S(1)}, u32[]{:S(2)}, u32[]{:S(2)}) collective-permute-start(bf16[672,256]{1,0:T(8,128)(2,1)} %get-tuple-element.11), channel_id=1, source_target_pairs={{0,4},{4,8},{8,12},{12,16},{16,20},{20,24},{24,28},{28,0},{1,5},{5... | collective-permute-start | bytes 1032200 | tf_op jit(solution)/shard_map/ppermute | solution.py:41
  99.9 8.8 %collective-permute-start.23 = (bf16[672,256]{1,0:T(8,128)(2,1)}, bf16[672,256]{1,0:T(8,128)(2,1)S(1)}, u32[]{:S(2)}, u32[]{:S(2)}) collective-permute-start(bf16[672,256]{1,0:T(8,128)(2,1)} %get-tuple-element.12), channel_id=1, source_target_pairs={{0,28},{4,0},{8,4},{12,8},{16,12},{20,16},{24,20},{28,24},{1,29},{... | collective-permute-start | bytes 1032200 | tf_op jit(solution)/shard_map/ppermute | solution.py:41
  107.2 5.0 %collective-permute-start.22 = (bf16[256,256]{1,0:T(8,128)(2,1)S(1)}, bf16[256,256]{1,0:T(8,128)(2,1)S(1)}, u32[]{:S(2)}, u32[]{:S(2)}) collective-permute-start(bf16[256,256]{1,0:T(8,128)(2,1)S(1)} %slice.36), channel_id=1, source_target_pairs={{0,4},{4,8},{8,12},{12,16},{16,20},{20,24},{24,28},{28,0},{1,5},{5... | collective-permute-start | bytes 393224 | tf_op jit(solution)/shard_map/ppermute | solution.py:41
  108.7 6.3 %collective-permute-start.24 = (bf16[256,256]{1,0:T(8,128)(2,1)S(1)}, bf16[256,256]{1,0:T(8,128)(2,1)S(1)}, u32[]{:S(2)}, u32[]{:S(2)}) collective-permute-start(bf16[256,256]{1,0:T(8,128)(2,1)S(1)} %slice.37), channel_id=1, source_target_pairs={{0,28},{4,0},{8,4},{12,8},{16,12},{20,16},{24,20},{28,24},{1,29},{... | collective-permute-start | bytes 393224 | tf_op jit(solution)/shard_map/ppermute | solution.py:41

commit v6 on v5

--- a/solution.py
+++ b/solution.py
@@ -47,11 +47,6 @@
 
 def first_hop(x):
     return exchange(x, 1), exchange(x, 3)
-
-
-def second_hop(a, b):
-    half = a.shape[0] // 2
-    return exchange(a[:half], 3), exchange(b[half:], 1)
 
 
 def normalise(mp, gain_ref, pieces, out_ref, rows):
@@ -111,16 +106,16 @@
     )(ids, *arrays, gain, w_kv, w_query, *tables, *after)
 
 
-def text_kernel(ids_ref, own, one_lo, one_hi, three_lo, three_hi, *refs):
-    twos = refs[:4]
-    gain, w_kv, cos, sin = refs[4:8]
+def text_kernel(ids_ref, own, one_a, one_b, three_a, three_b, two_a, two_b, two_c, *refs):
+    gain, w_kv, cos, sin = refs[:4]
     normed_ref, out_ref = refs[-2:]
     rows = own.shape[0]
-    for n in range(4):
-        @pl.when(pl.program_id(0) == n)
+    for n, others in enumerate(
+        ((one_a, three_a, two_a), (one_b, three_b, two_b), (one_b, three_b, two_c))
+    ):
+        @pl.when(jnp.minimum(pl.program_id(0), 2) == n)
         def _():
-            one, three = ((one_lo, three_lo), (one_hi, three_hi))[n // 2]
-            pieces = [own[...], one[...], three[...], twos[n][...]]
+            pieces = [own[...]] + [other[...] for other in others]
             normalise(ids_ref[0], gain, pieces, normed_ref, slice(0, rows))
 
     write_key_value(normed_ref[...], w_kv, cos[...], sin[...], out_ref, slice(0, rows))
@@ -130,9 +125,12 @@
     rows = arrays[0].shape[0]
     steps = 4
     tile = rows // steps
+
+    def block(skipped):
+        return pl.BlockSpec((tile, D // 4), lambda r: (jnp.maximum(r - skipped, 0), 0))
+
     whole = pl.BlockSpec(memory_space=VMEM)
-    low = pl.BlockSpec((tile, D // 4), lambda r: (jnp.minimum(r, 1), 0))
-    high = pl.BlockSpec((tile, D // 4), lambda r: (jnp.maximum(r - 2, 0), 0))
+    only = pl.BlockSpec((tile, D // 4), lambda r: (0, 0))
     table = pl.BlockSpec((tile, HD // 2), lambda r: (r, 0))
     return pl.pallas_call(
         text_kernel,
@@ -142,8 +140,8 @@
         ],
         grid=(steps,),
         in_specs=[pl.BlockSpec(memory_space=SMEM)]
-        + [pl.BlockSpec((tile, D // 4), lambda r: (r, 0)), low, high, low, high]
-        + [whole] * 6
+        + [block(0), only, block(1), only, block(1), only, only, block(2)]
+        + [whole] * 2
         + [table] * 2
         + [pl.BlockSpec(memory_space=pl.ANY)] * len(after),
         out_specs=[
@@ -156,23 +154,6 @@
     )(ids, *arrays, gain, w_kv, *tables, *after)
 
 
-def cut_kernel(starts, a_ref, b_ref, _, a_out, b_out):
-    for start, ref, out in zip(starts, (a_ref, b_ref), (a_out, b_out)):
-        out[...] = ref[start : start + out.shape[0], :]
-
-
-def cut_payloads(a, b, starts, rows, after):
-    whole = pl.BlockSpec(memory_space=VMEM)
-    return pl.pallas_call(
-        functools.partial(cut_kernel, starts),
-        out_shape=[jax.ShapeDtypeStruct((rows, a.shape[1]), a.dtype)] * 2,
-        in_specs=[whole] * 2 + [pl.BlockSpec(memory_space=pl.ANY)],
-        out_specs=[whole] * 2,
-        cost_estimate=pl.CostEstimate(flops=0, bytes_accessed=0, transcendentals=0),
-        name="cut_payloads",
-    )(a, b, after)
-
-
 def query_kernel(x_ref, w_ref, cos, sin, q_ref):
     product = jnp.dot(x_ref[...], w_ref[...], preferred_element_type=F32)
     for h in range(w_ref.shape[1] // HD):
@@ -180,17 +161,19 @@
         q_ref[:, span] = rotate(product[:, span], cos[...], sin[...]).astype(BF16)
 
 
-def query(normed, w_query, tables):
-    rows, columns, tile = normed.shape[0], w_query.shape[1], 2 * HD
+def query(normed, w_query, tables, part, parts):
+    rows, tile = normed.shape[0], 2 * HD
+    columns = w_query.shape[1] // parts
+    first = part * (columns // tile)
     whole = pl.BlockSpec(memory_space=VMEM)
     return pl.pallas_call(
         query_kernel,
         out_shape=jax.ShapeDtypeStruct((rows, columns), BF16),
         grid=(columns // tile,),
-        in_specs=[whole, pl.BlockSpec((D, tile), lambda n: (0, n))] + [whole] * 2,
+        in_specs=[whole, pl.BlockSpec((D, tile), lambda n: (0, first + n))] + [whole] * 2,
         out_specs=pl.BlockSpec((rows, tile), lambda n: (0, n)),
         compiler_params=pltpu.CompilerParams(vmem_limit_bytes=58 * 2**20),
-        cost_estimate=pl.CostEstimate(flops=8 * 10**9, bytes_accessed=10 * 2**20, transcendentals=0),
+        cost_estimate=pl.CostEstimate(flops=3 * 10**9, bytes_accessed=2**20, transcendentals=0),
         name="query",
     )(normed, w_query, *tables)
 
@@ -203,14 +186,15 @@
 
 
 def attention_kernel(tok, heads, ids_ref, counts_ref, starts_ref, *refs):
-    q_ref, own_e, own_l, f1, f2, f3, f4, f5, b1, b2, b3, b4, b5, out_ref = refs[:14]
-    q_buf, kv_buf, img_buf, s_buf, max_buf, sum_buf, acc_buf, sems = refs[14:]
+    q_one, q_two, own_e, own_l, f1, f2, f3, f4, f5, b1, b2, b3, b4, b5, out_ref = refs[:15]
+    q_buf, kv_buf, img_buf, s_buf, max_buf, sum_buf, acc_buf, sems = refs[15:]
     ctx, sample = ids_ref[1], ids_ref[2]
     factor = math.log2(math.e) / math.sqrt(HD)
 
     rows_e, rows_l = own_e.shape[0], own_l.shape[0]
     cut, part = rows_e // 2, rows_l // 2
-    moves = [(q_ref, q_buf)]
+    middle = heads * HD // 2
+    moves = [(q_one, q_buf.at[:, :middle]), (q_two, q_buf.at[:, middle:])]
     for d, array, base, first, count in (
         (0, own_e, 0, 0, rows_e),
         (1, f1, 0, 0, rows_e),
@@ -377,43 +361,46 @@
 
     my_slot, my_across, my_distance = source(sample)
     _, _, its_distance = source(sample ^ 1)
-    half = tok // 2
-    low, high = text_rows[:half], text_rows[half:]
-    one_lo, three_lo = first_hop(low)
-    routed = [visual_rows] + [shift(visual_rows, "dp", 2 * d, False) for d in (1, 2, 3)]
-    one_hi, three_hi = first_hop(high)
+    quarter = tok // 4
+    one_a, three_a = first_hop(text_rows[:quarter])
+    one_b, three_b = first_hop(text_rows[quarter:])
+    values = jnp.stack([one_a[0, 0], three_a[0, 0]]).astype(jnp.int32)
+    zero = jnp.minimum(jnp.sum(jnp.abs(values)), 0)
+    leaving = jnp.where(zero == 0, visual_rows, 0)
+    routed = [visual_rows] + [shift(leaving, "dp", 2 * d, False) for d in (1, 2, 3)]
     for_other = choose(its_distance, routed)
     from_other = lax.ppermute(for_other, "dp", [(i, i ^ 1) for i in range(SHARDS)])
     image = choose(jnp.where(my_across == 1, 4, my_distance), routed + [from_other])
-    twos_lo = second_hop(one_lo, three_lo)
     image_parts = [image] + [exchange(image, mask) for mask in (1, 3, 2)]
-    twos_hi = second_hop(one_hi, three_hi)
+    two_a = exchange(one_a, 3)
+    two_b = exchange(one_b[:quarter], 3)
+    two_c = exchange(three_b[quarter:], 1)
 
     mine = (every[:, None] == sample) & (every[None, :] == my_slot)
     my_start = jnp.sum(jnp.where(mine, image_starts, 0))
     text_tables = rotary_tables(ctx * tok + jnp.arange(tok, dtype=jnp.int32))
     image_tables = rotary_tables(my_start + jnp.arange(IMG_TOK, dtype=jnp.int32))
     own_e = project_image(
-        ids, image_parts, gain, w_kv, w_query, image_tables, (one_hi, three_hi)
+        ids, image_parts, gain, w_kv, w_query, image_tables,
+        (one_a, three_a, *text_tables),
     )
     normed, own_l = project_text(
-        ids, [text_rows, one_lo, one_hi, three_lo, three_hi, *twos_lo, *twos_hi],
+        ids, [text_rows, one_a, one_b, three_a, three_b, two_a, two_b, two_c],
         gain, w_kv, text_tables, (own_e,)
     )
-    q_all = query(normed, w_query, text_tables)
+    queries = [query(normed, w_query, text_tables, n, 2) for n in range(2)]
 
     cut, part = own_e.shape[0] // 2, tok // 2
     f1, b1 = shift(own_e, "ctx", 1, True), shift(own_e, "ctx", -1, True)
     f2 = shift(jnp.concatenate([f1, own_l], axis=0), "ctx", 1, True)
     b2 = shift(jnp.concatenate([own_l, b1], axis=0), "ctx", -1, True)
     f3, b3 = shift(f2, "ctx", 1, True), shift(b2, "ctx", -1, True)
-    onward = cut_payloads(f3, b3, (cut, 0), tok + cut, q_all)
-    f4, b4 = shift(onward[0], "ctx", 1, True), shift(onward[1], "ctx", -1, True)
+    f4, b4 = shift(f3[cut:], "ctx", 1, True), shift(b3[: tok + cut], "ctx", -1, True)
     f5 = shift(f4[cut : cut + part], "ctx", 1, True)
     b5 = shift(b4[part:tok], "ctx", -1, True)
     return attention(
         tok, heads, (ids, image_counts, image_starts),
-        [q_all, own_e, own_l, f1, f2, f3, f4, f5, b1, b2, b3, b4, b5],
+        [*queries, own_e, own_l, f1, f2, f3, f4, f5, b1, b2, b3, b4, b5],
     )
 
 

time: 150 us -> 143 us (0.953)
  waiting for transfers between devices: 28.7 us -> 20.2 us
    ppermute x11 -> x10, waiting for transfers between devices: 8.83 us -> 1.57 us  [exchange(): return lax.ppermute(x, 'mp', [(i, i ^ mask) for i in range(4)])]
    pallas_call x1 -> x2, Pallas kernels: 9.42 us -> 12.6 us  [query(): pl.pallas_call(query_kernel, out_shape=jax.ShapeDtypeStruct((rows, column...]
    ppermute x11 -> x10, starting transfers between devices: 14.8 us -> 12.6 us  [exchange(): return lax.ppermute(x, 'mp', [(i, i ^ mask) for i in range(4)])]
    pallas_call x1 -> x0, Pallas kernels: 2 us -> none  [cut_payloads(): pl.pallas_call(functools.partial(cut_kernel, starts), out_shape=[jax.Shap...]
    reduce_sum x0 -> x1, other arithmetic: none -> 1.95 us  [on_device(): zero = jnp.minimum(jnp.sum(jnp.abs(values)), 0)]
    slice x5 -> x8, local copies, waits for them, and re-layouts: 4.2 us -> 5.9 us  [the longest x1 2.06 us: on_device(): one_b, three_b = first_hop(text_rows[quarter:])]
    unnamed x43 -> x45, local copies, waits for them, and re-layouts: 4.55 us -> 3.82 us
  transfers between devices with their start and end apart: 25 -> 24, of which waited for: 6 -> 5; matrix products, arithmetic and copies ran while one was open for 9% -> 10% of each run, Pallas kernels for 17% -> 19%
where the time goes in v6:
time: 143 us
  Pallas kernels  60.7 us (42%)
  starting transfers between devices  38.8 us (27%)
  waiting for transfers between devices  20.2 us (14%)
  local copies, waits for them, and re-layouts  9.98 us (7%)
  other arithmetic  9.12 us (6%)
  between operations  3.71 us (3%)
    pallas_call x1, Pallas kernels, attention(): pl.pallas_call(functools.partial(attention_kernel, tok, heads), out_shape...  33 us
    ppermute x13, starting transfers between devices, shift(): return lax.ppermute(x, axis, pairs)  26.1 us
    ppermute x13, waiting for transfers between devices, shift(): return lax.ppermute(x, axis, pairs)  18.6 us
    ppermute x10, starting transfers between devices, exchange(): return lax.ppermute(x, 'mp', [(i, i ^ mask) for i in range(4)])  12.6 us
    pallas_call x2, Pallas kernels, query(): pl.pallas_call(query_kernel, out_shape=jax.ShapeDtypeStruct((rows, column...  12.6 us
    pallas_call x1, Pallas kernels, project_text(): pl.pallas_call(text_kernel, out_shape=[jax.ShapeDtypeStruct((rows, D), BF...  7.73 us
    pallas_call x1, Pallas kernels, project_image(): pl.pallas_call(image_kernel, out_shape=jax.ShapeDtypeStruct(((1 + steps)...  7.38 us
    unnamed x45, local copies, waits for them, and re-layouts  3.82 us
  transfers between devices with their start and end apart: 24, of which 5 were waited for; matrix products, arithmetic and copies ran while one was open for 10% of the time, Pallas kernels for 19%

profile of v6, /device:TPU:224, one launch (start us, length us, event | category | flops | bytes accessed | tf_op | source)
XLA Modules:
  0.0 142.5 jit_solution(12242343532465947070)
XLA Ops:
  0.0 1.7 %slice.30 = bf16[128,1024]{1,0:T(8,128)(2,1)} slice(bf16[512,1024]{1,0:T(8,128)(2,1)} %own.1), slice={[0:128], [0:1024]} | slice | bytes 524288 | tf_op jit(solution)/shard_map/slice | solution.py:365
  1.7 2.8 %collective-permute-start.2 = (bf16[128,1024]{1,0:T(8,128)(2,1)}, bf16[128,1024]{1,0:T(8,128)(2,1)S(1)}, u32[]{:S(2)}, u32[]{:S(2)}) collective-permute-start(bf16[128,1024]{1,0:T(8,128)(2,1)} %slice.30), channel_id=1, source_target_pairs={{0,3},{1,2},{2,1},{3,0},{4,7},{5,6},{6,5},{7,4},{8,11},{9,10},{10,... | collective-permute-start | bytes 786440 | tf_op jit(solution)/shard_map/ppermute | solution.py:45
  4.4 0.2 collective-permute-start
  4.6 2.1 %slice.31 = bf16[384,1024]{1,0:T(8,128)(2,1)} slice(bf16[512,1024]{1,0:T(8,128)(2,1)} %own.1), slice={[128:512], [0:1024]} | slice | bytes 1572864 | tf_op jit(solution)/shard_map/slice | solution.py:366
  6.7 1.1 collective-permute-start.3
  7.8 0.7 collective-permute-start.1
  8.5 1.5 %constant_dynamic-update-slice_fusion.1 = bf16[4096,256]{1,0:T(8,128)(2,1)S(1)} fusion(bf16[4096,128]{1,0:T(8,128)(2,1)} %param.14), kind=kLoop, calls=%fused_computation.10 | loop fusion | bytes 2097152
  10.0 0.0 copy-done.8
  10.1 0.2 constant_dynamic-update-slice_fusion.w_kv.refs_1_
  10.3 1.8 %multiply_sine_fusion = (f32[512,64]{1,0:T(8,128)}, f32[512,64]{1,0:T(8,128)}) fusion(f32[64]{0:T(128)S(1)} %multiply_exponential_fusion, f32[512]{0:T(512)S(1)} %add_convert_fusion), kind=kLoop, calls=%fused_computation.2 | loop fusion | flops 32768 | bytes 264448 | tf_op jit(solution)/shard_map/sin | solution.py:30
  12.2 0.6 slice.43
  12.7 1.1 collective-permute-done.refs_0_.one_a
  13.9 0.5 slice.42
  14.4 1.9 %fusion.3 = s32[]{:T(128)} fusion(bf16[1]{0:T(256)(128)(2,1)} %bitcast.5, bf16[1]{0:T(256)(128)(2,1)} %bitcast.4), kind=kLoop, calls=%fused_computation.20 | loop fusion | flops 11 | bytes 8 | tf_op jit(solution)/shard_map/reduce_sum | solution.py:368
  16.9 0.7 broadcast_select_fusion
  17.6 3.5 %collective-permute-start.9 = (bf16[64,1024]{1,0:T(8,128)(2,1)}, bf16[64,1024]{1,0:T(8,128)(2,1)S(1)}, u32[]{:S(2)}, u32[]{:S(2)}) collective-permute-start(bf16[64,1024]{1,0:T(8,128)(2,1)} %broadcast_select_fusion), channel_id=1, source_target_pairs={{0,64},{32,96},{64,128},{96,160},{128,192},{160,224},{1,65},{33,97... | collective-permute-start | bytes 393224 | tf_op jit(solution)/shard_map/ppermute | solution.py:41
  21.1 4.8 %collective-permute-start.8 = (bf16[64,1024]{1,0:T(8,128)(2,1)}, bf16[64,1024]{1,0:T(8,128)(2,1)S(1)}, u32[]{:S(2)}, u32[]{:S(2)}) collective-permute-start(bf16[64,1024]{1,0:T(8,128)(2,1)} %broadcast_select_fusion), channel_id=1, source_target_pairs={{0,128},{32,160},{64,192},{96,224},{1,129},{33,161},{65,193},{97,2... | collective-permute-start | bytes 393224 | tf_op jit(solution)/shard_map/ppermute | solution.py:41
  25.9 1.3 collective-permute-start.7
  27.2 0.7 fusion
  29.8 0.0 collective-permute-done.9
  29.8 0.0 collective-permute-done.8
  29.8 0.2 collective-permute-done.7
  30.1 0.1 collective-permute-start.10
  30.2 0.7 select_reduce_fusion
  31.5 0.6 add_convert_fusion.1
  32.2 0.0 collective-permute-done.10
  32.2 0.1 select_select_fusion.own
  32.2 1.9 %collective-permute-start.13 = (bf16[64,1024]{1,0:T(8,128)(2,1)S(1)}, bf16[64,1024]{1,0:T(8,128)(2,1)S(1)}, u32[]{:S(2)}, u32[]{:S(2)}) collective-permute-start(bf16[64,1024]{1,0:T(8,128)(2,1)S(1)} %select_select_fusion.own), channel_id=1, source_target_pairs={{0,2},{1,3},{2,0},{3,1},{4,6},{5,7},{6,4},{7,5},{8,10},{9,11},{10,... | collective-permute-start | bytes 393224 | tf_op jit(solution)/shard_map/ppermute | solution.py:45
  34.1 1.1 collective-permute-start.12
  35.3 0.6 collective-permute-start.11
  35.8 0.8 multiply_sine_fusion.1
  36.6 0.6 pad_add_fusion.ids_ref
  37.3 0.0 collective-permute-done.3.three_b
  37.3 1.8 %collective-permute-start.4 = (bf16[128,1024]{1,0:T(8,128)(2,1)}, bf16[128,1024]{1,0:T(8,128)(2,1)S(1)}, u32[]{:S(2)}, u32[]{:S(2)}) collective-permute-start(bf16[128,1024]{1,0:T(8,128)(2,1)} %copy-done.13), channel_id=1, source_target_pairs={{0,3},{1,2},{2,1},{3,0},{4,7},{5,6},{6,5},{7,4},{8,11},{9,10},{10,... | collective-permute-start | bytes 786440 | tf_op jit(solution)/shard_map/ppermute | solution.py:45
  39.1 0.0 collective-permute-done.1.one_b
  39.1 1.3 collective-permute-start.6
  40.4 1.0 slice.40
  41.3 0.0 collective-permute-done.13.two
  41.3 1.2 collective-permute-start.5
  42.6 0.4 collective-permute-done.12.three
  43.0 0.6 copy-done.20
  43.7 0.0 copy-done.21
  43.7 7.4 %project_image.1.refs_4_.refs_2_ = bf16[320,256]{1,0:T(8,128)(2,1)} custom-call(s32[3]{0:T(128)} %pad_add_fusion.ids_ref, bf16[64,1024]{1,0:T(8,128)(2,1)} %copy-done.16, bf16[64,1024]{1,0:T(8,128)(2,1)} %copy-done.21, bf16[64,1024]{1,0:T(8,128)(2,1)} %copy-done.20, bf16[64,1024]{1,0:T(8,128)(2,1)} %copy-done.19, f32[1,4096]{1,0:T(1,128)} %bitcast.6, ...), custom_call_target="tpu_custom_call" | custom-call | flops 8000000000 | bytes 10485760 | tf_op jit(solution)/shard_map/project_image/pallas_call | solution.py:92
  51.1 1.0 collective-permute-start.19
  52.1 2.2 %collective-permute-start.14 = (bf16[320,256]{1,0:T(8,128)(2,1)}, bf16[320,256]{1,0:T(8,128)(2,1)S(1)}, u32[]{:S(2)}, u32[]{:S(2)}) collective-permute-start(bf16[320,256]{1,0:T(8,128)(2,1)} %project_image.1.refs_4_.refs_2_), channel_id=1, source_target_pairs={{0,4},{4,8},{8,12},{12,16},{16,20},{20,24},{24,28},{28,0},{1,5},{5... | collective-permute-start | bytes 491528 | tf_op jit(solution)/shard_map/ppermute | solution.py:41
  54.3 0.0 collective-permute-done.4.two_a
  54.3 0.0 collective-permute-done.6.two_c
  54.4 0.7 copy-done.14
  55.0 0.1 copy-done.15
  55.1 0.8 copy-done.9
  55.9 7.7 %project_text.1 = (bf16[512,4096]{1,0:T(8,128)(2,1)}, bf16[512,256]{1,0:T(8,128)(2,1)}) custom-call(s32[3]{0:T(128)} %pad_add_fusion.ids_ref, bf16[512,1024]{1,0:T(8,128)(2,1)} %own.1, bf16[128,1024]{1,0:T(8,128)(2,1)} %copy-done.13, bf16[384,1024]{1,0:T(8,128)(2,1)} %collective-permute-done.1.one_b, bf16[128,1024]{1,0:T(8,128)(2,1)} %copy-done.12, ...), custom_call_target="tpu_custom_call" | custom-call | tf_op jit(solution)/shard_map/project_text/pallas_call | solution.py:135
  63.7 1.1 pad_maximum_fusion.1
  64.8 0.9 collective-permute-start.20
  65.7 2.4 %collective-permute-start.15 = (bf16[832,256]{1,0:T(8,128)(2,1)S(1)}, bf16[832,256]{1,0:T(8,128)(2,1)S(1)}, u32[]{:S(2)}, u32[]{:S(2)}) collective-permute-start(bf16[832,256]{1,0:T(8,128)(2,1)S(1)} %get-tuple-element.12), channel_id=1, source_target_pairs={{0,4},{4,8},{8,12},{12,16},{16,20},{20,24},{24,28},{28,0},{1,5},{5... | collective-permute-start | bytes 1277960 | tf_op jit(solution)/shard_map/ppermute | solution.py:41
  68.1 9.6 %collective-permute-done.20.refs_10_ = bf16[832,256]{1,0:T(8,128)(2,1)S(1)} collective-permute-done((bf16[832,256]{1,0:T(8,128)(2,1)S(1)}, bf16[832,256]{1,0:T(8,128)(2,1)S(1)}, u32[]{:S(2)}, u32[]{:S(2)}) %collective-permute-start.20) | collective-permute-done | bytes 426016 | tf_op jit(solution)/shard_map/ppermute | solution.py:41
  77.8 3.2 %collective-permute-start.16 = (bf16[832,256]{1,0:T(8,128)(2,1)S(1)}, bf16[832,256]{1,0:T(8,128)(2,1)S(1)}, u32[]{:S(2)}, u32[]{:S(2)}) collective-permute-start(bf16[832,256]{1,0:T(8,128)(2,1)S(1)} %collective-permute-done.15.refs_5_), channel_id=1, source_target_pairs={{0,4},{4,8},{8,12},{12,16},{16,20},{20,24},{24,28},{28,0},{1,5},{5... | collective-permute-start | bytes 1277960 | tf_op jit(solution)/shard_map/ppermute | solution.py:41
  81.0 8.8 %collective-permute-done.21.refs_11_ = bf16[832,256]{1,0:T(8,128)(2,1)S(1)} collective-permute-done((bf16[832,256]{1,0:T(8,128)(2,1)S(1)}, bf16[832,256]{1,0:T(8,128)(2,1)S(1)}, u32[]{:S(2)}, u32[]{:S(2)}) %collective-permute-start.21) | collective-permute-done | bytes 426016 | tf_op jit(solution)/shard_map/ppermute | solution.py:41
  89.8 0.1 collective-permute-start.22
  89.9 3.3 %collective-permute-start.17 = (bf16[672,256]{1,0:T(8,128)(2,1)S(1)}, bf16[672,256]{1,0:T(8,128)(2,1)S(1)}, u32[]{:S(2)}, u32[]{:S(2)}) collective-permute-start(bf16[672,256]{1,0:T(8,128)(2,1)S(1)} %slice.44), channel_id=1, source_target_pairs={{0,4},{4,8},{8,12},{12,16},{16,20},{20,24},{24,28},{28,0},{1,5},{5... | collective-permute-start | bytes 1032200 | tf_op jit(solution)/shard_map/ppermute | solution.py:41
  93.2 6.3 %query.3.refs_1_ = bf16[512,512]{1,0:T(8,128)(2,1)} custom-call(bf16[512,4096]{1,0:T(8,128)(2,1)} %get-tuple-element.7.x_ref, bf16[4096,1024]{1,0:T(8,128)(2,1)} %w_ref.3, f32[512,64]{1,0:T(8,128)} %get-tuple-element.14.refs_2_.cos, f32[512,64]{1,0:T(8,128)} %get-tuple-element.13.refs_3_.sin), custom_call_target="tpu_custom_call" | custom-call | flops 3000000000 | bytes 1048576 | tf_op jit(solution)/shard_map/query/pallas_call | solution.py:169
  99.6 0.1 collective-permute-start.23
  99.7 3.3 %collective-permute-start.18 = (bf16[256,256]{1,0:T(8,128)(2,1)S(1)}, bf16[256,256]{1,0:T(8,128)(2,1)S(1)}, u32[]{:S(2)}, u32[]{:S(2)}) collective-permute-start(bf16[256,256]{1,0:T(8,128)(2,1)S(1)} %slice.45), channel_id=1, source_target_pairs={{0,4},{4,8},{8,12},{12,16},{16,20},{20,24},{24,28},{28,0},{1,5},{5... | collective-permute-start | bytes 393224 | tf_op jit(solution)/shard_map/ppermute | solution.py:41
  103.0 6.3 %query.2.refs_0_ = bf16[512,512]{1,0:T(8,128)(2,1)} custom-call(bf16[512,4096]{1,0:T(8,128)(2,1)} %get-tuple-element.7.x_ref, bf16[4096,1024]{1,0:T(8,128)(2,1)} %w_ref.3, f32[512,64]{1,0:T(8,128)} %get-tuple-element.14.refs_2_.cos, f32[512,64]{1,0:T(8,128)} %get-tuple-element.13.refs_3_.sin), custom_call_target="tpu_custom_call" | custom-call | flops 3000000000 | bytes 1048576 | tf_op jit(solution)/shard_map/query/pallas_call | solution.py:169
  109.4 33.0 %attention.1 = bf16[512,1024]{1,0:T(8,128)(2,1)} custom-call(s32[3]{0:T(128)S(1)} %copy-done.3, s32[8]{0:T(128)S(1)} %copy-done.4, s32[8,8]{1,0:T(8,128)S(1)} %copy-done.2, bf16[512,512]{1,0:T(8,128)(2,1)} %query.2.refs_0_, bf16[512,512]{1,0:T(8,128)(2,1)} %query.3.refs_1_, bf16[320,256]{1,0:T(8,128)(2,1)S(1)} %copy-done.1, bf16[512,256]{1,0:T(8,128)(2,1)S(1)} %copy-done, ...), custom_call_target="tpu_custom_call" | custom-call | flops 8589934592 | bytes 8388608 | tf_op jit(solution)/shard_map/attention/pallas_call | solution.py:310
  (59 shorter events, 0.3 us)
Async XLA Ops:
  1.7 10.5 %collective-permute-start.2 = (bf16[128,1024]{1,0:T(8,128)(2,1)}, bf16[128,1024]{1,0:T(8,128)(2,1)S(1)}, u32[]{:S(2)}, u32[]{:S(2)}) collective-permute-start(bf16[128,1024]{1,0:T(8,128)(2,1)} %slice.30), channel_id=1, source_target_pairs={{0,3},{1,2},{2,1},{3,0},{4,7},{5,6},{6,5},{7,4},{8,11},{9,10},{10,... | collective-permute-start | bytes 786440 | tf_op jit(solution)/shard_map/ppermute | solution.py:45
  4.4 9.4 %collective-permute-start = (bf16[128,1024]{1,0:T(8,128)(2,1)}, bf16[128,1024]{1,0:T(8,128)(2,1)S(1)}, u32[]{:S(2)}, u32[]{:S(2)}) collective-permute-start(bf16[128,1024]{1,0:T(8,128)(2,1)} %slice.30), channel_id=1, source_target_pairs={{0,1},{1,0},{2,3},{3,2},{4,5},{5,4},{6,7},{7,6},{8,9},{9,8},{10,11... | collective-permute-start | bytes 786440 | tf_op jit(solution)/shard_map/ppermute | solution.py:45
  6.7 30.6 %collective-permute-start.3 = (bf16[384,1024]{1,0:T(8,128)(2,1)}, bf16[384,1024]{1,0:T(8,128)(2,1)S(1)}, u32[]{:S(2)}, u32[]{:S(2)}) collective-permute-start(bf16[384,1024]{1,0:T(8,128)(2,1)} %slice.31), channel_id=1, source_target_pairs={{0,3},{1,2},{2,1},{3,0},{4,7},{5,6},{6,5},{7,4},{8,11},{9,10},{10,... | collective-permute-start | bytes 2359304 | tf_op jit(solution)/shard_map/ppermute | solution.py:45
  7.8 31.2 %collective-permute-start.1 = (bf16[384,1024]{1,0:T(8,128)(2,1)}, bf16[384,1024]{1,0:T(8,128)(2,1)}, u32[]{:S(2)}, u32[]{:S(2)}) collective-permute-start(bf16[384,1024]{1,0:T(8,128)(2,1)} %slice.31), channel_id=1, source_target_pairs={{0,1},{1,0},{2,3},{3,2},{4,5},{5,4},{6,7},{7,6},{8,9},{9,8},{10,11... | collective-permute-start | bytes 2359304 | tf_op jit(solution)/shard_map/ppermute | solution.py:45
  8.5 1.5 %copy-start.8 = (bf16[4096,128]{1,0:T(8,128)(2,1)S(1)}, bf16[4096,128]{1,0:T(8,128)(2,1)}, u32[]{:S(2)}) copy-start(bf16[4096,128]{1,0:T(8,128)(2,1)} %param.15) | copy-start | bytes 3145732
  8.5 8.4 %copy-start.7 = (bf16[64,1024]{1,0:T(8,128)(2,1)S(1)}, bf16[64,1024]{1,0:T(8,128)(2,1)}, u32[]{:S(2)}) copy-start(bf16[64,1024]{1,0:T(8,128)(2,1)} %param.9) | copy-start | bytes 393220
  8.5 18.7 %copy-start.4 = (s32[8]{0:T(128)S(1)}, s32[8]{0:T(128)}, u32[]{:S(2)}) copy-start(s32[8]{0:T(128)} %counts_ref.1) | copy-start | bytes 100
  10.1 20.1 %copy-start.2 = (s32[8,8]{1,0:T(8,128)S(1)}, s32[8,8]{1,0:T(8,128)}, u32[]{:S(2)}) copy-start(s32[8,8]{1,0:T(8,128)} %starts_ref.1) | copy-start | bytes 772
  10.3 32.7 %copy-start.5 = (bf16[4096,256]{1,0:T(8,128)(2,1)}, bf16[4096,256]{1,0:T(8,128)(2,1)S(1)}, u32[]{:S(2)}) copy-start(bf16[4096,256]{1,0:T(8,128)(2,1)S(1)} %constant_dynamic-update-slice_fusion.w_kv.refs_1_) | copy-start | bytes 6291460
  12.2 4.8 %copy-start.12 = (bf16[128,1024]{1,0:T(8,128)(2,1)}, bf16[128,1024]{1,0:T(8,128)(2,1)S(1)}, u32[]{:S(2)}) copy-start(bf16[128,1024]{1,0:T(8,128)(2,1)S(1)} %collective-permute-done.2.refs_1_.three_a) | copy-start | bytes 786436
  13.9 7.2 %copy-start.13 = (bf16[128,1024]{1,0:T(8,128)(2,1)}, bf16[128,1024]{1,0:T(8,128)(2,1)S(1)}, u32[]{:S(2)}) copy-start(bf16[128,1024]{1,0:T(8,128)(2,1)S(1)} %collective-permute-done.refs_0_.one_a) | copy-start | bytes 786436
  17.6 12.2 %collective-permute-start.9 = (bf16[64,1024]{1,0:T(8,128)(2,1)}, bf16[64,1024]{1,0:T(8,128)(2,1)S(1)}, u32[]{:S(2)}, u32[]{:S(2)}) collective-permute-start(bf16[64,1024]{1,0:T(8,128)(2,1)} %broadcast_select_fusion), channel_id=1, source_target_pairs={{0,64},{32,96},{64,128},{96,160},{128,192},{160,224},{1,65},{33,97... | collective-permute-start | bytes 393224 | tf_op jit(solution)/shard_map/ppermute | solution.py:41
  21.1 8.7 %collective-permute-start.8 = (bf16[64,1024]{1,0:T(8,128)(2,1)}, bf16[64,1024]{1,0:T(8,128)(2,1)S(1)}, u32[]{:S(2)}, u32[]{:S(2)}) collective-permute-start(bf16[64,1024]{1,0:T(8,128)(2,1)} %broadcast_select_fusion), channel_id=1, source_target_pairs={{0,128},{32,160},{64,192},{96,224},{1,129},{33,161},{65,193},{97,2... | collective-permute-start | bytes 393224 | tf_op jit(solution)/shard_map/ppermute | solution.py:41
  25.9 4.1 %collective-permute-start.7 = (bf16[64,1024]{1,0:T(8,128)(2,1)}, bf16[64,1024]{1,0:T(8,128)(2,1)S(1)}, u32[]{:S(2)}, u32[]{:S(2)}) collective-permute-start(bf16[64,1024]{1,0:T(8,128)(2,1)} %broadcast_select_fusion), channel_id=1, source_target_pairs={{0,192},{32,224},{1,193},{33,225},{2,194},{34,226},{3,195},{35,227... | collective-permute-start | bytes 393224 | tf_op jit(solution)/shard_map/ppermute | solution.py:41
  30.1 2.1 %collective-permute-start.10 = (bf16[64,1024]{1,0:T(8,128)(2,1)S(1)}, bf16[64,1024]{1,0:T(8,128)(2,1)}, u32[]{:S(2)}, u32[]{:S(2)}) collective-permute-start(bf16[64,1024]{1,0:T(8,128)(2,1)S(1)} %select_select_fusion.1), channel_id=1, source_target_pairs={{0,32},{32,0},{64,96},{96,64},{128,160},{160,128},{192,224},{224,1... | collective-permute-start | bytes 393224 | tf_op jit(solution)/shard_map/ppermute | solution.py:372
  32.2 10.8 %copy-start.16 = (bf16[64,1024]{1,0:T(8,128)(2,1)}, bf16[64,1024]{1,0:T(8,128)(2,1)S(1)}, u32[]{:S(2)}) copy-start(bf16[64,1024]{1,0:T(8,128)(2,1)S(1)} %select_select_fusion.own) | copy-start | bytes 393220
  32.2 9.1 %collective-permute-start.13 = (bf16[64,1024]{1,0:T(8,128)(2,1)S(1)}, bf16[64,1024]{1,0:T(8,128)(2,1)S(1)}, u32[]{:S(2)}, u32[]{:S(2)}) collective-permute-start(bf16[64,1024]{1,0:T(8,128)(2,1)S(1)} %select_select_fusion.own), channel_id=1, source_target_pairs={{0,2},{1,3},{2,0},{3,1},{4,6},{5,7},{6,4},{7,5},{8,10},{9,11},{10,... | collective-permute-start | bytes 393224 | tf_op jit(solution)/shard_map/ppermute | solution.py:45
  34.1 8.9 %collective-permute-start.12 = (bf16[64,1024]{1,0:T(8,128)(2,1)S(1)}, bf16[64,1024]{1,0:T(8,128)(2,1)S(1)}, u32[]{:S(2)}, u32[]{:S(2)}) collective-permute-start(bf16[64,1024]{1,0:T(8,128)(2,1)S(1)} %select_select_fusion.own), channel_id=1, source_target_pairs={{0,3},{1,2},{2,1},{3,0},{4,7},{5,6},{6,5},{7,4},{8,11},{9,10},{10,... | collective-permute-start | bytes 393224 | tf_op jit(solution)/shard_map/ppermute | solution.py:45
  35.3 7.8 %collective-permute-start.11 = (bf16[64,1024]{1,0:T(8,128)(2,1)S(1)}, bf16[64,1024]{1,0:T(8,128)(2,1)S(1)}, u32[]{:S(2)}, u32[]{:S(2)}) collective-permute-start(bf16[64,1024]{1,0:T(8,128)(2,1)S(1)} %select_select_fusion.own), channel_id=1, source_target_pairs={{0,1},{1,0},{2,3},{3,2},{4,5},{5,4},{6,7},{7,6},{8,9},{9,8},{10,11... | collective-permute-start | bytes 393224 | tf_op jit(solution)/shard_map/ppermute | solution.py:45
  37.3 13.8 %copy-start.6 = (bf16[384,1024]{1,0:T(8,128)(2,1)}, bf16[384,1024]{1,0:T(8,128)(2,1)S(1)}, u32[]{:S(2)}) copy-start(bf16[384,1024]{1,0:T(8,128)(2,1)S(1)} %collective-permute-done.3.three_b) | copy-start | bytes 2359300
  37.3 17.1 %collective-permute-start.4 = (bf16[128,1024]{1,0:T(8,128)(2,1)}, bf16[128,1024]{1,0:T(8,128)(2,1)S(1)}, u32[]{:S(2)}, u32[]{:S(2)}) collective-permute-start(bf16[128,1024]{1,0:T(8,128)(2,1)} %copy-done.13), channel_id=1, source_target_pairs={{0,3},{1,2},{2,1},{3,0},{4,7},{5,6},{6,5},{7,4},{8,11},{9,10},{10,... | collective-permute-start | bytes 786440 | tf_op jit(solution)/shard_map/ppermute | solution.py:45
  39.1 15.3 %collective-permute-start.6 = (bf16[256,1024]{1,0:T(8,128)(2,1)S(1)}, bf16[256,1024]{1,0:T(8,128)(2,1)S(1)}, u32[]{:S(2)}, u32[]{:S(2)}) collective-permute-start(bf16[256,1024]{1,0:T(8,128)(2,1)S(1)} %slice.41), channel_id=1, source_target_pairs={{0,1},{1,0},{2,3},{3,2},{4,5},{5,4},{6,7},{7,6},{8,9},{9,8},{10,11... | collective-permute-start | bytes 1572872 | tf_op jit(solution)/shard_map/ppermute | solution.py:45
  41.3 1.7 %copy-start.19 = (bf16[64,1024]{1,0:T(8,128)(2,1)}, bf16[64,1024]{1,0:T(8,128)(2,1)S(1)}, u32[]{:S(2)}) copy-start(bf16[64,1024]{1,0:T(8,128)(2,1)S(1)} %collective-permute-done.13.two) | copy-start | bytes 393220
  41.3 13.0 %collective-permute-start.5 = (bf16[128,1024]{1,0:T(8,128)(2,1)S(1)}, bf16[128,1024]{1,0:T(8,128)(2,1)S(1)}, u32[]{:S(2)}, u32[]{:S(2)}) collective-permute-start(bf16[128,1024]{1,0:T(8,128)(2,1)S(1)} %slice.40), channel_id=1, source_target_pairs={{0,3},{1,2},{2,1},{3,0},{4,7},{5,6},{6,5},{7,4},{8,11},{9,10},{10,... | collective-permute-start | bytes 786440 | tf_op jit(solution)/shard_map/ppermute | solution.py:45
  43.0 0.7 copy-start.20
  43.0 0.7 copy-start.21
  51.1 12.6 %collective-permute-start.19 = (bf16[320,256]{1,0:T(8,128)(2,1)}, bf16[320,256]{1,0:T(8,128)(2,1)S(1)}, u32[]{:S(2)}, u32[]{:S(2)}) collective-permute-start(bf16[320,256]{1,0:T(8,128)(2,1)} %project_image.1.refs_4_.refs_2_), channel_id=1, source_target_pairs={{0,28},{4,0},{8,4},{12,8},{16,12},{20,16},{24,20},{28,24},{1,29},{... | collective-permute-start | bytes 491528 | tf_op jit(solution)/shard_map/ppermute | solution.py:41
  52.1 11.6 %collective-permute-start.14 = (bf16[320,256]{1,0:T(8,128)(2,1)}, bf16[320,256]{1,0:T(8,128)(2,1)S(1)}, u32[]{:S(2)}, u32[]{:S(2)}) collective-permute-start(bf16[320,256]{1,0:T(8,128)(2,1)} %project_image.1.refs_4_.refs_2_), channel_id=1, source_target_pairs={{0,4},{4,8},{8,12},{12,16},{16,20},{20,24},{24,28},{28,0},{1,5},{5... | collective-permute-start | bytes 491528 | tf_op jit(solution)/shard_map/ppermute | solution.py:41
  54.3 0.7 copy-start.14
  54.3 0.8 copy-start.15
  55.1 0.8 copy-start.9
  64.8 12.9 %collective-permute-start.20 = (bf16[832,256]{1,0:T(8,128)(2,1)S(1)}, bf16[832,256]{1,0:T(8,128)(2,1)S(1)}, u32[]{:S(2)}, u32[]{:S(2)}) collective-permute-start(bf16[832,256]{1,0:T(8,128)(2,1)S(1)} %get-tuple-element.11), channel_id=1, source_target_pairs={{0,28},{4,0},{8,4},{12,8},{16,12},{20,16},{24,20},{28,24},{1,29},{... | collective-permute-start | bytes 1277960 | tf_op jit(solution)/shard_map/ppermute | solution.py:41
  65.7 12.0 %collective-permute-start.15 = (bf16[832,256]{1,0:T(8,128)(2,1)S(1)}, bf16[832,256]{1,0:T(8,128)(2,1)S(1)}, u32[]{:S(2)}, u32[]{:S(2)}) collective-permute-start(bf16[832,256]{1,0:T(8,128)(2,1)S(1)} %get-tuple-element.12), channel_id=1, source_target_pairs={{0,4},{4,8},{8,12},{12,16},{16,20},{20,24},{24,28},{28,0},{1,5},{5... | collective-permute-start | bytes 1277960 | tf_op jit(solution)/shard_map/ppermute | solution.py:41
  77.7 21.8 %copy-start.17 = (bf16[832,256]{1,0:T(8,128)(2,1)}, bf16[832,256]{1,0:T(8,128)(2,1)S(1)}, u32[]{:S(2)}) copy-start(bf16[832,256]{1,0:T(8,128)(2,1)S(1)} %collective-permute-done.20.refs_10_) | copy-start | bytes 1277956
  77.7 12.0 %collective-permute-start.21 = (bf16[832,256]{1,0:T(8,128)(2,1)S(1)}, bf16[832,256]{1,0:T(8,128)(2,1)S(1)}, u32[]{:S(2)}, u32[]{:S(2)}) collective-permute-start(bf16[832,256]{1,0:T(8,128)(2,1)S(1)} %collective-permute-done.20.refs_10_), channel_id=1, source_target_pairs={{0,28},{4,0},{8,4},{12,8},{16,12},{20,16},{24,20},{28,24},{1,29},{... | collective-permute-start | bytes 1277960 | tf_op jit(solution)/shard_map/ppermute | solution.py:41
  77.8 21.8 %copy-start.18 = (bf16[832,256]{1,0:T(8,128)(2,1)}, bf16[832,256]{1,0:T(8,128)(2,1)S(1)}, u32[]{:S(2)}) copy-start(bf16[832,256]{1,0:T(8,128)(2,1)S(1)} %collective-permute-done.15.refs_5_) | copy-start | bytes 1277956
  77.8 12.1 %collective-permute-start.16 = (bf16[832,256]{1,0:T(8,128)(2,1)S(1)}, bf16[832,256]{1,0:T(8,128)(2,1)S(1)}, u32[]{:S(2)}, u32[]{:S(2)}) collective-permute-start(bf16[832,256]{1,0:T(8,128)(2,1)S(1)} %collective-permute-done.15.refs_5_), channel_id=1, source_target_pairs={{0,4},{4,8},{8,12},{12,16},{16,20},{20,24},{24,28},{28,0},{1,5},{5... | collective-permute-start | bytes 1277960 | tf_op jit(solution)/shard_map/ppermute | solution.py:41
  89.8 9.8 %copy-start.10 = (bf16[832,256]{1,0:T(8,128)(2,1)}, bf16[832,256]{1,0:T(8,128)(2,1)S(1)}, u32[]{:S(2)}) copy-start(bf16[832,256]{1,0:T(8,128)(2,1)S(1)} %collective-permute-done.21.refs_11_) | copy-start | bytes 1277956
  89.8 9.8 %collective-permute-start.22 = (bf16[672,256]{1,0:T(8,128)(2,1)S(1)}, bf16[672,256]{1,0:T(8,128)(2,1)S(1)}, u32[]{:S(2)}, u32[]{:S(2)}) collective-permute-start(bf16[672,256]{1,0:T(8,128)(2,1)S(1)} %slice.46), channel_id=1, source_target_pairs={{0,28},{4,0},{8,4},{12,8},{16,12},{20,16},{24,20},{28,24},{1,29},{... | collective-permute-start | bytes 1032200 | tf_op jit(solution)/shard_map/ppermute | solution.py:41
  89.9 9.6 %copy-start.11 = (bf16[832,256]{1,0:T(8,128)(2,1)}, bf16[832,256]{1,0:T(8,128)(2,1)S(1)}, u32[]{:S(2)}) copy-start(bf16[832,256]{1,0:T(8,128)(2,1)S(1)} %collective-permute-done.16.refs_6_) | copy-start | bytes 1277956
  89.9 9.7 %collective-permute-start.17 = (bf16[672,256]{1,0:T(8,128)(2,1)S(1)}, bf16[672,256]{1,0:T(8,128)(2,1)S(1)}, u32[]{:S(2)}, u32[]{:S(2)}) collective-permute-start(bf16[672,256]{1,0:T(8,128)(2,1)S(1)} %slice.44), channel_id=1, source_target_pairs={{0,4},{4,8},{8,12},{12,16},{16,20},{20,24},{24,28},{28,0},{1,5},{5... | collective-permute-start | bytes 1032200 | tf_op jit(solution)/shard_map/ppermute | solution.py:41
  99.6 9.8 %collective-permute-start.23 = (bf16[256,256]{1,0:T(8,128)(2,1)S(1)}, bf16[256,256]{1,0:T(8,128)(2,1)S(1)}, u32[]{:S(2)}, u32[]{:S(2)}) collective-permute-start(bf16[256,256]{1,0:T(8,128)(2,1)S(1)} %slice.47), channel_id=1, source_target_pairs={{0,28},{4,0},{8,4},{12,8},{16,12},{20,16},{24,20},{28,24},{1,29},{... | collective-permute-start | bytes 393224 | tf_op jit(solution)/shard_map/ppermute | solution.py:41
  99.7 9.6 %copy-start = (bf16[512,256]{1,0:T(8,128)(2,1)S(1)}, bf16[512,256]{1,0:T(8,128)(2,1)}, u32[]{:S(2)}) copy-start(bf16[512,256]{1,0:T(8,128)(2,1)} %get-tuple-element.8.refs_3_) | copy-start | bytes 786436
  99.7 9.6 %copy-start.1 = (bf16[320,256]{1,0:T(8,128)(2,1)S(1)}, bf16[320,256]{1,0:T(8,128)(2,1)}, u32[]{:S(2)}) copy-start(bf16[320,256]{1,0:T(8,128)(2,1)} %project_image.1.refs_4_.refs_2_) | copy-start | bytes 491524
  99.7 9.6 %copy-start.3 = (s32[3]{0:T(128)S(1)}, s32[3]{0:T(128)}, u32[]{:S(2)}) copy-start(s32[3]{0:T(128)} %pad_add_fusion.ids_ref) | copy-start | bytes 40
  99.7 9.6 %collective-permute-start.18 = (bf16[256,256]{1,0:T(8,128)(2,1)S(1)}, bf16[256,256]{1,0:T(8,128)(2,1)S(1)}, u32[]{:S(2)}, u32[]{:S(2)}) collective-permute-start(bf16[256,256]{1,0:T(8,128)(2,1)S(1)} %slice.45), channel_id=1, source_target_pairs={{0,4},{4,8},{8,12},{12,16},{16,20},{20,24},{24,28},{28,0},{1,5},{5... | collective-permute-start | bytes 393224 | tf_op jit(solution)/shard_map/ppermute | solution.py:41

commit v7 on v6

--- a/solution.py
+++ b/solution.py
@@ -186,44 +186,23 @@
 
 
 def attention_kernel(tok, heads, ids_ref, counts_ref, starts_ref, *refs):
-    q_one, q_two, own_e, own_l, f1, f2, f3, f4, f5, b1, b2, b3, b4, b5, out_ref = refs[:15]
-    q_buf, kv_buf, img_buf, s_buf, max_buf, sum_buf, acc_buf, sems = refs[15:]
+    q_one, q_two = refs[:2]
+    images, texts = refs[2 : 3 + SHARDS], refs[3 + SHARDS : 4 + 2 * SHARDS]
+    out_ref = refs[4 + 2 * SHARDS]
+    q_buf, kv_buf, img_buf, s_buf, max_buf, sum_buf, acc_buf, sems = refs[5 + 2 * SHARDS :]
     ctx, sample = ids_ref[1], ids_ref[2]
     factor = math.log2(math.e) / math.sqrt(HD)
 
-    rows_e, rows_l = own_e.shape[0], own_l.shape[0]
-    cut, part = rows_e // 2, rows_l // 2
     middle = heads * HD // 2
     moves = [(q_one, q_buf.at[:, :middle]), (q_two, q_buf.at[:, middle:])]
-    for d, array, base, first, count in (
-        (0, own_e, 0, 0, rows_e),
-        (1, f1, 0, 0, rows_e),
-        (2, f2, 0, 0, rows_e),
-        (3, f3, 0, 0, rows_e),
-        (4, f4, 0, cut, cut),
-        (4, b4, rows_l, 0, cut),
-        (5, b3, rows_l, 0, rows_e),
-        (6, b2, rows_l, 0, rows_e),
-        (7, b1, 0, 0, rows_e),
-    ):
+    for n, d in enumerate((0, 1, 2, 3, 4, 4, 5, 6, 7)):
         shard = (ctx - d) & (SHARDS - 1)
-        moves.append(
-            (array.at[pl.ds(base, count), :], img_buf.at[shard, pl.ds(first, count), :])
-        )
-    for d, array, base, first, count in (
-        (0, own_l, 0, 0, rows_l),
-        (1, f2, rows_e, 0, rows_l),
-        (2, f3, rows_e, 0, rows_l),
-        (3, f4, cut, 0, rows_l),
-        (4, f5, 0, 0, part),
-        (4, b5, 0, part, part),
-        (5, b4, 0, 0, rows_l),
-        (6, b3, 0, 0, rows_l),
-        (7, b2, 0, 0, rows_l),
-    ):
-        shard = (ctx - d) & (SHARDS - 1)
-        place = pl.ds(pl.multiple_of(shard * tok + first, part), count)
-        moves.append((array.at[pl.ds(base, count), :], kv_buf.at[place, :]))
+        first = images[4].shape[0] if n == 5 else 0
+        rows = pl.ds(first, images[n].shape[0])
+        moves.append((images[n], img_buf.at[shard, rows, :]))
+        first = texts[4].shape[0] if n == 5 else 0
+        place = pl.multiple_of(shard * tok + first, texts[4].shape[0])
+        moves.append((texts[n], kv_buf.at[pl.ds(place, texts[n].shape[0]), :]))
     copies = [
         pltpu.make_async_copy(source, target, sems.at[n])
         for n, (source, target) in enumerate(moves)
@@ -390,17 +369,17 @@
     )
     queries = [query(normed, w_query, text_tables, n, 2) for n in range(2)]
 
-    cut, part = own_e.shape[0] // 2, tok // 2
-    f1, b1 = shift(own_e, "ctx", 1, True), shift(own_e, "ctx", -1, True)
-    f2 = shift(jnp.concatenate([f1, own_l], axis=0), "ctx", 1, True)
-    b2 = shift(jnp.concatenate([own_l, b1], axis=0), "ctx", -1, True)
-    f3, b3 = shift(f2, "ctx", 1, True), shift(b2, "ctx", -1, True)
-    f4, b4 = shift(f3[cut:], "ctx", 1, True), shift(b3[: tok + cut], "ctx", -1, True)
-    f5 = shift(f4[cut : cut + part], "ctx", 1, True)
-    b5 = shift(b4[part:tok], "ctx", -1, True)
+    def ring(own):
+        cut = own.shape[0] // 2
+        ups, downs = [own], [own]
+        for _ in range(3):
+            ups.append(shift(ups[-1], "ctx", 1, True))
+            downs.append(shift(downs[-1], "ctx", -1, True))
+        last = [shift(ups[3][:cut], "ctx", 1, True), shift(downs[3][cut:], "ctx", -1, True)]
+        return [own, *ups[1:], *last, *downs[:0:-1]]
+
     return attention(
-        tok, heads, (ids, image_counts, image_starts),
-        [*queries, own_e, own_l, f1, f2, f3, f4, f5, b1, b2, b3, b4, b5],
+        tok, heads, (ids, image_counts, image_starts), [*queries, *ring(own_e), *ring(own_l)]
     )
 
 

time: 143 us -> 150 us (1.049)
  starting transfers between devices: 38.8 us -> 48.9 us
  waiting for transfers between devices: 20.2 us -> 17.3 us
    ppermute x13 -> x19, starting transfers between devices: 26.1 us -> 36.1 us  [shift(): return lax.ppermute(x, axis, pairs)]
    ppermute x13 -> x19, waiting for transfers between devices: 18.6 us -> 12.7 us  [shift(): return lax.ppermute(x, axis, pairs)]
    ppermute x10, waiting for transfers between devices: 1.57 us -> 4.58 us  [exchange(): return lax.ppermute(x, 'mp', [(i, i ^ mask) for i in range(4)])]
    unnamed x45 -> x49, local copies, waits for them, and re-layouts: 3.82 us -> 3.76 us
  transfers between devices with their start and end apart: 24 -> 30, of which waited for: 5 -> 7; matrix products, arithmetic and copies ran while one was open for 10% -> 9% of each run, Pallas kernels for 19% -> 13%
where the time goes in v7:
time: 150 us
  Pallas kernels  61.6 us (41%)
  starting transfers between devices  48.9 us (33%)
  waiting for transfers between devices  17.3 us (12%)
  local copies, waits for them, and re-layouts  10 us (7%)
  other arithmetic  8.03 us (5%)
  between operations  3.84 us (3%)
    ppermute x19, starting transfers between devices, shift(): return lax.ppermute(x, axis, pairs)  36.1 us
    pallas_call x1, Pallas kernels, attention(): pl.pallas_call(functools.partial(attention_kernel, tok, heads), out_shape...  33.8 us
    ppermute x19, waiting for transfers between devices, shift(): return lax.ppermute(x, axis, pairs)  12.7 us
    ppermute x10, starting transfers between devices, exchange(): return lax.ppermute(x, 'mp', [(i, i ^ mask) for i in range(4)])  12.7 us
    pallas_call x2, Pallas kernels, query(): pl.pallas_call(query_kernel, out_shape=jax.ShapeDtypeStruct((rows, column...  12.7 us
    pallas_call x1, Pallas kernels, project_text(): pl.pallas_call(text_kernel, out_shape=[jax.ShapeDtypeStruct((rows, D), BF...  7.69 us
    pallas_call x1, Pallas kernels, project_image(): pl.pallas_call(image_kernel, out_shape=jax.ShapeDtypeStruct(((1 + steps)...  7.45 us
    ppermute x10, waiting for transfers between devices, exchange(): return lax.ppermute(x, 'mp', [(i, i ^ mask) for i in range(4)])  4.58 us
  transfers between devices with their start and end apart: 30, of which 7 were waited for; matrix products, arithmetic and copies ran while one was open for 9% of the time, Pallas kernels for 13%

profile of v7, /device:TPU:224, one launch (start us, length us, event | category | flops | bytes accessed | tf_op | source)
XLA Modules:
  0.0 149.7 jit_solution(13840643114558559584)
XLA Ops:
  0.0 1.7 %slice.30 = bf16[128,1024]{1,0:T(8,128)(2,1)} slice(bf16[512,1024]{1,0:T(8,128)(2,1)} %own.1), slice={[0:128], [0:1024]} | slice | bytes 524288 | tf_op jit(solution)/shard_map/slice | solution.py:344
  1.7 2.8 %collective-permute-start.2 = (bf16[128,1024]{1,0:T(8,128)(2,1)}, bf16[128,1024]{1,0:T(8,128)(2,1)S(1)}, u32[]{:S(2)}, u32[]{:S(2)}) collective-permute-start(bf16[128,1024]{1,0:T(8,128)(2,1)} %slice.30), channel_id=1, source_target_pairs={{0,3},{1,2},{2,1},{3,0},{4,7},{5,6},{6,5},{7,4},{8,11},{9,10},{10,... | collective-permute-start | bytes 786440 | tf_op jit(solution)/shard_map/ppermute | solution.py:45
  4.4 0.2 collective-permute-start
  4.6 2.1 %slice.31 = bf16[384,1024]{1,0:T(8,128)(2,1)} slice(bf16[512,1024]{1,0:T(8,128)(2,1)} %own.1), slice={[128:512], [0:1024]} | slice | bytes 1572864 | tf_op jit(solution)/shard_map/slice | solution.py:345
  6.7 1.1 collective-permute-start.3
  7.8 0.7 collective-permute-start.1
  8.5 1.5 %constant_dynamic-update-slice_fusion.1 = bf16[4096,256]{1,0:T(8,128)(2,1)S(1)} fusion(bf16[4096,128]{1,0:T(8,128)(2,1)} %param.14), kind=kLoop, calls=%fused_computation.8 | loop fusion | bytes 2097152
  10.0 0.0 copy-done.8
  10.1 0.2 constant_dynamic-update-slice_fusion.w_kv.refs_1_
  10.3 1.8 %multiply_sine_fusion = (f32[512,64]{1,0:T(8,128)}, f32[512,64]{1,0:T(8,128)}) fusion(f32[64]{0:T(128)S(1)} %multiply_exponential_fusion, f32[512]{0:T(512)S(1)} %add_convert_fusion), kind=kLoop, calls=%fused_computation | loop fusion | flops 32768 | bytes 264448 | tf_op jit(solution)/shard_map/sin | solution.py:30
  12.2 0.6 slice.43
  12.8 1.1 collective-permute-done.refs_0_.one_a
  13.9 0.6 slice.42
  14.5 2.0 %fusion.3 = s32[]{:T(128)} fusion(bf16[1]{0:T(256)(128)(2,1)} %bitcast.5, bf16[1]{0:T(256)(128)(2,1)} %bitcast.4), kind=kLoop, calls=%fused_computation.18 | loop fusion | flops 11 | bytes 8 | tf_op jit(solution)/shard_map/reduce_sum | solution.py:347
  17.0 0.6 broadcast_select_fusion
  17.7 3.5 %collective-permute-start.9 = (bf16[64,1024]{1,0:T(8,128)(2,1)}, bf16[64,1024]{1,0:T(8,128)(2,1)S(1)}, u32[]{:S(2)}, u32[]{:S(2)}) collective-permute-start(bf16[64,1024]{1,0:T(8,128)(2,1)} %broadcast_select_fusion), channel_id=1, source_target_pairs={{0,64},{32,96},{64,128},{96,160},{128,192},{160,224},{1,65},{33,97... | collective-permute-start | bytes 393224 | tf_op jit(solution)/shard_map/ppermute | solution.py:41
  21.2 4.8 %collective-permute-start.8 = (bf16[64,1024]{1,0:T(8,128)(2,1)}, bf16[64,1024]{1,0:T(8,128)(2,1)S(1)}, u32[]{:S(2)}, u32[]{:S(2)}) collective-permute-start(bf16[64,1024]{1,0:T(8,128)(2,1)} %broadcast_select_fusion), channel_id=1, source_target_pairs={{0,128},{32,160},{64,192},{96,224},{1,129},{33,161},{65,193},{97,2... | collective-permute-start | bytes 393224 | tf_op jit(solution)/shard_map/ppermute | solution.py:41
  26.0 1.3 collective-permute-start.7
  27.3 0.7 fusion
  30.0 0.0 collective-permute-done.9
  30.0 0.0 collective-permute-done.8
  30.0 0.1 collective-permute-done.7
  30.1 0.1 collective-permute-start.10
  30.2 0.8 select_reduce_fusion
  31.7 0.6 add_convert_fusion.1
  32.3 0.1 select_select_fusion.own
  32.4 1.9 %collective-permute-start.13 = (bf16[64,1024]{1,0:T(8,128)(2,1)S(1)}, bf16[64,1024]{1,0:T(8,128)(2,1)S(1)}, u32[]{:S(2)}, u32[]{:S(2)}) collective-permute-start(bf16[64,1024]{1,0:T(8,128)(2,1)S(1)} %select_select_fusion.own), channel_id=1, source_target_pairs={{0,2},{1,3},{2,0},{3,1},{4,6},{5,7},{6,4},{7,5},{8,10},{9,11},{10,... | collective-permute-start | bytes 393224 | tf_op jit(solution)/shard_map/ppermute | solution.py:45
  34.3 1.1 collective-permute-start.12
  35.5 0.5 collective-permute-start.11
  36.0 0.8 multiply_sine_fusion.1
  36.8 0.6 pad_add_fusion.ids_ref
  37.4 0.0 collective-permute-done.3.three_b
  37.4 1.8 %collective-permute-start.4 = (bf16[128,1024]{1,0:T(8,128)(2,1)}, bf16[128,1024]{1,0:T(8,128)(2,1)S(1)}, u32[]{:S(2)}, u32[]{:S(2)}) collective-permute-start(bf16[128,1024]{1,0:T(8,128)(2,1)} %copy-done.11), channel_id=1, source_target_pairs={{0,3},{1,2},{2,1},{3,0},{4,7},{5,6},{6,5},{7,4},{8,11},{9,10},{10,... | collective-permute-start | bytes 786440 | tf_op jit(solution)/shard_map/ppermute | solution.py:45
  39.2 0.0 collective-permute-done.1.one_b
  39.2 1.3 collective-permute-start.6
  40.5 1.0 slice.40
  41.5 0.0 collective-permute-done.13.two
  41.5 1.2 collective-permute-start.5
  42.7 0.4 collective-permute-done.12.three
  43.2 0.0 collective-permute-done.11.one
  43.2 0.6 copy-done.22
  43.8 0.0 copy-done.23
  43.9 7.4 %project_image.1.refs_4_.refs_2_ = bf16[320,256]{1,0:T(8,128)(2,1)} custom-call(s32[3]{0:T(128)} %pad_add_fusion.ids_ref, bf16[64,1024]{1,0:T(8,128)(2,1)} %copy-done.14, bf16[64,1024]{1,0:T(8,128)(2,1)} %copy-done.23, bf16[64,1024]{1,0:T(8,128)(2,1)} %copy-done.22, bf16[64,1024]{1,0:T(8,128)(2,1)} %copy-done.21, f32[1,4096]{1,0:T(1,128)} %bitcast.6, ...), custom_call_target="tpu_custom_call" | custom-call | flops 8000000000 | bytes 10485760 | tf_op jit(solution)/shard_map/project_image/pallas_call | solution.py:92
  51.3 0.0 collective-permute-done.4.two_a
  51.4 3.1 %collective-permute-done.5.two_b = bf16[128,1024]{1,0:T(8,128)(2,1)S(1)} collective-permute-done((bf16[128,1024]{1,0:T(8,128)(2,1)S(1)}, bf16[128,1024]{1,0:T(8,128)(2,1)S(1)}, u32[]{:S(2)}, u32[]{:S(2)}) %collective-permute-start.5) | collective-permute-done | bytes 262176 | tf_op jit(solution)/shard_map/ppermute | solution.py:45
  54.4 0.7 copy-done.13
  55.1 0.8 copy-done.9
  55.9 7.7 %project_text.1 = (bf16[512,4096]{1,0:T(8,128)(2,1)}, bf16[512,256]{1,0:T(8,128)(2,1)}) custom-call(s32[3]{0:T(128)} %pad_add_fusion.ids_ref, bf16[512,1024]{1,0:T(8,128)(2,1)} %own.1, bf16[128,1024]{1,0:T(8,128)(2,1)} %copy-done.11, bf16[384,1024]{1,0:T(8,128)(2,1)} %collective-permute-done.1.one_b, bf16[128,1024]{1,0:T(8,128)(2,1)} %copy-done.10, ...), custom_call_target="tpu_custom_call" | custom-call | tf_op jit(solution)/shard_map/project_text/pallas_call | solution.py:135
  63.6 1.1 collective-permute-start.26
  64.7 2.2 %collective-permute-start.22 = (bf16[512,256]{1,0:T(8,128)(2,1)}, bf16[512,256]{1,0:T(8,128)(2,1)S(1)}, u32[]{:S(2)}, u32[]{:S(2)}) collective-permute-start(bf16[512,256]{1,0:T(8,128)(2,1)} %get-tuple-element.8.refs_11_), channel_id=1, source_target_pairs={{0,4},{4,8},{8,12},{12,16},{16,20},{20,24},{24,28},{28,0},{1,5},{5... | collective-permute-start | bytes 786440 | tf_op jit(solution)/shard_map/ppermute | solution.py:41
  66.9 3.2 %collective-permute-start.14 = (bf16[320,256]{1,0:T(8,128)(2,1)S(1)}, bf16[320,256]{1,0:T(8,128)(2,1)S(1)}, u32[]{:S(2)}, u32[]{:S(2)}) collective-permute-start(bf16[320,256]{1,0:T(8,128)(2,1)S(1)} %copy-done), channel_id=1, source_target_pairs={{0,4},{4,8},{8,12},{12,16},{16,20},{20,24},{24,28},{28,0},{1,5},{5... | collective-permute-start | bytes 491528 | tf_op jit(solution)/shard_map/ppermute | solution.py:41
  70.2 6.8 %collective-permute-done.18.refs_10_ = bf16[320,256]{1,0:T(8,128)(2,1)S(1)} collective-permute-done((bf16[320,256]{1,0:T(8,128)(2,1)S(1)}, bf16[320,256]{1,0:T(8,128)(2,1)S(1)}, u32[]{:S(2)}, u32[]{:S(2)}) %collective-permute-start.18) | collective-permute-done | bytes 163872 | tf_op jit(solution)/shard_map/ppermute | solution.py:41
  76.9 3.2 %collective-permute-start.15 = (bf16[320,256]{1,0:T(8,128)(2,1)S(1)}, bf16[320,256]{1,0:T(8,128)(2,1)S(1)}, u32[]{:S(2)}, u32[]{:S(2)}) collective-permute-start(bf16[320,256]{1,0:T(8,128)(2,1)S(1)} %collective-permute-done.14.refs_3_), channel_id=1, source_target_pairs={{0,4},{4,8},{8,12},{12,16},{16,20},{20,24},{24,28},{28,0},{1,5},{5... | collective-permute-start | bytes 491528 | tf_op jit(solution)/shard_map/ppermute | solution.py:41
  80.2 3.2 %collective-permute-start.23 = (bf16[512,256]{1,0:T(8,128)(2,1)S(1)}, bf16[512,256]{1,0:T(8,128)(2,1)S(1)}, u32[]{:S(2)}, u32[]{:S(2)}) collective-permute-start(bf16[512,256]{1,0:T(8,128)(2,1)S(1)} %collective-permute-done.22.refs_12_), channel_id=1, source_target_pairs={{0,4},{4,8},{8,12},{12,16},{16,20},{20,24},{24,28},{28,0},{1,5},{5... | collective-permute-start | bytes 786440 | tf_op jit(solution)/shard_map/ppermute | solution.py:41
  83.4 0.9 collective-permute-done.19.refs_9_
  84.4 3.4 %collective-permute-start.16 = (bf16[320,256]{1,0:T(8,128)(2,1)S(1)}, bf16[320,256]{1,0:T(8,128)(2,1)S(1)}, u32[]{:S(2)}, u32[]{:S(2)}) collective-permute-start(bf16[320,256]{1,0:T(8,128)(2,1)S(1)} %collective-permute-done.15.refs_4_), channel_id=1, source_target_pairs={{0,4},{4,8},{8,12},{12,16},{16,20},{20,24},{24,28},{28,0},{1,5},{5... | collective-permute-start | bytes 491528 | tf_op jit(solution)/shard_map/ppermute | solution.py:41
  87.8 4.9 %collective-permute-done.20.refs_8_ = bf16[320,256]{1,0:T(8,128)(2,1)S(1)} collective-permute-done((bf16[320,256]{1,0:T(8,128)(2,1)S(1)}, bf16[320,256]{1,0:T(8,128)(2,1)S(1)}, u32[]{:S(2)}, u32[]{:S(2)}) %collective-permute-start.20) | collective-permute-done | bytes 163872 | tf_op jit(solution)/shard_map/ppermute | solution.py:41
  92.7 3.3 %collective-permute-start.17 = (bf16[160,256]{1,0:T(8,128)(2,1)S(1)}, bf16[160,256]{1,0:T(8,128)(2,1)S(1)}, u32[]{:S(2)}, u32[]{:S(2)}) collective-permute-start(bf16[160,256]{1,0:T(8,128)(2,1)S(1)} %slice.44), channel_id=1, source_target_pairs={{0,4},{4,8},{8,12},{12,16},{16,20},{20,24},{24,28},{28,0},{1,5},{5... | collective-permute-start | bytes 245768 | tf_op jit(solution)/shard_map/ppermute | solution.py:41
  96.0 3.2 %collective-permute-start.24 = (bf16[512,256]{1,0:T(8,128)(2,1)S(1)}, bf16[512,256]{1,0:T(8,128)(2,1)S(1)}, u32[]{:S(2)}, u32[]{:S(2)}) collective-permute-start(bf16[512,256]{1,0:T(8,128)(2,1)S(1)} %collective-permute-done.23.refs_13_), channel_id=1, source_target_pairs={{0,4},{4,8},{8,12},{12,16},{16,20},{20,24},{24,28},{28,0},{1,5},{5... | collective-permute-start | bytes 786440 | tf_op jit(solution)/shard_map/ppermute | solution.py:41
  99.3 6.3 %query.3.refs_1_ = bf16[512,512]{1,0:T(8,128)(2,1)} custom-call(bf16[512,4096]{1,0:T(8,128)(2,1)} %get-tuple-element.7.x_ref, bf16[4096,1024]{1,0:T(8,128)(2,1)} %w_ref.3, f32[512,64]{1,0:T(8,128)} %get-tuple-element.12.refs_2_.cos, f32[512,64]{1,0:T(8,128)} %get-tuple-element.11.refs_3_.sin), custom_call_target="tpu_custom_call" | custom-call | flops 3000000000 | bytes 1048576 | tf_op jit(solution)/shard_map/query/pallas_call | solution.py:169
  105.7 0.1 collective-permute-start.29
  105.8 3.5 %collective-permute-start.25 = (bf16[256,256]{1,0:T(8,128)(2,1)S(1)}, bf16[256,256]{1,0:T(8,128)(2,1)S(1)}, u32[]{:S(2)}, u32[]{:S(2)}) collective-permute-start(bf16[256,256]{1,0:T(8,128)(2,1)S(1)} %slice.46), channel_id=1, source_target_pairs={{0,4},{4,8},{8,12},{12,16},{16,20},{20,24},{24,28},{28,0},{1,5},{5... | collective-permute-start | bytes 393224 | tf_op jit(solution)/shard_map/ppermute | solution.py:41
  109.3 6.3 %query.2.refs_0_ = bf16[512,512]{1,0:T(8,128)(2,1)} custom-call(bf16[512,4096]{1,0:T(8,128)(2,1)} %get-tuple-element.7.x_ref, bf16[4096,1024]{1,0:T(8,128)(2,1)} %w_ref.3, f32[512,64]{1,0:T(8,128)} %get-tuple-element.12.refs_2_.cos, f32[512,64]{1,0:T(8,128)} %get-tuple-element.11.refs_3_.sin), custom_call_target="tpu_custom_call" | custom-call | flops 3000000000 | bytes 1048576 | tf_op jit(solution)/shard_map/query/pallas_call | solution.py:169
  115.7 33.8 %attention.1 = bf16[512,1024]{1,0:T(8,128)(2,1)} custom-call(s32[3]{0:T(128)S(1)} %copy-done.2, s32[8]{0:T(128)S(1)} %copy-done.3, s32[8,8]{1,0:T(8,128)S(1)} %copy-done.1, bf16[512,512]{1,0:T(8,128)(2,1)} %query.2.refs_0_, bf16[512,512]{1,0:T(8,128)(2,1)} %query.3.refs_1_, bf16[320,256]{1,0:T(8,128)(2,1)S(1)} %copy-done, ...), custom_call_target="tpu_custom_call" | custom-call | flops 8589934592 | bytes 8388608 | tf_op jit(solution)/shard_map/attention/pallas_call | solution.py:289
  (74 shorter events, 0.3 us)
Async XLA Ops:
  1.7 10.5 %collective-permute-start.2 = (bf16[128,1024]{1,0:T(8,128)(2,1)}, bf16[128,1024]{1,0:T(8,128)(2,1)S(1)}, u32[]{:S(2)}, u32[]{:S(2)}) collective-permute-start(bf16[128,1024]{1,0:T(8,128)(2,1)} %slice.30), channel_id=1, source_target_pairs={{0,3},{1,2},{2,1},{3,0},{4,7},{5,6},{6,5},{7,4},{8,11},{9,10},{10,... | collective-permute-start | bytes 786440 | tf_op jit(solution)/shard_map/ppermute | solution.py:45
  4.4 9.4 %collective-permute-start = (bf16[128,1024]{1,0:T(8,128)(2,1)}, bf16[128,1024]{1,0:T(8,128)(2,1)S(1)}, u32[]{:S(2)}, u32[]{:S(2)}) collective-permute-start(bf16[128,1024]{1,0:T(8,128)(2,1)} %slice.30), channel_id=1, source_target_pairs={{0,1},{1,0},{2,3},{3,2},{4,5},{5,4},{6,7},{7,6},{8,9},{9,8},{10,11... | collective-permute-start | bytes 786440 | tf_op jit(solution)/shard_map/ppermute | solution.py:45
  6.7 30.7 %collective-permute-start.3 = (bf16[384,1024]{1,0:T(8,128)(2,1)}, bf16[384,1024]{1,0:T(8,128)(2,1)S(1)}, u32[]{:S(2)}, u32[]{:S(2)}) collective-permute-start(bf16[384,1024]{1,0:T(8,128)(2,1)} %slice.31), channel_id=1, source_target_pairs={{0,3},{1,2},{2,1},{3,0},{4,7},{5,6},{6,5},{7,4},{8,11},{9,10},{10,... | collective-permute-start | bytes 2359304 | tf_op jit(solution)/shard_map/ppermute | solution.py:45
  7.8 31.4 %collective-permute-start.1 = (bf16[384,1024]{1,0:T(8,128)(2,1)}, bf16[384,1024]{1,0:T(8,128)(2,1)}, u32[]{:S(2)}, u32[]{:S(2)}) collective-permute-start(bf16[384,1024]{1,0:T(8,128)(2,1)} %slice.31), channel_id=1, source_target_pairs={{0,1},{1,0},{2,3},{3,2},{4,5},{5,4},{6,7},{7,6},{8,9},{9,8},{10,11... | collective-permute-start | bytes 2359304 | tf_op jit(solution)/shard_map/ppermute | solution.py:45
  8.5 1.5 %copy-start.8 = (bf16[4096,128]{1,0:T(8,128)(2,1)S(1)}, bf16[4096,128]{1,0:T(8,128)(2,1)}, u32[]{:S(2)}) copy-start(bf16[4096,128]{1,0:T(8,128)(2,1)} %param.15) | copy-start | bytes 3145732
  8.5 8.5 %copy-start.7 = (bf16[64,1024]{1,0:T(8,128)(2,1)S(1)}, bf16[64,1024]{1,0:T(8,128)(2,1)}, u32[]{:S(2)}) copy-start(bf16[64,1024]{1,0:T(8,128)(2,1)} %param.9) | copy-start | bytes 393220
  8.5 18.8 %copy-start.3 = (s32[8]{0:T(128)S(1)}, s32[8]{0:T(128)}, u32[]{:S(2)}) copy-start(s32[8]{0:T(128)} %counts_ref.1) | copy-start | bytes 100
  10.1 20.2 %copy-start.1 = (s32[8,8]{1,0:T(8,128)S(1)}, s32[8,8]{1,0:T(8,128)}, u32[]{:S(2)}) copy-start(s32[8,8]{1,0:T(8,128)} %starts_ref.1) | copy-start | bytes 772
  10.3 32.9 %copy-start.5 = (bf16[4096,256]{1,0:T(8,128)(2,1)}, bf16[4096,256]{1,0:T(8,128)(2,1)S(1)}, u32[]{:S(2)}) copy-start(bf16[4096,256]{1,0:T(8,128)(2,1)S(1)} %constant_dynamic-update-slice_fusion.w_kv.refs_1_) | copy-start | bytes 6291460
  12.2 4.8 %copy-start.10 = (bf16[128,1024]{1,0:T(8,128)(2,1)}, bf16[128,1024]{1,0:T(8,128)(2,1)S(1)}, u32[]{:S(2)}) copy-start(bf16[128,1024]{1,0:T(8,128)(2,1)S(1)} %collective-permute-done.2.refs_1_.three_a) | copy-start | bytes 786436
  13.9 7.3 %copy-start.11 = (bf16[128,1024]{1,0:T(8,128)(2,1)}, bf16[128,1024]{1,0:T(8,128)(2,1)S(1)}, u32[]{:S(2)}) copy-start(bf16[128,1024]{1,0:T(8,128)(2,1)S(1)} %collective-permute-done.refs_0_.one_a) | copy-start | bytes 786436
  17.7 12.3 %collective-permute-start.9 = (bf16[64,1024]{1,0:T(8,128)(2,1)}, bf16[64,1024]{1,0:T(8,128)(2,1)S(1)}, u32[]{:S(2)}, u32[]{:S(2)}) collective-permute-start(bf16[64,1024]{1,0:T(8,128)(2,1)} %broadcast_select_fusion), channel_id=1, source_target_pairs={{0,64},{32,96},{64,128},{96,160},{128,192},{160,224},{1,65},{33,97... | collective-permute-start | bytes 393224 | tf_op jit(solution)/shard_map/ppermute | solution.py:41
  21.2 8.8 %collective-permute-start.8 = (bf16[64,1024]{1,0:T(8,128)(2,1)}, bf16[64,1024]{1,0:T(8,128)(2,1)S(1)}, u32[]{:S(2)}, u32[]{:S(2)}) collective-permute-start(bf16[64,1024]{1,0:T(8,128)(2,1)} %broadcast_select_fusion), channel_id=1, source_target_pairs={{0,128},{32,160},{64,192},{96,224},{1,129},{33,161},{65,193},{97,2... | collective-permute-start | bytes 393224 | tf_op jit(solution)/shard_map/ppermute | solution.py:41
  26.0 4.1 %collective-permute-start.7 = (bf16[64,1024]{1,0:T(8,128)(2,1)}, bf16[64,1024]{1,0:T(8,128)(2,1)S(1)}, u32[]{:S(2)}, u32[]{:S(2)}) collective-permute-start(bf16[64,1024]{1,0:T(8,128)(2,1)} %broadcast_select_fusion), channel_id=1, source_target_pairs={{0,192},{32,224},{1,193},{33,225},{2,194},{34,226},{3,195},{35,227... | collective-permute-start | bytes 393224 | tf_op jit(solution)/shard_map/ppermute | solution.py:41
  30.1 2.2 %collective-permute-start.10 = (bf16[64,1024]{1,0:T(8,128)(2,1)S(1)}, bf16[64,1024]{1,0:T(8,128)(2,1)}, u32[]{:S(2)}, u32[]{:S(2)}) collective-permute-start(bf16[64,1024]{1,0:T(8,128)(2,1)S(1)} %select_select_fusion.1), channel_id=1, source_target_pairs={{0,32},{32,0},{64,96},{96,64},{128,160},{160,128},{192,224},{224,1... | collective-permute-start | bytes 393224 | tf_op jit(solution)/shard_map/ppermute | solution.py:351
  32.4 10.8 %copy-start.14 = (bf16[64,1024]{1,0:T(8,128)(2,1)}, bf16[64,1024]{1,0:T(8,128)(2,1)S(1)}, u32[]{:S(2)}) copy-start(bf16[64,1024]{1,0:T(8,128)(2,1)S(1)} %select_select_fusion.own) | copy-start | bytes 393220
  32.4 9.1 %collective-permute-start.13 = (bf16[64,1024]{1,0:T(8,128)(2,1)S(1)}, bf16[64,1024]{1,0:T(8,128)(2,1)S(1)}, u32[]{:S(2)}, u32[]{:S(2)}) collective-permute-start(bf16[64,1024]{1,0:T(8,128)(2,1)S(1)} %select_select_fusion.own), channel_id=1, source_target_pairs={{0,2},{1,3},{2,0},{3,1},{4,6},{5,7},{6,4},{7,5},{8,10},{9,11},{10,... | collective-permute-start | bytes 393224 | tf_op jit(solution)/shard_map/ppermute | solution.py:45
  34.3 8.8 %collective-permute-start.12 = (bf16[64,1024]{1,0:T(8,128)(2,1)S(1)}, bf16[64,1024]{1,0:T(8,128)(2,1)S(1)}, u32[]{:S(2)}, u32[]{:S(2)}) collective-permute-start(bf16[64,1024]{1,0:T(8,128)(2,1)S(1)} %select_select_fusion.own), channel_id=1, source_target_pairs={{0,3},{1,2},{2,1},{3,0},{4,7},{5,6},{6,5},{7,4},{8,11},{9,10},{10,... | collective-permute-start | bytes 393224 | tf_op jit(solution)/shard_map/ppermute | solution.py:45
  35.5 7.7 %collective-permute-start.11 = (bf16[64,1024]{1,0:T(8,128)(2,1)S(1)}, bf16[64,1024]{1,0:T(8,128)(2,1)S(1)}, u32[]{:S(2)}, u32[]{:S(2)}) collective-permute-start(bf16[64,1024]{1,0:T(8,128)(2,1)S(1)} %select_select_fusion.own), channel_id=1, source_target_pairs={{0,1},{1,0},{2,3},{3,2},{4,5},{5,4},{6,7},{7,6},{8,9},{9,8},{10,11... | collective-permute-start | bytes 393224 | tf_op jit(solution)/shard_map/ppermute | solution.py:45
  37.4 14.0 %copy-start.6 = (bf16[384,1024]{1,0:T(8,128)(2,1)}, bf16[384,1024]{1,0:T(8,128)(2,1)S(1)}, u32[]{:S(2)}) copy-start(bf16[384,1024]{1,0:T(8,128)(2,1)S(1)} %collective-permute-done.3.three_b) | copy-start | bytes 2359300
  37.4 14.0 %collective-permute-start.4 = (bf16[128,1024]{1,0:T(8,128)(2,1)}, bf16[128,1024]{1,0:T(8,128)(2,1)S(1)}, u32[]{:S(2)}, u32[]{:S(2)}) collective-permute-start(bf16[128,1024]{1,0:T(8,128)(2,1)} %copy-done.11), channel_id=1, source_target_pairs={{0,3},{1,2},{2,1},{3,0},{4,7},{5,6},{6,5},{7,4},{8,11},{9,10},{10,... | collective-permute-start | bytes 786440 | tf_op jit(solution)/shard_map/ppermute | solution.py:45
  39.2 15.2 %collective-permute-start.6 = (bf16[256,1024]{1,0:T(8,128)(2,1)S(1)}, bf16[256,1024]{1,0:T(8,128)(2,1)S(1)}, u32[]{:S(2)}, u32[]{:S(2)}) collective-permute-start(bf16[256,1024]{1,0:T(8,128)(2,1)S(1)} %slice.41), channel_id=1, source_target_pairs={{0,1},{1,0},{2,3},{3,2},{4,5},{5,4},{6,7},{7,6},{8,9},{9,8},{10,11... | collective-permute-start | bytes 1572872 | tf_op jit(solution)/shard_map/ppermute | solution.py:45
  41.5 1.7 %copy-start.21 = (bf16[64,1024]{1,0:T(8,128)(2,1)}, bf16[64,1024]{1,0:T(8,128)(2,1)S(1)}, u32[]{:S(2)}) copy-start(bf16[64,1024]{1,0:T(8,128)(2,1)S(1)} %collective-permute-done.13.two) | copy-start | bytes 393220
  41.5 12.9 %collective-permute-start.5 = (bf16[128,1024]{1,0:T(8,128)(2,1)S(1)}, bf16[128,1024]{1,0:T(8,128)(2,1)S(1)}, u32[]{:S(2)}, u32[]{:S(2)}) collective-permute-start(bf16[128,1024]{1,0:T(8,128)(2,1)S(1)} %slice.40), channel_id=1, source_target_pairs={{0,3},{1,2},{2,1},{3,0},{4,7},{5,6},{6,5},{7,4},{8,11},{9,10},{10,... | collective-permute-start | bytes 786440 | tf_op jit(solution)/shard_map/ppermute | solution.py:45
  43.2 0.7 copy-start.22
  43.2 0.7 copy-start.23
  51.3 15.6 %copy-start = (bf16[320,256]{1,0:T(8,128)(2,1)S(1)}, bf16[320,256]{1,0:T(8,128)(2,1)}, u32[]{:S(2)}) copy-start(bf16[320,256]{1,0:T(8,128)(2,1)} %project_image.1.refs_4_.refs_2_) | copy-start | bytes 491524
  51.3 3.1 %copy-start.12 = (bf16[128,1024]{1,0:T(8,128)(2,1)}, bf16[128,1024]{1,0:T(8,128)(2,1)S(1)}, u32[]{:S(2)}) copy-start(bf16[128,1024]{1,0:T(8,128)(2,1)S(1)} %collective-permute-done.4.two_a) | copy-start | bytes 786436
  54.4 0.7 copy-start.13
  55.1 0.8 copy-start.9
  63.6 16.6 %collective-permute-start.26 = (bf16[512,256]{1,0:T(8,128)(2,1)}, bf16[512,256]{1,0:T(8,128)(2,1)S(1)}, u32[]{:S(2)}, u32[]{:S(2)}) collective-permute-start(bf16[512,256]{1,0:T(8,128)(2,1)} %get-tuple-element.8.refs_11_), channel_id=1, source_target_pairs={{0,28},{4,0},{8,4},{12,8},{16,12},{20,16},{24,20},{28,24},{1,29},{... | collective-permute-start | bytes 786440 | tf_op jit(solution)/shard_map/ppermute | solution.py:41
  64.7 15.5 %collective-permute-start.22 = (bf16[512,256]{1,0:T(8,128)(2,1)}, bf16[512,256]{1,0:T(8,128)(2,1)S(1)}, u32[]{:S(2)}, u32[]{:S(2)}) collective-permute-start(bf16[512,256]{1,0:T(8,128)(2,1)} %get-tuple-element.8.refs_11_), channel_id=1, source_target_pairs={{0,4},{4,8},{8,12},{12,16},{16,20},{20,24},{24,28},{28,0},{1,5},{5... | collective-permute-start | bytes 786440 | tf_op jit(solution)/shard_map/ppermute | solution.py:41
  66.9 10.0 %collective-permute-start.18 = (bf16[320,256]{1,0:T(8,128)(2,1)S(1)}, bf16[320,256]{1,0:T(8,128)(2,1)S(1)}, u32[]{:S(2)}, u32[]{:S(2)}) collective-permute-start(bf16[320,256]{1,0:T(8,128)(2,1)S(1)} %copy-done), channel_id=1, source_target_pairs={{0,28},{4,0},{8,4},{12,8},{16,12},{20,16},{24,20},{28,24},{1,29},{... | collective-permute-start | bytes 491528 | tf_op jit(solution)/shard_map/ppermute | solution.py:41
  66.9 10.0 %collective-permute-start.14 = (bf16[320,256]{1,0:T(8,128)(2,1)S(1)}, bf16[320,256]{1,0:T(8,128)(2,1)S(1)}, u32[]{:S(2)}, u32[]{:S(2)}) collective-permute-start(bf16[320,256]{1,0:T(8,128)(2,1)S(1)} %copy-done), channel_id=1, source_target_pairs={{0,4},{4,8},{8,12},{12,16},{16,20},{20,24},{24,28},{28,0},{1,5},{5... | collective-permute-start | bytes 491528 | tf_op jit(solution)/shard_map/ppermute | solution.py:41
  76.9 7.4 %collective-permute-start.19 = (bf16[320,256]{1,0:T(8,128)(2,1)S(1)}, bf16[320,256]{1,0:T(8,128)(2,1)S(1)}, u32[]{:S(2)}, u32[]{:S(2)}) collective-permute-start(bf16[320,256]{1,0:T(8,128)(2,1)S(1)} %collective-permute-done.18.refs_10_), channel_id=1, source_target_pairs={{0,28},{4,0},{8,4},{12,8},{16,12},{20,16},{24,20},{28,24},{1,29},{... | collective-permute-start | bytes 491528 | tf_op jit(solution)/shard_map/ppermute | solution.py:41
  76.9 7.4 %collective-permute-start.15 = (bf16[320,256]{1,0:T(8,128)(2,1)S(1)}, bf16[320,256]{1,0:T(8,128)(2,1)S(1)}, u32[]{:S(2)}, u32[]{:S(2)}) collective-permute-start(bf16[320,256]{1,0:T(8,128)(2,1)S(1)} %collective-permute-done.14.refs_3_), channel_id=1, source_target_pairs={{0,4},{4,8},{8,12},{12,16},{16,20},{20,24},{24,28},{28,0},{1,5},{5... | collective-permute-start | bytes 491528 | tf_op jit(solution)/shard_map/ppermute | solution.py:41
  80.2 25.4 %copy-start.17 = (bf16[512,256]{1,0:T(8,128)(2,1)}, bf16[512,256]{1,0:T(8,128)(2,1)S(1)}, u32[]{:S(2)}) copy-start(bf16[512,256]{1,0:T(8,128)(2,1)S(1)} %collective-permute-done.26.refs_19_) | copy-start | bytes 786436
  80.2 15.8 %collective-permute-start.27 = (bf16[512,256]{1,0:T(8,128)(2,1)S(1)}, bf16[512,256]{1,0:T(8,128)(2,1)S(1)}, u32[]{:S(2)}, u32[]{:S(2)}) collective-permute-start(bf16[512,256]{1,0:T(8,128)(2,1)S(1)} %collective-permute-done.26.refs_19_), channel_id=1, source_target_pairs={{0,28},{4,0},{8,4},{12,8},{16,12},{20,16},{24,20},{28,24},{1,29},{... | collective-permute-start | bytes 786440 | tf_op jit(solution)/shard_map/ppermute | solution.py:41
  80.2 25.4 %copy-start.18 = (bf16[512,256]{1,0:T(8,128)(2,1)}, bf16[512,256]{1,0:T(8,128)(2,1)S(1)}, u32[]{:S(2)}) copy-start(bf16[512,256]{1,0:T(8,128)(2,1)S(1)} %collective-permute-done.22.refs_12_) | copy-start | bytes 786436
  80.2 15.8 %collective-permute-start.23 = (bf16[512,256]{1,0:T(8,128)(2,1)S(1)}, bf16[512,256]{1,0:T(8,128)(2,1)S(1)}, u32[]{:S(2)}, u32[]{:S(2)}) collective-permute-start(bf16[512,256]{1,0:T(8,128)(2,1)S(1)} %collective-permute-done.22.refs_12_), channel_id=1, source_target_pairs={{0,4},{4,8},{8,12},{12,16},{16,20},{20,24},{24,28},{28,0},{1,5},{5... | collective-permute-start | bytes 786440 | tf_op jit(solution)/shard_map/ppermute | solution.py:41
  84.4 8.3 %collective-permute-start.20 = (bf16[320,256]{1,0:T(8,128)(2,1)S(1)}, bf16[320,256]{1,0:T(8,128)(2,1)S(1)}, u32[]{:S(2)}, u32[]{:S(2)}) collective-permute-start(bf16[320,256]{1,0:T(8,128)(2,1)S(1)} %collective-permute-done.19.refs_9_), channel_id=1, source_target_pairs={{0,28},{4,0},{8,4},{12,8},{16,12},{20,16},{24,20},{28,24},{1,29},{... | collective-permute-start | bytes 491528 | tf_op jit(solution)/shard_map/ppermute | solution.py:41
  84.4 8.3 %collective-permute-start.16 = (bf16[320,256]{1,0:T(8,128)(2,1)S(1)}, bf16[320,256]{1,0:T(8,128)(2,1)S(1)}, u32[]{:S(2)}, u32[]{:S(2)}) collective-permute-start(bf16[320,256]{1,0:T(8,128)(2,1)S(1)} %collective-permute-done.15.refs_4_), channel_id=1, source_target_pairs={{0,4},{4,8},{8,12},{12,16},{16,20},{20,24},{24,28},{28,0},{1,5},{5... | collective-permute-start | bytes 491528 | tf_op jit(solution)/shard_map/ppermute | solution.py:41
  92.7 23.0 %collective-permute-start.21 = (bf16[160,256]{1,0:T(8,128)(2,1)S(1)}, bf16[160,256]{1,0:T(8,128)(2,1)S(1)}, u32[]{:S(2)}, u32[]{:S(2)}) collective-permute-start(bf16[160,256]{1,0:T(8,128)(2,1)S(1)} %slice.45), channel_id=1, source_target_pairs={{0,28},{4,0},{8,4},{12,8},{16,12},{20,16},{24,20},{28,24},{1,29},{... | collective-permute-start | bytes 245768 | tf_op jit(solution)/shard_map/ppermute | solution.py:41
  92.7 22.9 %collective-permute-start.17 = (bf16[160,256]{1,0:T(8,128)(2,1)S(1)}, bf16[160,256]{1,0:T(8,128)(2,1)S(1)}, u32[]{:S(2)}, u32[]{:S(2)}) collective-permute-start(bf16[160,256]{1,0:T(8,128)(2,1)S(1)} %slice.44), channel_id=1, source_target_pairs={{0,4},{4,8},{8,12},{12,16},{16,20},{20,24},{24,28},{28,0},{1,5},{5... | collective-permute-start | bytes 245768 | tf_op jit(solution)/shard_map/ppermute | solution.py:41
  96.0 9.6 %copy-start.19 = (bf16[512,256]{1,0:T(8,128)(2,1)}, bf16[512,256]{1,0:T(8,128)(2,1)S(1)}, u32[]{:S(2)}) copy-start(bf16[512,256]{1,0:T(8,128)(2,1)S(1)} %collective-permute-done.27.refs_18_) | copy-start | bytes 786436
  96.0 9.6 %collective-permute-start.28 = (bf16[512,256]{1,0:T(8,128)(2,1)S(1)}, bf16[512,256]{1,0:T(8,128)(2,1)S(1)}, u32[]{:S(2)}, u32[]{:S(2)}) collective-permute-start(bf16[512,256]{1,0:T(8,128)(2,1)S(1)} %collective-permute-done.27.refs_18_), channel_id=1, source_target_pairs={{0,28},{4,0},{8,4},{12,8},{16,12},{20,16},{24,20},{28,24},{1,29},{... | collective-permute-start | bytes 786440 | tf_op jit(solution)/shard_map/ppermute | solution.py:41
  96.0 9.6 %copy-start.20 = (bf16[512,256]{1,0:T(8,128)(2,1)}, bf16[512,256]{1,0:T(8,128)(2,1)S(1)}, u32[]{:S(2)}) copy-start(bf16[512,256]{1,0:T(8,128)(2,1)S(1)} %collective-permute-done.23.refs_13_) | copy-start | bytes 786436
  96.0 9.7 %collective-permute-start.24 = (bf16[512,256]{1,0:T(8,128)(2,1)S(1)}, bf16[512,256]{1,0:T(8,128)(2,1)S(1)}, u32[]{:S(2)}, u32[]{:S(2)}) collective-permute-start(bf16[512,256]{1,0:T(8,128)(2,1)S(1)} %collective-permute-done.23.refs_13_), channel_id=1, source_target_pairs={{0,4},{4,8},{8,12},{12,16},{16,20},{20,24},{24,28},{28,0},{1,5},{5... | collective-permute-start | bytes 786440 | tf_op jit(solution)/shard_map/ppermute | solution.py:41
  105.6 10.0 %copy-start.15 = (bf16[512,256]{1,0:T(8,128)(2,1)}, bf16[512,256]{1,0:T(8,128)(2,1)S(1)}, u32[]{:S(2)}) copy-start(bf16[512,256]{1,0:T(8,128)(2,1)S(1)} %collective-permute-done.28.refs_17_) | copy-start | bytes 786436
  105.7 10.0 %collective-permute-start.29 = (bf16[256,256]{1,0:T(8,128)(2,1)S(1)}, bf16[256,256]{1,0:T(8,128)(2,1)S(1)}, u32[]{:S(2)}, u32[]{:S(2)}) collective-permute-start(bf16[256,256]{1,0:T(8,128)(2,1)S(1)} %slice.47), channel_id=1, source_target_pairs={{0,28},{4,0},{8,4},{12,8},{16,12},{20,16},{24,20},{28,24},{1,29},{... | collective-permute-start | bytes 393224 | tf_op jit(solution)/shard_map/ppermute | solution.py:41
  105.8 9.9 %copy-start.16 = (bf16[512,256]{1,0:T(8,128)(2,1)}, bf16[512,256]{1,0:T(8,128)(2,1)S(1)}, u32[]{:S(2)}) copy-start(bf16[512,256]{1,0:T(8,128)(2,1)S(1)} %collective-permute-done.24.refs_14_) | copy-start | bytes 786436
  105.8 9.9 %copy-start.2 = (s32[3]{0:T(128)S(1)}, s32[3]{0:T(128)}, u32[]{:S(2)}) copy-start(s32[3]{0:T(128)} %pad_add_fusion.ids_ref) | copy-start | bytes 40
  105.8 9.9 %copy-start.4 = (bf16[512,256]{1,0:T(8,128)(2,1)S(1)}, bf16[512,256]{1,0:T(8,128)(2,1)}, u32[]{:S(2)}) copy-start(bf16[512,256]{1,0:T(8,128)(2,1)} %get-tuple-element.8.refs_11_) | copy-start | bytes 786436
  105.8 9.9 %collective-permute-start.25 = (bf16[256,256]{1,0:T(8,128)(2,1)S(1)}, bf16[256,256]{1,0:T(8,128)(2,1)S(1)}, u32[]{:S(2)}, u32[]{:S(2)}) collective-permute-start(bf16[256,256]{1,0:T(8,128)(2,1)S(1)} %slice.46), channel_id=1, source_target_pairs={{0,4},{4,8},{8,12},{12,16},{16,20},{20,24},{24,28},{28,0},{1,5},{5... | collective-permute-start | bytes 393224 | tf_op jit(solution)/shard_map/ppermute | solution.py:41

commit v8 on v6

--- a/solution.py
+++ b/solution.py
@@ -104,6 +104,22 @@
         cost_estimate=pl.CostEstimate(flops=8 * 10**9, bytes_accessed=10 * 2**20, transcendentals=0),
         name="project_image",
     )(ids, *arrays, gain, w_kv, w_query, *tables, *after)
+
+
+def hold_kernel(x_ref, *refs):
+    refs[-1][...] = x_ref[...]
+
+
+def hold(x, after):
+    whole = pl.BlockSpec(memory_space=VMEM)
+    return pl.pallas_call(
+        hold_kernel,
+        out_shape=jax.ShapeDtypeStruct(x.shape, x.dtype),
+        in_specs=[whole] + [pl.BlockSpec(memory_space=pl.ANY)] * len(after),
+        out_specs=whole,
+        cost_estimate=pl.CostEstimate(flops=0, bytes_accessed=0, transcendentals=0),
+        name="hold",
+    )(x, *after)
 
 
 def text_kernel(ids_ref, own, one_a, one_b, three_a, three_b, two_a, two_b, two_c, *refs):
@@ -186,15 +202,18 @@
 
 
 def attention_kernel(tok, heads, ids_ref, counts_ref, starts_ref, *refs):
-    q_one, q_two, own_e, own_l, f1, f2, f3, f4, f5, b1, b2, b3, b4, b5, out_ref = refs[:15]
-    q_buf, kv_buf, img_buf, s_buf, max_buf, sum_buf, acc_buf, sems = refs[15:]
+    queries, refs = refs[:4], refs[4:]
+    own_e, own_l, f1, f2, f3, f4, f5, b1, b2, b3, b4, b5, out_ref = refs[:13]
+    q_buf, kv_buf, img_buf, s_buf, max_buf, sum_buf, acc_buf, sems = refs[13:]
     ctx, sample = ids_ref[1], ids_ref[2]
     factor = math.log2(math.e) / math.sqrt(HD)
 
     rows_e, rows_l = own_e.shape[0], own_l.shape[0]
     cut, part = rows_e // 2, rows_l // 2
-    middle = heads * HD // 2
-    moves = [(q_one, q_buf.at[:, :middle]), (q_two, q_buf.at[:, middle:])]
+    moves = []
+    for n, q_ref in enumerate(queries):
+        width = q_ref.shape[1]
+        moves.append((q_ref, q_buf.at[:, n * width : (n + 1) * width]))
     for d, array, base, first, count in (
         (0, own_e, 0, 0, rows_e),
         (1, f1, 0, 0, rows_e),
@@ -362,11 +381,10 @@
     my_slot, my_across, my_distance = source(sample)
     _, _, its_distance = source(sample ^ 1)
     quarter = tok // 4
-    one_a, three_a = first_hop(text_rows[:quarter])
-    one_b, three_b = first_hop(text_rows[quarter:])
-    values = jnp.stack([one_a[0, 0], three_a[0, 0]]).astype(jnp.int32)
-    zero = jnp.minimum(jnp.sum(jnp.abs(values)), 0)
-    leaving = jnp.where(zero == 0, visual_rows, 0)
+    group_a, group_b = text_rows[:quarter], text_rows[quarter:]
+    one_a, three_a = first_hop(group_a)
+    one_b, three_b = first_hop(group_b)
+    leaving = hold(visual_rows, (one_a, three_a))
     routed = [visual_rows] + [shift(leaving, "dp", 2 * d, False) for d in (1, 2, 3)]
     for_other = choose(its_distance, routed)
     from_other = lax.ppermute(for_other, "dp", [(i, i ^ 1) for i in range(SHARDS)])
@@ -388,7 +406,7 @@
         ids, [text_rows, one_a, one_b, three_a, three_b, two_a, two_b, two_c],
         gain, w_kv, text_tables, (own_e,)
     )
-    queries = [query(normed, w_query, text_tables, n, 2) for n in range(2)]
+    queries = [query(normed, w_query, text_tables, n, 4) for n in range(4)]
 
     cut, part = own_e.shape[0] // 2, tok // 2
     f1, b1 = shift(own_e, "ctx", 1, True), shift(own_e, "ctx", -1, True)

time: 143 us -> 145 us (1.014)
  Pallas kernels: 60.7 us -> 69.3 us
  waiting for transfers between devices: 20.2 us -> 16.5 us
  other arithmetic: 9.12 us -> 6.6 us
    pallas_call x2 -> x4, Pallas kernels: 12.6 us -> 19.8 us  [query(): pl.pallas_call(query_kernel, out_shape=jax.ShapeDtypeStruct((rows, column...]
    ppermute x13, waiting for transfers between devices: 18.6 us -> 14 us  [shift(): return lax.ppermute(x, axis, pairs)]
    reduce_sum x1 -> x0, other arithmetic: 1.95 us -> none  [on_device(): zero = jnp.minimum(jnp.sum(jnp.abs(values)), 0)]
    pallas_call x0 -> x1, Pallas kernels: none -> 1.56 us  [hold(): pl.pallas_call(hold_kernel, out_shape=jax.ShapeDtypeStruct(x.shape, x.dty...]
    slice x4 -> x2, local copies, waits for them, and re-layouts: 4.85 us -> 3.72 us  [on_device(): group_a, group_b = (text_rows[:quarter], text_rows[quarter:])]
    unnamed x45 -> x49, local copies, waits for them, and re-layouts: 3.82 us -> 4.76 us
  transfers between devices with their start and end apart: 24 -> 24, of which waited for: 5 -> 6; matrix products, arithmetic and copies ran while one was open for 10% -> 7% of each run, Pallas kernels for 19% -> 25%
where the time goes in v8:
time: 145 us
  Pallas kernels  69.3 us (48%)
  starting transfers between devices  39.2 us (27%)
  waiting for transfers between devices  16.5 us (11%)
  local copies, waits for them, and re-layouts  9.8 us (7%)
  other arithmetic  6.6 us (5%)
  between operations  3.15 us (2%)
    pallas_call x1, Pallas kernels, attention(): pl.pallas_call(functools.partial(attention_kernel, tok, heads), out_shape...  32.8 us
    ppermute x13, starting transfers between devices, shift(): return lax.ppermute(x, axis, pairs)  26.3 us
    pallas_call x4, Pallas kernels, query(): pl.pallas_call(query_kernel, out_shape=jax.ShapeDtypeStruct((rows, column...  19.8 us
    ppermute x13, waiting for transfers between devices, shift(): return lax.ppermute(x, axis, pairs)  14 us
    ppermute x10, starting transfers between devices, exchange(): return lax.ppermute(x, 'mp', [(i, i ^ mask) for i in range(4)])  12.8 us
    pallas_call x1, Pallas kernels, project_text(): pl.pallas_call(text_kernel, out_shape=[jax.ShapeDtypeStruct((rows, D), BF...  7.7 us
    pallas_call x1, Pallas kernels, project_image(): pl.pallas_call(image_kernel, out_shape=jax.ShapeDtypeStruct(((1 + steps)...  7.43 us
    unnamed x49, local copies, waits for them, and re-layouts  4.76 us
  transfers between devices with their start and end apart: 24, of which 6 were waited for; matrix products, arithmetic and copies ran while one was open for 7% of the time, Pallas kernels for 25%

profile of v8, /device:TPU:224, one launch (start us, length us, event | category | flops | bytes accessed | tf_op | source)
XLA Modules:
  0.0 144.6 jit_solution(6378929591694125237)
XLA Ops:
  0.0 1.7 %slice.24 = bf16[128,1024]{1,0:T(8,128)(2,1)} slice(bf16[512,1024]{1,0:T(8,128)(2,1)} %own.1), slice={[0:128], [0:1024]} | slice | bytes 524288 | tf_op jit(solution)/shard_map/slice | solution.py:384
  1.7 2.8 %collective-permute-start.2 = (bf16[128,1024]{1,0:T(8,128)(2,1)}, bf16[128,1024]{1,0:T(8,128)(2,1)S(1)}, u32[]{:S(2)}, u32[]{:S(2)}) collective-permute-start(bf16[128,1024]{1,0:T(8,128)(2,1)} %slice.24), channel_id=1, source_target_pairs={{0,3},{1,2},{2,1},{3,0},{4,7},{5,6},{6,5},{7,4},{8,11},{9,10},{10,... | collective-permute-start | bytes 786440 | tf_op jit(solution)/shard_map/ppermute | solution.py:45
  4.4 0.2 collective-permute-start
  4.6 2.1 %slice.25 = bf16[384,1024]{1,0:T(8,128)(2,1)} slice(bf16[512,1024]{1,0:T(8,128)(2,1)} %own.1), slice={[128:512], [0:1024]} | slice | bytes 1572864 | tf_op jit(solution)/shard_map/slice | solution.py:384
  6.7 1.1 collective-permute-start.3
  7.8 0.7 collective-permute-start.1
  8.5 1.5 %constant_dynamic-update-slice_fusion.1 = bf16[4096,256]{1,0:T(8,128)(2,1)S(1)} fusion(bf16[4096,128]{1,0:T(8,128)(2,1)} %param.14), kind=kLoop, calls=%fused_computation.9 | loop fusion | bytes 2097152
  10.0 0.0 copy-done.13
  10.1 0.2 constant_dynamic-update-slice_fusion.w_kv.refs_1_
  10.3 1.8 %multiply_sine_fusion = (f32[512,64]{1,0:T(8,128)}, f32[512,64]{1,0:T(8,128)}) fusion(f32[64]{0:T(128)S(1)} %multiply_exponential_fusion, f32[512]{0:T(512)S(1)} %add_convert_fusion), kind=kLoop, calls=%fused_computation.2 | loop fusion | flops 32768 | bytes 264448 | tf_op jit(solution)/shard_map/sin | solution.py:30
  12.2 0.0 collective-permute-done.2.refs_1_.three_a
  12.2 1.7 %collective-permute-done.refs_0_.one_a = bf16[128,1024]{1,0:T(8,128)(2,1)S(1)} collective-permute-done((bf16[128,1024]{1,0:T(8,128)(2,1)}, bf16[128,1024]{1,0:T(8,128)(2,1)S(1)}, u32[]{:S(2)}, u32[]{:S(2)}) %collective-permute-start) | collective-permute-done | bytes 262176 | tf_op jit(solution)/shard_map/ppermute | solution.py:45
  13.9 0.7 copy-done.12
  14.6 1.6 %hold.1 = bf16[64,1024]{1,0:T(8,128)(2,1)} custom-call(bf16[64,1024]{1,0:T(8,128)(2,1)} %x_ref.1, bf16[128,1024]{1,0:T(8,128)(2,1)} %copy-done.12, bf16[128,1024]{1,0:T(8,128)(2,1)} %copy-done.11), custom_call_target="tpu_custom_call" | custom-call | tf_op jit(solution)/shard_map/hold/pallas_call | solution.py:115
  16.1 3.5 %collective-permute-start.9 = (bf16[64,1024]{1,0:T(8,128)(2,1)}, bf16[64,1024]{1,0:T(8,128)(2,1)S(1)}, u32[]{:S(2)}, u32[]{:S(2)}) collective-permute-start(bf16[64,1024]{1,0:T(8,128)(2,1)} %hold.1), channel_id=1, source_target_pairs={{0,64},{32,96},{64,128},{96,160},{128,192},{160,224},{1,65},{33,97... | collective-permute-start | bytes 393224 | tf_op jit(solution)/shard_map/ppermute | solution.py:41
  19.6 4.8 %collective-permute-start.8 = (bf16[64,1024]{1,0:T(8,128)(2,1)}, bf16[64,1024]{1,0:T(8,128)(2,1)S(1)}, u32[]{:S(2)}, u32[]{:S(2)}) collective-permute-start(bf16[64,1024]{1,0:T(8,128)(2,1)} %hold.1), channel_id=1, source_target_pairs={{0,128},{32,160},{64,192},{96,224},{1,129},{33,161},{65,193},{97,2... | collective-permute-start | bytes 393224 | tf_op jit(solution)/shard_map/ppermute | solution.py:41
  24.4 1.3 collective-permute-start.7
  25.8 0.7 fusion
  28.4 0.0 collective-permute-done.9
  28.4 0.0 collective-permute-done.8
  28.4 0.2 collective-permute-done.7
  28.6 0.1 collective-permute-start.10
  28.7 0.7 select_reduce_fusion
  30.1 0.6 add_convert_fusion.1
  30.7 0.1 select_select_fusion.own
  30.8 2.0 %collective-permute-start.13 = (bf16[64,1024]{1,0:T(8,128)(2,1)S(1)}, bf16[64,1024]{1,0:T(8,128)(2,1)}, u32[]{:S(2)}, u32[]{:S(2)}) collective-permute-start(bf16[64,1024]{1,0:T(8,128)(2,1)S(1)} %select_select_fusion.own), channel_id=1, source_target_pairs={{0,2},{1,3},{2,0},{3,1},{4,6},{5,7},{6,4},{7,5},{8,10},{9,11},{10,... | collective-permute-start | bytes 393224 | tf_op jit(solution)/shard_map/ppermute | solution.py:45
  32.8 1.1 collective-permute-start.12
  34.0 0.4 collective-permute-start.11
  34.4 0.8 multiply_sine_fusion.1
  35.2 0.7 pad_add_fusion.ids_ref
  35.9 0.0 collective-permute-done.3.three_b
  35.9 1.9 %collective-permute-start.4 = (bf16[128,1024]{1,0:T(8,128)(2,1)}, bf16[128,1024]{1,0:T(8,128)(2,1)S(1)}, u32[]{:S(2)}, u32[]{:S(2)}) collective-permute-start(bf16[128,1024]{1,0:T(8,128)(2,1)} %copy-done.12), channel_id=1, source_target_pairs={{0,3},{1,2},{2,1},{3,0},{4,7},{5,6},{6,5},{7,4},{8,11},{9,10},{10,... | collective-permute-start | bytes 786440 | tf_op jit(solution)/shard_map/ppermute | solution.py:45
  37.8 1.3 collective-permute-start.6
  39.1 1.0 slice.32
  40.1 0.0 collective-permute-done.13.two
  40.1 1.2 collective-permute-start.5
  41.3 0.4 collective-permute-done.12.three
  41.7 0.0 collective-permute-done.11.one
  41.7 7.4 %project_image.1.refs_4_ = bf16[320,256]{1,0:T(8,128)(2,1)} custom-call(s32[3]{0:T(128)} %pad_add_fusion.ids_ref, bf16[64,1024]{1,0:T(8,128)(2,1)} %copy-done.19, bf16[64,1024]{1,0:T(8,128)(2,1)} %collective-permute-done.11.one, bf16[64,1024]{1,0:T(8,128)(2,1)} %collective-permute-done.12.three, bf16[64,1024]{1,0:T(8,128)(2,1)} %collective-permute-done.13.two, ...), custom_call_target="tpu_custom_call" | custom-call | flops 8000000000 | bytes 10485760 | tf_op jit(solution)/shard_map/project_image/pallas_call | solution.py:92
  49.1 0.7 collective-permute-start.19
  49.8 2.6 %collective-permute-start.14 = (bf16[320,256]{1,0:T(8,128)(2,1)}, bf16[320,256]{1,0:T(8,128)(2,1)S(1)}, u32[]{:S(2)}, u32[]{:S(2)}) collective-permute-start(bf16[320,256]{1,0:T(8,128)(2,1)} %project_image.1.refs_4_), channel_id=1, source_target_pairs={{0,4},{4,8},{8,12},{12,16},{16,20},{20,24},{24,28},{28,0},{1,5},{5... | collective-permute-start | bytes 491528 | tf_op jit(solution)/shard_map/ppermute | solution.py:41
  52.4 0.4 collective-permute-done.5.two_b
  52.8 0.2 copy-done.17
  53.1 0.5 copy-done.18
  53.5 0.8 copy-done.14
  54.3 7.7 %project_text.1 = (bf16[512,4096]{1,0:T(8,128)(2,1)}, bf16[512,256]{1,0:T(8,128)(2,1)}) custom-call(s32[3]{0:T(128)} %pad_add_fusion.ids_ref, bf16[512,1024]{1,0:T(8,128)(2,1)} %own.1, bf16[128,1024]{1,0:T(8,128)(2,1)} %copy-done.12, bf16[384,1024]{1,0:T(8,128)(2,1)} %collective-permute-done.1.one_b, bf16[128,1024]{1,0:T(8,128)(2,1)} %copy-done.11, ...), custom_call_target="tpu_custom_call" | custom-call | tf_op jit(solution)/shard_map/project_text/pallas_call | solution.py:151
  62.0 0.0 collective-permute-done.14.refs_6_
  62.0 1.1 pad_maximum_fusion.1
  63.2 0.6 collective-permute-start.20
  63.8 2.7 %collective-permute-start.15 = (bf16[832,256]{1,0:T(8,128)(2,1)S(1)}, bf16[832,256]{1,0:T(8,128)(2,1)S(1)}, u32[]{:S(2)}, u32[]{:S(2)}) collective-permute-start(bf16[832,256]{1,0:T(8,128)(2,1)S(1)} %get-tuple-element.12), channel_id=1, source_target_pairs={{0,4},{4,8},{8,12},{12,16},{16,20},{20,24},{24,28},{28,0},{1,5},{5... | collective-permute-start | bytes 1277960 | tf_op jit(solution)/shard_map/ppermute | solution.py:41
  66.5 9.8 %collective-permute-done.20.refs_12_ = bf16[832,256]{1,0:T(8,128)(2,1)S(1)} collective-permute-done((bf16[832,256]{1,0:T(8,128)(2,1)S(1)}, bf16[832,256]{1,0:T(8,128)(2,1)S(1)}, u32[]{:S(2)}, u32[]{:S(2)}) %collective-permute-start.20) | collective-permute-done | bytes 426016 | tf_op jit(solution)/shard_map/ppermute | solution.py:41
  76.3 3.2 %collective-permute-start.16 = (bf16[832,256]{1,0:T(8,128)(2,1)S(1)}, bf16[832,256]{1,0:T(8,128)(2,1)S(1)}, u32[]{:S(2)}, u32[]{:S(2)}) collective-permute-start(bf16[832,256]{1,0:T(8,128)(2,1)S(1)} %collective-permute-done.15.refs_7_), channel_id=1, source_target_pairs={{0,4},{4,8},{8,12},{12,16},{16,20},{20,24},{24,28},{28,0},{1,5},{5... | collective-permute-start | bytes 1277960 | tf_op jit(solution)/shard_map/ppermute | solution.py:41
  79.5 4.9 %query.7.refs_3_ = bf16[512,256]{1,0:T(8,128)(2,1)} custom-call(bf16[512,4096]{1,0:T(8,128)(2,1)} %get-tuple-element.7.x_ref, bf16[4096,1024]{1,0:T(8,128)(2,1)} %w_ref.7, f32[512,64]{1,0:T(8,128)} %get-tuple-element.14.refs_2_.cos, f32[512,64]{1,0:T(8,128)} %get-tuple-element.13.refs_3_.sin), custom_call_target="tpu_custom_call" | custom-call | flops 3000000000 | bytes 1048576 | tf_op jit(solution)/shard_map/query/pallas_call | solution.py:185
  84.5 4.0 %collective-permute-done.21.refs_13_ = bf16[832,256]{1,0:T(8,128)(2,1)S(1)} collective-permute-done((bf16[832,256]{1,0:T(8,128)(2,1)S(1)}, bf16[832,256]{1,0:T(8,128)(2,1)S(1)}, u32[]{:S(2)}, u32[]{:S(2)}) %collective-permute-start.21) | collective-permute-done | bytes 426016 | tf_op jit(solution)/shard_map/ppermute | solution.py:41
  88.5 0.1 collective-permute-start.22
  88.7 3.3 %collective-permute-start.17 = (bf16[672,256]{1,0:T(8,128)(2,1)S(1)}, bf16[672,256]{1,0:T(8,128)(2,1)S(1)}, u32[]{:S(2)}, u32[]{:S(2)}) collective-permute-start(bf16[672,256]{1,0:T(8,128)(2,1)S(1)} %slice.34), channel_id=1, source_target_pairs={{0,4},{4,8},{8,12},{12,16},{16,20},{20,24},{24,28},{28,0},{1,5},{5... | collective-permute-start | bytes 1032200 | tf_op jit(solution)/shard_map/ppermute | solution.py:41
  92.0 4.9 %query.6.refs_2_ = bf16[512,256]{1,0:T(8,128)(2,1)} custom-call(bf16[512,4096]{1,0:T(8,128)(2,1)} %get-tuple-element.7.x_ref, bf16[4096,1024]{1,0:T(8,128)(2,1)} %w_ref.7, f32[512,64]{1,0:T(8,128)} %get-tuple-element.14.refs_2_.cos, f32[512,64]{1,0:T(8,128)} %get-tuple-element.13.refs_3_.sin), custom_call_target="tpu_custom_call" | custom-call | flops 3000000000 | bytes 1048576 | tf_op jit(solution)/shard_map/query/pallas_call | solution.py:185
  96.9 5.0 %query.5.refs_1_ = bf16[512,256]{1,0:T(8,128)(2,1)} custom-call(bf16[512,4096]{1,0:T(8,128)(2,1)} %get-tuple-element.7.x_ref, bf16[4096,1024]{1,0:T(8,128)(2,1)} %w_ref.7, f32[512,64]{1,0:T(8,128)} %get-tuple-element.14.refs_2_.cos, f32[512,64]{1,0:T(8,128)} %get-tuple-element.13.refs_3_.sin), custom_call_target="tpu_custom_call" | custom-call | flops 3000000000 | bytes 1048576 | tf_op jit(solution)/shard_map/query/pallas_call | solution.py:185
  101.9 0.1 collective-permute-start.23
  102.1 3.5 %collective-permute-start.18 = (bf16[256,256]{1,0:T(8,128)(2,1)S(1)}, bf16[256,256]{1,0:T(8,128)(2,1)S(1)}, u32[]{:S(2)}, u32[]{:S(2)}) collective-permute-start(bf16[256,256]{1,0:T(8,128)(2,1)S(1)} %slice.35), channel_id=1, source_target_pairs={{0,4},{4,8},{8,12},{12,16},{16,20},{20,24},{24,28},{28,0},{1,5},{5... | collective-permute-start | bytes 393224 | tf_op jit(solution)/shard_map/ppermute | solution.py:41
  105.6 5.0 %query.4.refs_0_ = bf16[512,256]{1,0:T(8,128)(2,1)} custom-call(bf16[512,4096]{1,0:T(8,128)(2,1)} %get-tuple-element.7.x_ref, bf16[4096,1024]{1,0:T(8,128)(2,1)} %w_ref.7, f32[512,64]{1,0:T(8,128)} %get-tuple-element.14.refs_2_.cos, f32[512,64]{1,0:T(8,128)} %get-tuple-element.13.refs_3_.sin), custom_call_target="tpu_custom_call" | custom-call | flops 3000000000 | bytes 1048576 | tf_op jit(solution)/shard_map/query/pallas_call | solution.py:185
  110.6 0.0 copy-start.3
  110.6 0.9 copy-done.3
  111.6 32.8 %attention.1 = bf16[512,1024]{1,0:T(8,128)(2,1)} custom-call(s32[3]{0:T(128)S(1)} %copy-done.6, s32[8]{0:T(128)S(1)} %copy-done.7, s32[8,8]{1,0:T(8,128)S(1)} %copy-done.5, bf16[512,256]{1,0:T(8,128)(2,1)S(1)} %copy-done.3, bf16[512,256]{1,0:T(8,128)(2,1)S(1)} %copy-done.2, bf16[512,256]{1,0:T(8,128)(2,1)S(1)} %copy-done.1, bf16[512,256]{1,0:T(8,128)(2,1)S(1)} %copy-done, ...), custom_call_target="tpu_custom_call" | custom-call | flops 8589934592 | bytes 8388608 | tf_op jit(solution)/shard_map/attention/pallas_call | solution.py:329
  (62 shorter events, 0.3 us)
Async XLA Ops:
  1.7 10.5 %collective-permute-start.2 = (bf16[128,1024]{1,0:T(8,128)(2,1)}, bf16[128,1024]{1,0:T(8,128)(2,1)S(1)}, u32[]{:S(2)}, u32[]{:S(2)}) collective-permute-start(bf16[128,1024]{1,0:T(8,128)(2,1)} %slice.24), channel_id=1, source_target_pairs={{0,3},{1,2},{2,1},{3,0},{4,7},{5,6},{6,5},{7,4},{8,11},{9,10},{10,... | collective-permute-start | bytes 786440 | tf_op jit(solution)/shard_map/ppermute | solution.py:45
  4.4 9.4 %collective-permute-start = (bf16[128,1024]{1,0:T(8,128)(2,1)}, bf16[128,1024]{1,0:T(8,128)(2,1)S(1)}, u32[]{:S(2)}, u32[]{:S(2)}) collective-permute-start(bf16[128,1024]{1,0:T(8,128)(2,1)} %slice.24), channel_id=1, source_target_pairs={{0,1},{1,0},{2,3},{3,2},{4,5},{5,4},{6,7},{7,6},{8,9},{9,8},{10,11... | collective-permute-start | bytes 786440 | tf_op jit(solution)/shard_map/ppermute | solution.py:45
  6.7 29.2 %collective-permute-start.3 = (bf16[384,1024]{1,0:T(8,128)(2,1)}, bf16[384,1024]{1,0:T(8,128)(2,1)S(1)}, u32[]{:S(2)}, u32[]{:S(2)}) collective-permute-start(bf16[384,1024]{1,0:T(8,128)(2,1)} %slice.25), channel_id=1, source_target_pairs={{0,3},{1,2},{2,1},{3,0},{4,7},{5,6},{6,5},{7,4},{8,11},{9,10},{10,... | collective-permute-start | bytes 2359304 | tf_op jit(solution)/shard_map/ppermute | solution.py:45
  7.8 30.0 %collective-permute-start.1 = (bf16[384,1024]{1,0:T(8,128)(2,1)}, bf16[384,1024]{1,0:T(8,128)(2,1)}, u32[]{:S(2)}, u32[]{:S(2)}) collective-permute-start(bf16[384,1024]{1,0:T(8,128)(2,1)} %slice.25), channel_id=1, source_target_pairs={{0,1},{1,0},{2,3},{3,2},{4,5},{5,4},{6,7},{7,6},{8,9},{9,8},{10,11... | collective-permute-start | bytes 2359304 | tf_op jit(solution)/shard_map/ppermute | solution.py:45
  8.5 1.5 %copy-start.13 = (bf16[4096,128]{1,0:T(8,128)(2,1)S(1)}, bf16[4096,128]{1,0:T(8,128)(2,1)}, u32[]{:S(2)}) copy-start(bf16[4096,128]{1,0:T(8,128)(2,1)} %param.15) | copy-start | bytes 3145732
  10.1 15.7 %copy-start.7 = (s32[8]{0:T(128)S(1)}, s32[8]{0:T(128)}, u32[]{:S(2)}) copy-start(s32[8]{0:T(128)} %counts_ref.1) | copy-start | bytes 100
  10.1 18.5 %copy-start.10 = (bf16[64,1024]{1,0:T(8,128)(2,1)S(1)}, bf16[64,1024]{1,0:T(8,128)(2,1)}, u32[]{:S(2)}) copy-start(bf16[64,1024]{1,0:T(8,128)(2,1)} %x_ref.1) | copy-start | bytes 393220
  10.1 18.6 %copy-start.5 = (s32[8,8]{1,0:T(8,128)S(1)}, s32[8,8]{1,0:T(8,128)}, u32[]{:S(2)}) copy-start(s32[8,8]{1,0:T(8,128)} %starts_ref.1) | copy-start | bytes 772
  10.3 29.8 %copy-start.8 = (bf16[4096,256]{1,0:T(8,128)(2,1)}, bf16[4096,256]{1,0:T(8,128)(2,1)S(1)}, u32[]{:S(2)}) copy-start(bf16[4096,256]{1,0:T(8,128)(2,1)S(1)} %constant_dynamic-update-slice_fusion.w_kv.refs_1_) | copy-start | bytes 6291460
  12.2 1.7 %copy-start.11 = (bf16[128,1024]{1,0:T(8,128)(2,1)}, bf16[128,1024]{1,0:T(8,128)(2,1)S(1)}, u32[]{:S(2)}) copy-start(bf16[128,1024]{1,0:T(8,128)(2,1)S(1)} %collective-permute-done.2.refs_1_.three_a) | copy-start | bytes 786436
  13.9 0.7 copy-start.12
  16.1 12.2 %collective-permute-start.9 = (bf16[64,1024]{1,0:T(8,128)(2,1)}, bf16[64,1024]{1,0:T(8,128)(2,1)S(1)}, u32[]{:S(2)}, u32[]{:S(2)}) collective-permute-start(bf16[64,1024]{1,0:T(8,128)(2,1)} %hold.1), channel_id=1, source_target_pairs={{0,64},{32,96},{64,128},{96,160},{128,192},{160,224},{1,65},{33,97... | collective-permute-start | bytes 393224 | tf_op jit(solution)/shard_map/ppermute | solution.py:41
  19.6 8.8 %collective-permute-start.8 = (bf16[64,1024]{1,0:T(8,128)(2,1)}, bf16[64,1024]{1,0:T(8,128)(2,1)S(1)}, u32[]{:S(2)}, u32[]{:S(2)}) collective-permute-start(bf16[64,1024]{1,0:T(8,128)(2,1)} %hold.1), channel_id=1, source_target_pairs={{0,128},{32,160},{64,192},{96,224},{1,129},{33,161},{65,193},{97,2... | collective-permute-start | bytes 393224 | tf_op jit(solution)/shard_map/ppermute | solution.py:41
  24.4 4.1 %collective-permute-start.7 = (bf16[64,1024]{1,0:T(8,128)(2,1)}, bf16[64,1024]{1,0:T(8,128)(2,1)S(1)}, u32[]{:S(2)}, u32[]{:S(2)}) collective-permute-start(bf16[64,1024]{1,0:T(8,128)(2,1)} %hold.1), channel_id=1, source_target_pairs={{0,192},{32,224},{1,193},{33,225},{2,194},{34,226},{3,195},{35,227... | collective-permute-start | bytes 393224 | tf_op jit(solution)/shard_map/ppermute | solution.py:41
  28.6 2.1 %collective-permute-start.10 = (bf16[64,1024]{1,0:T(8,128)(2,1)S(1)}, bf16[64,1024]{1,0:T(8,128)(2,1)}, u32[]{:S(2)}, u32[]{:S(2)}) collective-permute-start(bf16[64,1024]{1,0:T(8,128)(2,1)S(1)} %select_select_fusion.1), channel_id=1, source_target_pairs={{0,32},{32,0},{64,96},{96,64},{128,160},{160,128},{192,224},{224,1... | collective-permute-start | bytes 393224 | tf_op jit(solution)/shard_map/ppermute | solution.py:390
  30.8 10.9 %copy-start.19 = (bf16[64,1024]{1,0:T(8,128)(2,1)}, bf16[64,1024]{1,0:T(8,128)(2,1)S(1)}, u32[]{:S(2)}) copy-start(bf16[64,1024]{1,0:T(8,128)(2,1)S(1)} %select_select_fusion.own) | copy-start | bytes 393220
  30.8 9.3 %collective-permute-start.13 = (bf16[64,1024]{1,0:T(8,128)(2,1)S(1)}, bf16[64,1024]{1,0:T(8,128)(2,1)}, u32[]{:S(2)}, u32[]{:S(2)}) collective-permute-start(bf16[64,1024]{1,0:T(8,128)(2,1)S(1)} %select_select_fusion.own), channel_id=1, source_target_pairs={{0,2},{1,3},{2,0},{3,1},{4,6},{5,7},{6,4},{7,5},{8,10},{9,11},{10,... | collective-permute-start | bytes 393224 | tf_op jit(solution)/shard_map/ppermute | solution.py:45
  32.8 8.8 %collective-permute-start.12 = (bf16[64,1024]{1,0:T(8,128)(2,1)S(1)}, bf16[64,1024]{1,0:T(8,128)(2,1)}, u32[]{:S(2)}, u32[]{:S(2)}) collective-permute-start(bf16[64,1024]{1,0:T(8,128)(2,1)S(1)} %select_select_fusion.own), channel_id=1, source_target_pairs={{0,3},{1,2},{2,1},{3,0},{4,7},{5,6},{6,5},{7,4},{8,11},{9,10},{10,... | collective-permute-start | bytes 393224 | tf_op jit(solution)/shard_map/ppermute | solution.py:45
  34.0 7.7 %collective-permute-start.11 = (bf16[64,1024]{1,0:T(8,128)(2,1)S(1)}, bf16[64,1024]{1,0:T(8,128)(2,1)}, u32[]{:S(2)}, u32[]{:S(2)}) collective-permute-start(bf16[64,1024]{1,0:T(8,128)(2,1)S(1)} %select_select_fusion.own), channel_id=1, source_target_pairs={{0,1},{1,0},{2,3},{3,2},{4,5},{5,4},{6,7},{7,6},{8,9},{9,8},{10,11... | collective-permute-start | bytes 393224 | tf_op jit(solution)/shard_map/ppermute | solution.py:45
  35.9 13.2 %copy-start.9 = (bf16[384,1024]{1,0:T(8,128)(2,1)}, bf16[384,1024]{1,0:T(8,128)(2,1)S(1)}, u32[]{:S(2)}) copy-start(bf16[384,1024]{1,0:T(8,128)(2,1)S(1)} %collective-permute-done.3.three_b) | copy-start | bytes 2359300
  35.9 16.5 %collective-permute-start.4 = (bf16[128,1024]{1,0:T(8,128)(2,1)}, bf16[128,1024]{1,0:T(8,128)(2,1)S(1)}, u32[]{:S(2)}, u32[]{:S(2)}) collective-permute-start(bf16[128,1024]{1,0:T(8,128)(2,1)} %copy-done.12), channel_id=1, source_target_pairs={{0,3},{1,2},{2,1},{3,0},{4,7},{5,6},{6,5},{7,4},{8,11},{9,10},{10,... | collective-permute-start | bytes 786440 | tf_op jit(solution)/shard_map/ppermute | solution.py:45
  37.8 15.0 %collective-permute-start.6 = (bf16[256,1024]{1,0:T(8,128)(2,1)S(1)}, bf16[256,1024]{1,0:T(8,128)(2,1)S(1)}, u32[]{:S(2)}, u32[]{:S(2)}) collective-permute-start(bf16[256,1024]{1,0:T(8,128)(2,1)S(1)} %slice.33), channel_id=1, source_target_pairs={{0,1},{1,0},{2,3},{3,2},{4,5},{5,4},{6,7},{7,6},{8,9},{9,8},{10,11... | collective-permute-start | bytes 1572872 | tf_op jit(solution)/shard_map/ppermute | solution.py:45
  40.1 12.7 %collective-permute-start.5 = (bf16[128,1024]{1,0:T(8,128)(2,1)S(1)}, bf16[128,1024]{1,0:T(8,128)(2,1)S(1)}, u32[]{:S(2)}, u32[]{:S(2)}) collective-permute-start(bf16[128,1024]{1,0:T(8,128)(2,1)S(1)} %slice.32), channel_id=1, source_target_pairs={{0,3},{1,2},{2,1},{3,0},{4,7},{5,6},{6,5},{7,4},{8,11},{9,10},{10,... | collective-permute-start | bytes 786440 | tf_op jit(solution)/shard_map/ppermute | solution.py:45
  49.1 12.9 %collective-permute-start.19 = (bf16[320,256]{1,0:T(8,128)(2,1)}, bf16[320,256]{1,0:T(8,128)(2,1)S(1)}, u32[]{:S(2)}, u32[]{:S(2)}) collective-permute-start(bf16[320,256]{1,0:T(8,128)(2,1)} %project_image.1.refs_4_), channel_id=1, source_target_pairs={{0,28},{4,0},{8,4},{12,8},{16,12},{20,16},{24,20},{28,24},{1,29},{... | collective-permute-start | bytes 491528 | tf_op jit(solution)/shard_map/ppermute | solution.py:41
  49.8 12.2 %collective-permute-start.14 = (bf16[320,256]{1,0:T(8,128)(2,1)}, bf16[320,256]{1,0:T(8,128)(2,1)S(1)}, u32[]{:S(2)}, u32[]{:S(2)}) collective-permute-start(bf16[320,256]{1,0:T(8,128)(2,1)} %project_image.1.refs_4_), channel_id=1, source_target_pairs={{0,4},{4,8},{8,12},{12,16},{16,20},{20,24},{24,28},{28,0},{1,5},{5... | collective-permute-start | bytes 491528 | tf_op jit(solution)/shard_map/ppermute | solution.py:41
  52.4 0.7 copy-start.17
  52.8 0.7 copy-start.18
  53.5 0.8 copy-start.14
  63.2 13.1 %collective-permute-start.20 = (bf16[832,256]{1,0:T(8,128)(2,1)S(1)}, bf16[832,256]{1,0:T(8,128)(2,1)S(1)}, u32[]{:S(2)}, u32[]{:S(2)}) collective-permute-start(bf16[832,256]{1,0:T(8,128)(2,1)S(1)} %get-tuple-element.11), channel_id=1, source_target_pairs={{0,28},{4,0},{8,4},{12,8},{16,12},{20,16},{24,20},{28,24},{1,29},{... | collective-permute-start | bytes 1277960 | tf_op jit(solution)/shard_map/ppermute | solution.py:41
  63.8 12.5 %collective-permute-start.15 = (bf16[832,256]{1,0:T(8,128)(2,1)S(1)}, bf16[832,256]{1,0:T(8,128)(2,1)S(1)}, u32[]{:S(2)}, u32[]{:S(2)}) collective-permute-start(bf16[832,256]{1,0:T(8,128)(2,1)S(1)} %get-tuple-element.12), channel_id=1, source_target_pairs={{0,4},{4,8},{8,12},{12,16},{16,20},{20,24},{24,28},{28,0},{1,5},{5... | collective-permute-start | bytes 1277960 | tf_op jit(solution)/shard_map/ppermute | solution.py:41
  76.3 8.2 %copy-start.22 = (bf16[832,256]{1,0:T(8,128)(2,1)}, bf16[832,256]{1,0:T(8,128)(2,1)S(1)}, u32[]{:S(2)}) copy-start(bf16[832,256]{1,0:T(8,128)(2,1)S(1)} %collective-permute-done.20.refs_12_) | copy-start | bytes 1277956
  76.3 12.2 %collective-permute-start.21 = (bf16[832,256]{1,0:T(8,128)(2,1)S(1)}, bf16[832,256]{1,0:T(8,128)(2,1)S(1)}, u32[]{:S(2)}, u32[]{:S(2)}) collective-permute-start(bf16[832,256]{1,0:T(8,128)(2,1)S(1)} %collective-permute-done.20.refs_12_), channel_id=1, source_target_pairs={{0,28},{4,0},{8,4},{12,8},{16,12},{20,16},{24,20},{28,24},{1,29},{... | collective-permute-start | bytes 1277960 | tf_op jit(solution)/shard_map/ppermute | solution.py:41
  76.3 8.2 %copy-start.23 = (bf16[832,256]{1,0:T(8,128)(2,1)}, bf16[832,256]{1,0:T(8,128)(2,1)S(1)}, u32[]{:S(2)}) copy-start(bf16[832,256]{1,0:T(8,128)(2,1)S(1)} %collective-permute-done.15.refs_7_) | copy-start | bytes 1277956
  76.3 12.3 %collective-permute-start.16 = (bf16[832,256]{1,0:T(8,128)(2,1)S(1)}, bf16[832,256]{1,0:T(8,128)(2,1)S(1)}, u32[]{:S(2)}, u32[]{:S(2)}) collective-permute-start(bf16[832,256]{1,0:T(8,128)(2,1)S(1)} %collective-permute-done.15.refs_7_), channel_id=1, source_target_pairs={{0,4},{4,8},{8,12},{12,16},{16,20},{20,24},{24,28},{28,0},{1,5},{5... | collective-permute-start | bytes 1277960 | tf_op jit(solution)/shard_map/ppermute | solution.py:41
  88.5 8.4 %copy-start.15 = (bf16[832,256]{1,0:T(8,128)(2,1)}, bf16[832,256]{1,0:T(8,128)(2,1)S(1)}, u32[]{:S(2)}) copy-start(bf16[832,256]{1,0:T(8,128)(2,1)S(1)} %collective-permute-done.21.refs_13_) | copy-start | bytes 1277956
  88.5 13.3 %collective-permute-start.22 = (bf16[672,256]{1,0:T(8,128)(2,1)S(1)}, bf16[672,256]{1,0:T(8,128)(2,1)S(1)}, u32[]{:S(2)}, u32[]{:S(2)}) collective-permute-start(bf16[672,256]{1,0:T(8,128)(2,1)S(1)} %slice.36), channel_id=1, source_target_pairs={{0,28},{4,0},{8,4},{12,8},{16,12},{20,16},{24,20},{28,24},{1,29},{... | collective-permute-start | bytes 1032200 | tf_op jit(solution)/shard_map/ppermute | solution.py:41
  88.6 8.3 %copy-start.16 = (bf16[832,256]{1,0:T(8,128)(2,1)}, bf16[832,256]{1,0:T(8,128)(2,1)S(1)}, u32[]{:S(2)}) copy-start(bf16[832,256]{1,0:T(8,128)(2,1)S(1)} %collective-permute-done.16.refs_8_) | copy-start | bytes 1277956
  88.7 13.3 %collective-permute-start.17 = (bf16[672,256]{1,0:T(8,128)(2,1)S(1)}, bf16[672,256]{1,0:T(8,128)(2,1)S(1)}, u32[]{:S(2)}, u32[]{:S(2)}) collective-permute-start(bf16[672,256]{1,0:T(8,128)(2,1)S(1)} %slice.34), channel_id=1, source_target_pairs={{0,4},{4,8},{8,12},{12,16},{16,20},{20,24},{24,28},{28,0},{1,5},{5... | collective-permute-start | bytes 1032200 | tf_op jit(solution)/shard_map/ppermute | solution.py:41
  101.9 8.7 %copy-start.20 = (bf16[672,256]{1,0:T(8,128)(2,1)}, bf16[672,256]{1,0:T(8,128)(2,1)S(1)}, u32[]{:S(2)}) copy-start(bf16[672,256]{1,0:T(8,128)(2,1)S(1)} %collective-permute-done.22.refs_14_) | copy-start | bytes 1032196
  101.9 8.7 %collective-permute-start.23 = (bf16[256,256]{1,0:T(8,128)(2,1)S(1)}, bf16[256,256]{1,0:T(8,128)(2,1)S(1)}, u32[]{:S(2)}, u32[]{:S(2)}) collective-permute-start(bf16[256,256]{1,0:T(8,128)(2,1)S(1)} %slice.37), channel_id=1, source_target_pairs={{0,28},{4,0},{8,4},{12,8},{16,12},{20,16},{24,20},{28,24},{1,29},{... | collective-permute-start | bytes 393224 | tf_op jit(solution)/shard_map/ppermute | solution.py:41
  102.0 8.6 %copy-start.21 = (bf16[672,256]{1,0:T(8,128)(2,1)}, bf16[672,256]{1,0:T(8,128)(2,1)S(1)}, u32[]{:S(2)}) copy-start(bf16[672,256]{1,0:T(8,128)(2,1)S(1)} %collective-permute-done.17.refs_9_) | copy-start | bytes 1032196
  102.0 8.5 %copy-start = (bf16[512,256]{1,0:T(8,128)(2,1)S(1)}, bf16[512,256]{1,0:T(8,128)(2,1)}, u32[]{:S(2)}) copy-start(bf16[512,256]{1,0:T(8,128)(2,1)} %query.7.refs_3_) | copy-start | bytes 786436
  102.0 8.5 %copy-start.1 = (bf16[512,256]{1,0:T(8,128)(2,1)S(1)}, bf16[512,256]{1,0:T(8,128)(2,1)}, u32[]{:S(2)}) copy-start(bf16[512,256]{1,0:T(8,128)(2,1)} %query.6.refs_2_) | copy-start | bytes 786436
  102.0 8.5 %copy-start.2 = (bf16[512,256]{1,0:T(8,128)(2,1)S(1)}, bf16[512,256]{1,0:T(8,128)(2,1)}, u32[]{:S(2)}) copy-start(bf16[512,256]{1,0:T(8,128)(2,1)} %query.5.refs_1_) | copy-start | bytes 786436
  102.0 8.5 %copy-start.4 = (bf16[320,256]{1,0:T(8,128)(2,1)S(1)}, bf16[320,256]{1,0:T(8,128)(2,1)}, u32[]{:S(2)}) copy-start(bf16[320,256]{1,0:T(8,128)(2,1)} %project_image.1.refs_4_) | copy-start | bytes 491524
  102.0 8.5 %copy-start.6 = (s32[3]{0:T(128)S(1)}, s32[3]{0:T(128)}, u32[]{:S(2)}) copy-start(s32[3]{0:T(128)} %pad_add_fusion.ids_ref) | copy-start | bytes 40
  102.1 8.5 %collective-permute-start.18 = (bf16[256,256]{1,0:T(8,128)(2,1)S(1)}, bf16[256,256]{1,0:T(8,128)(2,1)S(1)}, u32[]{:S(2)}, u32[]{:S(2)}) collective-permute-start(bf16[256,256]{1,0:T(8,128)(2,1)S(1)} %slice.35), channel_id=1, source_target_pairs={{0,4},{4,8},{8,12},{12,16},{16,20},{20,24},{24,28},{28,0},{1,5},{5... | collective-permute-start | bytes 393224 | tf_op jit(solution)/shard_map/ppermute | solution.py:41
  110.6 1.0 copy-start.3

commit v9 on v8

--- a/solution.py
+++ b/solution.py
@@ -13,7 +13,7 @@
 MAX_IMG = 8
 D = 4096
 SHARDS = 8
-BLOCK = 2048
+BLOCK = 1792
 rope_base = 500000.0
 eps = 1e-05
 BF16 = jnp.bfloat16
@@ -189,7 +189,7 @@
         in_specs=[whole, pl.BlockSpec((D, tile), lambda n: (0, first + n))] + [whole] * 2,
         out_specs=pl.BlockSpec((rows, tile), lambda n: (0, n)),
         compiler_params=pltpu.CompilerParams(vmem_limit_bytes=58 * 2**20),
-        cost_estimate=pl.CostEstimate(flops=3 * 10**9, bytes_accessed=2**20, transcendentals=0),
+        cost_estimate=pl.CostEstimate(flops=6 * 10**9, bytes_accessed=2**20, transcendentals=0),
         name="query",
     )(normed, w_query, *tables)
 
@@ -201,19 +201,26 @@
     return total
 
 
+def image_starts_of(ids_ref, counts_ref, starts_ref):
+    sample = ids_ref[2]
+    before = images_before(counts_ref, sample)
+    for c in range(SHARDS):
+        slot = (c - before) & (MAX_IMG - 1)
+        yield c, jnp.where(slot < counts_ref[sample], starts_ref[sample, slot], -1)
+
+
 def attention_kernel(tok, heads, ids_ref, counts_ref, starts_ref, *refs):
-    queries, refs = refs[:4], refs[4:]
-    own_e, own_l, f1, f2, f3, f4, f5, b1, b2, b3, b4, b5, out_ref = refs[:13]
-    q_buf, kv_buf, img_buf, s_buf, max_buf, sum_buf, acc_buf, sems = refs[13:]
-    ctx, sample = ids_ref[1], ids_ref[2]
+    q_one, q_two, own_e, own_l, f1, f2, f3, f4, b1, b2, b3, b4 = refs[:12]
+    q_buf, img_kv, acc_out, max_out, sum_out = refs[12:17]
+    kv_buf, img_buf, s_buf, max_buf, sum_buf, acc_buf, sems = refs[17:]
+    ctx = ids_ref[1]
     factor = math.log2(math.e) / math.sqrt(HD)
-
+    shift_by = tok.bit_length() - 1
     rows_e, rows_l = own_e.shape[0], own_l.shape[0]
-    cut, part = rows_e // 2, rows_l // 2
-    moves = []
-    for n, q_ref in enumerate(queries):
-        width = q_ref.shape[1]
-        moves.append((q_ref, q_buf.at[:, n * width : (n + 1) * width]))
+    cut = rows_e // 2
+
+    middle = heads * HD // 2
+    moves = [(q_one, q_buf.at[:, :middle]), (q_two, q_buf.at[:, middle:])]
     for d, array, base, first, count in (
         (0, own_e, 0, 0, rows_e),
         (1, f1, 0, 0, rows_e),
@@ -226,23 +233,10 @@
         (7, b1, 0, 0, rows_e),
     ):
         shard = (ctx - d) & (SHARDS - 1)
-        moves.append(
-            (array.at[pl.ds(base, count), :], img_buf.at[shard, pl.ds(first, count), :])
-        )
-    for d, array, base, first, count in (
-        (0, own_l, 0, 0, rows_l),
-        (1, f2, rows_e, 0, rows_l),
-        (2, f3, rows_e, 0, rows_l),
-        (3, f4, cut, 0, rows_l),
-        (4, f5, 0, 0, part),
-        (4, b5, 0, part, part),
-        (5, b4, 0, 0, rows_l),
-        (6, b3, 0, 0, rows_l),
-        (7, b2, 0, 0, rows_l),
-    ):
-        shard = (ctx - d) & (SHARDS - 1)
-        place = pl.ds(pl.multiple_of(shard * tok + first, part), count)
-        moves.append((array.at[pl.ds(base, count), :], kv_buf.at[place, :]))
+        moves.append((array.at[pl.ds(base, count), :], img_buf.at[shard, pl.ds(first, count), :]))
+    texts = ((own_l, 0), (f2, rows_e), (f3, rows_e), (f4, cut), (b4, 0), (b3, 0), (b2, 0))
+    for n, (array, base) in enumerate(texts):
+        moves.append((array.at[pl.ds(base, rows_l), :], kv_buf.at[pl.ds(n * tok, tok), :]))
     copies = [
         pltpu.make_async_copy(source, target, sems.at[n])
         for n, (source, target) in enumerate(moves)
@@ -251,23 +245,26 @@
         copy.start()
     for copy in copies:
         copy.wait()
-    before = images_before(counts_ref, sample)
-    for c in range(SHARDS):
-        slot = (c - before) & (MAX_IMG - 1)
-        start = jnp.where(slot < counts_ref[sample], starts_ref[sample, slot], -1)
-
-        @pl.when(start >= 0)
+    for c, start in image_starts_of(ids_ref, counts_ref, starts_ref):
+        img_kv[c] = img_buf[c, :IMG_TOK, :]
+        shard, row = start >> shift_by, start & (tok - 1)
+        distance = ctx - shard
+
+        @pl.when((start >= 0) & (distance >= 0) & (distance != 4))
         def _():
-            rows = pl.ds(pl.multiple_of(start, IMG_TOK), IMG_TOK)
-            kv_buf[rows, :] = img_buf[c, :IMG_TOK, :]
-
-        @pl.when((start >= ctx * tok) & (start < ctx * tok + tok))
+            place = jnp.where(distance > 4, distance - 1, distance) * tok + row
+            kv_buf[pl.ds(pl.multiple_of(place, IMG_TOK), IMG_TOK), :] = img_buf[c, :IMG_TOK, :]
+
+        @pl.when((start >= 0) & (distance == 0))
         def _():
-            rows = pl.ds(pl.multiple_of(start - ctx * tok, IMG_TOK), IMG_TOK)
+            rows = pl.ds(pl.multiple_of(row, IMG_TOK), IMG_TOK)
             for n in range(heads // 2):
                 q_buf[rows, n * 2 * HD : (n + 1) * 2 * HD] = img_buf[
                     c, IMG_TOK * (n + 1) : IMG_TOK * (n + 2), :
                 ]
+
+    max_out[...] = jnp.zeros((tok, HD), F32)
+    sum_out[...] = jnp.zeros((tok, HD), F32)
 
     def phase(step, do_score, do_mix):
         slot = lax.rem(step, 2)
@@ -283,12 +280,16 @@
                     (((1,), (1,)), ((), ())),
                     preferred_element_type=F32,
                 )
-                row = lax.broadcasted_iota(jnp.int32, (tok, HD), 0) + (ctx * tok - j * BLOCK)
+                row = lax.broadcasted_iota(jnp.int32, (tok, HD), 0)
                 column = lax.broadcasted_iota(jnp.int32, (tok, HD), 1)
                 top = max_buf[slot]
                 for g in range(BLOCK // HD):
+                    place = j * BLOCK + g * HD
+                    nth = place >> shift_by
+                    earlier = nth + jnp.where(nth > 3, 1, 0) <= ctx
+                    ahead = jnp.where(nth == 0, place, jnp.where(earlier, -tok, tok))
                     seen = s[:, g * HD : (g + 1) * HD]
-                    seen = jnp.where(column + g * HD <= row, seen, -1e30)
+                    seen = jnp.where(column + ahead <= row, seen, -1e30)
                     s_buf[slot, j, :, g * HD : (g + 1) * HD] = seen
                     top = jnp.maximum(top, seen)
                 max_buf[slot] = top
@@ -310,14 +311,17 @@
         if do_mix:
             sum_buf[...] = jnp.zeros((tok, HD), F32)
             acc_buf[...] = jnp.zeros((tok, HD), F32)
-        pl.loop(0, (ctx * tok + tok + BLOCK - 1) // BLOCK)(block)
+        pl.loop(0, jnp.where(ctx * tok + tok > BLOCK, 2, 1))(block)
         if do_score:
             top = jnp.max(max_buf[slot], axis=1, keepdims=True) * factor
             max_buf[slot] = jnp.broadcast_to(top, (tok, HD))
         if do_mix:
+            head = step - 1
+            here = lax.broadcasted_iota(jnp.int32, (tok, HD), 1) == head
+            max_out[...] = jnp.where(here, max_buf[other], max_out[...])
             total = jnp.sum(sum_buf[...], axis=1, keepdims=True)
-            columns = pl.ds(pl.multiple_of((step - 1) * HD, HD), HD)
-            out_ref[:, columns] = (acc_buf[...] / total).astype(BF16)
+            sum_out[...] = jnp.where(here, total, sum_out[...])
+            acc_out[:, pl.ds(pl.multiple_of(head * HD, HD), HD)] = acc_buf[...]
 
     phase(jnp.int32(0), True, False)
     pl.loop(1, heads)(lambda step: phase(step, True, True))
@@ -326,17 +330,23 @@
 
 def attention(tok, heads, scalars, arrays):
     img_rows = IMG_TOK * (1 + heads // 2)
+    keys = (SHARDS - 1) * tok
     return pl.pallas_call(
         functools.partial(attention_kernel, tok, heads),
-        out_shape=jax.ShapeDtypeStruct((tok, heads * HD), BF16),
+        out_shape=[
+            jax.ShapeDtypeStruct((tok, heads * HD), BF16),
+            jax.ShapeDtypeStruct((SHARDS, IMG_TOK, 2 * HD), BF16),
+            jax.ShapeDtypeStruct((tok, heads * HD), F32),
+            jax.ShapeDtypeStruct((tok, HD), F32),
+            jax.ShapeDtypeStruct((tok, HD), F32),
+        ],
         in_specs=[pl.BlockSpec(memory_space=SMEM)] * 3
         + [pl.BlockSpec(memory_space=pl.ANY)] * len(arrays),
-        out_specs=pl.BlockSpec(memory_space=VMEM),
+        out_specs=[pl.BlockSpec(memory_space=VMEM)] * 5,
         scratch_shapes=[
-            pltpu.VMEM((tok, heads * HD), BF16),
-            pltpu.VMEM((SHARDS * tok, 2 * HD), BF16),
+            pltpu.VMEM((keys, 2 * HD), BF16),
             pltpu.VMEM((SHARDS, img_rows, 2 * HD), BF16),
-            pltpu.VMEM((2, SHARDS * tok // BLOCK, tok, BLOCK), F32),
+            pltpu.VMEM((2, keys // BLOCK, tok, BLOCK), F32),
             pltpu.VMEM((2, tok, HD), F32),
             pltpu.VMEM((tok, HD), F32),
             pltpu.VMEM((tok, HD), F32),
@@ -344,12 +354,81 @@
         ],
         compiler_params=pltpu.CompilerParams(vmem_limit_bytes=52 * 2**20),
         cost_estimate=pl.CostEstimate(
-            flops=4 * tok * heads * SHARDS * tok * HD,
+            flops=4 * tok * heads * keys * HD,
             bytes_accessed=8 * 2**20,
-            transcendentals=tok * heads * SHARDS * tok,
+            transcendentals=tok * heads * keys,
         ),
         name="attention",
     )(*scalars, *arrays)
+
+
+def finish_kernel(tok, ids_ref, counts_ref, starts_ref, *refs):
+    q_ref, img_kv, lower, upper, acc_ref, max_ref, sum_ref, out_ref, kv_buf = refs
+    ctx = ids_ref[1]
+    step = pl.program_id(0)
+    factor = math.log2(math.e) / math.sqrt(HD)
+    shift_by = tok.bit_length() - 1
+
+    @pl.when(step == 0)
+    def _():
+        half = lower.shape[0]
+        kv_buf[:half, :] = lower[...]
+        kv_buf[half:, :] = upper[...]
+        for c, start in image_starts_of(ids_ref, counts_ref, starts_ref):
+            @pl.when((start >= 0) & (ctx - (start >> shift_by) == 4))
+            def _():
+                rows = pl.ds(pl.multiple_of(start & (tok - 1), IMG_TOK), IMG_TOK)
+                kv_buf[rows, :] = img_kv[c]
+
+    def of_head(ref, head):
+        here = lax.broadcasted_iota(jnp.int32, (tok, HD), 1) == head
+        return jnp.sum(jnp.where(here, ref[...], 0.0), axis=1, keepdims=True)
+
+    count = out_ref.shape[1] // HD
+
+    @pl.when(ctx >= 4)
+    def _():
+        for n in range(count):
+            span = slice(n * HD, (n + 1) * HD)
+            s = lax.dot_general(
+                q_ref[:, span],
+                kv_buf[:, :HD],
+                (((1,), (1,)), ((), ())),
+                preferred_element_type=F32,
+            )
+            before = of_head(max_ref, step * count + n)
+            top = jnp.maximum(before, jnp.max(s, axis=1, keepdims=True) * factor)
+            scale = jnp.exp2(before - top)
+            w = jnp.exp2(s * factor - top)
+            total = of_head(sum_ref, step * count + n) * scale + jnp.sum(w, axis=1, keepdims=True)
+            mixed = jnp.dot(w.astype(BF16), kv_buf[:, HD:], preferred_element_type=F32)
+            out_ref[:, span] = ((acc_ref[:, span] * scale + mixed) / total).astype(BF16)
+
+    @pl.when(ctx < 4)
+    def _():
+        for n in range(count):
+            span = slice(n * HD, (n + 1) * HD)
+            total = of_head(sum_ref, step * count + n)
+            out_ref[:, span] = (acc_ref[:, span] / total).astype(BF16)
+
+
+def finish(tok, heads, scalars, q_all, img_kv, lower, upper, state):
+    width = 2 * HD
+    whole = pl.BlockSpec(memory_space=VMEM)
+    block = pl.BlockSpec((tok, width), lambda n: (0, n))
+    return pl.pallas_call(
+        functools.partial(finish_kernel, tok),
+        out_shape=jax.ShapeDtypeStruct((tok, heads * HD), BF16),
+        grid=(heads * HD // width,),
+        in_specs=[pl.BlockSpec(memory_space=SMEM)] * 3 + [block] + [whole] * 3 + [block] + [whole] * 2,
+        out_specs=block,
+        scratch_shapes=[pltpu.VMEM((tok, 2 * HD), BF16)],
+        compiler_params=pltpu.CompilerParams(vmem_limit_bytes=40 * 2**20),
+        cost_estimate=pl.CostEstimate(
+            flops=4 * tok * heads * tok * HD, bytes_accessed=6 * 2**20, transcendentals=0
+        ),
+        name="finish",
+    )(*scalars, q_all, img_kv, lower, upper, *state)
 
 
 def on_device(
@@ -406,7 +485,7 @@
         ids, [text_rows, one_a, one_b, three_a, three_b, two_a, two_b, two_c],
         gain, w_kv, text_tables, (own_e,)
     )
-    queries = [query(normed, w_query, text_tables, n, 4) for n in range(4)]
+    queries = [query(normed, w_query, text_tables, n, 2) for n in range(2)]
 
     cut, part = own_e.shape[0] // 2, tok // 2
     f1, b1 = shift(own_e, "ctx", 1, True), shift(own_e, "ctx", -1, True)
@@ -416,10 +495,11 @@
     f4, b4 = shift(f3[cut:], "ctx", 1, True), shift(b3[: tok + cut], "ctx", -1, True)
     f5 = shift(f4[cut : cut + part], "ctx", 1, True)
     b5 = shift(b4[part:tok], "ctx", -1, True)
-    return attention(
-        tok, heads, (ids, image_counts, image_starts),
-        [*queries, own_e, own_l, f1, f2, f3, f4, f5, b1, b2, b3, b4, b5],
+    scalars = (ids, image_counts, image_starts)
+    q_all, img_kv, *state = attention(
+        tok, heads, scalars, [*queries, own_e, own_l, f1, f2, f3, f4, b1, b2, b3, b4]
     )
+    return finish(tok, heads, scalars, q_all, img_kv, f5, b5, state)
 
 
 def solution(mesh):

time: 145 us -> 143 us (0.986)
  Pallas kernels: 69.3 us -> 67.3 us
  local copies, waits for them, and re-layouts: 9.8 us -> 11.7 us
    pallas_call x4 -> x2, Pallas kernels: 19.8 us -> 12.7 us  [query(): pl.pallas_call(query_kernel, out_shape=jax.ShapeDtypeStruct((rows, column...]
    pallas_call x0 -> x1, Pallas kernels: none -> 5.94 us  [finish(): pl.pallas_call(functools.partial(finish_kernel, tok), out_shape=jax.Shape...]
    unnamed x49 -> x45, local copies, waits for them, and re-layouts: 4.76 us -> 6.62 us
  transfers between devices with their start and end apart: 24 -> 24, of which waited for: 6 -> 6; matrix products, arithmetic and copies ran while one was open for 7% -> 7% of each run, Pallas kernels for 25% -> 43%
where the time goes in v9:
time: 143 us
  Pallas kernels  67.3 us (47%)
  starting transfers between devices  38.9 us (27%)
  waiting for transfers between devices  15.2 us (11%)
  local copies, waits for them, and re-layouts  11.7 us (8%)
  other arithmetic  6.54 us (5%)
  between operations  2.9 us (2%)
    pallas_call x1, Pallas kernels, attention(): pl.pallas_call(functools.partial(attention_kernel, tok, heads), out_shape...  32 us
    ppermute x13, starting transfers between devices, shift(): return lax.ppermute(x, axis, pairs)  26.1 us
    ppermute x10, starting transfers between devices, exchange(): return lax.ppermute(x, 'mp', [(i, i ^ mask) for i in range(4)])  12.8 us
    pallas_call x2, Pallas kernels, query(): pl.pallas_call(query_kernel, out_shape=jax.ShapeDtypeStruct((rows, column...  12.7 us
    ppermute x13, waiting for transfers between devices, shift(): return lax.ppermute(x, axis, pairs)  12.6 us
    pallas_call x1, Pallas kernels, project_text(): pl.pallas_call(text_kernel, out_shape=[jax.ShapeDtypeStruct((rows, D), BF...  7.7 us
    pallas_call x1, Pallas kernels, project_image(): pl.pallas_call(image_kernel, out_shape=jax.ShapeDtypeStruct(((1 + steps)...  7.44 us
    unnamed x45, local copies, waits for them, and re-layouts  6.62 us
  transfers between devices with their start and end apart: 24, of which 6 were waited for; matrix products, arithmetic and copies ran while one was open for 7% of the time, Pallas kernels for 43%

profile of v9, /device:TPU:224, one launch (start us, length us, event | category | flops | bytes accessed | tf_op | source)
XLA Modules:
  0.0 142.5 jit_solution(118231791322832773)
XLA Ops:
  0.0 1.7 %slice.24 = bf16[128,1024]{1,0:T(8,128)(2,1)} slice(bf16[512,1024]{1,0:T(8,128)(2,1)} %own.1), slice={[0:128], [0:1024]} | slice | bytes 524288 | tf_op jit(solution)/shard_map/slice | solution.py:463
  1.7 2.8 %collective-permute-start.2 = (bf16[128,1024]{1,0:T(8,128)(2,1)}, bf16[128,1024]{1,0:T(8,128)(2,1)S(1)}, u32[]{:S(2)}, u32[]{:S(2)}) collective-permute-start(bf16[128,1024]{1,0:T(8,128)(2,1)} %slice.24), channel_id=1, source_target_pairs={{0,3},{1,2},{2,1},{3,0},{4,7},{5,6},{6,5},{7,4},{8,11},{9,10},{10,... | collective-permute-start | bytes 786440 | tf_op jit(solution)/shard_map/ppermute | solution.py:45
  4.4 0.2 collective-permute-start
  4.7 2.1 %slice.25 = bf16[384,1024]{1,0:T(8,128)(2,1)} slice(bf16[512,1024]{1,0:T(8,128)(2,1)} %own.1), slice={[128:512], [0:1024]} | slice | bytes 1572864 | tf_op jit(solution)/shard_map/slice | solution.py:463
  6.7 1.1 collective-permute-start.3
  7.9 0.7 collective-permute-start.1
  8.5 1.5 %constant_dynamic-update-slice_fusion.1 = bf16[4096,256]{1,0:T(8,128)(2,1)S(1)} fusion(bf16[4096,128]{1,0:T(8,128)(2,1)} %param.14), kind=kLoop, calls=%fused_computation.9 | loop fusion | bytes 2097152
  10.0 0.0 copy-done.12
  10.1 0.2 constant_dynamic-update-slice_fusion.w_kv.refs_1_
  10.4 1.8 %multiply_sine_fusion = (f32[512,64]{1,0:T(8,128)}, f32[512,64]{1,0:T(8,128)}) fusion(f32[64]{0:T(128)S(1)} %multiply_exponential_fusion, f32[512]{0:T(512)S(1)} %add_convert_fusion), kind=kLoop, calls=%fused_computation.2 | loop fusion | flops 32768 | bytes 264448 | tf_op jit(solution)/shard_map/sin | solution.py:30
  12.2 0.0 collective-permute-done.2.refs_1_.three_a
  12.2 1.7 %collective-permute-done.refs_0_.one_a = bf16[128,1024]{1,0:T(8,128)(2,1)S(1)} collective-permute-done((bf16[128,1024]{1,0:T(8,128)(2,1)}, bf16[128,1024]{1,0:T(8,128)(2,1)S(1)}, u32[]{:S(2)}, u32[]{:S(2)}) %collective-permute-start) | collective-permute-done | bytes 262176 | tf_op jit(solution)/shard_map/ppermute | solution.py:45
  13.9 0.7 copy-done.11
  14.6 1.6 %hold.1 = bf16[64,1024]{1,0:T(8,128)(2,1)} custom-call(bf16[64,1024]{1,0:T(8,128)(2,1)} %x_ref.1, bf16[128,1024]{1,0:T(8,128)(2,1)} %copy-done.11, bf16[128,1024]{1,0:T(8,128)(2,1)} %copy-done.10), custom_call_target="tpu_custom_call" | custom-call | tf_op jit(solution)/shard_map/hold/pallas_call | solution.py:115
  16.2 3.5 %collective-permute-start.9 = (bf16[64,1024]{1,0:T(8,128)(2,1)}, bf16[64,1024]{1,0:T(8,128)(2,1)S(1)}, u32[]{:S(2)}, u32[]{:S(2)}) collective-permute-start(bf16[64,1024]{1,0:T(8,128)(2,1)} %hold.1), channel_id=1, source_target_pairs={{0,64},{32,96},{64,128},{96,160},{128,192},{160,224},{1,65},{33,97... | collective-permute-start | bytes 393224 | tf_op jit(solution)/shard_map/ppermute | solution.py:41
  19.6 4.8 %collective-permute-start.8 = (bf16[64,1024]{1,0:T(8,128)(2,1)}, bf16[64,1024]{1,0:T(8,128)(2,1)S(1)}, u32[]{:S(2)}, u32[]{:S(2)}) collective-permute-start(bf16[64,1024]{1,0:T(8,128)(2,1)} %hold.1), channel_id=1, source_target_pairs={{0,128},{32,160},{64,192},{96,224},{1,129},{33,161},{65,193},{97,2... | collective-permute-start | bytes 393224 | tf_op jit(solution)/shard_map/ppermute | solution.py:41
  24.5 1.3 collective-permute-start.7
  25.8 0.7 fusion
  28.4 0.0 collective-permute-done.8
  28.4 0.2 collective-permute-done.7
  28.6 0.1 collective-permute-start.10
  28.7 0.8 select_reduce_fusion
  30.1 0.6 add_convert_fusion.1
  30.8 0.0 collective-permute-done.10
  30.8 0.1 select_select_fusion.own
  30.8 2.0 %collective-permute-start.13 = (bf16[64,1024]{1,0:T(8,128)(2,1)S(1)}, bf16[64,1024]{1,0:T(8,128)(2,1)}, u32[]{:S(2)}, u32[]{:S(2)}) collective-permute-start(bf16[64,1024]{1,0:T(8,128)(2,1)S(1)} %select_select_fusion.own), channel_id=1, source_target_pairs={{0,2},{1,3},{2,0},{3,1},{4,6},{5,7},{6,4},{7,5},{8,10},{9,11},{10,... | collective-permute-start | bytes 393224 | tf_op jit(solution)/shard_map/ppermute | solution.py:45
  32.8 1.1 collective-permute-start.12
  34.0 0.4 collective-permute-start.11
  34.4 0.8 multiply_sine_fusion.1
  35.2 0.6 pad_add_fusion.ids_ref
  35.8 1.9 %collective-permute-start.4 = (bf16[128,1024]{1,0:T(8,128)(2,1)}, bf16[128,1024]{1,0:T(8,128)(2,1)S(1)}, u32[]{:S(2)}, u32[]{:S(2)}) collective-permute-start(bf16[128,1024]{1,0:T(8,128)(2,1)} %copy-done.11), channel_id=1, source_target_pairs={{0,3},{1,2},{2,1},{3,0},{4,7},{5,6},{6,5},{7,4},{8,11},{9,10},{10,... | collective-permute-start | bytes 786440 | tf_op jit(solution)/shard_map/ppermute | solution.py:45
  37.7 0.0 collective-permute-done.1.one_b
  37.8 1.3 collective-permute-start.6
  39.0 1.0 slice.32
  40.0 1.2 collective-permute-start.5
  41.3 0.4 collective-permute-done.12.three
  41.7 7.4 %project_image.1.refs_4_.refs_2_ = bf16[320,256]{1,0:T(8,128)(2,1)} custom-call(s32[3]{0:T(128)} %pad_add_fusion.ids_ref, bf16[64,1024]{1,0:T(8,128)(2,1)} %copy-done.18, bf16[64,1024]{1,0:T(8,128)(2,1)} %collective-permute-done.11.one, bf16[64,1024]{1,0:T(8,128)(2,1)} %collective-permute-done.12.three, bf16[64,1024]{1,0:T(8,128)(2,1)} %collective-permute-done.13.two, ...), custom_call_target="tpu_custom_call" | custom-call | flops 8000000000 | bytes 10485760 | tf_op jit(solution)/shard_map/project_image/pallas_call | solution.py:92
  49.2 1.0 collective-permute-start.18
  50.2 2.2 %collective-permute-start.14 = (bf16[320,256]{1,0:T(8,128)(2,1)}, bf16[320,256]{1,0:T(8,128)(2,1)S(1)}, u32[]{:S(2)}, u32[]{:S(2)}) collective-permute-start(bf16[320,256]{1,0:T(8,128)(2,1)} %project_image.1.refs_4_.refs_2_), channel_id=1, source_target_pairs={{0,4},{4,8},{8,12},{12,16},{16,20},{20,24},{24,28},{28,0},{1,5},{5... | collective-permute-start | bytes 491528 | tf_op jit(solution)/shard_map/ppermute | solution.py:41
  52.4 0.4 collective-permute-done.5.two_b
  52.8 0.0 collective-permute-done.6.two_c
  52.8 0.3 copy-done.16
  53.1 0.4 copy-done.17
  53.5 0.8 copy-done.13
  54.3 7.7 %project_text.1 = (bf16[512,4096]{1,0:T(8,128)(2,1)}, bf16[512,256]{1,0:T(8,128)(2,1)}) custom-call(s32[3]{0:T(128)} %pad_add_fusion.ids_ref, bf16[512,1024]{1,0:T(8,128)(2,1)} %own.1, bf16[128,1024]{1,0:T(8,128)(2,1)} %copy-done.11, bf16[384,1024]{1,0:T(8,128)(2,1)} %collective-permute-done.1.one_b, bf16[128,1024]{1,0:T(8,128)(2,1)} %copy-done.10, ...), custom_call_target="tpu_custom_call" | custom-call | tf_op jit(solution)/shard_map/project_text/pallas_call | solution.py:151
  62.0 0.0 collective-permute-done.18.refs_8_
  62.1 1.1 pad_maximum_fusion.1
  63.2 1.1 collective-permute-start.19
  64.3 2.2 %collective-permute-start.15 = (bf16[832,256]{1,0:T(8,128)(2,1)S(1)}, bf16[832,256]{1,0:T(8,128)(2,1)S(1)}, u32[]{:S(2)}, u32[]{:S(2)}) collective-permute-start(bf16[832,256]{1,0:T(8,128)(2,1)S(1)} %get-tuple-element.22), channel_id=1, source_target_pairs={{0,4},{4,8},{8,12},{12,16},{16,20},{20,24},{24,28},{28,0},{1,5},{5... | collective-permute-start | bytes 1277960 | tf_op jit(solution)/shard_map/ppermute | solution.py:41
  66.5 9.8 %collective-permute-done.19.refs_9_ = bf16[832,256]{1,0:T(8,128)(2,1)S(1)} collective-permute-done((bf16[832,256]{1,0:T(8,128)(2,1)S(1)}, bf16[832,256]{1,0:T(8,128)(2,1)S(1)}, u32[]{:S(2)}, u32[]{:S(2)}) %collective-permute-start.19) | collective-permute-done | bytes 426016 | tf_op jit(solution)/shard_map/ppermute | solution.py:41
  76.3 3.2 %collective-permute-start.16 = (bf16[832,256]{1,0:T(8,128)(2,1)S(1)}, bf16[832,256]{1,0:T(8,128)(2,1)S(1)}, u32[]{:S(2)}, u32[]{:S(2)}) collective-permute-start(bf16[832,256]{1,0:T(8,128)(2,1)S(1)} %collective-permute-done.15.refs_5_), channel_id=1, source_target_pairs={{0,4},{4,8},{8,12},{12,16},{16,20},{20,24},{24,28},{28,0},{1,5},{5... | collective-permute-start | bytes 1277960 | tf_op jit(solution)/shard_map/ppermute | solution.py:41
  79.6 6.4 %query.3.refs_1_ = bf16[512,512]{1,0:T(8,128)(2,1)} custom-call(bf16[512,4096]{1,0:T(8,128)(2,1)} %get-tuple-element.12.x_ref, bf16[4096,1024]{1,0:T(8,128)(2,1)} %w_ref.3, f32[512,64]{1,0:T(8,128)} %get-tuple-element.24.refs_2_.cos, f32[512,64]{1,0:T(8,128)} %get-tuple-element.23.refs_3_.sin), custom_call_target="tpu_custom_call" | custom-call | flops 6000000000 | bytes 1048576 | tf_op jit(solution)/shard_map/query/pallas_call | solution.py:185
  85.9 2.6 %collective-permute-done.20.refs_10_ = bf16[832,256]{1,0:T(8,128)(2,1)S(1)} collective-permute-done((bf16[832,256]{1,0:T(8,128)(2,1)S(1)}, bf16[832,256]{1,0:T(8,128)(2,1)S(1)}, u32[]{:S(2)}, u32[]{:S(2)}) %collective-permute-start.20) | collective-permute-done | bytes 426016 | tf_op jit(solution)/shard_map/ppermute | solution.py:41
  88.6 0.1 collective-permute-start.21
  88.6 0.0 collective-permute-done.16.refs_6_
  88.7 3.3 %collective-permute-start.17 = (bf16[672,256]{1,0:T(8,128)(2,1)S(1)}, bf16[672,256]{1,0:T(8,128)(2,1)S(1)}, u32[]{:S(2)}, u32[]{:S(2)}) collective-permute-start(bf16[672,256]{1,0:T(8,128)(2,1)S(1)} %slice.34), channel_id=1, source_target_pairs={{0,4},{4,8},{8,12},{12,16},{16,20},{20,24},{24,28},{28,0},{1,5},{5... | collective-permute-start | bytes 1032200 | tf_op jit(solution)/shard_map/ppermute | solution.py:41
  92.0 6.3 %query.2.refs_0_ = bf16[512,512]{1,0:T(8,128)(2,1)} custom-call(bf16[512,4096]{1,0:T(8,128)(2,1)} %get-tuple-element.12.x_ref, bf16[4096,1024]{1,0:T(8,128)(2,1)} %w_ref.3, f32[512,64]{1,0:T(8,128)} %get-tuple-element.24.refs_2_.cos, f32[512,64]{1,0:T(8,128)} %get-tuple-element.23.refs_3_.sin), custom_call_target="tpu_custom_call" | custom-call | flops 6000000000 | bytes 1048576 | tf_op jit(solution)/shard_map/query/pallas_call | solution.py:185
  98.4 0.1 collective-permute-start.23
  98.5 0.0 collective-permute-done.17.refs_7_
  98.5 3.3 %collective-permute-start.22 = (bf16[256,256]{1,0:T(8,128)(2,1)S(1)}, bf16[256,256]{1,0:T(8,128)(2,1)S(1)}, u32[]{:S(2)}, u32[]{:S(2)}) collective-permute-start(bf16[256,256]{1,0:T(8,128)(2,1)S(1)} %slice.36), channel_id=1, source_target_pairs={{0,4},{4,8},{8,12},{12,16},{16,20},{20,24},{24,28},{28,0},{1,5},{5... | collective-permute-start | bytes 393224 | tf_op jit(solution)/shard_map/ppermute | solution.py:41
  101.8 32.0 %attention.1 = (bf16[512,1024]{1,0:T(8,128)(2,1)}, bf16[8,64,256]{2,1,0:T(8,128)(2,1)S(1)}, f32[512,1024]{1,0:T(8,128)}, f32[512,128]{1,0:T(8,128)S(1)}, f32[512,128]{1,0:T(8,128)S(1)}) custom-call(s32[3]{0:T(128)S(1)} %copy-done.5, s32[8]{0:T(128)S(1)} %copy-done.6, s32[8,8]{1,0:T(8,128)S(1)} %copy-done.4, bf16[512,512]{1,0:T(8,128)(2,1)} %query.2.refs_0_, ...), custom_call_target="tpu_custom_call" | custom-call | flops 7516192768 | bytes 8388608 | tf_op jit(solution)/shard_map/attention/pallas_call | solution.py:334
  133.8 1.6 %copy-done = f32[512,1024]{1,0:T(8,128)S(1)} copy-done((f32[512,1024]{1,0:T(8,128)S(1)}, f32[512,1024]{1,0:T(8,128)}, u32[]{:S(2)}) %copy-start) | copy-done | bytes 2097176
  135.4 1.2 copy-done.1
  136.6 5.9 %finish.1 = bf16[512,1024]{1,0:T(8,128)(2,1)} custom-call(s32[3]{0:T(128)S(1)} %copy-done.5, s32[8]{0:T(128)S(1)} %copy-done.6, s32[8,8]{1,0:T(8,128)S(1)} %copy-done.4, bf16[512,1024]{1,0:T(8,128)(2,1)S(1)} %copy-done.1, bf16[8,64,256]{2,1,0:T(8,128)(2,1)S(1)} %get-tuple-element.15.refs_1_, bf16[256,256]{1,0:T(8,128)(2,1)S(1)} %collective-permute-done.22.refs_2_, ...), custom_call_target="tpu_custom_call" | custom-call | flops 1073741824 | bytes 6291456 | tf_op jit(solution)/shard_map/finish/pallas_call | solution.py:419
  (57 shorter events, 0.2 us)
Async XLA Ops:
  1.7 10.5 %collective-permute-start.2 = (bf16[128,1024]{1,0:T(8,128)(2,1)}, bf16[128,1024]{1,0:T(8,128)(2,1)S(1)}, u32[]{:S(2)}, u32[]{:S(2)}) collective-permute-start(bf16[128,1024]{1,0:T(8,128)(2,1)} %slice.24), channel_id=1, source_target_pairs={{0,3},{1,2},{2,1},{3,0},{4,7},{5,6},{6,5},{7,4},{8,11},{9,10},{10,... | collective-permute-start | bytes 786440 | tf_op jit(solution)/shard_map/ppermute | solution.py:45
  4.4 9.4 %collective-permute-start = (bf16[128,1024]{1,0:T(8,128)(2,1)}, bf16[128,1024]{1,0:T(8,128)(2,1)S(1)}, u32[]{:S(2)}, u32[]{:S(2)}) collective-permute-start(bf16[128,1024]{1,0:T(8,128)(2,1)} %slice.24), channel_id=1, source_target_pairs={{0,1},{1,0},{2,3},{3,2},{4,5},{5,4},{6,7},{7,6},{8,9},{9,8},{10,11... | collective-permute-start | bytes 786440 | tf_op jit(solution)/shard_map/ppermute | solution.py:45
  6.7 29.1 %collective-permute-start.3 = (bf16[384,1024]{1,0:T(8,128)(2,1)}, bf16[384,1024]{1,0:T(8,128)(2,1)S(1)}, u32[]{:S(2)}, u32[]{:S(2)}) collective-permute-start(bf16[384,1024]{1,0:T(8,128)(2,1)} %slice.25), channel_id=1, source_target_pairs={{0,3},{1,2},{2,1},{3,0},{4,7},{5,6},{6,5},{7,4},{8,11},{9,10},{10,... | collective-permute-start | bytes 2359304 | tf_op jit(solution)/shard_map/ppermute | solution.py:45
  7.9 29.9 %collective-permute-start.1 = (bf16[384,1024]{1,0:T(8,128)(2,1)}, bf16[384,1024]{1,0:T(8,128)(2,1)}, u32[]{:S(2)}, u32[]{:S(2)}) collective-permute-start(bf16[384,1024]{1,0:T(8,128)(2,1)} %slice.25), channel_id=1, source_target_pairs={{0,1},{1,0},{2,3},{3,2},{4,5},{5,4},{6,7},{7,6},{8,9},{9,8},{10,11... | collective-permute-start | bytes 2359304 | tf_op jit(solution)/shard_map/ppermute | solution.py:45
  8.5 1.5 %copy-start.12 = (bf16[4096,128]{1,0:T(8,128)(2,1)S(1)}, bf16[4096,128]{1,0:T(8,128)(2,1)}, u32[]{:S(2)}) copy-start(bf16[4096,128]{1,0:T(8,128)(2,1)} %param.15) | copy-start | bytes 3145732
  10.1 15.7 %copy-start.6 = (s32[8]{0:T(128)S(1)}, s32[8]{0:T(128)}, u32[]{:S(2)}) copy-start(s32[8]{0:T(128)} %counts_ref.3) | copy-start | bytes 100
  10.1 18.5 %copy-start.9 = (bf16[64,1024]{1,0:T(8,128)(2,1)S(1)}, bf16[64,1024]{1,0:T(8,128)(2,1)}, u32[]{:S(2)}) copy-start(bf16[64,1024]{1,0:T(8,128)(2,1)} %x_ref.1) | copy-start | bytes 393220
  10.1 18.6 %copy-start.4 = (s32[8,8]{1,0:T(8,128)S(1)}, s32[8,8]{1,0:T(8,128)}, u32[]{:S(2)}) copy-start(s32[8,8]{1,0:T(8,128)} %starts_ref.3) | copy-start | bytes 772
  10.3 29.7 %copy-start.7 = (bf16[4096,256]{1,0:T(8,128)(2,1)}, bf16[4096,256]{1,0:T(8,128)(2,1)S(1)}, u32[]{:S(2)}) copy-start(bf16[4096,256]{1,0:T(8,128)(2,1)S(1)} %constant_dynamic-update-slice_fusion.w_kv.refs_1_) | copy-start | bytes 6291460
  12.2 1.7 %copy-start.10 = (bf16[128,1024]{1,0:T(8,128)(2,1)}, bf16[128,1024]{1,0:T(8,128)(2,1)S(1)}, u32[]{:S(2)}) copy-start(bf16[128,1024]{1,0:T(8,128)(2,1)S(1)} %collective-permute-done.2.refs_1_.three_a) | copy-start | bytes 786436
  13.9 0.7 copy-start.11
  16.2 12.2 %collective-permute-start.9 = (bf16[64,1024]{1,0:T(8,128)(2,1)}, bf16[64,1024]{1,0:T(8,128)(2,1)S(1)}, u32[]{:S(2)}, u32[]{:S(2)}) collective-permute-start(bf16[64,1024]{1,0:T(8,128)(2,1)} %hold.1), channel_id=1, source_target_pairs={{0,64},{32,96},{64,128},{96,160},{128,192},{160,224},{1,65},{33,97... | collective-permute-start | bytes 393224 | tf_op jit(solution)/shard_map/ppermute | solution.py:41
  19.6 8.7 %collective-permute-start.8 = (bf16[64,1024]{1,0:T(8,128)(2,1)}, bf16[64,1024]{1,0:T(8,128)(2,1)S(1)}, u32[]{:S(2)}, u32[]{:S(2)}) collective-permute-start(bf16[64,1024]{1,0:T(8,128)(2,1)} %hold.1), channel_id=1, source_target_pairs={{0,128},{32,160},{64,192},{96,224},{1,129},{33,161},{65,193},{97,2... | collective-permute-start | bytes 393224 | tf_op jit(solution)/shard_map/ppermute | solution.py:41
  24.5 4.1 %collective-permute-start.7 = (bf16[64,1024]{1,0:T(8,128)(2,1)}, bf16[64,1024]{1,0:T(8,128)(2,1)S(1)}, u32[]{:S(2)}, u32[]{:S(2)}) collective-permute-start(bf16[64,1024]{1,0:T(8,128)(2,1)} %hold.1), channel_id=1, source_target_pairs={{0,192},{32,224},{1,193},{33,225},{2,194},{34,226},{3,195},{35,227... | collective-permute-start | bytes 393224 | tf_op jit(solution)/shard_map/ppermute | solution.py:41
  28.6 2.1 %collective-permute-start.10 = (bf16[64,1024]{1,0:T(8,128)(2,1)S(1)}, bf16[64,1024]{1,0:T(8,128)(2,1)}, u32[]{:S(2)}, u32[]{:S(2)}) collective-permute-start(bf16[64,1024]{1,0:T(8,128)(2,1)S(1)} %select_select_fusion.1), channel_id=1, source_target_pairs={{0,32},{32,0},{64,96},{96,64},{128,160},{160,128},{192,224},{224,1... | collective-permute-start | bytes 393224 | tf_op jit(solution)/shard_map/ppermute | solution.py:469
  30.8 10.9 %copy-start.18 = (bf16[64,1024]{1,0:T(8,128)(2,1)}, bf16[64,1024]{1,0:T(8,128)(2,1)S(1)}, u32[]{:S(2)}) copy-start(bf16[64,1024]{1,0:T(8,128)(2,1)S(1)} %select_select_fusion.own) | copy-start | bytes 393220
  30.8 9.2 %collective-permute-start.13 = (bf16[64,1024]{1,0:T(8,128)(2,1)S(1)}, bf16[64,1024]{1,0:T(8,128)(2,1)}, u32[]{:S(2)}, u32[]{:S(2)}) collective-permute-start(bf16[64,1024]{1,0:T(8,128)(2,1)S(1)} %select_select_fusion.own), channel_id=1, source_target_pairs={{0,2},{1,3},{2,0},{3,1},{4,6},{5,7},{6,4},{7,5},{8,10},{9,11},{10,... | collective-permute-start | bytes 393224 | tf_op jit(solution)/shard_map/ppermute | solution.py:45
  32.8 8.9 %collective-permute-start.12 = (bf16[64,1024]{1,0:T(8,128)(2,1)S(1)}, bf16[64,1024]{1,0:T(8,128)(2,1)}, u32[]{:S(2)}, u32[]{:S(2)}) collective-permute-start(bf16[64,1024]{1,0:T(8,128)(2,1)S(1)} %select_select_fusion.own), channel_id=1, source_target_pairs={{0,3},{1,2},{2,1},{3,0},{4,7},{5,6},{6,5},{7,4},{8,11},{9,10},{10,... | collective-permute-start | bytes 393224 | tf_op jit(solution)/shard_map/ppermute | solution.py:45
  34.0 7.7 %collective-permute-start.11 = (bf16[64,1024]{1,0:T(8,128)(2,1)S(1)}, bf16[64,1024]{1,0:T(8,128)(2,1)}, u32[]{:S(2)}, u32[]{:S(2)}) collective-permute-start(bf16[64,1024]{1,0:T(8,128)(2,1)S(1)} %select_select_fusion.own), channel_id=1, source_target_pairs={{0,1},{1,0},{2,3},{3,2},{4,5},{5,4},{6,7},{7,6},{8,9},{9,8},{10,11... | collective-permute-start | bytes 393224 | tf_op jit(solution)/shard_map/ppermute | solution.py:45
  35.8 13.3 %copy-start.8 = (bf16[384,1024]{1,0:T(8,128)(2,1)}, bf16[384,1024]{1,0:T(8,128)(2,1)S(1)}, u32[]{:S(2)}) copy-start(bf16[384,1024]{1,0:T(8,128)(2,1)S(1)} %collective-permute-done.3.three_b) | copy-start | bytes 2359300
  35.8 16.6 %collective-permute-start.4 = (bf16[128,1024]{1,0:T(8,128)(2,1)}, bf16[128,1024]{1,0:T(8,128)(2,1)S(1)}, u32[]{:S(2)}, u32[]{:S(2)}) collective-permute-start(bf16[128,1024]{1,0:T(8,128)(2,1)} %copy-done.11), channel_id=1, source_target_pairs={{0,3},{1,2},{2,1},{3,0},{4,7},{5,6},{6,5},{7,4},{8,11},{9,10},{10,... | collective-permute-start | bytes 786440 | tf_op jit(solution)/shard_map/ppermute | solution.py:45
  37.8 15.1 %collective-permute-start.6 = (bf16[256,1024]{1,0:T(8,128)(2,1)S(1)}, bf16[256,1024]{1,0:T(8,128)(2,1)S(1)}, u32[]{:S(2)}, u32[]{:S(2)}) collective-permute-start(bf16[256,1024]{1,0:T(8,128)(2,1)S(1)} %slice.33), channel_id=1, source_target_pairs={{0,1},{1,0},{2,3},{3,2},{4,5},{5,4},{6,7},{7,6},{8,9},{9,8},{10,11... | collective-permute-start | bytes 1572872 | tf_op jit(solution)/shard_map/ppermute | solution.py:45
  40.0 12.8 %collective-permute-start.5 = (bf16[128,1024]{1,0:T(8,128)(2,1)S(1)}, bf16[128,1024]{1,0:T(8,128)(2,1)S(1)}, u32[]{:S(2)}, u32[]{:S(2)}) collective-permute-start(bf16[128,1024]{1,0:T(8,128)(2,1)S(1)} %slice.32), channel_id=1, source_target_pairs={{0,3},{1,2},{2,1},{3,0},{4,7},{5,6},{6,5},{7,4},{8,11},{9,10},{10,... | collective-permute-start | bytes 786440 | tf_op jit(solution)/shard_map/ppermute | solution.py:45
  49.2 12.9 %collective-permute-start.18 = (bf16[320,256]{1,0:T(8,128)(2,1)}, bf16[320,256]{1,0:T(8,128)(2,1)S(1)}, u32[]{:S(2)}, u32[]{:S(2)}) collective-permute-start(bf16[320,256]{1,0:T(8,128)(2,1)} %project_image.1.refs_4_.refs_2_), channel_id=1, source_target_pairs={{0,28},{4,0},{8,4},{12,8},{16,12},{20,16},{24,20},{28,24},{1,29},{... | collective-permute-start | bytes 491528 | tf_op jit(solution)/shard_map/ppermute | solution.py:41
  50.2 11.9 %collective-permute-start.14 = (bf16[320,256]{1,0:T(8,128)(2,1)}, bf16[320,256]{1,0:T(8,128)(2,1)S(1)}, u32[]{:S(2)}, u32[]{:S(2)}) collective-permute-start(bf16[320,256]{1,0:T(8,128)(2,1)} %project_image.1.refs_4_.refs_2_), channel_id=1, source_target_pairs={{0,4},{4,8},{8,12},{12,16},{16,20},{20,24},{24,28},{28,0},{1,5},{5... | collective-permute-start | bytes 491528 | tf_op jit(solution)/shard_map/ppermute | solution.py:41
  52.4 0.7 copy-start.16
  52.8 0.7 copy-start.17
  53.5 0.8 copy-start.13
  63.2 13.1 %collective-permute-start.19 = (bf16[832,256]{1,0:T(8,128)(2,1)S(1)}, bf16[832,256]{1,0:T(8,128)(2,1)S(1)}, u32[]{:S(2)}, u32[]{:S(2)}) collective-permute-start(bf16[832,256]{1,0:T(8,128)(2,1)S(1)} %get-tuple-element.21), channel_id=1, source_target_pairs={{0,28},{4,0},{8,4},{12,8},{16,12},{20,16},{24,20},{28,24},{1,29},{... | collective-permute-start | bytes 1277960 | tf_op jit(solution)/shard_map/ppermute | solution.py:41
  64.3 12.0 %collective-permute-start.15 = (bf16[832,256]{1,0:T(8,128)(2,1)S(1)}, bf16[832,256]{1,0:T(8,128)(2,1)S(1)}, u32[]{:S(2)}, u32[]{:S(2)}) collective-permute-start(bf16[832,256]{1,0:T(8,128)(2,1)S(1)} %get-tuple-element.22), channel_id=1, source_target_pairs={{0,4},{4,8},{8,12},{12,16},{16,20},{20,24},{24,28},{28,0},{1,5},{5... | collective-permute-start | bytes 1277960 | tf_op jit(solution)/shard_map/ppermute | solution.py:41
  76.3 9.6 %copy-start.20 = (bf16[832,256]{1,0:T(8,128)(2,1)}, bf16[832,256]{1,0:T(8,128)(2,1)S(1)}, u32[]{:S(2)}) copy-start(bf16[832,256]{1,0:T(8,128)(2,1)S(1)} %collective-permute-done.19.refs_9_) | copy-start | bytes 1277956
  76.3 12.2 %collective-permute-start.20 = (bf16[832,256]{1,0:T(8,128)(2,1)S(1)}, bf16[832,256]{1,0:T(8,128)(2,1)S(1)}, u32[]{:S(2)}, u32[]{:S(2)}) collective-permute-start(bf16[832,256]{1,0:T(8,128)(2,1)S(1)} %collective-permute-done.19.refs_9_), channel_id=1, source_target_pairs={{0,28},{4,0},{8,4},{12,8},{16,12},{20,16},{24,20},{28,24},{1,29},{... | collective-permute-start | bytes 1277960 | tf_op jit(solution)/shard_map/ppermute | solution.py:41
  76.3 9.6 %copy-start.21 = (bf16[832,256]{1,0:T(8,128)(2,1)}, bf16[832,256]{1,0:T(8,128)(2,1)S(1)}, u32[]{:S(2)}) copy-start(bf16[832,256]{1,0:T(8,128)(2,1)S(1)} %collective-permute-done.15.refs_5_) | copy-start | bytes 1277956
  76.3 12.3 %collective-permute-start.16 = (bf16[832,256]{1,0:T(8,128)(2,1)S(1)}, bf16[832,256]{1,0:T(8,128)(2,1)S(1)}, u32[]{:S(2)}, u32[]{:S(2)}) collective-permute-start(bf16[832,256]{1,0:T(8,128)(2,1)S(1)} %collective-permute-done.15.refs_5_), channel_id=1, source_target_pairs={{0,4},{4,8},{8,12},{12,16},{16,20},{20,24},{24,28},{28,0},{1,5},{5... | collective-permute-start | bytes 1277960 | tf_op jit(solution)/shard_map/ppermute | solution.py:41
  88.5 9.8 %copy-start.14 = (bf16[832,256]{1,0:T(8,128)(2,1)}, bf16[832,256]{1,0:T(8,128)(2,1)S(1)}, u32[]{:S(2)}) copy-start(bf16[832,256]{1,0:T(8,128)(2,1)S(1)} %collective-permute-done.20.refs_10_) | copy-start | bytes 1277956
  88.6 9.8 %collective-permute-start.21 = (bf16[672,256]{1,0:T(8,128)(2,1)S(1)}, bf16[672,256]{1,0:T(8,128)(2,1)S(1)}, u32[]{:S(2)}, u32[]{:S(2)}) collective-permute-start(bf16[672,256]{1,0:T(8,128)(2,1)S(1)} %slice.35), channel_id=1, source_target_pairs={{0,28},{4,0},{8,4},{12,8},{16,12},{20,16},{24,20},{28,24},{1,29},{... | collective-permute-start | bytes 1032200 | tf_op jit(solution)/shard_map/ppermute | solution.py:41
  88.7 9.7 %copy-start.15 = (bf16[832,256]{1,0:T(8,128)(2,1)}, bf16[832,256]{1,0:T(8,128)(2,1)S(1)}, u32[]{:S(2)}) copy-start(bf16[832,256]{1,0:T(8,128)(2,1)S(1)} %collective-permute-done.16.refs_6_) | copy-start | bytes 1277956
  88.7 13.1 %copy-start.2 = (bf16[512,256]{1,0:T(8,128)(2,1)S(1)}, bf16[512,256]{1,0:T(8,128)(2,1)}, u32[]{:S(2)}) copy-start(bf16[512,256]{1,0:T(8,128)(2,1)} %get-tuple-element.13.refs_3_) | copy-start | bytes 786436
  88.7 13.1 %copy-start.3 = (bf16[320,256]{1,0:T(8,128)(2,1)S(1)}, bf16[320,256]{1,0:T(8,128)(2,1)}, u32[]{:S(2)}) copy-start(bf16[320,256]{1,0:T(8,128)(2,1)} %project_image.1.refs_4_.refs_2_) | copy-start | bytes 491524
  88.7 13.1 %copy-start.5 = (s32[3]{0:T(128)S(1)}, s32[3]{0:T(128)}, u32[]{:S(2)}) copy-start(s32[3]{0:T(128)} %pad_add_fusion.ids_ref) | copy-start | bytes 40
  88.7 9.7 %collective-permute-start.17 = (bf16[672,256]{1,0:T(8,128)(2,1)S(1)}, bf16[672,256]{1,0:T(8,128)(2,1)S(1)}, u32[]{:S(2)}, u32[]{:S(2)}) collective-permute-start(bf16[672,256]{1,0:T(8,128)(2,1)S(1)} %slice.34), channel_id=1, source_target_pairs={{0,4},{4,8},{8,12},{12,16},{16,20},{20,24},{24,28},{28,0},{1,5},{5... | collective-permute-start | bytes 1032200 | tf_op jit(solution)/shard_map/ppermute | solution.py:41
  98.3 3.4 %copy-start.19 = (bf16[672,256]{1,0:T(8,128)(2,1)}, bf16[672,256]{1,0:T(8,128)(2,1)S(1)}, u32[]{:S(2)}) copy-start(bf16[672,256]{1,0:T(8,128)(2,1)S(1)} %collective-permute-done.21.refs_11_) | copy-start | bytes 1032196
  98.4 35.4 %collective-permute-start.23 = (bf16[256,256]{1,0:T(8,128)(2,1)S(1)}, bf16[256,256]{1,0:T(8,128)(2,1)S(1)}, u32[]{:S(2)}, u32[]{:S(2)}) collective-permute-start(bf16[256,256]{1,0:T(8,128)(2,1)S(1)} %slice.37), channel_id=1, source_target_pairs={{0,28},{4,0},{8,4},{12,8},{16,12},{20,16},{24,20},{28,24},{1,29},{... | collective-permute-start | bytes 393224 | tf_op jit(solution)/shard_map/ppermute | solution.py:41
  98.5 35.3 %collective-permute-start.22 = (bf16[256,256]{1,0:T(8,128)(2,1)S(1)}, bf16[256,256]{1,0:T(8,128)(2,1)S(1)}, u32[]{:S(2)}, u32[]{:S(2)}) collective-permute-start(bf16[256,256]{1,0:T(8,128)(2,1)S(1)} %slice.36), channel_id=1, source_target_pairs={{0,4},{4,8},{8,12},{12,16},{16,20},{20,24},{24,28},{28,0},{1,5},{5... | collective-permute-start | bytes 393224 | tf_op jit(solution)/shard_map/ppermute | solution.py:41
  133.8 1.6 %copy-start = (f32[512,1024]{1,0:T(8,128)S(1)}, f32[512,1024]{1,0:T(8,128)}, u32[]{:S(2)}) copy-start(f32[512,1024]{1,0:T(8,128)} %get-tuple-element.16.refs_4_) | copy-start | bytes 6291460
  135.4 1.2 copy-start.1

commit v10 on v9

--- a/solution.py
+++ b/solution.py
@@ -352,7 +352,7 @@
             pltpu.VMEM((tok, HD), F32),
             pltpu.SemaphoreType.DMA((32,)),
         ],
-        compiler_params=pltpu.CompilerParams(vmem_limit_bytes=52 * 2**20),
+        compiler_params=pltpu.CompilerParams(vmem_limit_bytes=34 * 2**20),
         cost_estimate=pl.CostEstimate(
             flops=4 * tok * heads * keys * HD,
             bytes_accessed=8 * 2**20,
@@ -423,7 +423,7 @@
         in_specs=[pl.BlockSpec(memory_space=SMEM)] * 3 + [block] + [whole] * 3 + [block] + [whole] * 2,
         out_specs=block,
         scratch_shapes=[pltpu.VMEM((tok, 2 * HD), BF16)],
-        compiler_params=pltpu.CompilerParams(vmem_limit_bytes=40 * 2**20),
+        compiler_params=pltpu.CompilerParams(vmem_limit_bytes=24 * 2**20),
         cost_estimate=pl.CostEstimate(
             flops=4 * tok * heads * tok * HD, bytes_accessed=6 * 2**20, transcendentals=0
         ),
@@ -459,11 +459,15 @@
 
     my_slot, my_across, my_distance = source(sample)
     _, _, its_distance = source(sample ^ 1)
+    mine = (every[:, None] == sample) & (every[None, :] == my_slot)
+    my_start = jnp.sum(jnp.where(mine, image_starts, 0))
+    text_tables = rotary_tables(ctx * tok + jnp.arange(tok, dtype=jnp.int32))
+    image_tables = rotary_tables(my_start + jnp.arange(IMG_TOK, dtype=jnp.int32))
     quarter = tok // 4
     group_a, group_b = text_rows[:quarter], text_rows[quarter:]
     one_a, three_a = first_hop(group_a)
     one_b, three_b = first_hop(group_b)
-    leaving = hold(visual_rows, (one_a, three_a))
+    leaving = hold(visual_rows, (one_a, three_a, ids, *image_tables))
     routed = [visual_rows] + [shift(leaving, "dp", 2 * d, False) for d in (1, 2, 3)]
     for_other = choose(its_distance, routed)
     from_other = lax.ppermute(for_other, "dp", [(i, i ^ 1) for i in range(SHARDS)])
@@ -473,10 +477,6 @@
     two_b = exchange(one_b[:quarter], 3)
     two_c = exchange(three_b[quarter:], 1)
 
-    mine = (every[:, None] == sample) & (every[None, :] == my_slot)
-    my_start = jnp.sum(jnp.where(mine, image_starts, 0))
-    text_tables = rotary_tables(ctx * tok + jnp.arange(tok, dtype=jnp.int32))
-    image_tables = rotary_tables(my_start + jnp.arange(IMG_TOK, dtype=jnp.int32))
     own_e = project_image(
         ids, image_parts, gain, w_kv, w_query, image_tables,
         (one_a, three_a, *text_tables),

time: 143 us -> 140 us (0.979)
  waiting for transfers between devices: 15.2 us -> 12.3 us
  Pallas kernels: 67.3 us -> 65.8 us
    ppermute x10, waiting for transfers between devices: 2.58 us -> 0.98 us  [exchange(): return lax.ppermute(x, 'mp', [(i, i ^ mask) for i in range(4)])]
    unnamed x45 -> x41, local copies, waits for them, and re-layouts: 6.62 us -> 5.46 us
  transfers between devices with their start and end apart: 24 -> 24, of which waited for: 6 -> 3; matrix products, arithmetic and copies ran while one was open for 7% -> 9% of each run, Pallas kernels for 43% -> 43%
where the time goes in v10:
time: 140 us; the launch traced here: 139 us
  Pallas kernels  65.8 us (47%)
  starting transfers between devices  39.8 us (28%)
  waiting for transfers between devices  12.3 us (9%)
  local copies, waits for them, and re-layouts  11.1 us (8%)
  other arithmetic  7.34 us (5%)
  between operations  2.81 us (2%)
    pallas_call x1, Pallas kernels, attention(): pl.pallas_call(functools.partial(attention_kernel, tok, heads), out_shape...  30.5 us
    ppermute x13, starting transfers between devices, shift(): return lax.ppermute(x, axis, pairs)  26.8 us
    ppermute x10, starting transfers between devices, exchange(): return lax.ppermute(x, 'mp', [(i, i ^ mask) for i in range(4)])  13.1 us
    pallas_call x2, Pallas kernels, query(): pl.pallas_call(query_kernel, out_shape=jax.ShapeDtypeStruct((rows, column...  12.6 us
    ppermute x13, waiting for transfers between devices, shift(): return lax.ppermute(x, axis, pairs)  11.3 us
    pallas_call x1, Pallas kernels, project_text(): pl.pallas_call(text_kernel, out_shape=[jax.ShapeDtypeStruct((rows, D), BF...  7.74 us
    pallas_call x1, Pallas kernels, project_image(): pl.pallas_call(image_kernel, out_shape=jax.ShapeDtypeStruct(((1 + steps)...  7.43 us
    pallas_call x1, Pallas kernels, finish(): pl.pallas_call(functools.partial(finish_kernel, tok), out_shape=jax.Shape...  5.98 us
  transfers between devices with their start and end apart: 24, of which 3 were waited for; matrix products, arithmetic and copies ran while one was open for 9% of the time, Pallas kernels for 43%

profile of v10, /device:TPU:224, one launch (start us, length us, event | category | flops | bytes accessed | tf_op | source)
XLA Modules:
  0.0 139.2 jit_solution(16037939196141144666)
XLA Ops:
  0.0 1.0 slice.24
  1.0 0.0 copy-start.9
  1.0 2.8 %collective-permute-start.2 = (bf16[128,1024]{1,0:T(8,128)(2,1)S(1)}, bf16[128,1024]{1,0:T(8,128)(2,1)S(1)}, u32[]{:S(2)}, u32[]{:S(2)}) collective-permute-start(bf16[128,1024]{1,0:T(8,128)(2,1)S(1)} %slice.24), channel_id=1, source_target_pairs={{0,3},{1,2},{2,1},{3,0},{4,7},{5,6},{6,5},{7,4},{8,11},{9,10},{10,... | collective-permute-start | bytes 786440 | tf_op jit(solution)/shard_map/ppermute | solution.py:45
  3.9 0.2 collective-permute-start
  4.1 2.1 %slice.25 = bf16[384,1024]{1,0:T(8,128)(2,1)} slice(bf16[512,1024]{1,0:T(8,128)(2,1)} %own.1), slice={[128:512], [0:1024]} | slice | bytes 1572864 | tf_op jit(solution)/shard_map/slice | solution.py:467
  6.1 1.1 collective-permute-start.3
  7.3 0.7 collective-permute-start.1
  8.0 0.7 fusion.1
  9.2 0.8 select_reduce_fusion
  10.0 0.7 add_convert_fusion.1
  10.7 0.6 pad_add_fusion.refs_2_.ids_ref
  11.3 0.8 multiply_sine_fusion.1
  12.1 1.0 collective-permute-done.refs_0_.one_a
  13.1 0.7 copy-done.11
  13.8 1.6 %hold.1 = bf16[64,1024]{1,0:T(8,128)(2,1)} custom-call(bf16[64,1024]{1,0:T(8,128)(2,1)} %x_ref.1, bf16[128,1024]{1,0:T(8,128)(2,1)} %copy-done.11, bf16[128,1024]{1,0:T(8,128)(2,1)} %copy-done.10, s32[3]{0:T(128)} %pad_add_fusion.refs_2_.ids_ref, f32[64,64]{1,0:T(8,128)} %get-tuple-element.26.refs_3_.cos, f32[64,64]{1,0:T(8,128)} %get-tuple-element.25.refs_4_.sin), custom_call_target="tpu_custom_call" | custom-call | tf_op jit(solution)/shard_map/hold/pallas_call | solution.py:115
  15.4 3.5 %collective-permute-start.9 = (bf16[64,1024]{1,0:T(8,128)(2,1)}, bf16[64,1024]{1,0:T(8,128)(2,1)S(1)}, u32[]{:S(2)}, u32[]{:S(2)}) collective-permute-start(bf16[64,1024]{1,0:T(8,128)(2,1)} %hold.1), channel_id=1, source_target_pairs={{0,64},{32,96},{64,128},{96,160},{128,192},{160,224},{1,65},{33,97... | collective-permute-start | bytes 393224 | tf_op jit(solution)/shard_map/ppermute | solution.py:41
  18.9 4.8 %collective-permute-start.8 = (bf16[64,1024]{1,0:T(8,128)(2,1)}, bf16[64,1024]{1,0:T(8,128)(2,1)S(1)}, u32[]{:S(2)}, u32[]{:S(2)}) collective-permute-start(bf16[64,1024]{1,0:T(8,128)(2,1)} %hold.1), channel_id=1, source_target_pairs={{0,128},{32,160},{64,192},{96,224},{1,129},{33,161},{65,193},{97,2... | collective-permute-start | bytes 393224 | tf_op jit(solution)/shard_map/ppermute | solution.py:41
  23.7 1.9 %collective-permute-start.7 = (bf16[64,1024]{1,0:T(8,128)(2,1)}, bf16[64,1024]{1,0:T(8,128)(2,1)}, u32[]{:S(2)}, u32[]{:S(2)}) collective-permute-start(bf16[64,1024]{1,0:T(8,128)(2,1)} %hold.1), channel_id=1, source_target_pairs={{0,192},{32,224},{1,193},{33,225},{2,194},{34,226},{3,195},{35,227... | collective-permute-start | bytes 393224 | tf_op jit(solution)/shard_map/ppermute | solution.py:41
  25.7 1.4 %constant_dynamic-update-slice_fusion.1 = bf16[4096,256]{1,0:T(8,128)(2,1)S(1)} fusion(bf16[4096,128]{1,0:T(8,128)(2,1)} %param.14), kind=kLoop, calls=%fused_computation.9 | loop fusion | bytes 2097152
  28.4 0.0 collective-permute-done.8
  28.4 0.0 collective-permute-done.7
  28.4 0.7 select_select_fusion.1
  29.1 1.5 %constant_dynamic-update-slice_fusion.w_kv.refs_1_ = bf16[4096,256]{1,0:T(8,128)(2,1)S(1)} fusion(bf16[4096,256]{1,0:T(8,128)(2,1)S(1)} %constant_dynamic-update-slice_fusion.1, bf16[4096,128]{1,0:T(8,128)(2,1)} %param.15), kind=kLoop, calls=%fused_computation.8 | loop fusion | bytes 2097152 | tf_op jit(solution)/shard_map/concatenate | solution.py:444
  31.2 0.0 collective-permute-done.10
  31.2 0.1 select_select_fusion.own
  31.3 2.1 %collective-permute-start.13 = (bf16[64,1024]{1,0:T(8,128)(2,1)S(1)}, bf16[64,1024]{1,0:T(8,128)(2,1)S(1)}, u32[]{:S(2)}, u32[]{:S(2)}) collective-permute-start(bf16[64,1024]{1,0:T(8,128)(2,1)S(1)} %select_select_fusion.own), channel_id=1, source_target_pairs={{0,2},{1,3},{2,0},{3,1},{4,6},{5,7},{6,4},{7,5},{8,10},{9,11},{10,... | collective-permute-start | bytes 393224 | tf_op jit(solution)/shard_map/ppermute | solution.py:45
  33.4 1.1 collective-permute-start.12
  34.6 0.3 collective-permute-start.11
  34.9 1.8 %multiply_sine_fusion = (f32[512,64]{1,0:T(8,128)}, f32[512,64]{1,0:T(8,128)}) fusion(f32[64]{0:T(128)S(1)} %multiply_exponential_fusion, f32[512]{0:T(512)S(1)} %add_convert_fusion), kind=kLoop, calls=%fused_computation.2 | loop fusion | flops 32768 | bytes 264448 | tf_op jit(solution)/shard_map/sin | solution.py:30
  36.7 0.0 collective-permute-done.3.three_b
  36.7 1.9 %collective-permute-start.4 = (bf16[128,1024]{1,0:T(8,128)(2,1)S(1)}, bf16[128,1024]{1,0:T(8,128)(2,1)S(1)}, u32[]{:S(2)}, u32[]{:S(2)}) collective-permute-start(bf16[128,1024]{1,0:T(8,128)(2,1)S(1)} %copy-done.12), channel_id=1, source_target_pairs={{0,3},{1,2},{2,1},{3,0},{4,7},{5,6},{6,5},{7,4},{8,11},{9,10},{10,... | collective-permute-start | bytes 786440 | tf_op jit(solution)/shard_map/ppermute | solution.py:45
  38.6 1.5 %collective-permute-start.6 = (bf16[256,1024]{1,0:T(8,128)(2,1)S(1)}, bf16[256,1024]{1,0:T(8,128)(2,1)S(1)}, u32[]{:S(2)}, u32[]{:S(2)}) collective-permute-start(bf16[256,1024]{1,0:T(8,128)(2,1)S(1)} %slice.33), channel_id=1, source_target_pairs={{0,1},{1,0},{2,3},{3,2},{4,5},{5,4},{6,7},{7,6},{8,9},{9,8},{10,11... | collective-permute-start | bytes 1572872 | tf_op jit(solution)/shard_map/ppermute | solution.py:45
  40.2 1.0 slice.32
  41.1 0.0 collective-permute-done.13.two
  41.1 1.2 collective-permute-start.5
  42.4 0.0 collective-permute-done.12.three
  42.4 0.0 copy-start.19
  42.4 0.6 copy-done.18
  43.0 0.0 copy-done.19
  43.1 7.4 %project_image.1.refs_4_.refs_2_ = bf16[320,256]{1,0:T(8,128)(2,1)} custom-call(s32[3]{0:T(128)} %pad_add_fusion.refs_2_.ids_ref, bf16[64,1024]{1,0:T(8,128)(2,1)} %copy-done.16, bf16[64,1024]{1,0:T(8,128)(2,1)} %copy-done.19, bf16[64,1024]{1,0:T(8,128)(2,1)} %copy-done.18, bf16[64,1024]{1,0:T(8,128)(2,1)} %copy-done.17, f32[1,4096]{1,0:T(1,128)} %bitcast.4, ...), custom_call_target="tpu_custom_call" | custom-call | flops 8000000000 | bytes 10485760 | tf_op jit(solution)/shard_map/project_image/pallas_call | solution.py:92
  50.5 1.0 collective-permute-start.18
  51.5 2.2 %collective-permute-start.14 = (bf16[320,256]{1,0:T(8,128)(2,1)}, bf16[320,256]{1,0:T(8,128)(2,1)S(1)}, u32[]{:S(2)}, u32[]{:S(2)}) collective-permute-start(bf16[320,256]{1,0:T(8,128)(2,1)} %project_image.1.refs_4_.refs_2_), channel_id=1, source_target_pairs={{0,4},{4,8},{8,12},{12,16},{16,20},{20,24},{24,28},{28,0},{1,5},{5... | collective-permute-start | bytes 491528 | tf_op jit(solution)/shard_map/ppermute | solution.py:41
  53.7 0.0 collective-permute-done.4.two_a
  53.8 0.0 collective-permute-done.5.two_b
  53.8 0.7 copy-done.14
  54.5 0.1 copy-done.15
  54.6 0.8 copy-done.13
  55.3 7.7 %project_text.1 = (bf16[512,4096]{1,0:T(8,128)(2,1)}, bf16[512,256]{1,0:T(8,128)(2,1)}) custom-call(s32[3]{0:T(128)} %pad_add_fusion.refs_2_.ids_ref, bf16[512,1024]{1,0:T(8,128)(2,1)} %own.1, bf16[128,1024]{1,0:T(8,128)(2,1)} %copy-done.11, bf16[384,1024]{1,0:T(8,128)(2,1)} %collective-permute-done.1.one_b, bf16[128,1024]{1,0:T(8,128)(2,1)} %copy-done.10, ...), custom_call_target="tpu_custom_call" | custom-call | tf_op jit(solution)/shard_map/project_text/pallas_call | solution.py:151
  63.1 1.1 pad_maximum_fusion.1
  64.2 0.5 collective-permute-start.19
  64.8 2.8 %collective-permute-start.15 = (bf16[832,256]{1,0:T(8,128)(2,1)S(1)}, bf16[832,256]{1,0:T(8,128)(2,1)S(1)}, u32[]{:S(2)}, u32[]{:S(2)}) collective-permute-start(bf16[832,256]{1,0:T(8,128)(2,1)S(1)} %get-tuple-element.22), channel_id=1, source_target_pairs={{0,4},{4,8},{8,12},{12,16},{16,20},{20,24},{24,28},{28,0},{1,5},{5... | collective-permute-start | bytes 1277960 | tf_op jit(solution)/shard_map/ppermute | solution.py:41
  67.5 9.2 %collective-permute-done.19.refs_9_ = bf16[832,256]{1,0:T(8,128)(2,1)S(1)} collective-permute-done((bf16[832,256]{1,0:T(8,128)(2,1)S(1)}, bf16[832,256]{1,0:T(8,128)(2,1)S(1)}, u32[]{:S(2)}, u32[]{:S(2)}) %collective-permute-start.19) | collective-permute-done | bytes 426016 | tf_op jit(solution)/shard_map/ppermute | solution.py:41
  76.8 3.2 %collective-permute-start.16 = (bf16[832,256]{1,0:T(8,128)(2,1)S(1)}, bf16[832,256]{1,0:T(8,128)(2,1)S(1)}, u32[]{:S(2)}, u32[]{:S(2)}) collective-permute-start(bf16[832,256]{1,0:T(8,128)(2,1)S(1)} %collective-permute-done.15.refs_5_), channel_id=1, source_target_pairs={{0,4},{4,8},{8,12},{12,16},{16,20},{20,24},{24,28},{28,0},{1,5},{5... | collective-permute-start | bytes 1277960 | tf_op jit(solution)/shard_map/ppermute | solution.py:41
  80.0 6.3 %query.3.refs_1_ = bf16[512,512]{1,0:T(8,128)(2,1)} custom-call(bf16[512,4096]{1,0:T(8,128)(2,1)} %get-tuple-element.12.x_ref, bf16[4096,1024]{1,0:T(8,128)(2,1)} %w_ref.3, f32[512,64]{1,0:T(8,128)} %get-tuple-element.24.refs_2_.cos, f32[512,64]{1,0:T(8,128)} %get-tuple-element.23.refs_3_.sin), custom_call_target="tpu_custom_call" | custom-call | flops 6000000000 | bytes 1048576 | tf_op jit(solution)/shard_map/query/pallas_call | solution.py:185
  86.3 2.0 %collective-permute-done.20.refs_10_ = bf16[832,256]{1,0:T(8,128)(2,1)S(1)} collective-permute-done((bf16[832,256]{1,0:T(8,128)(2,1)S(1)}, bf16[832,256]{1,0:T(8,128)(2,1)S(1)}, u32[]{:S(2)}, u32[]{:S(2)}) %collective-permute-start.20) | collective-permute-done | bytes 426016 | tf_op jit(solution)/shard_map/ppermute | solution.py:41
  88.4 0.1 collective-permute-start.21
  88.6 3.3 %collective-permute-start.17 = (bf16[672,256]{1,0:T(8,128)(2,1)S(1)}, bf16[672,256]{1,0:T(8,128)(2,1)S(1)}, u32[]{:S(2)}, u32[]{:S(2)}) collective-permute-start(bf16[672,256]{1,0:T(8,128)(2,1)S(1)} %slice.34), channel_id=1, source_target_pairs={{0,4},{4,8},{8,12},{12,16},{16,20},{20,24},{24,28},{28,0},{1,5},{5... | collective-permute-start | bytes 1032200 | tf_op jit(solution)/shard_map/ppermute | solution.py:41
  91.9 6.3 %query.2.refs_0_ = bf16[512,512]{1,0:T(8,128)(2,1)} custom-call(bf16[512,4096]{1,0:T(8,128)(2,1)} %get-tuple-element.12.x_ref, bf16[4096,1024]{1,0:T(8,128)(2,1)} %w_ref.3, f32[512,64]{1,0:T(8,128)} %get-tuple-element.24.refs_2_.cos, f32[512,64]{1,0:T(8,128)} %get-tuple-element.23.refs_3_.sin), custom_call_target="tpu_custom_call" | custom-call | flops 6000000000 | bytes 1048576 | tf_op jit(solution)/shard_map/query/pallas_call | solution.py:185
  98.1 0.1 collective-permute-start.23
  98.3 3.3 %collective-permute-start.22 = (bf16[256,256]{1,0:T(8,128)(2,1)S(1)}, bf16[256,256]{1,0:T(8,128)(2,1)S(1)}, u32[]{:S(2)}, u32[]{:S(2)}) collective-permute-start(bf16[256,256]{1,0:T(8,128)(2,1)S(1)} %slice.36), channel_id=1, source_target_pairs={{0,4},{4,8},{8,12},{12,16},{16,20},{20,24},{24,28},{28,0},{1,5},{5... | collective-permute-start | bytes 393224 | tf_op jit(solution)/shard_map/ppermute | solution.py:41
  101.6 0.0 copy-start.6
  101.6 1.0 copy-done.6
  102.6 30.5 %attention.1 = (bf16[512,1024]{1,0:T(8,128)(2,1)S(1)}, bf16[8,64,256]{2,1,0:T(8,128)(2,1)S(1)}, f32[512,1024]{1,0:T(8,128)S(1)}, f32[512,128]{1,0:T(8,128)S(1)}, f32[512,128]{1,0:T(8,128)S(1)}) custom-call(s32[3]{0:T(128)S(1)} %copy-done.3, s32[8]{0:T(128)S(1)} %copy-done.4, s32[8,8]{1,0:T(8,128)S(1)} %copy-done.2, bf16[512,512]{1,0:T(8,128)(2,1)S(1)} %copy-done.6, ...), custom_call_target="tpu_custom_call" | custom-call | flops 7516192768 | bytes 8388608 | tf_op jit(solution)/shard_map/attention/pallas_call | solution.py:334
  133.2 6.0 %finish.1 = bf16[512,1024]{1,0:T(8,128)(2,1)} custom-call(s32[3]{0:T(128)S(1)} %copy-done.3, s32[8]{0:T(128)S(1)} %copy-done.4, s32[8,8]{1,0:T(8,128)S(1)} %copy-done.2, bf16[512,1024]{1,0:T(8,128)(2,1)S(1)} %get-tuple-element.14.refs_0_, bf16[8,64,256]{2,1,0:T(8,128)(2,1)S(1)} %get-tuple-element.15.refs_1_, ...), custom_call_target="tpu_custom_call" | custom-call | flops 1073741824 | bytes 6291456 | tf_op jit(solution)/shard_map/finish/pallas_call | solution.py:419
  (53 shorter events, 0.2 us)
Async XLA Ops:
  0.0 8.0 %copy-start.4 = (s32[8]{0:T(128)S(1)}, s32[8]{0:T(128)}, u32[]{:S(2)}) copy-start(s32[8]{0:T(128)} %counts_ref.3) | copy-start | bytes 100
  0.0 9.2 %copy-start.2 = (s32[8,8]{1,0:T(8,128)S(1)}, s32[8,8]{1,0:T(8,128)}, u32[]{:S(2)}) copy-start(s32[8,8]{1,0:T(8,128)} %starts_ref.3) | copy-start | bytes 772
  1.0 27.4 %copy-start.9 = (bf16[64,1024]{1,0:T(8,128)(2,1)S(1)}, bf16[64,1024]{1,0:T(8,128)(2,1)}, u32[]{:S(2)}) copy-start(bf16[64,1024]{1,0:T(8,128)(2,1)} %x_ref.1) | copy-start | bytes 393220
  1.0 11.1 %collective-permute-start.2 = (bf16[128,1024]{1,0:T(8,128)(2,1)S(1)}, bf16[128,1024]{1,0:T(8,128)(2,1)S(1)}, u32[]{:S(2)}, u32[]{:S(2)}) collective-permute-start(bf16[128,1024]{1,0:T(8,128)(2,1)S(1)} %slice.24), channel_id=1, source_target_pairs={{0,3},{1,2},{2,1},{3,0},{4,7},{5,6},{6,5},{7,4},{8,11},{9,10},{10,... | collective-permute-start | bytes 786440 | tf_op jit(solution)/shard_map/ppermute | solution.py:45
  3.9 9.2 %collective-permute-start = (bf16[128,1024]{1,0:T(8,128)(2,1)S(1)}, bf16[128,1024]{1,0:T(8,128)(2,1)S(1)}, u32[]{:S(2)}, u32[]{:S(2)}) collective-permute-start(bf16[128,1024]{1,0:T(8,128)(2,1)S(1)} %slice.24), channel_id=1, source_target_pairs={{0,1},{1,0},{2,3},{3,2},{4,5},{5,4},{6,7},{7,6},{8,9},{9,8},{10,11... | collective-permute-start | bytes 786440 | tf_op jit(solution)/shard_map/ppermute | solution.py:45
  6.1 30.6 %collective-permute-start.3 = (bf16[384,1024]{1,0:T(8,128)(2,1)}, bf16[384,1024]{1,0:T(8,128)(2,1)S(1)}, u32[]{:S(2)}, u32[]{:S(2)}) collective-permute-start(bf16[384,1024]{1,0:T(8,128)(2,1)} %slice.25), channel_id=1, source_target_pairs={{0,3},{1,2},{2,1},{3,0},{4,7},{5,6},{6,5},{7,4},{8,11},{9,10},{10,... | collective-permute-start | bytes 2359304 | tf_op jit(solution)/shard_map/ppermute | solution.py:45
  7.3 31.3 %collective-permute-start.1 = (bf16[384,1024]{1,0:T(8,128)(2,1)}, bf16[384,1024]{1,0:T(8,128)(2,1)}, u32[]{:S(2)}, u32[]{:S(2)}) collective-permute-start(bf16[384,1024]{1,0:T(8,128)(2,1)} %slice.25), channel_id=1, source_target_pairs={{0,1},{1,0},{2,3},{3,2},{4,5},{5,4},{6,7},{7,6},{8,9},{9,8},{10,11... | collective-permute-start | bytes 2359304 | tf_op jit(solution)/shard_map/ppermute | solution.py:45
  12.1 1.0 copy-start.10
  13.1 0.8 copy-start.11
  15.4 13.0 %collective-permute-start.9 = (bf16[64,1024]{1,0:T(8,128)(2,1)}, bf16[64,1024]{1,0:T(8,128)(2,1)S(1)}, u32[]{:S(2)}, u32[]{:S(2)}) collective-permute-start(bf16[64,1024]{1,0:T(8,128)(2,1)} %hold.1), channel_id=1, source_target_pairs={{0,64},{32,96},{64,128},{96,160},{128,192},{160,224},{1,65},{33,97... | collective-permute-start | bytes 393224 | tf_op jit(solution)/shard_map/ppermute | solution.py:41
  18.9 9.5 %collective-permute-start.8 = (bf16[64,1024]{1,0:T(8,128)(2,1)}, bf16[64,1024]{1,0:T(8,128)(2,1)S(1)}, u32[]{:S(2)}, u32[]{:S(2)}) collective-permute-start(bf16[64,1024]{1,0:T(8,128)(2,1)} %hold.1), channel_id=1, source_target_pairs={{0,128},{32,160},{64,192},{96,224},{1,129},{33,161},{65,193},{97,2... | collective-permute-start | bytes 393224 | tf_op jit(solution)/shard_map/ppermute | solution.py:41
  23.7 4.7 %collective-permute-start.7 = (bf16[64,1024]{1,0:T(8,128)(2,1)}, bf16[64,1024]{1,0:T(8,128)(2,1)}, u32[]{:S(2)}, u32[]{:S(2)}) collective-permute-start(bf16[64,1024]{1,0:T(8,128)(2,1)} %hold.1), channel_id=1, source_target_pairs={{0,192},{32,224},{1,193},{33,225},{2,194},{34,226},{3,195},{35,227... | collective-permute-start | bytes 393224 | tf_op jit(solution)/shard_map/ppermute | solution.py:41
  27.1 9.6 %copy-start.12 = (bf16[128,1024]{1,0:T(8,128)(2,1)S(1)}, bf16[128,1024]{1,0:T(8,128)(2,1)}, u32[]{:S(2)}) copy-start(bf16[128,1024]{1,0:T(8,128)(2,1)} %copy-done.11) | copy-start | bytes 786436
  29.1 2.1 %collective-permute-start.10 = (bf16[64,1024]{1,0:T(8,128)(2,1)}, bf16[64,1024]{1,0:T(8,128)(2,1)}, u32[]{:S(2)}, u32[]{:S(2)}) collective-permute-start(bf16[64,1024]{1,0:T(8,128)(2,1)} %select_select_fusion.1), channel_id=1, source_target_pairs={{0,32},{32,0},{64,96},{96,64},{128,160},{160,128},{192,224},{224,1... | collective-permute-start | bytes 393224 | tf_op jit(solution)/shard_map/ppermute | solution.py:473
  30.6 11.8 %copy-start.7 = (bf16[4096,256]{1,0:T(8,128)(2,1)}, bf16[4096,256]{1,0:T(8,128)(2,1)S(1)}, u32[]{:S(2)}) copy-start(bf16[4096,256]{1,0:T(8,128)(2,1)S(1)} %constant_dynamic-update-slice_fusion.w_kv.refs_1_) | copy-start | bytes 6291460
  31.3 11.1 %copy-start.16 = (bf16[64,1024]{1,0:T(8,128)(2,1)}, bf16[64,1024]{1,0:T(8,128)(2,1)S(1)}, u32[]{:S(2)}) copy-start(bf16[64,1024]{1,0:T(8,128)(2,1)S(1)} %select_select_fusion.own) | copy-start | bytes 393220
  31.3 9.8 %collective-permute-start.13 = (bf16[64,1024]{1,0:T(8,128)(2,1)S(1)}, bf16[64,1024]{1,0:T(8,128)(2,1)S(1)}, u32[]{:S(2)}, u32[]{:S(2)}) collective-permute-start(bf16[64,1024]{1,0:T(8,128)(2,1)S(1)} %select_select_fusion.own), channel_id=1, source_target_pairs={{0,2},{1,3},{2,0},{3,1},{4,6},{5,7},{6,4},{7,5},{8,10},{9,11},{10,... | collective-permute-start | bytes 393224 | tf_op jit(solution)/shard_map/ppermute | solution.py:45
  33.4 9.0 %collective-permute-start.12 = (bf16[64,1024]{1,0:T(8,128)(2,1)S(1)}, bf16[64,1024]{1,0:T(8,128)(2,1)S(1)}, u32[]{:S(2)}, u32[]{:S(2)}) collective-permute-start(bf16[64,1024]{1,0:T(8,128)(2,1)S(1)} %select_select_fusion.own), channel_id=1, source_target_pairs={{0,3},{1,2},{2,1},{3,0},{4,7},{5,6},{6,5},{7,4},{8,11},{9,10},{10,... | collective-permute-start | bytes 393224 | tf_op jit(solution)/shard_map/ppermute | solution.py:45
  34.6 7.8 %collective-permute-start.11 = (bf16[64,1024]{1,0:T(8,128)(2,1)S(1)}, bf16[64,1024]{1,0:T(8,128)(2,1)S(1)}, u32[]{:S(2)}, u32[]{:S(2)}) collective-permute-start(bf16[64,1024]{1,0:T(8,128)(2,1)S(1)} %select_select_fusion.own), channel_id=1, source_target_pairs={{0,1},{1,0},{2,3},{3,2},{4,5},{5,4},{6,7},{7,6},{8,9},{9,8},{10,11... | collective-permute-start | bytes 393224 | tf_op jit(solution)/shard_map/ppermute | solution.py:45
  36.7 13.8 %copy-start.8 = (bf16[384,1024]{1,0:T(8,128)(2,1)}, bf16[384,1024]{1,0:T(8,128)(2,1)S(1)}, u32[]{:S(2)}) copy-start(bf16[384,1024]{1,0:T(8,128)(2,1)S(1)} %collective-permute-done.3.three_b) | copy-start | bytes 2359300
  36.7 17.0 %collective-permute-start.4 = (bf16[128,1024]{1,0:T(8,128)(2,1)S(1)}, bf16[128,1024]{1,0:T(8,128)(2,1)S(1)}, u32[]{:S(2)}, u32[]{:S(2)}) collective-permute-start(bf16[128,1024]{1,0:T(8,128)(2,1)S(1)} %copy-done.12), channel_id=1, source_target_pairs={{0,3},{1,2},{2,1},{3,0},{4,7},{5,6},{6,5},{7,4},{8,11},{9,10},{10,... | collective-permute-start | bytes 786440 | tf_op jit(solution)/shard_map/ppermute | solution.py:45
  38.6 15.1 %collective-permute-start.6 = (bf16[256,1024]{1,0:T(8,128)(2,1)S(1)}, bf16[256,1024]{1,0:T(8,128)(2,1)S(1)}, u32[]{:S(2)}, u32[]{:S(2)}) collective-permute-start(bf16[256,1024]{1,0:T(8,128)(2,1)S(1)} %slice.33), channel_id=1, source_target_pairs={{0,1},{1,0},{2,3},{3,2},{4,5},{5,4},{6,7},{7,6},{8,9},{9,8},{10,11... | collective-permute-start | bytes 1572872 | tf_op jit(solution)/shard_map/ppermute | solution.py:45
  41.1 1.3 copy-start.17
  41.1 12.6 %collective-permute-start.5 = (bf16[128,1024]{1,0:T(8,128)(2,1)S(1)}, bf16[128,1024]{1,0:T(8,128)(2,1)S(1)}, u32[]{:S(2)}, u32[]{:S(2)}) collective-permute-start(bf16[128,1024]{1,0:T(8,128)(2,1)S(1)} %slice.32), channel_id=1, source_target_pairs={{0,3},{1,2},{2,1},{3,0},{4,7},{5,6},{6,5},{7,4},{8,11},{9,10},{10,... | collective-permute-start | bytes 786440 | tf_op jit(solution)/shard_map/ppermute | solution.py:45
  42.4 0.6 copy-start.18
  42.4 0.7 copy-start.19
  50.5 12.6 %collective-permute-start.18 = (bf16[320,256]{1,0:T(8,128)(2,1)}, bf16[320,256]{1,0:T(8,128)(2,1)S(1)}, u32[]{:S(2)}, u32[]{:S(2)}) collective-permute-start(bf16[320,256]{1,0:T(8,128)(2,1)} %project_image.1.refs_4_.refs_2_), channel_id=1, source_target_pairs={{0,28},{4,0},{8,4},{12,8},{16,12},{20,16},{24,20},{28,24},{1,29},{... | collective-permute-start | bytes 491528 | tf_op jit(solution)/shard_map/ppermute | solution.py:41
  51.5 11.6 %collective-permute-start.14 = (bf16[320,256]{1,0:T(8,128)(2,1)}, bf16[320,256]{1,0:T(8,128)(2,1)S(1)}, u32[]{:S(2)}, u32[]{:S(2)}) collective-permute-start(bf16[320,256]{1,0:T(8,128)(2,1)} %project_image.1.refs_4_.refs_2_), channel_id=1, source_target_pairs={{0,4},{4,8},{8,12},{12,16},{16,20},{20,24},{24,28},{28,0},{1,5},{5... | collective-permute-start | bytes 491528 | tf_op jit(solution)/shard_map/ppermute | solution.py:41
  53.8 0.7 copy-start.14
  53.8 0.8 copy-start.15
  54.6 0.8 copy-start.13
  64.2 12.6 %collective-permute-start.19 = (bf16[832,256]{1,0:T(8,128)(2,1)S(1)}, bf16[832,256]{1,0:T(8,128)(2,1)S(1)}, u32[]{:S(2)}, u32[]{:S(2)}) collective-permute-start(bf16[832,256]{1,0:T(8,128)(2,1)S(1)} %get-tuple-element.21), channel_id=1, source_target_pairs={{0,28},{4,0},{8,4},{12,8},{16,12},{20,16},{24,20},{28,24},{1,29},{... | collective-permute-start | bytes 1277960 | tf_op jit(solution)/shard_map/ppermute | solution.py:41
  64.8 12.0 %collective-permute-start.15 = (bf16[832,256]{1,0:T(8,128)(2,1)S(1)}, bf16[832,256]{1,0:T(8,128)(2,1)S(1)}, u32[]{:S(2)}, u32[]{:S(2)}) collective-permute-start(bf16[832,256]{1,0:T(8,128)(2,1)S(1)} %get-tuple-element.22), channel_id=1, source_target_pairs={{0,4},{4,8},{8,12},{12,16},{16,20},{20,24},{24,28},{28,0},{1,5},{5... | collective-permute-start | bytes 1277960 | tf_op jit(solution)/shard_map/ppermute | solution.py:41
  76.8 11.6 %collective-permute-start.20 = (bf16[832,256]{1,0:T(8,128)(2,1)S(1)}, bf16[832,256]{1,0:T(8,128)(2,1)S(1)}, u32[]{:S(2)}, u32[]{:S(2)}) collective-permute-start(bf16[832,256]{1,0:T(8,128)(2,1)S(1)} %collective-permute-done.19.refs_9_), channel_id=1, source_target_pairs={{0,28},{4,0},{8,4},{12,8},{16,12},{20,16},{24,20},{28,24},{1,29},{... | collective-permute-start | bytes 1277960 | tf_op jit(solution)/shard_map/ppermute | solution.py:41
  76.8 11.7 %collective-permute-start.16 = (bf16[832,256]{1,0:T(8,128)(2,1)S(1)}, bf16[832,256]{1,0:T(8,128)(2,1)S(1)}, u32[]{:S(2)}, u32[]{:S(2)}) collective-permute-start(bf16[832,256]{1,0:T(8,128)(2,1)S(1)} %collective-permute-done.15.refs_5_), channel_id=1, source_target_pairs={{0,4},{4,8},{8,12},{12,16},{16,20},{20,24},{24,28},{28,0},{1,5},{5... | collective-permute-start | bytes 1277960 | tf_op jit(solution)/shard_map/ppermute | solution.py:41
  88.4 9.7 %collective-permute-start.21 = (bf16[672,256]{1,0:T(8,128)(2,1)S(1)}, bf16[672,256]{1,0:T(8,128)(2,1)S(1)}, u32[]{:S(2)}, u32[]{:S(2)}) collective-permute-start(bf16[672,256]{1,0:T(8,128)(2,1)S(1)} %slice.35), channel_id=1, source_target_pairs={{0,28},{4,0},{8,4},{12,8},{16,12},{20,16},{24,20},{28,24},{1,29},{... | collective-permute-start | bytes 1032200 | tf_op jit(solution)/shard_map/ppermute | solution.py:41
  88.5 13.0 %copy-start = (bf16[512,256]{1,0:T(8,128)(2,1)S(1)}, bf16[512,256]{1,0:T(8,128)(2,1)}, u32[]{:S(2)}) copy-start(bf16[512,256]{1,0:T(8,128)(2,1)} %get-tuple-element.13.refs_3_) | copy-start | bytes 786436
  88.5 13.0 %copy-start.1 = (bf16[320,256]{1,0:T(8,128)(2,1)S(1)}, bf16[320,256]{1,0:T(8,128)(2,1)}, u32[]{:S(2)}) copy-start(bf16[320,256]{1,0:T(8,128)(2,1)} %project_image.1.refs_4_.refs_2_) | copy-start | bytes 491524
  88.5 13.0 %copy-start.3 = (s32[3]{0:T(128)S(1)}, s32[3]{0:T(128)}, u32[]{:S(2)}) copy-start(s32[3]{0:T(128)} %pad_add_fusion.refs_2_.ids_ref) | copy-start | bytes 40
  88.6 13.0 %copy-start.5 = (bf16[512,512]{1,0:T(8,128)(2,1)S(1)}, bf16[512,512]{1,0:T(8,128)(2,1)}, u32[]{:S(2)}) copy-start(bf16[512,512]{1,0:T(8,128)(2,1)} %query.3.refs_1_) | copy-start | bytes 1572868
  88.6 9.7 %collective-permute-start.17 = (bf16[672,256]{1,0:T(8,128)(2,1)S(1)}, bf16[672,256]{1,0:T(8,128)(2,1)S(1)}, u32[]{:S(2)}, u32[]{:S(2)}) collective-permute-start(bf16[672,256]{1,0:T(8,128)(2,1)S(1)} %slice.34), channel_id=1, source_target_pairs={{0,4},{4,8},{8,12},{12,16},{16,20},{20,24},{24,28},{28,0},{1,5},{5... | collective-permute-start | bytes 1032200 | tf_op jit(solution)/shard_map/ppermute | solution.py:41
  98.1 35.0 %collective-permute-start.23 = (bf16[256,256]{1,0:T(8,128)(2,1)S(1)}, bf16[256,256]{1,0:T(8,128)(2,1)S(1)}, u32[]{:S(2)}, u32[]{:S(2)}) collective-permute-start(bf16[256,256]{1,0:T(8,128)(2,1)S(1)} %slice.37), channel_id=1, source_target_pairs={{0,28},{4,0},{8,4},{12,8},{16,12},{20,16},{24,20},{28,24},{1,29},{... | collective-permute-start | bytes 393224 | tf_op jit(solution)/shard_map/ppermute | solution.py:41
  98.3 34.9 %collective-permute-start.22 = (bf16[256,256]{1,0:T(8,128)(2,1)S(1)}, bf16[256,256]{1,0:T(8,128)(2,1)S(1)}, u32[]{:S(2)}, u32[]{:S(2)}) collective-permute-start(bf16[256,256]{1,0:T(8,128)(2,1)S(1)} %slice.36), channel_id=1, source_target_pairs={{0,4},{4,8},{8,12},{12,16},{16,20},{20,24},{24,28},{28,0},{1,5},{5... | collective-permute-start | bytes 393224 | tf_op jit(solution)/shard_map/ppermute | solution.py:41
  101.6 1.0 copy-start.6

commit v11 on v10

--- a/solution.py
+++ b/solution.py
@@ -124,17 +124,28 @@
 
 def text_kernel(ids_ref, own, one_a, one_b, three_a, three_b, two_a, two_b, two_c, *refs):
     gain, w_kv, cos, sin = refs[:4]
-    normed_ref, out_ref = refs[-2:]
+    normed_ref, out_ref, held = refs[-3:]
     rows = own.shape[0]
-    for n, others in enumerate(
-        ((one_a, three_a, two_a), (one_b, three_b, two_b), (one_b, three_b, two_c))
-    ):
-        @pl.when(jnp.minimum(pl.program_id(0), 2) == n)
-        def _():
-            pieces = [own[...]] + [other[...] for other in others]
-            normalise(ids_ref[0], gain, pieces, normed_ref, slice(0, rows))
-
-    write_key_value(normed_ref[...], w_kv, cos[...], sin[...], out_ref, slice(0, rows))
+    step = pl.program_id(0)
+    last = pl.num_programs(0) - 1
+    slot = lax.rem(step, 2)
+
+    def phase(do_norm, do_product):
+        if do_norm:
+            pieces = [
+                own[...],
+                jnp.where(step == 0, one_a[...], one_b[...]),
+                jnp.where(step == 0, three_a[...], three_b[...]),
+                jnp.where(step == 0, two_a[...], jnp.where(step == 1, two_b[...], two_c[...])),
+            ]
+            normalise(ids_ref[0], gain, pieces, held.at[slot], slice(0, rows))
+            normed_ref[...] = held[slot]
+        if do_product:
+            write_key_value(held[1 - slot], w_kv, cos[...], sin[...], out_ref, slice(0, rows))
+
+    pl.when(step == 0)(lambda: phase(True, False))
+    pl.when((step > 0) & (step < last))(lambda: phase(True, True))
+    pl.when(step == last)(lambda: phase(False, True))
 
 
 def project_text(ids, arrays, gain, w_kv, tables, after):
@@ -143,27 +154,30 @@
     tile = rows // steps
 
     def block(skipped):
-        return pl.BlockSpec((tile, D // 4), lambda r: (jnp.maximum(r - skipped, 0), 0))
+        return pl.BlockSpec(
+            (tile, D // 4), lambda r: (jnp.clip(r - skipped, 0, steps - 1 - skipped), 0)
+        )
 
     whole = pl.BlockSpec(memory_space=VMEM)
     only = pl.BlockSpec((tile, D // 4), lambda r: (0, 0))
-    table = pl.BlockSpec((tile, HD // 2), lambda r: (r, 0))
+    table = pl.BlockSpec((tile, HD // 2), lambda r: (jnp.maximum(r - 1, 0), 0))
     return pl.pallas_call(
         text_kernel,
         out_shape=[
             jax.ShapeDtypeStruct((rows, D), BF16),
             jax.ShapeDtypeStruct((rows, 2 * HD), BF16),
         ],
-        grid=(steps,),
+        grid=(steps + 1,),
         in_specs=[pl.BlockSpec(memory_space=SMEM)]
         + [block(0), only, block(1), only, block(1), only, only, block(2)]
         + [whole] * 2
         + [table] * 2
         + [pl.BlockSpec(memory_space=pl.ANY)] * len(after),
         out_specs=[
-            pl.BlockSpec((tile, D), lambda r: (r, 0)),
-            pl.BlockSpec((tile, 2 * HD), lambda r: (r, 0)),
+            pl.BlockSpec((tile, D), lambda r: (jnp.minimum(r, steps - 1), 0)),
+            pl.BlockSpec((tile, 2 * HD), lambda r: (jnp.maximum(r - 1, 0), 0)),
         ],
+        scratch_shapes=[pltpu.VMEM((2, tile, D), BF16)],
         compiler_params=pltpu.CompilerParams(vmem_limit_bytes=58 * 2**20),
         cost_estimate=pl.CostEstimate(flops=0, bytes_accessed=0, transcendentals=0),
         name="project_text",
@@ -243,26 +257,33 @@
     ]
     for copy in copies:
         copy.start()
-    for copy in copies:
+    for copy in copies[:-3]:
         copy.wait()
-    for c, start in image_starts_of(ids_ref, counts_ref, starts_ref):
-        img_kv[c] = img_buf[c, :IMG_TOK, :]
-        shard, row = start >> shift_by, start & (tok - 1)
-        distance = ctx - shard
-
-        @pl.when((start >= 0) & (distance >= 0) & (distance != 4))
-        def _():
-            place = jnp.where(distance > 4, distance - 1, distance) * tok + row
-            kv_buf[pl.ds(pl.multiple_of(place, IMG_TOK), IMG_TOK), :] = img_buf[c, :IMG_TOK, :]
-
-        @pl.when((start >= 0) & (distance == 0))
-        def _():
-            rows = pl.ds(pl.multiple_of(row, IMG_TOK), IMG_TOK)
-            for n in range(heads // 2):
-                q_buf[rows, n * 2 * HD : (n + 1) * 2 * HD] = img_buf[
-                    c, IMG_TOK * (n + 1) : IMG_TOK * (n + 2), :
-                ]
-
+
+    def place_images(near):
+        for c, start in image_starts_of(ids_ref, counts_ref, starts_ref):
+            shard, row = start >> shift_by, start & (tok - 1)
+            distance = ctx - shard
+            taken = (distance >= 0) & (distance < 4) if near else distance > 4
+
+            @pl.when((start >= 0) & taken)
+            def _():
+                place = (distance if near else distance - 1) * tok + row
+                rows = pl.ds(pl.multiple_of(place, IMG_TOK), IMG_TOK)
+                kv_buf[rows, :] = img_buf[c, :IMG_TOK, :]
+
+            if near:
+                img_kv[c] = img_buf[c, :IMG_TOK, :]
+
+                @pl.when((start >= 0) & (distance == 0))
+                def _():
+                    rows = pl.ds(pl.multiple_of(row, IMG_TOK), IMG_TOK)
+                    for n in range(heads // 2):
+                        q_buf[rows, n * 2 * HD : (n + 1) * 2 * HD] = img_buf[
+                            c, IMG_TOK * (n + 1) : IMG_TOK * (n + 2), :
+                        ]
+
+    place_images(True)
     max_out[...] = jnp.zeros((tok, HD), F32)
     sum_out[...] = jnp.zeros((tok, HD), F32)
 
@@ -311,7 +332,15 @@
         if do_mix:
             sum_buf[...] = jnp.zeros((tok, HD), F32)
             acc_buf[...] = jnp.zeros((tok, HD), F32)
-        pl.loop(0, jnp.where(ctx * tok + tok > BLOCK, 2, 1))(block)
+        blocks = jnp.where(ctx * tok + tok > BLOCK, 2, 1)
+        if do_mix:
+            pl.loop(0, blocks)(block)
+        else:
+            block(jnp.int32(0))
+            for copy in copies[-3:]:
+                copy.wait()
+            place_images(False)
+            pl.loop(1, blocks)(block)
         if do_score:
             top = jnp.max(max_buf[slot], axis=1, keepdims=True) * factor
             max_buf[slot] = jnp.broadcast_to(top, (tok, HD))
@@ -413,7 +442,7 @@
 
 
 def finish(tok, heads, scalars, q_all, img_kv, lower, upper, state):
-    width = 2 * HD
+    width = 4 * HD
     whole = pl.BlockSpec(memory_space=VMEM)
     block = pl.BlockSpec((tok, width), lambda n: (0, n))
     return pl.pallas_call(
@@ -467,7 +496,7 @@
     group_a, group_b = text_rows[:quarter], text_rows[quarter:]
     one_a, three_a = first_hop(group_a)
     one_b, three_b = first_hop(group_b)
-    leaving = hold(visual_rows, (one_a, three_a, ids, *image_tables))
+    leaving = hold(visual_rows, (one_a, three_a, ids, *image_tables, *text_tables))
     routed = [visual_rows] + [shift(leaving, "dp", 2 * d, False) for d in (1, 2, 3)]
     for_other = choose(its_distance, routed)
     from_other = lax.ppermute(for_other, "dp", [(i, i ^ 1) for i in range(SHARDS)])

time: 140 us -> 151 us (1.079)
  waiting for transfers between devices: 12.3 us -> 24.1 us
    ppermute x10, waiting for transfers between devices: 0.98 us -> 11.7 us  [exchange(): return lax.ppermute(x, 'mp', [(i, i ^ mask) for i in range(4)])]
    unnamed x41 -> x45, local copies, waits for them, and re-layouts: 5.46 us -> 5.46 us
  transfers between devices with their start and end apart: 24 -> 24, of which waited for: 3 -> 6; matrix products, arithmetic and copies ran while one was open for 9% -> 8% of each run, Pallas kernels for 43% -> 39%
where the time goes in v11:
time: 151 us
  Pallas kernels  65.8 us (44%)
  starting transfers between devices  39.4 us (26%)
  waiting for transfers between devices  24.1 us (16%)
  local copies, waits for them, and re-layouts  10 us (7%)
  other arithmetic  8.51 us (6%)
  between operations  2.96 us (2%)
    pallas_call x1, Pallas kernels, attention(): pl.pallas_call(functools.partial(attention_kernel, tok, heads), out_shape...  30 us
    ppermute x13, starting transfers between devices, shift(): return lax.ppermute(x, axis, pairs)  26.6 us
    ppermute x10, starting transfers between devices, exchange(): return lax.ppermute(x, 'mp', [(i, i ^ mask) for i in range(4)])  12.8 us
    pallas_call x2, Pallas kernels, query(): pl.pallas_call(query_kernel, out_shape=jax.ShapeDtypeStruct((rows, column...  12.6 us
    ppermute x13, waiting for transfers between devices, shift(): return lax.ppermute(x, axis, pairs)  12.5 us
    ppermute x10, waiting for transfers between devices, exchange(): return lax.ppermute(x, 'mp', [(i, i ^ mask) for i in range(4)])  11.7 us
    pallas_call x1, Pallas kernels, project_text(): pl.pallas_call(text_kernel, out_shape=[jax.ShapeDtypeStruct((rows, D), BF...  8.63 us
    pallas_call x1, Pallas kernels, project_image(): pl.pallas_call(image_kernel, out_shape=jax.ShapeDtypeStruct(((1 + steps)...  7.42 us
  transfers between devices with their start and end apart: 24, of which 6 were waited for; matrix products, arithmetic and copies ran while one was open for 8% of the time, Pallas kernels for 39%

profile of v11, /device:TPU:224, one launch (start us, length us, event | category | flops | bytes accessed | tf_op | source)
XLA Modules:
  0.0 150.8 jit_solution(15872067493273673235)
XLA Ops:
  0.0 1.1 slice.24
  1.1 2.8 %collective-permute-start.2 = (bf16[128,1024]{1,0:T(8,128)(2,1)S(1)}, bf16[128,1024]{1,0:T(8,128)(2,1)S(1)}, u32[]{:S(2)}, u32[]{:S(2)}) collective-permute-start(bf16[128,1024]{1,0:T(8,128)(2,1)S(1)} %slice.24), channel_id=1, source_target_pairs={{0,3},{1,2},{2,1},{3,0},{4,7},{5,6},{6,5},{7,4},{8,11},{9,10},{10,... | collective-permute-start | bytes 786440 | tf_op jit(solution)/shard_map/ppermute | solution.py:45
  3.9 0.2 collective-permute-start
  4.2 1.4 fusion.1
  6.1 1.5 select_reduce_fusion
  7.6 0.6 add_convert_fusion.1
  8.2 0.8 multiply_sine_fusion.1
  9.0 0.6 pad_add_fusion.refs_2_.ids_ref
  9.6 1.8 %multiply_sine_fusion = (f32[512,64]{1,0:T(8,128)}, f32[512,64]{1,0:T(8,128)}) fusion(f32[64]{0:T(128)S(1)} %multiply_exponential_fusion, f32[512]{0:T(512)S(1)} %add_convert_fusion), kind=kLoop, calls=%fused_computation.2 | loop fusion | flops 32768 | bytes 264448 | tf_op jit(solution)/shard_map/sin | solution.py:30
  11.4 0.3 collective-permute-done.refs_0_.one_a
  11.7 0.5 copy-done.11
  12.1 0.2 copy-done.12
  12.4 1.6 %hold.1 = bf16[64,1024]{1,0:T(8,128)(2,1)} custom-call(bf16[64,1024]{1,0:T(8,128)(2,1)} %x_ref.1, bf16[128,1024]{1,0:T(8,128)(2,1)} %copy-done.12, bf16[128,1024]{1,0:T(8,128)(2,1)} %copy-done.11, s32[3]{0:T(128)} %pad_add_fusion.refs_2_.ids_ref, f32[64,64]{1,0:T(8,128)} %get-tuple-element.26.refs_3_.cos, f32[64,64]{1,0:T(8,128)} %get-tuple-element.25.refs_4_.sin, ...), custom_call_target="tpu_custom_call" | custom-call | tf_op jit(solution)/shard_map/hold/pallas_call | solution.py:115
  14.0 3.5 %collective-permute-start.9 = (bf16[64,1024]{1,0:T(8,128)(2,1)}, bf16[64,1024]{1,0:T(8,128)(2,1)S(1)}, u32[]{:S(2)}, u32[]{:S(2)}) collective-permute-start(bf16[64,1024]{1,0:T(8,128)(2,1)} %hold.1), channel_id=1, source_target_pairs={{0,64},{32,96},{64,128},{96,160},{128,192},{160,224},{1,65},{33,97... | collective-permute-start | bytes 393224 | tf_op jit(solution)/shard_map/ppermute | solution.py:41
  17.4 4.8 %collective-permute-start.8 = (bf16[64,1024]{1,0:T(8,128)(2,1)}, bf16[64,1024]{1,0:T(8,128)(2,1)S(1)}, u32[]{:S(2)}, u32[]{:S(2)}) collective-permute-start(bf16[64,1024]{1,0:T(8,128)(2,1)} %hold.1), channel_id=1, source_target_pairs={{0,128},{32,160},{64,192},{96,224},{1,129},{33,161},{65,193},{97,2... | collective-permute-start | bytes 393224 | tf_op jit(solution)/shard_map/ppermute | solution.py:41
  22.3 1.3 collective-permute-start.7
  23.6 0.9 slice.25
  24.5 1.6 %collective-permute-start.3 = (bf16[384,1024]{1,0:T(8,128)(2,1)}, bf16[384,1024]{1,0:T(8,128)(2,1)S(1)}, u32[]{:S(2)}, u32[]{:S(2)}) collective-permute-start(bf16[384,1024]{1,0:T(8,128)(2,1)} %slice.25), channel_id=1, source_target_pairs={{0,3},{1,2},{2,1},{3,0},{4,7},{5,6},{6,5},{7,4},{8,11},{9,10},{10,... | collective-permute-start | bytes 2359304 | tf_op jit(solution)/shard_map/ppermute | solution.py:45
  26.1 0.1 collective-permute-start.1
  27.6 0.0 collective-permute-done.9
  27.6 0.7 select_select_fusion.1
  28.3 1.4 constant_dynamic-update-slice_fusion.1
  30.4 0.0 collective-permute-done.10
  30.4 3.1 %collective-permute-start.13 = (bf16[64,1024]{1,0:T(8,128)(2,1)S(1)}, bf16[64,1024]{1,0:T(8,128)(2,1)S(1)}, u32[]{:S(2)}, u32[]{:S(2)}) collective-permute-start(bf16[64,1024]{1,0:T(8,128)(2,1)S(1)} %select_select_fusion.own), channel_id=1, source_target_pairs={{0,2},{1,3},{2,0},{3,1},{4,6},{5,7},{6,4},{7,5},{8,10},{9,11},{10,... | collective-permute-start | bytes 393224 | tf_op jit(solution)/shard_map/ppermute | solution.py:45
  33.6 1.6 %collective-permute-start.12 = (bf16[64,1024]{1,0:T(8,128)(2,1)S(1)}, bf16[64,1024]{1,0:T(8,128)(2,1)S(1)}, u32[]{:S(2)}, u32[]{:S(2)}) collective-permute-start(bf16[64,1024]{1,0:T(8,128)(2,1)S(1)} %select_select_fusion.own), channel_id=1, source_target_pairs={{0,3},{1,2},{2,1},{3,0},{4,7},{5,6},{6,5},{7,4},{8,11},{9,10},{10,... | collective-permute-start | bytes 393224 | tf_op jit(solution)/shard_map/ppermute | solution.py:45
  35.2 1.5 constant_dynamic-update-slice_fusion.w_kv.refs_1_
  36.7 11.2 %collective-permute-done.3.three_b = bf16[384,1024]{1,0:T(8,128)(2,1)S(1)} collective-permute-done((bf16[384,1024]{1,0:T(8,128)(2,1)}, bf16[384,1024]{1,0:T(8,128)(2,1)S(1)}, u32[]{:S(2)}, u32[]{:S(2)}) %collective-permute-start.3) | collective-permute-done | bytes 786464 | tf_op jit(solution)/shard_map/ppermute | solution.py:45
  47.8 1.6 %collective-permute-start.4 = (bf16[128,1024]{1,0:T(8,128)(2,1)S(1)}, bf16[128,1024]{1,0:T(8,128)(2,1)S(1)}, u32[]{:S(2)}, u32[]{:S(2)}) collective-permute-start(bf16[128,1024]{1,0:T(8,128)(2,1)S(1)} %copy-done.13), channel_id=1, source_target_pairs={{0,3},{1,2},{2,1},{3,0},{4,7},{5,6},{6,5},{7,4},{8,11},{9,10},{10,... | collective-permute-start | bytes 786440 | tf_op jit(solution)/shard_map/ppermute | solution.py:45
  49.5 0.0 collective-permute-done.1.one_b
  49.5 0.1 collective-permute-start.6
  49.6 1.0 slice.32
  50.5 0.1 collective-permute-done.13.two
  50.7 1.6 %collective-permute-start.5 = (bf16[128,1024]{1,0:T(8,128)(2,1)S(1)}, bf16[128,1024]{1,0:T(8,128)(2,1)S(1)}, u32[]{:S(2)}, u32[]{:S(2)}) collective-permute-start(bf16[128,1024]{1,0:T(8,128)(2,1)S(1)} %slice.32), channel_id=1, source_target_pairs={{0,3},{1,2},{2,1},{3,0},{4,7},{5,6},{6,5},{7,4},{8,11},{9,10},{10,... | collective-permute-start | bytes 786440 | tf_op jit(solution)/shard_map/ppermute | solution.py:45
  52.3 0.0 collective-permute-done.12.three
  52.3 0.1 collective-permute-done.11.one
  52.4 0.5 copy-done.20
  52.9 0.1 copy-done.21
  53.1 7.4 %project_image.1.refs_4_.refs_2_ = bf16[320,256]{1,0:T(8,128)(2,1)} custom-call(s32[3]{0:T(128)} %pad_add_fusion.refs_2_.ids_ref, bf16[64,1024]{1,0:T(8,128)(2,1)} %copy-done.18, bf16[64,1024]{1,0:T(8,128)(2,1)} %copy-done.21, bf16[64,1024]{1,0:T(8,128)(2,1)} %copy-done.20, bf16[64,1024]{1,0:T(8,128)(2,1)} %copy-done.19, f32[1,4096]{1,0:T(1,128)} %bitcast.4, ...), custom_call_target="tpu_custom_call" | custom-call | flops 8000000000 | bytes 10485760 | tf_op jit(solution)/shard_map/project_image/pallas_call | solution.py:92
  60.5 1.0 collective-permute-start.18
  61.5 2.2 %collective-permute-start.14 = (bf16[320,256]{1,0:T(8,128)(2,1)}, bf16[320,256]{1,0:T(8,128)(2,1)S(1)}, u32[]{:S(2)}, u32[]{:S(2)}) collective-permute-start(bf16[320,256]{1,0:T(8,128)(2,1)} %project_image.1.refs_4_.refs_2_), channel_id=1, source_target_pairs={{0,4},{4,8},{8,12},{12,16},{16,20},{20,24},{24,28},{28,0},{1,5},{5... | collective-permute-start | bytes 491528 | tf_op jit(solution)/shard_map/ppermute | solution.py:41
  63.7 0.0 collective-permute-done.4.two_a
  63.8 0.0 collective-permute-done.6.two_c
  63.8 0.7 copy-done.16
  64.5 0.1 copy-done.17
  64.5 0.8 copy-done.15
  65.3 8.6 %project_text.1 = (bf16[512,4096]{1,0:T(8,128)(2,1)}, bf16[512,256]{1,0:T(8,128)(2,1)}) custom-call(s32[3]{0:T(128)} %pad_add_fusion.refs_2_.ids_ref, bf16[512,1024]{1,0:T(8,128)(2,1)} %own.1, bf16[128,1024]{1,0:T(8,128)(2,1)} %copy-done.12, bf16[384,1024]{1,0:T(8,128)(2,1)} %collective-permute-done.1.one_b, bf16[128,1024]{1,0:T(8,128)(2,1)} %copy-done.11, ...), custom_call_target="tpu_custom_call" | custom-call | tf_op jit(solution)/shard_map/project_text/pallas_call | solution.py:164
  74.0 1.1 pad_maximum_fusion.1
  75.1 0.1 collective-permute-start.19
  75.2 3.2 %collective-permute-start.15 = (bf16[832,256]{1,0:T(8,128)(2,1)S(1)}, bf16[832,256]{1,0:T(8,128)(2,1)S(1)}, u32[]{:S(2)}, u32[]{:S(2)}) collective-permute-start(bf16[832,256]{1,0:T(8,128)(2,1)S(1)} %get-tuple-element.22), channel_id=1, source_target_pairs={{0,4},{4,8},{8,12},{12,16},{16,20},{20,24},{24,28},{28,0},{1,5},{5... | collective-permute-start | bytes 1277960 | tf_op jit(solution)/shard_map/ppermute | solution.py:41
  78.4 9.3 %collective-permute-done.19.refs_9_ = bf16[832,256]{1,0:T(8,128)(2,1)S(1)} collective-permute-done((bf16[832,256]{1,0:T(8,128)(2,1)S(1)}, bf16[832,256]{1,0:T(8,128)(2,1)S(1)}, u32[]{:S(2)}, u32[]{:S(2)}) %collective-permute-start.19) | collective-permute-done | bytes 426016 | tf_op jit(solution)/shard_map/ppermute | solution.py:41
  87.7 3.5 %collective-permute-start.16 = (bf16[832,256]{1,0:T(8,128)(2,1)S(1)}, bf16[832,256]{1,0:T(8,128)(2,1)S(1)}, u32[]{:S(2)}, u32[]{:S(2)}) collective-permute-start(bf16[832,256]{1,0:T(8,128)(2,1)S(1)} %collective-permute-done.15.refs_5_), channel_id=1, source_target_pairs={{0,4},{4,8},{8,12},{12,16},{16,20},{20,24},{24,28},{28,0},{1,5},{5... | collective-permute-start | bytes 1277960 | tf_op jit(solution)/shard_map/ppermute | solution.py:41
  91.2 6.3 %query.3.refs_1_ = bf16[512,512]{1,0:T(8,128)(2,1)} custom-call(bf16[512,4096]{1,0:T(8,128)(2,1)} %get-tuple-element.12.x_ref, bf16[4096,1024]{1,0:T(8,128)(2,1)} %w_ref.3, f32[512,64]{1,0:T(8,128)} %get-tuple-element.24.refs_5_.refs_2_.cos, f32[512,64]{1,0:T(8,128)} %get-tuple-element.23.refs_6_.refs_3_.sin), custom_call_target="tpu_custom_call" | custom-call | flops 6000000000 | bytes 1048576 | tf_op jit(solution)/shard_map/query/pallas_call | solution.py:199
  97.5 3.2 %collective-permute-done.20.refs_10_ = bf16[832,256]{1,0:T(8,128)(2,1)S(1)} collective-permute-done((bf16[832,256]{1,0:T(8,128)(2,1)S(1)}, bf16[832,256]{1,0:T(8,128)(2,1)S(1)}, u32[]{:S(2)}, u32[]{:S(2)}) %collective-permute-start.20) | collective-permute-done | bytes 426016 | tf_op jit(solution)/shard_map/ppermute | solution.py:41
  100.7 0.1 collective-permute-start.21
  100.9 0.0 copy-start.2
  100.9 0.0 copy-start.4
  100.9 3.5 %collective-permute-start.17 = (bf16[672,256]{1,0:T(8,128)(2,1)S(1)}, bf16[672,256]{1,0:T(8,128)(2,1)S(1)}, u32[]{:S(2)}, u32[]{:S(2)}) collective-permute-start(bf16[672,256]{1,0:T(8,128)(2,1)S(1)} %slice.34), channel_id=1, source_target_pairs={{0,4},{4,8},{8,12},{12,16},{16,20},{20,24},{24,28},{28,0},{1,5},{5... | collective-permute-start | bytes 1032200 | tf_op jit(solution)/shard_map/ppermute | solution.py:41
  104.4 6.3 %query.2.refs_0_ = bf16[512,512]{1,0:T(8,128)(2,1)} custom-call(bf16[512,4096]{1,0:T(8,128)(2,1)} %get-tuple-element.12.x_ref, bf16[4096,1024]{1,0:T(8,128)(2,1)} %w_ref.3, f32[512,64]{1,0:T(8,128)} %get-tuple-element.24.refs_5_.refs_2_.cos, f32[512,64]{1,0:T(8,128)} %get-tuple-element.23.refs_6_.refs_3_.sin), custom_call_target="tpu_custom_call" | custom-call | flops 6000000000 | bytes 1048576 | tf_op jit(solution)/shard_map/query/pallas_call | solution.py:199
  110.7 0.1 collective-permute-start.23
  110.8 3.3 %collective-permute-start.22 = (bf16[256,256]{1,0:T(8,128)(2,1)S(1)}, bf16[256,256]{1,0:T(8,128)(2,1)S(1)}, u32[]{:S(2)}, u32[]{:S(2)}) collective-permute-start(bf16[256,256]{1,0:T(8,128)(2,1)S(1)} %slice.36), channel_id=1, source_target_pairs={{0,4},{4,8},{8,12},{12,16},{16,20},{20,24},{24,28},{28,0},{1,5},{5... | collective-permute-start | bytes 393224 | tf_op jit(solution)/shard_map/ppermute | solution.py:41
  114.2 0.0 copy-start.6
  114.2 1.0 copy-done.6
  115.2 30.0 %attention.1 = (bf16[512,1024]{1,0:T(8,128)(2,1)S(1)}, bf16[8,64,256]{2,1,0:T(8,128)(2,1)S(1)}, f32[512,1024]{1,0:T(8,128)S(1)}, f32[512,128]{1,0:T(8,128)S(1)}, f32[512,128]{1,0:T(8,128)S(1)}) custom-call(s32[3]{0:T(128)S(1)} %copy-done.3, s32[8]{0:T(128)S(1)} %copy-done.4, s32[8,8]{1,0:T(8,128)S(1)} %copy-done.2, bf16[512,512]{1,0:T(8,128)(2,1)S(1)} %copy-done.6, ...), custom_call_target="tpu_custom_call" | custom-call | flops 7516192768 | bytes 8388608 | tf_op jit(solution)/shard_map/attention/pallas_call | solution.py:363
  145.2 5.6 %finish.1 = bf16[512,1024]{1,0:T(8,128)(2,1)} custom-call(s32[3]{0:T(128)S(1)} %copy-done.3, s32[8]{0:T(128)S(1)} %copy-done.4, s32[8,8]{1,0:T(8,128)S(1)} %copy-done.2, bf16[512,1024]{1,0:T(8,128)(2,1)S(1)} %get-tuple-element.14.refs_0_, bf16[8,64,256]{2,1,0:T(8,128)(2,1)S(1)} %get-tuple-element.15.refs_1_, ...), custom_call_target="tpu_custom_call" | custom-call | flops 1073741824 | bytes 6291456 | tf_op jit(solution)/shard_map/finish/pallas_call | solution.py:448
  (57 shorter events, 0.3 us)
Async XLA Ops:
  0.0 23.6 %copy-start.8 = (bf16[512,1024]{1,0:T(8,128)(2,1)S(1)}, bf16[512,1024]{1,0:T(8,128)(2,1)}, u32[]{:S(2)}) copy-start(bf16[512,1024]{1,0:T(8,128)(2,1)} %own.1) | copy-start | bytes 3145732
  0.0 27.6 %copy-start.10 = (bf16[64,1024]{1,0:T(8,128)(2,1)S(1)}, bf16[64,1024]{1,0:T(8,128)(2,1)}, u32[]{:S(2)}) copy-start(bf16[64,1024]{1,0:T(8,128)(2,1)} %x_ref.1) | copy-start | bytes 393220
  1.1 10.4 %collective-permute-start.2 = (bf16[128,1024]{1,0:T(8,128)(2,1)S(1)}, bf16[128,1024]{1,0:T(8,128)(2,1)S(1)}, u32[]{:S(2)}, u32[]{:S(2)}) collective-permute-start(bf16[128,1024]{1,0:T(8,128)(2,1)S(1)} %slice.24), channel_id=1, source_target_pairs={{0,3},{1,2},{2,1},{3,0},{4,7},{5,6},{6,5},{7,4},{8,11},{9,10},{10,... | collective-permute-start | bytes 786440 | tf_op jit(solution)/shard_map/ppermute | solution.py:45
  3.9 7.8 %collective-permute-start = (bf16[128,1024]{1,0:T(8,128)(2,1)S(1)}, bf16[128,1024]{1,0:T(8,128)(2,1)S(1)}, u32[]{:S(2)}, u32[]{:S(2)}) collective-permute-start(bf16[128,1024]{1,0:T(8,128)(2,1)S(1)} %slice.24), channel_id=1, source_target_pairs={{0,1},{1,0},{2,3},{3,2},{4,5},{5,4},{6,7},{7,6},{8,9},{9,8},{10,11... | collective-permute-start | bytes 786440 | tf_op jit(solution)/shard_map/ppermute | solution.py:45
  11.4 0.7 copy-start.11
  11.7 0.7 copy-start.12
  14.0 13.6 %collective-permute-start.9 = (bf16[64,1024]{1,0:T(8,128)(2,1)}, bf16[64,1024]{1,0:T(8,128)(2,1)S(1)}, u32[]{:S(2)}, u32[]{:S(2)}) collective-permute-start(bf16[64,1024]{1,0:T(8,128)(2,1)} %hold.1), channel_id=1, source_target_pairs={{0,64},{32,96},{64,128},{96,160},{128,192},{160,224},{1,65},{33,97... | collective-permute-start | bytes 393224 | tf_op jit(solution)/shard_map/ppermute | solution.py:41
  17.4 10.1 %collective-permute-start.8 = (bf16[64,1024]{1,0:T(8,128)(2,1)}, bf16[64,1024]{1,0:T(8,128)(2,1)S(1)}, u32[]{:S(2)}, u32[]{:S(2)}) collective-permute-start(bf16[64,1024]{1,0:T(8,128)(2,1)} %hold.1), channel_id=1, source_target_pairs={{0,128},{32,160},{64,192},{96,224},{1,129},{33,161},{65,193},{97,2... | collective-permute-start | bytes 393224 | tf_op jit(solution)/shard_map/ppermute | solution.py:41
  22.3 5.3 %collective-permute-start.7 = (bf16[64,1024]{1,0:T(8,128)(2,1)}, bf16[64,1024]{1,0:T(8,128)(2,1)S(1)}, u32[]{:S(2)}, u32[]{:S(2)}) collective-permute-start(bf16[64,1024]{1,0:T(8,128)(2,1)} %hold.1), channel_id=1, source_target_pairs={{0,192},{32,224},{1,193},{33,225},{2,194},{34,226},{3,195},{35,227... | collective-permute-start | bytes 393224 | tf_op jit(solution)/shard_map/ppermute | solution.py:41
  24.5 23.3 %collective-permute-start.3 = (bf16[384,1024]{1,0:T(8,128)(2,1)}, bf16[384,1024]{1,0:T(8,128)(2,1)S(1)}, u32[]{:S(2)}, u32[]{:S(2)}) collective-permute-start(bf16[384,1024]{1,0:T(8,128)(2,1)} %slice.25), channel_id=1, source_target_pairs={{0,3},{1,2},{2,1},{3,0},{4,7},{5,6},{6,5},{7,4},{8,11},{9,10},{10,... | collective-permute-start | bytes 2359304 | tf_op jit(solution)/shard_map/ppermute | solution.py:45
  26.1 23.3 %collective-permute-start.1 = (bf16[384,1024]{1,0:T(8,128)(2,1)}, bf16[384,1024]{1,0:T(8,128)(2,1)}, u32[]{:S(2)}, u32[]{:S(2)}) collective-permute-start(bf16[384,1024]{1,0:T(8,128)(2,1)} %slice.25), channel_id=1, source_target_pairs={{0,1},{1,0},{2,3},{3,2},{4,5},{5,4},{6,7},{7,6},{8,9},{9,8},{10,11... | collective-permute-start | bytes 2359304 | tf_op jit(solution)/shard_map/ppermute | solution.py:45
  27.6 0.7 copy-start.14
  28.3 19.5 %copy-start.13 = (bf16[128,1024]{1,0:T(8,128)(2,1)S(1)}, bf16[128,1024]{1,0:T(8,128)(2,1)}, u32[]{:S(2)}) copy-start(bf16[128,1024]{1,0:T(8,128)(2,1)} %copy-done.12) | copy-start | bytes 786436
  28.3 2.0 %collective-permute-start.10 = (bf16[64,1024]{1,0:T(8,128)(2,1)}, bf16[64,1024]{1,0:T(8,128)(2,1)}, u32[]{:S(2)}, u32[]{:S(2)}) collective-permute-start(bf16[64,1024]{1,0:T(8,128)(2,1)} %select_select_fusion.1), channel_id=1, source_target_pairs={{0,32},{32,0},{64,96},{96,64},{128,160},{160,128},{192,224},{224,1... | collective-permute-start | bytes 393224 | tf_op jit(solution)/shard_map/ppermute | solution.py:502
  30.4 22.0 %copy-start.18 = (bf16[64,1024]{1,0:T(8,128)(2,1)}, bf16[64,1024]{1,0:T(8,128)(2,1)S(1)}, u32[]{:S(2)}) copy-start(bf16[64,1024]{1,0:T(8,128)(2,1)S(1)} %select_select_fusion.own) | copy-start | bytes 393220
  30.4 20.2 %collective-permute-start.13 = (bf16[64,1024]{1,0:T(8,128)(2,1)S(1)}, bf16[64,1024]{1,0:T(8,128)(2,1)S(1)}, u32[]{:S(2)}, u32[]{:S(2)}) collective-permute-start(bf16[64,1024]{1,0:T(8,128)(2,1)S(1)} %select_select_fusion.own), channel_id=1, source_target_pairs={{0,2},{1,3},{2,0},{3,1},{4,6},{5,7},{6,4},{7,5},{8,10},{9,11},{10,... | collective-permute-start | bytes 393224 | tf_op jit(solution)/shard_map/ppermute | solution.py:45
  33.6 18.7 %collective-permute-start.12 = (bf16[64,1024]{1,0:T(8,128)(2,1)S(1)}, bf16[64,1024]{1,0:T(8,128)(2,1)S(1)}, u32[]{:S(2)}, u32[]{:S(2)}) collective-permute-start(bf16[64,1024]{1,0:T(8,128)(2,1)S(1)} %select_select_fusion.own), channel_id=1, source_target_pairs={{0,3},{1,2},{2,1},{3,0},{4,7},{5,6},{6,5},{7,4},{8,11},{9,10},{10,... | collective-permute-start | bytes 393224 | tf_op jit(solution)/shard_map/ppermute | solution.py:45
  35.2 17.3 %collective-permute-start.11 = (bf16[64,1024]{1,0:T(8,128)(2,1)S(1)}, bf16[64,1024]{1,0:T(8,128)(2,1)S(1)}, u32[]{:S(2)}, u32[]{:S(2)}) collective-permute-start(bf16[64,1024]{1,0:T(8,128)(2,1)S(1)} %select_select_fusion.own), channel_id=1, source_target_pairs={{0,1},{1,0},{2,3},{3,2},{4,5},{5,4},{6,7},{7,6},{8,9},{9,8},{10,11... | collective-permute-start | bytes 393224 | tf_op jit(solution)/shard_map/ppermute | solution.py:45
  36.6 15.8 %copy-start.7 = (bf16[4096,256]{1,0:T(8,128)(2,1)}, bf16[4096,256]{1,0:T(8,128)(2,1)S(1)}, u32[]{:S(2)}) copy-start(bf16[4096,256]{1,0:T(8,128)(2,1)S(1)} %constant_dynamic-update-slice_fusion.w_kv.refs_1_) | copy-start | bytes 6291460
  47.8 12.7 %copy-start.9 = (bf16[384,1024]{1,0:T(8,128)(2,1)}, bf16[384,1024]{1,0:T(8,128)(2,1)S(1)}, u32[]{:S(2)}) copy-start(bf16[384,1024]{1,0:T(8,128)(2,1)S(1)} %collective-permute-done.3.three_b) | copy-start | bytes 2359300
  47.8 15.9 %collective-permute-start.4 = (bf16[128,1024]{1,0:T(8,128)(2,1)S(1)}, bf16[128,1024]{1,0:T(8,128)(2,1)S(1)}, u32[]{:S(2)}, u32[]{:S(2)}) collective-permute-start(bf16[128,1024]{1,0:T(8,128)(2,1)S(1)} %copy-done.13), channel_id=1, source_target_pairs={{0,3},{1,2},{2,1},{3,0},{4,7},{5,6},{6,5},{7,4},{8,11},{9,10},{10,... | collective-permute-start | bytes 786440 | tf_op jit(solution)/shard_map/ppermute | solution.py:45
  49.5 14.3 %collective-permute-start.6 = (bf16[256,1024]{1,0:T(8,128)(2,1)S(1)}, bf16[256,1024]{1,0:T(8,128)(2,1)S(1)}, u32[]{:S(2)}, u32[]{:S(2)}) collective-permute-start(bf16[256,1024]{1,0:T(8,128)(2,1)S(1)} %slice.33), channel_id=1, source_target_pairs={{0,1},{1,0},{2,3},{3,2},{4,5},{5,4},{6,7},{7,6},{8,9},{9,8},{10,11... | collective-permute-start | bytes 1572872 | tf_op jit(solution)/shard_map/ppermute | solution.py:45
  50.7 1.8 %copy-start.19 = (bf16[64,1024]{1,0:T(8,128)(2,1)}, bf16[64,1024]{1,0:T(8,128)(2,1)S(1)}, u32[]{:S(2)}) copy-start(bf16[64,1024]{1,0:T(8,128)(2,1)S(1)} %collective-permute-done.13.two) | copy-start | bytes 393220
  50.7 13.1 %collective-permute-start.5 = (bf16[128,1024]{1,0:T(8,128)(2,1)S(1)}, bf16[128,1024]{1,0:T(8,128)(2,1)S(1)}, u32[]{:S(2)}, u32[]{:S(2)}) collective-permute-start(bf16[128,1024]{1,0:T(8,128)(2,1)S(1)} %slice.32), channel_id=1, source_target_pairs={{0,3},{1,2},{2,1},{3,0},{4,7},{5,6},{6,5},{7,4},{8,11},{9,10},{10,... | collective-permute-start | bytes 786440 | tf_op jit(solution)/shard_map/ppermute | solution.py:45
  52.3 0.7 copy-start.20
  52.4 0.7 copy-start.21
  60.5 13.5 %collective-permute-start.18 = (bf16[320,256]{1,0:T(8,128)(2,1)}, bf16[320,256]{1,0:T(8,128)(2,1)S(1)}, u32[]{:S(2)}, u32[]{:S(2)}) collective-permute-start(bf16[320,256]{1,0:T(8,128)(2,1)} %project_image.1.refs_4_.refs_2_), channel_id=1, source_target_pairs={{0,28},{4,0},{8,4},{12,8},{16,12},{20,16},{24,20},{28,24},{1,29},{... | collective-permute-start | bytes 491528 | tf_op jit(solution)/shard_map/ppermute | solution.py:41
  61.5 12.5 %collective-permute-start.14 = (bf16[320,256]{1,0:T(8,128)(2,1)}, bf16[320,256]{1,0:T(8,128)(2,1)S(1)}, u32[]{:S(2)}, u32[]{:S(2)}) collective-permute-start(bf16[320,256]{1,0:T(8,128)(2,1)} %project_image.1.refs_4_.refs_2_), channel_id=1, source_target_pairs={{0,4},{4,8},{8,12},{12,16},{16,20},{20,24},{24,28},{28,0},{1,5},{5... | collective-permute-start | bytes 491528 | tf_op jit(solution)/shard_map/ppermute | solution.py:41
  63.7 0.7 copy-start.16
  63.7 0.8 copy-start.17
  64.5 0.8 copy-start.15
  75.1 12.6 %collective-permute-start.19 = (bf16[832,256]{1,0:T(8,128)(2,1)S(1)}, bf16[832,256]{1,0:T(8,128)(2,1)S(1)}, u32[]{:S(2)}, u32[]{:S(2)}) collective-permute-start(bf16[832,256]{1,0:T(8,128)(2,1)S(1)} %get-tuple-element.21), channel_id=1, source_target_pairs={{0,28},{4,0},{8,4},{12,8},{16,12},{20,16},{24,20},{28,24},{1,29},{... | collective-permute-start | bytes 1277960 | tf_op jit(solution)/shard_map/ppermute | solution.py:41
  75.2 12.5 %collective-permute-start.15 = (bf16[832,256]{1,0:T(8,128)(2,1)S(1)}, bf16[832,256]{1,0:T(8,128)(2,1)S(1)}, u32[]{:S(2)}, u32[]{:S(2)}) collective-permute-start(bf16[832,256]{1,0:T(8,128)(2,1)S(1)} %get-tuple-element.22), channel_id=1, source_target_pairs={{0,4},{4,8},{8,12},{12,16},{16,20},{20,24},{24,28},{28,0},{1,5},{5... | collective-permute-start | bytes 1277960 | tf_op jit(solution)/shard_map/ppermute | solution.py:41
  87.7 13.0 %collective-permute-start.20 = (bf16[832,256]{1,0:T(8,128)(2,1)S(1)}, bf16[832,256]{1,0:T(8,128)(2,1)S(1)}, u32[]{:S(2)}, u32[]{:S(2)}) collective-permute-start(bf16[832,256]{1,0:T(8,128)(2,1)S(1)} %collective-permute-done.19.refs_9_), channel_id=1, source_target_pairs={{0,28},{4,0},{8,4},{12,8},{16,12},{20,16},{24,20},{28,24},{1,29},{... | collective-permute-start | bytes 1277960 | tf_op jit(solution)/shard_map/ppermute | solution.py:41
  87.7 13.1 %collective-permute-start.16 = (bf16[832,256]{1,0:T(8,128)(2,1)S(1)}, bf16[832,256]{1,0:T(8,128)(2,1)S(1)}, u32[]{:S(2)}, u32[]{:S(2)}) collective-permute-start(bf16[832,256]{1,0:T(8,128)(2,1)S(1)} %collective-permute-done.15.refs_5_), channel_id=1, source_target_pairs={{0,4},{4,8},{8,12},{12,16},{16,20},{20,24},{24,28},{28,0},{1,5},{5... | collective-permute-start | bytes 1277960 | tf_op jit(solution)/shard_map/ppermute | solution.py:41
  100.7 10.0 %collective-permute-start.21 = (bf16[672,256]{1,0:T(8,128)(2,1)S(1)}, bf16[672,256]{1,0:T(8,128)(2,1)S(1)}, u32[]{:S(2)}, u32[]{:S(2)}) collective-permute-start(bf16[672,256]{1,0:T(8,128)(2,1)S(1)} %slice.35), channel_id=1, source_target_pairs={{0,28},{4,0},{8,4},{12,8},{16,12},{20,16},{24,20},{28,24},{1,29},{... | collective-permute-start | bytes 1032200 | tf_op jit(solution)/shard_map/ppermute | solution.py:41
  100.8 13.3 %copy-start = (bf16[512,256]{1,0:T(8,128)(2,1)S(1)}, bf16[512,256]{1,0:T(8,128)(2,1)}, u32[]{:S(2)}) copy-start(bf16[512,256]{1,0:T(8,128)(2,1)} %get-tuple-element.13.refs_3_) | copy-start | bytes 786436
  100.9 13.3 %copy-start.1 = (bf16[320,256]{1,0:T(8,128)(2,1)S(1)}, bf16[320,256]{1,0:T(8,128)(2,1)}, u32[]{:S(2)}) copy-start(bf16[320,256]{1,0:T(8,128)(2,1)} %project_image.1.refs_4_.refs_2_) | copy-start | bytes 491524
  100.9 13.3 %copy-start.2 = (s32[8,8]{1,0:T(8,128)S(1)}, s32[8,8]{1,0:T(8,128)}, u32[]{:S(2)}) copy-start(s32[8,8]{1,0:T(8,128)} %starts_ref.3) | copy-start | bytes 772
  100.9 13.3 %copy-start.3 = (s32[3]{0:T(128)S(1)}, s32[3]{0:T(128)}, u32[]{:S(2)}) copy-start(s32[3]{0:T(128)} %pad_add_fusion.refs_2_.ids_ref) | copy-start | bytes 40
  100.9 13.3 %copy-start.4 = (s32[8]{0:T(128)S(1)}, s32[8]{0:T(128)}, u32[]{:S(2)}) copy-start(s32[8]{0:T(128)} %counts_ref.3) | copy-start | bytes 100
  100.9 13.3 %copy-start.5 = (bf16[512,512]{1,0:T(8,128)(2,1)S(1)}, bf16[512,512]{1,0:T(8,128)(2,1)}, u32[]{:S(2)}) copy-start(bf16[512,512]{1,0:T(8,128)(2,1)} %query.3.refs_1_) | copy-start | bytes 1572868
  100.9 9.9 %collective-permute-start.17 = (bf16[672,256]{1,0:T(8,128)(2,1)S(1)}, bf16[672,256]{1,0:T(8,128)(2,1)S(1)}, u32[]{:S(2)}, u32[]{:S(2)}) collective-permute-start(bf16[672,256]{1,0:T(8,128)(2,1)S(1)} %slice.34), channel_id=1, source_target_pairs={{0,4},{4,8},{8,12},{12,16},{16,20},{20,24},{24,28},{28,0},{1,5},{5... | collective-permute-start | bytes 1032200 | tf_op jit(solution)/shard_map/ppermute | solution.py:41
  110.7 34.5 %collective-permute-start.23 = (bf16[256,256]{1,0:T(8,128)(2,1)S(1)}, bf16[256,256]{1,0:T(8,128)(2,1)S(1)}, u32[]{:S(2)}, u32[]{:S(2)}) collective-permute-start(bf16[256,256]{1,0:T(8,128)(2,1)S(1)} %slice.37), channel_id=1, source_target_pairs={{0,28},{4,0},{8,4},{12,8},{16,12},{20,16},{24,20},{28,24},{1,29},{... | collective-permute-start | bytes 393224 | tf_op jit(solution)/shard_map/ppermute | solution.py:41
  110.8 34.4 %collective-permute-start.22 = (bf16[256,256]{1,0:T(8,128)(2,1)S(1)}, bf16[256,256]{1,0:T(8,128)(2,1)S(1)}, u32[]{:S(2)}, u32[]{:S(2)}) collective-permute-start(bf16[256,256]{1,0:T(8,128)(2,1)S(1)} %slice.36), channel_id=1, source_target_pairs={{0,4},{4,8},{8,12},{12,16},{16,20},{20,24},{24,28},{28,0},{1,5},{5... | collective-permute-start | bytes 393224 | tf_op jit(solution)/shard_map/ppermute | solution.py:41
  114.2 1.0 copy-start.6

commit v12 on v11

--- a/solution.py
+++ b/solution.py
@@ -124,28 +124,17 @@
 
 def text_kernel(ids_ref, own, one_a, one_b, three_a, three_b, two_a, two_b, two_c, *refs):
     gain, w_kv, cos, sin = refs[:4]
-    normed_ref, out_ref, held = refs[-3:]
+    normed_ref, out_ref = refs[-2:]
     rows = own.shape[0]
-    step = pl.program_id(0)
-    last = pl.num_programs(0) - 1
-    slot = lax.rem(step, 2)
-
-    def phase(do_norm, do_product):
-        if do_norm:
-            pieces = [
-                own[...],
-                jnp.where(step == 0, one_a[...], one_b[...]),
-                jnp.where(step == 0, three_a[...], three_b[...]),
-                jnp.where(step == 0, two_a[...], jnp.where(step == 1, two_b[...], two_c[...])),
-            ]
-            normalise(ids_ref[0], gain, pieces, held.at[slot], slice(0, rows))
-            normed_ref[...] = held[slot]
-        if do_product:
-            write_key_value(held[1 - slot], w_kv, cos[...], sin[...], out_ref, slice(0, rows))
-
-    pl.when(step == 0)(lambda: phase(True, False))
-    pl.when((step > 0) & (step < last))(lambda: phase(True, True))
-    pl.when(step == last)(lambda: phase(False, True))
+    for n, others in enumerate(
+        ((one_a, three_a, two_a), (one_b, three_b, two_b), (one_b, three_b, two_c))
+    ):
+        @pl.when(jnp.minimum(pl.program_id(0), 2) == n)
+        def _():
+            pieces = [own[...]] + [other[...] for other in others]
+            normalise(ids_ref[0], gain, pieces, normed_ref, slice(0, rows))
+
+    write_key_value(normed_ref[...], w_kv, cos[...], sin[...], out_ref, slice(0, rows))
 
 
 def project_text(ids, arrays, gain, w_kv, tables, after):
@@ -154,30 +143,27 @@
     tile = rows // steps
 
     def block(skipped):
-        return pl.BlockSpec(
-            (tile, D // 4), lambda r: (jnp.clip(r - skipped, 0, steps - 1 - skipped), 0)
-        )
+        return pl.BlockSpec((tile, D // 4), lambda r: (jnp.maximum(r - skipped, 0), 0))
 
     whole = pl.BlockSpec(memory_space=VMEM)
     only = pl.BlockSpec((tile, D // 4), lambda r: (0, 0))
-    table = pl.BlockSpec((tile, HD // 2), lambda r: (jnp.maximum(r - 1, 0), 0))
+    table = pl.BlockSpec((tile, HD // 2), lambda r: (r, 0))
     return pl.pallas_call(
         text_kernel,
         out_shape=[
             jax.ShapeDtypeStruct((rows, D), BF16),
             jax.ShapeDtypeStruct((rows, 2 * HD), BF16),
         ],
-        grid=(steps + 1,),
+        grid=(steps,),
         in_specs=[pl.BlockSpec(memory_space=SMEM)]
         + [block(0), only, block(1), only, block(1), only, only, block(2)]
         + [whole] * 2
         + [table] * 2
         + [pl.BlockSpec(memory_space=pl.ANY)] * len(after),
         out_specs=[
-            pl.BlockSpec((tile, D), lambda r: (jnp.minimum(r, steps - 1), 0)),
-            pl.BlockSpec((tile, 2 * HD), lambda r: (jnp.maximum(r - 1, 0), 0)),
+            pl.BlockSpec((tile, D), lambda r: (r, 0)),
+            pl.BlockSpec((tile, 2 * HD), lambda r: (r, 0)),
         ],
-        scratch_shapes=[pltpu.VMEM((2, tile, D), BF16)],
         compiler_params=pltpu.CompilerParams(vmem_limit_bytes=58 * 2**20),
         cost_estimate=pl.CostEstimate(flops=0, bytes_accessed=0, transcendentals=0),
         name="project_text",
@@ -496,7 +482,7 @@
     group_a, group_b = text_rows[:quarter], text_rows[quarter:]
     one_a, three_a = first_hop(group_a)
     one_b, three_b = first_hop(group_b)
-    leaving = hold(visual_rows, (one_a, three_a, ids, *image_tables, *text_tables))
+    leaving = hold(visual_rows, (one_a, three_a, ids, *image_tables))
     routed = [visual_rows] + [shift(leaving, "dp", 2 * d, False) for d in (1, 2, 3)]
     for_other = choose(its_distance, routed)
     from_other = lax.ppermute(for_other, "dp", [(i, i ^ 1) for i in range(SHARDS)])

time: 151 us -> 140 us (0.927)
  waiting for transfers between devices: 24.1 us -> 12.3 us
    ppermute x10, waiting for transfers between devices: 11.7 us -> 0.98 us  [exchange(): return lax.ppermute(x, 'mp', [(i, i ^ mask) for i in range(4)])]
    unnamed x45 -> x41, local copies, waits for them, and re-layouts: 5.46 us -> 5.46 us
  transfers between devices with their start and end apart: 24 -> 24, of which waited for: 6 -> 3; matrix products, arithmetic and copies ran while one was open for 8% -> 9% of each run, Pallas kernels for 39% -> 43%
where the time goes in v12:
time: 140 us; the launch traced here: 139 us
  Pallas kernels  65.6 us (47%)
  starting transfers between devices  39.8 us (28%)
  waiting for transfers between devices  12.3 us (9%)
  local copies, waits for them, and re-layouts  11.1 us (8%)
  other arithmetic  7.34 us (5%)
  between operations  2.81 us (2%)
    pallas_call x1, Pallas kernels, attention(): pl.pallas_call(functools.partial(attention_kernel, tok, heads), out_shape...  30.6 us
    ppermute x13, starting transfers between devices, shift(): return lax.ppermute(x, axis, pairs)  26.8 us
    ppermute x10, starting transfers between devices, exchange(): return lax.ppermute(x, 'mp', [(i, i ^ mask) for i in range(4)])  13.1 us
    pallas_call x2, Pallas kernels, query(): pl.pallas_call(query_kernel, out_shape=jax.ShapeDtypeStruct((rows, column...  12.6 us
    ppermute x13, waiting for transfers between devices, shift(): return lax.ppermute(x, axis, pairs)  11.3 us
    pallas_call x1, Pallas kernels, project_text(): pl.pallas_call(text_kernel, out_shape=[jax.ShapeDtypeStruct((rows, D), BF...  7.74 us
    pallas_call x1, Pallas kernels, project_image(): pl.pallas_call(image_kernel, out_shape=jax.ShapeDtypeStruct(((1 + steps)...  7.43 us
    pallas_call x1, Pallas kernels, finish(): pl.pallas_call(functools.partial(finish_kernel, tok), out_shape=jax.Shape...  5.71 us
  transfers between devices with their start and end apart: 24, of which 3 were waited for; matrix products, arithmetic and copies ran while one was open for 9% of the time, Pallas kernels for 43%

profile of v12, /device:TPU:224, one launch (start us, length us, event | category | flops | bytes accessed | tf_op | source)
XLA Modules:
  0.0 139.0 jit_solution(3706987914098865635)
XLA Ops:
  0.0 1.0 slice.24
  1.0 0.0 copy-start.9
  1.0 2.8 %collective-permute-start.2 = (bf16[128,1024]{1,0:T(8,128)(2,1)S(1)}, bf16[128,1024]{1,0:T(8,128)(2,1)S(1)}, u32[]{:S(2)}, u32[]{:S(2)}) collective-permute-start(bf16[128,1024]{1,0:T(8,128)(2,1)S(1)} %slice.24), channel_id=1, source_target_pairs={{0,3},{1,2},{2,1},{3,0},{4,7},{5,6},{6,5},{7,4},{8,11},{9,10},{10,... | collective-permute-start | bytes 786440 | tf_op jit(solution)/shard_map/ppermute | solution.py:45
  3.9 0.2 collective-permute-start
  4.1 2.1 %slice.25 = bf16[384,1024]{1,0:T(8,128)(2,1)} slice(bf16[512,1024]{1,0:T(8,128)(2,1)} %own.1), slice={[128:512], [0:1024]} | slice | bytes 1572864 | tf_op jit(solution)/shard_map/slice | solution.py:482
  6.1 1.1 collective-permute-start.3
  7.3 0.7 collective-permute-start.1
  8.0 0.7 fusion.1
  9.2 0.8 select_reduce_fusion
  10.0 0.7 add_convert_fusion.1
  10.7 0.6 pad_add_fusion.refs_2_.ids_ref
  11.3 0.8 multiply_sine_fusion.1
  12.1 0.0 collective-permute-done.2.refs_1_.three_a
  12.1 1.0 collective-permute-done.refs_0_.one_a
  13.1 0.7 copy-done.11
  13.8 1.6 %hold.1 = bf16[64,1024]{1,0:T(8,128)(2,1)} custom-call(bf16[64,1024]{1,0:T(8,128)(2,1)} %x_ref.1, bf16[128,1024]{1,0:T(8,128)(2,1)} %copy-done.11, bf16[128,1024]{1,0:T(8,128)(2,1)} %copy-done.10, s32[3]{0:T(128)} %pad_add_fusion.refs_2_.ids_ref, f32[64,64]{1,0:T(8,128)} %get-tuple-element.26.refs_3_.cos, f32[64,64]{1,0:T(8,128)} %get-tuple-element.25.refs_4_.sin), custom_call_target="tpu_custom_call" | custom-call | tf_op jit(solution)/shard_map/hold/pallas_call | solution.py:115
  15.4 3.5 %collective-permute-start.9 = (bf16[64,1024]{1,0:T(8,128)(2,1)}, bf16[64,1024]{1,0:T(8,128)(2,1)S(1)}, u32[]{:S(2)}, u32[]{:S(2)}) collective-permute-start(bf16[64,1024]{1,0:T(8,128)(2,1)} %hold.1), channel_id=1, source_target_pairs={{0,64},{32,96},{64,128},{96,160},{128,192},{160,224},{1,65},{33,97... | collective-permute-start | bytes 393224 | tf_op jit(solution)/shard_map/ppermute | solution.py:41
  18.9 4.8 %collective-permute-start.8 = (bf16[64,1024]{1,0:T(8,128)(2,1)}, bf16[64,1024]{1,0:T(8,128)(2,1)S(1)}, u32[]{:S(2)}, u32[]{:S(2)}) collective-permute-start(bf16[64,1024]{1,0:T(8,128)(2,1)} %hold.1), channel_id=1, source_target_pairs={{0,128},{32,160},{64,192},{96,224},{1,129},{33,161},{65,193},{97,2... | collective-permute-start | bytes 393224 | tf_op jit(solution)/shard_map/ppermute | solution.py:41
  23.7 1.9 %collective-permute-start.7 = (bf16[64,1024]{1,0:T(8,128)(2,1)}, bf16[64,1024]{1,0:T(8,128)(2,1)}, u32[]{:S(2)}, u32[]{:S(2)}) collective-permute-start(bf16[64,1024]{1,0:T(8,128)(2,1)} %hold.1), channel_id=1, source_target_pairs={{0,192},{32,224},{1,193},{33,225},{2,194},{34,226},{3,195},{35,227... | collective-permute-start | bytes 393224 | tf_op jit(solution)/shard_map/ppermute | solution.py:41
  25.7 1.4 %constant_dynamic-update-slice_fusion.1 = bf16[4096,256]{1,0:T(8,128)(2,1)S(1)} fusion(bf16[4096,128]{1,0:T(8,128)(2,1)} %param.14), kind=kLoop, calls=%fused_computation.9 | loop fusion | bytes 2097152
  28.4 0.0 collective-permute-done.7
  28.4 0.7 select_select_fusion.1
  29.1 1.5 %constant_dynamic-update-slice_fusion.w_kv.refs_1_ = bf16[4096,256]{1,0:T(8,128)(2,1)S(1)} fusion(bf16[4096,256]{1,0:T(8,128)(2,1)S(1)} %constant_dynamic-update-slice_fusion.1, bf16[4096,128]{1,0:T(8,128)(2,1)} %param.15), kind=kLoop, calls=%fused_computation.8 | loop fusion | bytes 2097152 | tf_op jit(solution)/shard_map/concatenate | solution.py:459
  31.2 0.0 collective-permute-done.10
  31.2 0.1 select_select_fusion.own
  31.3 2.1 %collective-permute-start.13 = (bf16[64,1024]{1,0:T(8,128)(2,1)S(1)}, bf16[64,1024]{1,0:T(8,128)(2,1)S(1)}, u32[]{:S(2)}, u32[]{:S(2)}) collective-permute-start(bf16[64,1024]{1,0:T(8,128)(2,1)S(1)} %select_select_fusion.own), channel_id=1, source_target_pairs={{0,2},{1,3},{2,0},{3,1},{4,6},{5,7},{6,4},{7,5},{8,10},{9,11},{10,... | collective-permute-start | bytes 393224 | tf_op jit(solution)/shard_map/ppermute | solution.py:45
  33.4 1.1 collective-permute-start.12
  34.6 0.3 collective-permute-start.11
  34.9 1.8 %multiply_sine_fusion = (f32[512,64]{1,0:T(8,128)}, f32[512,64]{1,0:T(8,128)}) fusion(f32[64]{0:T(128)S(1)} %multiply_exponential_fusion, f32[512]{0:T(512)S(1)} %add_convert_fusion), kind=kLoop, calls=%fused_computation.2 | loop fusion | flops 32768 | bytes 264448 | tf_op jit(solution)/shard_map/sin | solution.py:30
  36.7 1.9 %collective-permute-start.4 = (bf16[128,1024]{1,0:T(8,128)(2,1)S(1)}, bf16[128,1024]{1,0:T(8,128)(2,1)S(1)}, u32[]{:S(2)}, u32[]{:S(2)}) collective-permute-start(bf16[128,1024]{1,0:T(8,128)(2,1)S(1)} %copy-done.12), channel_id=1, source_target_pairs={{0,3},{1,2},{2,1},{3,0},{4,7},{5,6},{6,5},{7,4},{8,11},{9,10},{10,... | collective-permute-start | bytes 786440 | tf_op jit(solution)/shard_map/ppermute | solution.py:45
  38.6 0.0 collective-permute-done.1.one_b
  38.6 1.5 %collective-permute-start.6 = (bf16[256,1024]{1,0:T(8,128)(2,1)S(1)}, bf16[256,1024]{1,0:T(8,128)(2,1)S(1)}, u32[]{:S(2)}, u32[]{:S(2)}) collective-permute-start(bf16[256,1024]{1,0:T(8,128)(2,1)S(1)} %slice.33), channel_id=1, source_target_pairs={{0,1},{1,0},{2,3},{3,2},{4,5},{5,4},{6,7},{7,6},{8,9},{9,8},{10,11... | collective-permute-start | bytes 1572872 | tf_op jit(solution)/shard_map/ppermute | solution.py:45
  40.2 1.0 slice.32
  41.1 0.0 collective-permute-done.13.two
  41.1 1.2 collective-permute-start.5
  42.4 0.0 collective-permute-done.12.three
  42.4 0.0 collective-permute-done.11.one
  42.4 0.0 copy-start.19
  42.4 0.6 copy-done.18
  43.0 0.0 copy-done.19
  43.1 7.4 %project_image.1.refs_4_.refs_2_ = bf16[320,256]{1,0:T(8,128)(2,1)} custom-call(s32[3]{0:T(128)} %pad_add_fusion.refs_2_.ids_ref, bf16[64,1024]{1,0:T(8,128)(2,1)} %copy-done.16, bf16[64,1024]{1,0:T(8,128)(2,1)} %copy-done.19, bf16[64,1024]{1,0:T(8,128)(2,1)} %copy-done.18, bf16[64,1024]{1,0:T(8,128)(2,1)} %copy-done.17, f32[1,4096]{1,0:T(1,128)} %bitcast.4, ...), custom_call_target="tpu_custom_call" | custom-call | flops 8000000000 | bytes 10485760 | tf_op jit(solution)/shard_map/project_image/pallas_call | solution.py:92
  50.5 1.0 collective-permute-start.18
  51.5 2.2 %collective-permute-start.14 = (bf16[320,256]{1,0:T(8,128)(2,1)}, bf16[320,256]{1,0:T(8,128)(2,1)S(1)}, u32[]{:S(2)}, u32[]{:S(2)}) collective-permute-start(bf16[320,256]{1,0:T(8,128)(2,1)} %project_image.1.refs_4_.refs_2_), channel_id=1, source_target_pairs={{0,4},{4,8},{8,12},{12,16},{16,20},{20,24},{24,28},{28,0},{1,5},{5... | collective-permute-start | bytes 491528 | tf_op jit(solution)/shard_map/ppermute | solution.py:41
  53.8 0.0 collective-permute-done.5.two_b
  53.8 0.7 copy-done.14
  54.5 0.1 copy-done.15
  54.6 0.8 copy-done.13
  55.3 7.7 %project_text.1 = (bf16[512,4096]{1,0:T(8,128)(2,1)}, bf16[512,256]{1,0:T(8,128)(2,1)}) custom-call(s32[3]{0:T(128)} %pad_add_fusion.refs_2_.ids_ref, bf16[512,1024]{1,0:T(8,128)(2,1)} %own.1, bf16[128,1024]{1,0:T(8,128)(2,1)} %copy-done.11, bf16[384,1024]{1,0:T(8,128)(2,1)} %collective-permute-done.1.one_b, bf16[128,1024]{1,0:T(8,128)(2,1)} %copy-done.10, ...), custom_call_target="tpu_custom_call" | custom-call | tf_op jit(solution)/shard_map/project_text/pallas_call | solution.py:151
  63.1 1.1 pad_maximum_fusion.1
  64.2 0.5 collective-permute-start.19
  64.8 2.8 %collective-permute-start.15 = (bf16[832,256]{1,0:T(8,128)(2,1)S(1)}, bf16[832,256]{1,0:T(8,128)(2,1)S(1)}, u32[]{:S(2)}, u32[]{:S(2)}) collective-permute-start(bf16[832,256]{1,0:T(8,128)(2,1)S(1)} %get-tuple-element.22), channel_id=1, source_target_pairs={{0,4},{4,8},{8,12},{12,16},{16,20},{20,24},{24,28},{28,0},{1,5},{5... | collective-permute-start | bytes 1277960 | tf_op jit(solution)/shard_map/ppermute | solution.py:41
  67.5 9.2 %collective-permute-done.19.refs_9_ = bf16[832,256]{1,0:T(8,128)(2,1)S(1)} collective-permute-done((bf16[832,256]{1,0:T(8,128)(2,1)S(1)}, bf16[832,256]{1,0:T(8,128)(2,1)S(1)}, u32[]{:S(2)}, u32[]{:S(2)}) %collective-permute-start.19) | collective-permute-done | bytes 426016 | tf_op jit(solution)/shard_map/ppermute | solution.py:41
  76.8 3.2 %collective-permute-start.16 = (bf16[832,256]{1,0:T(8,128)(2,1)S(1)}, bf16[832,256]{1,0:T(8,128)(2,1)S(1)}, u32[]{:S(2)}, u32[]{:S(2)}) collective-permute-start(bf16[832,256]{1,0:T(8,128)(2,1)S(1)} %collective-permute-done.15.refs_5_), channel_id=1, source_target_pairs={{0,4},{4,8},{8,12},{12,16},{16,20},{20,24},{24,28},{28,0},{1,5},{5... | collective-permute-start | bytes 1277960 | tf_op jit(solution)/shard_map/ppermute | solution.py:41
  80.0 6.3 %query.3.refs_1_ = bf16[512,512]{1,0:T(8,128)(2,1)} custom-call(bf16[512,4096]{1,0:T(8,128)(2,1)} %get-tuple-element.12.x_ref, bf16[4096,1024]{1,0:T(8,128)(2,1)} %w_ref.3, f32[512,64]{1,0:T(8,128)} %get-tuple-element.24.refs_2_.cos, f32[512,64]{1,0:T(8,128)} %get-tuple-element.23.refs_3_.sin), custom_call_target="tpu_custom_call" | custom-call | flops 6000000000 | bytes 1048576 | tf_op jit(solution)/shard_map/query/pallas_call | solution.py:185
  86.3 2.0 %collective-permute-done.20.refs_10_ = bf16[832,256]{1,0:T(8,128)(2,1)S(1)} collective-permute-done((bf16[832,256]{1,0:T(8,128)(2,1)S(1)}, bf16[832,256]{1,0:T(8,128)(2,1)S(1)}, u32[]{:S(2)}, u32[]{:S(2)}) %collective-permute-start.20) | collective-permute-done | bytes 426016 | tf_op jit(solution)/shard_map/ppermute | solution.py:41
  88.4 0.1 collective-permute-start.21
  88.6 3.3 %collective-permute-start.17 = (bf16[672,256]{1,0:T(8,128)(2,1)S(1)}, bf16[672,256]{1,0:T(8,128)(2,1)S(1)}, u32[]{:S(2)}, u32[]{:S(2)}) collective-permute-start(bf16[672,256]{1,0:T(8,128)(2,1)S(1)} %slice.34), channel_id=1, source_target_pairs={{0,4},{4,8},{8,12},{12,16},{16,20},{20,24},{24,28},{28,0},{1,5},{5... | collective-permute-start | bytes 1032200 | tf_op jit(solution)/shard_map/ppermute | solution.py:41
  91.9 6.3 %query.2.refs_0_ = bf16[512,512]{1,0:T(8,128)(2,1)} custom-call(bf16[512,4096]{1,0:T(8,128)(2,1)} %get-tuple-element.12.x_ref, bf16[4096,1024]{1,0:T(8,128)(2,1)} %w_ref.3, f32[512,64]{1,0:T(8,128)} %get-tuple-element.24.refs_2_.cos, f32[512,64]{1,0:T(8,128)} %get-tuple-element.23.refs_3_.sin), custom_call_target="tpu_custom_call" | custom-call | flops 6000000000 | bytes 1048576 | tf_op jit(solution)/shard_map/query/pallas_call | solution.py:185
  98.1 0.1 collective-permute-start.23
  98.3 3.3 %collective-permute-start.22 = (bf16[256,256]{1,0:T(8,128)(2,1)S(1)}, bf16[256,256]{1,0:T(8,128)(2,1)S(1)}, u32[]{:S(2)}, u32[]{:S(2)}) collective-permute-start(bf16[256,256]{1,0:T(8,128)(2,1)S(1)} %slice.36), channel_id=1, source_target_pairs={{0,4},{4,8},{8,12},{12,16},{16,20},{20,24},{24,28},{28,0},{1,5},{5... | collective-permute-start | bytes 393224 | tf_op jit(solution)/shard_map/ppermute | solution.py:41
  101.6 0.0 copy-start.6
  101.6 1.0 copy-done.6
  102.6 30.6 %attention.1 = (bf16[512,1024]{1,0:T(8,128)(2,1)S(1)}, bf16[8,64,256]{2,1,0:T(8,128)(2,1)S(1)}, f32[512,1024]{1,0:T(8,128)S(1)}, f32[512,128]{1,0:T(8,128)S(1)}, f32[512,128]{1,0:T(8,128)S(1)}) custom-call(s32[3]{0:T(128)S(1)} %copy-done.3, s32[8]{0:T(128)S(1)} %copy-done.4, s32[8,8]{1,0:T(8,128)S(1)} %copy-done.2, bf16[512,512]{1,0:T(8,128)(2,1)S(1)} %copy-done.6, ...), custom_call_target="tpu_custom_call" | custom-call | flops 7516192768 | bytes 8388608 | tf_op jit(solution)/shard_map/attention/pallas_call | solution.py:349
  133.3 5.7 %finish.1 = bf16[512,1024]{1,0:T(8,128)(2,1)} custom-call(s32[3]{0:T(128)S(1)} %copy-done.3, s32[8]{0:T(128)S(1)} %copy-done.4, s32[8,8]{1,0:T(8,128)S(1)} %copy-done.2, bf16[512,1024]{1,0:T(8,128)(2,1)S(1)} %get-tuple-element.14.refs_0_, bf16[8,64,256]{2,1,0:T(8,128)(2,1)S(1)} %get-tuple-element.15.refs_1_, ...), custom_call_target="tpu_custom_call" | custom-call | flops 1073741824 | bytes 6291456 | tf_op jit(solution)/shard_map/finish/pallas_call | solution.py:434
  (53 shorter events, 0.2 us)
Async XLA Ops:
  0.0 8.0 %copy-start.4 = (s32[8]{0:T(128)S(1)}, s32[8]{0:T(128)}, u32[]{:S(2)}) copy-start(s32[8]{0:T(128)} %counts_ref.3) | copy-start | bytes 100
  0.0 9.2 %copy-start.2 = (s32[8,8]{1,0:T(8,128)S(1)}, s32[8,8]{1,0:T(8,128)}, u32[]{:S(2)}) copy-start(s32[8,8]{1,0:T(8,128)} %starts_ref.3) | copy-start | bytes 772
  1.0 27.4 %copy-start.9 = (bf16[64,1024]{1,0:T(8,128)(2,1)S(1)}, bf16[64,1024]{1,0:T(8,128)(2,1)}, u32[]{:S(2)}) copy-start(bf16[64,1024]{1,0:T(8,128)(2,1)} %x_ref.1) | copy-start | bytes 393220
  1.0 11.1 %collective-permute-start.2 = (bf16[128,1024]{1,0:T(8,128)(2,1)S(1)}, bf16[128,1024]{1,0:T(8,128)(2,1)S(1)}, u32[]{:S(2)}, u32[]{:S(2)}) collective-permute-start(bf16[128,1024]{1,0:T(8,128)(2,1)S(1)} %slice.24), channel_id=1, source_target_pairs={{0,3},{1,2},{2,1},{3,0},{4,7},{5,6},{6,5},{7,4},{8,11},{9,10},{10,... | collective-permute-start | bytes 786440 | tf_op jit(solution)/shard_map/ppermute | solution.py:45
  3.9 9.2 %collective-permute-start = (bf16[128,1024]{1,0:T(8,128)(2,1)S(1)}, bf16[128,1024]{1,0:T(8,128)(2,1)S(1)}, u32[]{:S(2)}, u32[]{:S(2)}) collective-permute-start(bf16[128,1024]{1,0:T(8,128)(2,1)S(1)} %slice.24), channel_id=1, source_target_pairs={{0,1},{1,0},{2,3},{3,2},{4,5},{5,4},{6,7},{7,6},{8,9},{9,8},{10,11... | collective-permute-start | bytes 786440 | tf_op jit(solution)/shard_map/ppermute | solution.py:45
  6.1 30.6 %collective-permute-start.3 = (bf16[384,1024]{1,0:T(8,128)(2,1)}, bf16[384,1024]{1,0:T(8,128)(2,1)S(1)}, u32[]{:S(2)}, u32[]{:S(2)}) collective-permute-start(bf16[384,1024]{1,0:T(8,128)(2,1)} %slice.25), channel_id=1, source_target_pairs={{0,3},{1,2},{2,1},{3,0},{4,7},{5,6},{6,5},{7,4},{8,11},{9,10},{10,... | collective-permute-start | bytes 2359304 | tf_op jit(solution)/shard_map/ppermute | solution.py:45
  7.3 31.3 %collective-permute-start.1 = (bf16[384,1024]{1,0:T(8,128)(2,1)}, bf16[384,1024]{1,0:T(8,128)(2,1)}, u32[]{:S(2)}, u32[]{:S(2)}) collective-permute-start(bf16[384,1024]{1,0:T(8,128)(2,1)} %slice.25), channel_id=1, source_target_pairs={{0,1},{1,0},{2,3},{3,2},{4,5},{5,4},{6,7},{7,6},{8,9},{9,8},{10,11... | collective-permute-start | bytes 2359304 | tf_op jit(solution)/shard_map/ppermute | solution.py:45
  12.1 1.0 copy-start.10
  13.1 0.8 copy-start.11
  15.4 13.0 %collective-permute-start.9 = (bf16[64,1024]{1,0:T(8,128)(2,1)}, bf16[64,1024]{1,0:T(8,128)(2,1)S(1)}, u32[]{:S(2)}, u32[]{:S(2)}) collective-permute-start(bf16[64,1024]{1,0:T(8,128)(2,1)} %hold.1), channel_id=1, source_target_pairs={{0,64},{32,96},{64,128},{96,160},{128,192},{160,224},{1,65},{33,97... | collective-permute-start | bytes 393224 | tf_op jit(solution)/shard_map/ppermute | solution.py:41
  18.9 9.5 %collective-permute-start.8 = (bf16[64,1024]{1,0:T(8,128)(2,1)}, bf16[64,1024]{1,0:T(8,128)(2,1)S(1)}, u32[]{:S(2)}, u32[]{:S(2)}) collective-permute-start(bf16[64,1024]{1,0:T(8,128)(2,1)} %hold.1), channel_id=1, source_target_pairs={{0,128},{32,160},{64,192},{96,224},{1,129},{33,161},{65,193},{97,2... | collective-permute-start | bytes 393224 | tf_op jit(solution)/shard_map/ppermute | solution.py:41
  23.7 4.7 %collective-permute-start.7 = (bf16[64,1024]{1,0:T(8,128)(2,1)}, bf16[64,1024]{1,0:T(8,128)(2,1)}, u32[]{:S(2)}, u32[]{:S(2)}) collective-permute-start(bf16[64,1024]{1,0:T(8,128)(2,1)} %hold.1), channel_id=1, source_target_pairs={{0,192},{32,224},{1,193},{33,225},{2,194},{34,226},{3,195},{35,227... | collective-permute-start | bytes 393224 | tf_op jit(solution)/shard_map/ppermute | solution.py:41
  27.1 9.6 %copy-start.12 = (bf16[128,1024]{1,0:T(8,128)(2,1)S(1)}, bf16[128,1024]{1,0:T(8,128)(2,1)}, u32[]{:S(2)}) copy-start(bf16[128,1024]{1,0:T(8,128)(2,1)} %copy-done.11) | copy-start | bytes 786436
  29.1 2.1 %collective-permute-start.10 = (bf16[64,1024]{1,0:T(8,128)(2,1)}, bf16[64,1024]{1,0:T(8,128)(2,1)}, u32[]{:S(2)}, u32[]{:S(2)}) collective-permute-start(bf16[64,1024]{1,0:T(8,128)(2,1)} %select_select_fusion.1), channel_id=1, source_target_pairs={{0,32},{32,0},{64,96},{96,64},{128,160},{160,128},{192,224},{224,1... | collective-permute-start | bytes 393224 | tf_op jit(solution)/shard_map/ppermute | solution.py:488
  30.6 11.8 %copy-start.7 = (bf16[4096,256]{1,0:T(8,128)(2,1)}, bf16[4096,256]{1,0:T(8,128)(2,1)S(1)}, u32[]{:S(2)}) copy-start(bf16[4096,256]{1,0:T(8,128)(2,1)S(1)} %constant_dynamic-update-slice_fusion.w_kv.refs_1_) | copy-start | bytes 6291460
  31.3 11.1 %copy-start.16 = (bf16[64,1024]{1,0:T(8,128)(2,1)}, bf16[64,1024]{1,0:T(8,128)(2,1)S(1)}, u32[]{:S(2)}) copy-start(bf16[64,1024]{1,0:T(8,128)(2,1)S(1)} %select_select_fusion.own) | copy-start | bytes 393220
  31.3 9.8 %collective-permute-start.13 = (bf16[64,1024]{1,0:T(8,128)(2,1)S(1)}, bf16[64,1024]{1,0:T(8,128)(2,1)S(1)}, u32[]{:S(2)}, u32[]{:S(2)}) collective-permute-start(bf16[64,1024]{1,0:T(8,128)(2,1)S(1)} %select_select_fusion.own), channel_id=1, source_target_pairs={{0,2},{1,3},{2,0},{3,1},{4,6},{5,7},{6,4},{7,5},{8,10},{9,11},{10,... | collective-permute-start | bytes 393224 | tf_op jit(solution)/shard_map/ppermute | solution.py:45
  33.4 9.0 %collective-permute-start.12 = (bf16[64,1024]{1,0:T(8,128)(2,1)S(1)}, bf16[64,1024]{1,0:T(8,128)(2,1)S(1)}, u32[]{:S(2)}, u32[]{:S(2)}) collective-permute-start(bf16[64,1024]{1,0:T(8,128)(2,1)S(1)} %select_select_fusion.own), channel_id=1, source_target_pairs={{0,3},{1,2},{2,1},{3,0},{4,7},{5,6},{6,5},{7,4},{8,11},{9,10},{10,... | collective-permute-start | bytes 393224 | tf_op jit(solution)/shard_map/ppermute | solution.py:45
  34.6 7.8 %collective-permute-start.11 = (bf16[64,1024]{1,0:T(8,128)(2,1)S(1)}, bf16[64,1024]{1,0:T(8,128)(2,1)S(1)}, u32[]{:S(2)}, u32[]{:S(2)}) collective-permute-start(bf16[64,1024]{1,0:T(8,128)(2,1)S(1)} %select_select_fusion.own), channel_id=1, source_target_pairs={{0,1},{1,0},{2,3},{3,2},{4,5},{5,4},{6,7},{7,6},{8,9},{9,8},{10,11... | collective-permute-start | bytes 393224 | tf_op jit(solution)/shard_map/ppermute | solution.py:45
  36.7 13.8 %copy-start.8 = (bf16[384,1024]{1,0:T(8,128)(2,1)}, bf16[384,1024]{1,0:T(8,128)(2,1)S(1)}, u32[]{:S(2)}) copy-start(bf16[384,1024]{1,0:T(8,128)(2,1)S(1)} %collective-permute-done.3.three_b) | copy-start | bytes 2359300
  36.7 17.0 %collective-permute-start.4 = (bf16[128,1024]{1,0:T(8,128)(2,1)S(1)}, bf16[128,1024]{1,0:T(8,128)(2,1)S(1)}, u32[]{:S(2)}, u32[]{:S(2)}) collective-permute-start(bf16[128,1024]{1,0:T(8,128)(2,1)S(1)} %copy-done.12), channel_id=1, source_target_pairs={{0,3},{1,2},{2,1},{3,0},{4,7},{5,6},{6,5},{7,4},{8,11},{9,10},{10,... | collective-permute-start | bytes 786440 | tf_op jit(solution)/shard_map/ppermute | solution.py:45
  38.6 15.1 %collective-permute-start.6 = (bf16[256,1024]{1,0:T(8,128)(2,1)S(1)}, bf16[256,1024]{1,0:T(8,128)(2,1)S(1)}, u32[]{:S(2)}, u32[]{:S(2)}) collective-permute-start(bf16[256,1024]{1,0:T(8,128)(2,1)S(1)} %slice.33), channel_id=1, source_target_pairs={{0,1},{1,0},{2,3},{3,2},{4,5},{5,4},{6,7},{7,6},{8,9},{9,8},{10,11... | collective-permute-start | bytes 1572872 | tf_op jit(solution)/shard_map/ppermute | solution.py:45
  41.1 1.3 copy-start.17
  41.1 12.6 %collective-permute-start.5 = (bf16[128,1024]{1,0:T(8,128)(2,1)S(1)}, bf16[128,1024]{1,0:T(8,128)(2,1)S(1)}, u32[]{:S(2)}, u32[]{:S(2)}) collective-permute-start(bf16[128,1024]{1,0:T(8,128)(2,1)S(1)} %slice.32), channel_id=1, source_target_pairs={{0,3},{1,2},{2,1},{3,0},{4,7},{5,6},{6,5},{7,4},{8,11},{9,10},{10,... | collective-permute-start | bytes 786440 | tf_op jit(solution)/shard_map/ppermute | solution.py:45
  42.4 0.6 copy-start.18
  42.4 0.7 copy-start.19
  50.5 12.6 %collective-permute-start.18 = (bf16[320,256]{1,0:T(8,128)(2,1)}, bf16[320,256]{1,0:T(8,128)(2,1)S(1)}, u32[]{:S(2)}, u32[]{:S(2)}) collective-permute-start(bf16[320,256]{1,0:T(8,128)(2,1)} %project_image.1.refs_4_.refs_2_), channel_id=1, source_target_pairs={{0,28},{4,0},{8,4},{12,8},{16,12},{20,16},{24,20},{28,24},{1,29},{... | collective-permute-start | bytes 491528 | tf_op jit(solution)/shard_map/ppermute | solution.py:41
  51.5 11.6 %collective-permute-start.14 = (bf16[320,256]{1,0:T(8,128)(2,1)}, bf16[320,256]{1,0:T(8,128)(2,1)S(1)}, u32[]{:S(2)}, u32[]{:S(2)}) collective-permute-start(bf16[320,256]{1,0:T(8,128)(2,1)} %project_image.1.refs_4_.refs_2_), channel_id=1, source_target_pairs={{0,4},{4,8},{8,12},{12,16},{16,20},{20,24},{24,28},{28,0},{1,5},{5... | collective-permute-start | bytes 491528 | tf_op jit(solution)/shard_map/ppermute | solution.py:41
  53.8 0.7 copy-start.14
  53.8 0.8 copy-start.15
  54.6 0.8 copy-start.13
  64.2 12.6 %collective-permute-start.19 = (bf16[832,256]{1,0:T(8,128)(2,1)S(1)}, bf16[832,256]{1,0:T(8,128)(2,1)S(1)}, u32[]{:S(2)}, u32[]{:S(2)}) collective-permute-start(bf16[832,256]{1,0:T(8,128)(2,1)S(1)} %get-tuple-element.21), channel_id=1, source_target_pairs={{0,28},{4,0},{8,4},{12,8},{16,12},{20,16},{24,20},{28,24},{1,29},{... | collective-permute-start | bytes 1277960 | tf_op jit(solution)/shard_map/ppermute | solution.py:41
  64.8 12.0 %collective-permute-start.15 = (bf16[832,256]{1,0:T(8,128)(2,1)S(1)}, bf16[832,256]{1,0:T(8,128)(2,1)S(1)}, u32[]{:S(2)}, u32[]{:S(2)}) collective-permute-start(bf16[832,256]{1,0:T(8,128)(2,1)S(1)} %get-tuple-element.22), channel_id=1, source_target_pairs={{0,4},{4,8},{8,12},{12,16},{16,20},{20,24},{24,28},{28,0},{1,5},{5... | collective-permute-start | bytes 1277960 | tf_op jit(solution)/shard_map/ppermute | solution.py:41
  76.8 11.6 %collective-permute-start.20 = (bf16[832,256]{1,0:T(8,128)(2,1)S(1)}, bf16[832,256]{1,0:T(8,128)(2,1)S(1)}, u32[]{:S(2)}, u32[]{:S(2)}) collective-permute-start(bf16[832,256]{1,0:T(8,128)(2,1)S(1)} %collective-permute-done.19.refs_9_), channel_id=1, source_target_pairs={{0,28},{4,0},{8,4},{12,8},{16,12},{20,16},{24,20},{28,24},{1,29},{... | collective-permute-start | bytes 1277960 | tf_op jit(solution)/shard_map/ppermute | solution.py:41
  76.8 11.7 %collective-permute-start.16 = (bf16[832,256]{1,0:T(8,128)(2,1)S(1)}, bf16[832,256]{1,0:T(8,128)(2,1)S(1)}, u32[]{:S(2)}, u32[]{:S(2)}) collective-permute-start(bf16[832,256]{1,0:T(8,128)(2,1)S(1)} %collective-permute-done.15.refs_5_), channel_id=1, source_target_pairs={{0,4},{4,8},{8,12},{12,16},{16,20},{20,24},{24,28},{28,0},{1,5},{5... | collective-permute-start | bytes 1277960 | tf_op jit(solution)/shard_map/ppermute | solution.py:41
  88.4 9.7 %collective-permute-start.21 = (bf16[672,256]{1,0:T(8,128)(2,1)S(1)}, bf16[672,256]{1,0:T(8,128)(2,1)S(1)}, u32[]{:S(2)}, u32[]{:S(2)}) collective-permute-start(bf16[672,256]{1,0:T(8,128)(2,1)S(1)} %slice.35), channel_id=1, source_target_pairs={{0,28},{4,0},{8,4},{12,8},{16,12},{20,16},{24,20},{28,24},{1,29},{... | collective-permute-start | bytes 1032200 | tf_op jit(solution)/shard_map/ppermute | solution.py:41
  88.5 13.0 %copy-start = (bf16[512,256]{1,0:T(8,128)(2,1)S(1)}, bf16[512,256]{1,0:T(8,128)(2,1)}, u32[]{:S(2)}) copy-start(bf16[512,256]{1,0:T(8,128)(2,1)} %get-tuple-element.13.refs_3_) | copy-start | bytes 786436
  88.5 13.0 %copy-start.1 = (bf16[320,256]{1,0:T(8,128)(2,1)S(1)}, bf16[320,256]{1,0:T(8,128)(2,1)}, u32[]{:S(2)}) copy-start(bf16[320,256]{1,0:T(8,128)(2,1)} %project_image.1.refs_4_.refs_2_) | copy-start | bytes 491524
  88.5 13.0 %copy-start.3 = (s32[3]{0:T(128)S(1)}, s32[3]{0:T(128)}, u32[]{:S(2)}) copy-start(s32[3]{0:T(128)} %pad_add_fusion.refs_2_.ids_ref) | copy-start | bytes 40
  88.6 13.0 %copy-start.5 = (bf16[512,512]{1,0:T(8,128)(2,1)S(1)}, bf16[512,512]{1,0:T(8,128)(2,1)}, u32[]{:S(2)}) copy-start(bf16[512,512]{1,0:T(8,128)(2,1)} %query.3.refs_1_) | copy-start | bytes 1572868
  88.6 9.7 %collective-permute-start.17 = (bf16[672,256]{1,0:T(8,128)(2,1)S(1)}, bf16[672,256]{1,0:T(8,128)(2,1)S(1)}, u32[]{:S(2)}, u32[]{:S(2)}) collective-permute-start(bf16[672,256]{1,0:T(8,128)(2,1)S(1)} %slice.34), channel_id=1, source_target_pairs={{0,4},{4,8},{8,12},{12,16},{16,20},{20,24},{24,28},{28,0},{1,5},{5... | collective-permute-start | bytes 1032200 | tf_op jit(solution)/shard_map/ppermute | solution.py:41
  98.1 35.1 %collective-permute-start.23 = (bf16[256,256]{1,0:T(8,128)(2,1)S(1)}, bf16[256,256]{1,0:T(8,128)(2,1)S(1)}, u32[]{:S(2)}, u32[]{:S(2)}) collective-permute-start(bf16[256,256]{1,0:T(8,128)(2,1)S(1)} %slice.37), channel_id=1, source_target_pairs={{0,28},{4,0},{8,4},{12,8},{16,12},{20,16},{24,20},{28,24},{1,29},{... | collective-permute-start | bytes 393224 | tf_op jit(solution)/shard_map/ppermute | solution.py:41
  98.3 35.0 %collective-permute-start.22 = (bf16[256,256]{1,0:T(8,128)(2,1)S(1)}, bf16[256,256]{1,0:T(8,128)(2,1)S(1)}, u32[]{:S(2)}, u32[]{:S(2)}) collective-permute-start(bf16[256,256]{1,0:T(8,128)(2,1)S(1)} %slice.36), channel_id=1, source_target_pairs={{0,4},{4,8},{8,12},{12,16},{16,20},{20,24},{24,28},{28,0},{1,5},{5... | collective-permute-start | bytes 393224 | tf_op jit(solution)/shard_map/ppermute | solution.py:41
  101.6 1.0 copy-start.6

commit v13 on v12

--- a/solution.py
+++ b/solution.py
@@ -295,7 +295,7 @@
                     nth = place >> shift_by
                     earlier = nth + jnp.where(nth > 3, 1, 0) <= ctx
                     ahead = jnp.where(nth == 0, place, jnp.where(earlier, -tok, tok))
-                    seen = s[:, g * HD : (g + 1) * HD]
+                    seen = s[:, g * HD : (g + 1) * HD] * factor
                     seen = jnp.where(column + ahead <= row, seen, -1e30)
                     s_buf[slot, j, :, g * HD : (g + 1) * HD] = seen
                     top = jnp.maximum(top, seen)
@@ -305,7 +305,7 @@
                 total = sum_buf[...]
                 weights = []
                 for g in range(BLOCK // HD):
-                    w = jnp.exp2(s_buf[other, j, :, g * HD : (g + 1) * HD] * factor - shared)
+                    w = jnp.exp2(s_buf[other, j, :, g * HD : (g + 1) * HD] - shared)
                     total = total + w
                     weights.append(w.astype(BF16))
                 sum_buf[...] = total
@@ -328,7 +328,7 @@
             place_images(False)
             pl.loop(1, blocks)(block)
         if do_score:
-            top = jnp.max(max_buf[slot], axis=1, keepdims=True) * factor
+            top = jnp.max(max_buf[slot], axis=1, keepdims=True)
             max_buf[slot] = jnp.broadcast_to(top, (tok, HD))
         if do_mix:
             head = step - 1

time: 140 us -> 140 us (level)
  no operation moved by 1% of the time
where the time goes in v13:
time: 140 us
  Pallas kernels  66.5 us (48%)
  starting transfers between devices  39.8 us (28%)
  waiting for transfers between devices  12.3 us (9%)
  local copies, waits for them, and re-layouts  11.1 us (8%)
  other arithmetic  7.34 us (5%)
  between operations  2.81 us (2%)
    pallas_call x1, Pallas kernels, attention(): pl.pallas_call(functools.partial(attention_kernel, tok, heads), out_shape...  31.5 us
    ppermute x13, starting transfers between devices, shift(): return lax.ppermute(x, axis, pairs)  26.8 us
    ppermute x10, starting transfers between devices, exchange(): return lax.ppermute(x, 'mp', [(i, i ^ mask) for i in range(4)])  13.1 us
    pallas_call x2, Pallas kernels, query(): pl.pallas_call(query_kernel, out_shape=jax.ShapeDtypeStruct((rows, column...  12.6 us
    ppermute x13, waiting for transfers between devices, shift(): return lax.ppermute(x, axis, pairs)  11.3 us
    pallas_call x1, Pallas kernels, project_text(): pl.pallas_call(text_kernel, out_shape=[jax.ShapeDtypeStruct((rows, D), BF...  7.74 us
    pallas_call x1, Pallas kernels, project_image(): pl.pallas_call(image_kernel, out_shape=jax.ShapeDtypeStruct(((1 + steps)...  7.43 us
    pallas_call x1, Pallas kernels, finish(): pl.pallas_call(functools.partial(finish_kernel, tok), out_shape=jax.Shape...  5.71 us
  transfers between devices with their start and end apart: 24, of which 3 were waited for; matrix products, arithmetic and copies ran while one was open for 9% of the time, Pallas kernels for 43%

profile of v13, /device:TPU:224, one launch (start us, length us, event | category | flops | bytes accessed | tf_op | source)
XLA Modules:
  0.0 139.8 jit_solution(2055918200318673979)
XLA Ops:
  0.0 1.0 slice.24
  1.0 0.0 copy-start.9
  1.0 2.8 %collective-permute-start.2 = (bf16[128,1024]{1,0:T(8,128)(2,1)S(1)}, bf16[128,1024]{1,0:T(8,128)(2,1)S(1)}, u32[]{:S(2)}, u32[]{:S(2)}) collective-permute-start(bf16[128,1024]{1,0:T(8,128)(2,1)S(1)} %slice.24), channel_id=1, source_target_pairs={{0,3},{1,2},{2,1},{3,0},{4,7},{5,6},{6,5},{7,4},{8,11},{9,10},{10,... | collective-permute-start | bytes 786440 | tf_op jit(solution)/shard_map/ppermute | solution.py:45
  3.9 0.2 collective-permute-start
  4.1 2.1 %slice.25 = bf16[384,1024]{1,0:T(8,128)(2,1)} slice(bf16[512,1024]{1,0:T(8,128)(2,1)} %own.1), slice={[128:512], [0:1024]} | slice | bytes 1572864 | tf_op jit(solution)/shard_map/slice | solution.py:482
  6.1 1.1 collective-permute-start.3
  7.3 0.7 collective-permute-start.1
  8.0 0.7 fusion.1
  9.2 0.8 select_reduce_fusion
  10.0 0.7 add_convert_fusion.1
  10.7 0.6 pad_add_fusion.refs_2_.ids_ref
  11.3 0.8 multiply_sine_fusion.1
  12.1 1.0 collective-permute-done.refs_0_.one_a
  13.1 0.7 copy-done.11
  13.8 1.6 %hold.1 = bf16[64,1024]{1,0:T(8,128)(2,1)} custom-call(bf16[64,1024]{1,0:T(8,128)(2,1)} %x_ref.1, bf16[128,1024]{1,0:T(8,128)(2,1)} %copy-done.11, bf16[128,1024]{1,0:T(8,128)(2,1)} %copy-done.10, s32[3]{0:T(128)} %pad_add_fusion.refs_2_.ids_ref, f32[64,64]{1,0:T(8,128)} %get-tuple-element.26.refs_3_.cos, f32[64,64]{1,0:T(8,128)} %get-tuple-element.25.refs_4_.sin), custom_call_target="tpu_custom_call" | custom-call | tf_op jit(solution)/shard_map/hold/pallas_call | solution.py:115
  15.4 3.5 %collective-permute-start.9 = (bf16[64,1024]{1,0:T(8,128)(2,1)}, bf16[64,1024]{1,0:T(8,128)(2,1)S(1)}, u32[]{:S(2)}, u32[]{:S(2)}) collective-permute-start(bf16[64,1024]{1,0:T(8,128)(2,1)} %hold.1), channel_id=1, source_target_pairs={{0,64},{32,96},{64,128},{96,160},{128,192},{160,224},{1,65},{33,97... | collective-permute-start | bytes 393224 | tf_op jit(solution)/shard_map/ppermute | solution.py:41
  18.9 4.8 %collective-permute-start.8 = (bf16[64,1024]{1,0:T(8,128)(2,1)}, bf16[64,1024]{1,0:T(8,128)(2,1)S(1)}, u32[]{:S(2)}, u32[]{:S(2)}) collective-permute-start(bf16[64,1024]{1,0:T(8,128)(2,1)} %hold.1), channel_id=1, source_target_pairs={{0,128},{32,160},{64,192},{96,224},{1,129},{33,161},{65,193},{97,2... | collective-permute-start | bytes 393224 | tf_op jit(solution)/shard_map/ppermute | solution.py:41
  23.7 1.9 %collective-permute-start.7 = (bf16[64,1024]{1,0:T(8,128)(2,1)}, bf16[64,1024]{1,0:T(8,128)(2,1)}, u32[]{:S(2)}, u32[]{:S(2)}) collective-permute-start(bf16[64,1024]{1,0:T(8,128)(2,1)} %hold.1), channel_id=1, source_target_pairs={{0,192},{32,224},{1,193},{33,225},{2,194},{34,226},{3,195},{35,227... | collective-permute-start | bytes 393224 | tf_op jit(solution)/shard_map/ppermute | solution.py:41
  25.7 1.4 %constant_dynamic-update-slice_fusion.1 = bf16[4096,256]{1,0:T(8,128)(2,1)S(1)} fusion(bf16[4096,128]{1,0:T(8,128)(2,1)} %param.14), kind=kLoop, calls=%fused_computation.9 | loop fusion | bytes 2097152
  28.4 0.0 collective-permute-done.8
  28.4 0.7 select_select_fusion.1
  29.1 1.5 %constant_dynamic-update-slice_fusion.w_kv.refs_1_ = bf16[4096,256]{1,0:T(8,128)(2,1)S(1)} fusion(bf16[4096,256]{1,0:T(8,128)(2,1)S(1)} %constant_dynamic-update-slice_fusion.1, bf16[4096,128]{1,0:T(8,128)(2,1)} %param.15), kind=kLoop, calls=%fused_computation.8 | loop fusion | bytes 2097152 | tf_op jit(solution)/shard_map/concatenate | solution.py:459
  31.2 0.0 collective-permute-done.10
  31.2 0.1 select_select_fusion.own
  31.3 2.1 %collective-permute-start.13 = (bf16[64,1024]{1,0:T(8,128)(2,1)S(1)}, bf16[64,1024]{1,0:T(8,128)(2,1)S(1)}, u32[]{:S(2)}, u32[]{:S(2)}) collective-permute-start(bf16[64,1024]{1,0:T(8,128)(2,1)S(1)} %select_select_fusion.own), channel_id=1, source_target_pairs={{0,2},{1,3},{2,0},{3,1},{4,6},{5,7},{6,4},{7,5},{8,10},{9,11},{10,... | collective-permute-start | bytes 393224 | tf_op jit(solution)/shard_map/ppermute | solution.py:45
  33.4 1.1 collective-permute-start.12
  34.6 0.3 collective-permute-start.11
  34.9 1.8 %multiply_sine_fusion = (f32[512,64]{1,0:T(8,128)}, f32[512,64]{1,0:T(8,128)}) fusion(f32[64]{0:T(128)S(1)} %multiply_exponential_fusion, f32[512]{0:T(512)S(1)} %add_convert_fusion), kind=kLoop, calls=%fused_computation.2 | loop fusion | flops 32768 | bytes 264448 | tf_op jit(solution)/shard_map/sin | solution.py:30
  36.7 0.0 collective-permute-done.3.three_b
  36.7 1.9 %collective-permute-start.4 = (bf16[128,1024]{1,0:T(8,128)(2,1)S(1)}, bf16[128,1024]{1,0:T(8,128)(2,1)S(1)}, u32[]{:S(2)}, u32[]{:S(2)}) collective-permute-start(bf16[128,1024]{1,0:T(8,128)(2,1)S(1)} %copy-done.12), channel_id=1, source_target_pairs={{0,3},{1,2},{2,1},{3,0},{4,7},{5,6},{6,5},{7,4},{8,11},{9,10},{10,... | collective-permute-start | bytes 786440 | tf_op jit(solution)/shard_map/ppermute | solution.py:45
  38.6 1.5 %collective-permute-start.6 = (bf16[256,1024]{1,0:T(8,128)(2,1)S(1)}, bf16[256,1024]{1,0:T(8,128)(2,1)S(1)}, u32[]{:S(2)}, u32[]{:S(2)}) collective-permute-start(bf16[256,1024]{1,0:T(8,128)(2,1)S(1)} %slice.33), channel_id=1, source_target_pairs={{0,1},{1,0},{2,3},{3,2},{4,5},{5,4},{6,7},{7,6},{8,9},{9,8},{10,11... | collective-permute-start | bytes 1572872 | tf_op jit(solution)/shard_map/ppermute | solution.py:45
  40.2 1.0 slice.32
  41.1 0.0 collective-permute-done.13.two
  41.1 1.2 collective-permute-start.5
  42.4 0.0 collective-permute-done.12.three
  42.4 0.0 copy-start.19
  42.4 0.6 copy-done.18
  43.0 0.0 copy-done.19
  43.1 7.4 %project_image.1.refs_4_.refs_2_ = bf16[320,256]{1,0:T(8,128)(2,1)} custom-call(s32[3]{0:T(128)} %pad_add_fusion.refs_2_.ids_ref, bf16[64,1024]{1,0:T(8,128)(2,1)} %copy-done.16, bf16[64,1024]{1,0:T(8,128)(2,1)} %copy-done.19, bf16[64,1024]{1,0:T(8,128)(2,1)} %copy-done.18, bf16[64,1024]{1,0:T(8,128)(2,1)} %copy-done.17, f32[1,4096]{1,0:T(1,128)} %bitcast.4, ...), custom_call_target="tpu_custom_call" | custom-call | flops 8000000000 | bytes 10485760 | tf_op jit(solution)/shard_map/project_image/pallas_call | solution.py:92
  50.5 1.0 collective-permute-start.18
  51.5 2.2 %collective-permute-start.14 = (bf16[320,256]{1,0:T(8,128)(2,1)}, bf16[320,256]{1,0:T(8,128)(2,1)S(1)}, u32[]{:S(2)}, u32[]{:S(2)}) collective-permute-start(bf16[320,256]{1,0:T(8,128)(2,1)} %project_image.1.refs_4_.refs_2_), channel_id=1, source_target_pairs={{0,4},{4,8},{8,12},{12,16},{16,20},{20,24},{24,28},{28,0},{1,5},{5... | collective-permute-start | bytes 491528 | tf_op jit(solution)/shard_map/ppermute | solution.py:41
  53.7 0.0 collective-permute-done.4.two_a
  53.8 0.0 collective-permute-done.5.two_b
  53.8 0.7 copy-done.14
  54.5 0.1 copy-done.15
  54.6 0.8 copy-done.13
  55.3 7.7 %project_text.1 = (bf16[512,4096]{1,0:T(8,128)(2,1)}, bf16[512,256]{1,0:T(8,128)(2,1)}) custom-call(s32[3]{0:T(128)} %pad_add_fusion.refs_2_.ids_ref, bf16[512,1024]{1,0:T(8,128)(2,1)} %own.1, bf16[128,1024]{1,0:T(8,128)(2,1)} %copy-done.11, bf16[384,1024]{1,0:T(8,128)(2,1)} %collective-permute-done.1.one_b, bf16[128,1024]{1,0:T(8,128)(2,1)} %copy-done.10, ...), custom_call_target="tpu_custom_call" | custom-call | tf_op jit(solution)/shard_map/project_text/pallas_call | solution.py:151
  63.1 1.1 pad_maximum_fusion.1
  64.2 0.5 collective-permute-start.19
  64.8 2.8 %collective-permute-start.15 = (bf16[832,256]{1,0:T(8,128)(2,1)S(1)}, bf16[832,256]{1,0:T(8,128)(2,1)S(1)}, u32[]{:S(2)}, u32[]{:S(2)}) collective-permute-start(bf16[832,256]{1,0:T(8,128)(2,1)S(1)} %get-tuple-element.22), channel_id=1, source_target_pairs={{0,4},{4,8},{8,12},{12,16},{16,20},{20,24},{24,28},{28,0},{1,5},{5... | collective-permute-start | bytes 1277960 | tf_op jit(solution)/shard_map/ppermute | solution.py:41
  67.5 9.2 %collective-permute-done.19.refs_9_ = bf16[832,256]{1,0:T(8,128)(2,1)S(1)} collective-permute-done((bf16[832,256]{1,0:T(8,128)(2,1)S(1)}, bf16[832,256]{1,0:T(8,128)(2,1)S(1)}, u32[]{:S(2)}, u32[]{:S(2)}) %collective-permute-start.19) | collective-permute-done | bytes 426016 | tf_op jit(solution)/shard_map/ppermute | solution.py:41
  76.8 0.0 collective-permute-start.20
  76.8 3.2 %collective-permute-start.16 = (bf16[832,256]{1,0:T(8,128)(2,1)S(1)}, bf16[832,256]{1,0:T(8,128)(2,1)S(1)}, u32[]{:S(2)}, u32[]{:S(2)}) collective-permute-start(bf16[832,256]{1,0:T(8,128)(2,1)S(1)} %collective-permute-done.15.refs_5_), channel_id=1, source_target_pairs={{0,4},{4,8},{8,12},{12,16},{16,20},{20,24},{24,28},{28,0},{1,5},{5... | collective-permute-start | bytes 1277960 | tf_op jit(solution)/shard_map/ppermute | solution.py:41
  80.0 6.3 %query.3.refs_1_ = bf16[512,512]{1,0:T(8,128)(2,1)} custom-call(bf16[512,4096]{1,0:T(8,128)(2,1)} %get-tuple-element.12.x_ref, bf16[4096,1024]{1,0:T(8,128)(2,1)} %w_ref.3, f32[512,64]{1,0:T(8,128)} %get-tuple-element.24.refs_2_.cos, f32[512,64]{1,0:T(8,128)} %get-tuple-element.23.refs_3_.sin), custom_call_target="tpu_custom_call" | custom-call | flops 6000000000 | bytes 1048576 | tf_op jit(solution)/shard_map/query/pallas_call | solution.py:185
  86.3 2.0 %collective-permute-done.20.refs_10_ = bf16[832,256]{1,0:T(8,128)(2,1)S(1)} collective-permute-done((bf16[832,256]{1,0:T(8,128)(2,1)S(1)}, bf16[832,256]{1,0:T(8,128)(2,1)S(1)}, u32[]{:S(2)}, u32[]{:S(2)}) %collective-permute-start.20) | collective-permute-done | bytes 426016 | tf_op jit(solution)/shard_map/ppermute | solution.py:41
  88.4 0.1 collective-permute-start.21
  88.6 3.3 %collective-permute-start.17 = (bf16[672,256]{1,0:T(8,128)(2,1)S(1)}, bf16[672,256]{1,0:T(8,128)(2,1)S(1)}, u32[]{:S(2)}, u32[]{:S(2)}) collective-permute-start(bf16[672,256]{1,0:T(8,128)(2,1)S(1)} %slice.34), channel_id=1, source_target_pairs={{0,4},{4,8},{8,12},{12,16},{16,20},{20,24},{24,28},{28,0},{1,5},{5... | collective-permute-start | bytes 1032200 | tf_op jit(solution)/shard_map/ppermute | solution.py:41
  91.9 6.3 %query.2.refs_0_ = bf16[512,512]{1,0:T(8,128)(2,1)} custom-call(bf16[512,4096]{1,0:T(8,128)(2,1)} %get-tuple-element.12.x_ref, bf16[4096,1024]{1,0:T(8,128)(2,1)} %w_ref.3, f32[512,64]{1,0:T(8,128)} %get-tuple-element.24.refs_2_.cos, f32[512,64]{1,0:T(8,128)} %get-tuple-element.23.refs_3_.sin), custom_call_target="tpu_custom_call" | custom-call | flops 6000000000 | bytes 1048576 | tf_op jit(solution)/shard_map/query/pallas_call | solution.py:185
  98.1 0.1 collective-permute-start.23
  98.3 3.3 %collective-permute-start.22 = (bf16[256,256]{1,0:T(8,128)(2,1)S(1)}, bf16[256,256]{1,0:T(8,128)(2,1)S(1)}, u32[]{:S(2)}, u32[]{:S(2)}) collective-permute-start(bf16[256,256]{1,0:T(8,128)(2,1)S(1)} %slice.36), channel_id=1, source_target_pairs={{0,4},{4,8},{8,12},{12,16},{16,20},{20,24},{24,28},{28,0},{1,5},{5... | collective-permute-start | bytes 393224 | tf_op jit(solution)/shard_map/ppermute | solution.py:41
  101.6 0.0 copy-start.6
  101.6 1.0 copy-done.6
  102.6 31.5 %attention.1 = (bf16[512,1024]{1,0:T(8,128)(2,1)S(1)}, bf16[8,64,256]{2,1,0:T(8,128)(2,1)S(1)}, f32[512,1024]{1,0:T(8,128)S(1)}, f32[512,128]{1,0:T(8,128)S(1)}, f32[512,128]{1,0:T(8,128)S(1)}) custom-call(s32[3]{0:T(128)S(1)} %copy-done.3, s32[8]{0:T(128)S(1)} %copy-done.4, s32[8,8]{1,0:T(8,128)S(1)} %copy-done.2, bf16[512,512]{1,0:T(8,128)(2,1)S(1)} %copy-done.6, ...), custom_call_target="tpu_custom_call" | custom-call | flops 7516192768 | bytes 8388608 | tf_op jit(solution)/shard_map/attention/pallas_call | solution.py:349
  134.1 5.7 %finish.1 = bf16[512,1024]{1,0:T(8,128)(2,1)} custom-call(s32[3]{0:T(128)S(1)} %copy-done.3, s32[8]{0:T(128)S(1)} %copy-done.4, s32[8,8]{1,0:T(8,128)S(1)} %copy-done.2, bf16[512,1024]{1,0:T(8,128)(2,1)S(1)} %get-tuple-element.14.refs_0_, bf16[8,64,256]{2,1,0:T(8,128)(2,1)S(1)} %get-tuple-element.15.refs_1_, ...), custom_call_target="tpu_custom_call" | custom-call | flops 1073741824 | bytes 6291456 | tf_op jit(solution)/shard_map/finish/pallas_call | solution.py:434
  (53 shorter events, 0.2 us)
Async XLA Ops:
  0.0 8.0 %copy-start.4 = (s32[8]{0:T(128)S(1)}, s32[8]{0:T(128)}, u32[]{:S(2)}) copy-start(s32[8]{0:T(128)} %counts_ref.3) | copy-start | bytes 100
  0.0 9.2 %copy-start.2 = (s32[8,8]{1,0:T(8,128)S(1)}, s32[8,8]{1,0:T(8,128)}, u32[]{:S(2)}) copy-start(s32[8,8]{1,0:T(8,128)} %starts_ref.3) | copy-start | bytes 772
  1.0 27.4 %copy-start.9 = (bf16[64,1024]{1,0:T(8,128)(2,1)S(1)}, bf16[64,1024]{1,0:T(8,128)(2,1)}, u32[]{:S(2)}) copy-start(bf16[64,1024]{1,0:T(8,128)(2,1)} %x_ref.1) | copy-start | bytes 393220
  1.0 11.1 %collective-permute-start.2 = (bf16[128,1024]{1,0:T(8,128)(2,1)S(1)}, bf16[128,1024]{1,0:T(8,128)(2,1)S(1)}, u32[]{:S(2)}, u32[]{:S(2)}) collective-permute-start(bf16[128,1024]{1,0:T(8,128)(2,1)S(1)} %slice.24), channel_id=1, source_target_pairs={{0,3},{1,2},{2,1},{3,0},{4,7},{5,6},{6,5},{7,4},{8,11},{9,10},{10,... | collective-permute-start | bytes 786440 | tf_op jit(solution)/shard_map/ppermute | solution.py:45
  3.9 9.2 %collective-permute-start = (bf16[128,1024]{1,0:T(8,128)(2,1)S(1)}, bf16[128,1024]{1,0:T(8,128)(2,1)S(1)}, u32[]{:S(2)}, u32[]{:S(2)}) collective-permute-start(bf16[128,1024]{1,0:T(8,128)(2,1)S(1)} %slice.24), channel_id=1, source_target_pairs={{0,1},{1,0},{2,3},{3,2},{4,5},{5,4},{6,7},{7,6},{8,9},{9,8},{10,11... | collective-permute-start | bytes 786440 | tf_op jit(solution)/shard_map/ppermute | solution.py:45
  6.1 30.6 %collective-permute-start.3 = (bf16[384,1024]{1,0:T(8,128)(2,1)}, bf16[384,1024]{1,0:T(8,128)(2,1)S(1)}, u32[]{:S(2)}, u32[]{:S(2)}) collective-permute-start(bf16[384,1024]{1,0:T(8,128)(2,1)} %slice.25), channel_id=1, source_target_pairs={{0,3},{1,2},{2,1},{3,0},{4,7},{5,6},{6,5},{7,4},{8,11},{9,10},{10,... | collective-permute-start | bytes 2359304 | tf_op jit(solution)/shard_map/ppermute | solution.py:45
  7.3 31.3 %collective-permute-start.1 = (bf16[384,1024]{1,0:T(8,128)(2,1)}, bf16[384,1024]{1,0:T(8,128)(2,1)}, u32[]{:S(2)}, u32[]{:S(2)}) collective-permute-start(bf16[384,1024]{1,0:T(8,128)(2,1)} %slice.25), channel_id=1, source_target_pairs={{0,1},{1,0},{2,3},{3,2},{4,5},{5,4},{6,7},{7,6},{8,9},{9,8},{10,11... | collective-permute-start | bytes 2359304 | tf_op jit(solution)/shard_map/ppermute | solution.py:45
  12.1 1.0 copy-start.10
  13.1 0.8 copy-start.11
  15.4 13.0 %collective-permute-start.9 = (bf16[64,1024]{1,0:T(8,128)(2,1)}, bf16[64,1024]{1,0:T(8,128)(2,1)S(1)}, u32[]{:S(2)}, u32[]{:S(2)}) collective-permute-start(bf16[64,1024]{1,0:T(8,128)(2,1)} %hold.1), channel_id=1, source_target_pairs={{0,64},{32,96},{64,128},{96,160},{128,192},{160,224},{1,65},{33,97... | collective-permute-start | bytes 393224 | tf_op jit(solution)/shard_map/ppermute | solution.py:41
  18.9 9.5 %collective-permute-start.8 = (bf16[64,1024]{1,0:T(8,128)(2,1)}, bf16[64,1024]{1,0:T(8,128)(2,1)S(1)}, u32[]{:S(2)}, u32[]{:S(2)}) collective-permute-start(bf16[64,1024]{1,0:T(8,128)(2,1)} %hold.1), channel_id=1, source_target_pairs={{0,128},{32,160},{64,192},{96,224},{1,129},{33,161},{65,193},{97,2... | collective-permute-start | bytes 393224 | tf_op jit(solution)/shard_map/ppermute | solution.py:41
  23.7 4.7 %collective-permute-start.7 = (bf16[64,1024]{1,0:T(8,128)(2,1)}, bf16[64,1024]{1,0:T(8,128)(2,1)}, u32[]{:S(2)}, u32[]{:S(2)}) collective-permute-start(bf16[64,1024]{1,0:T(8,128)(2,1)} %hold.1), channel_id=1, source_target_pairs={{0,192},{32,224},{1,193},{33,225},{2,194},{34,226},{3,195},{35,227... | collective-permute-start | bytes 393224 | tf_op jit(solution)/shard_map/ppermute | solution.py:41
  27.1 9.6 %copy-start.12 = (bf16[128,1024]{1,0:T(8,128)(2,1)S(1)}, bf16[128,1024]{1,0:T(8,128)(2,1)}, u32[]{:S(2)}) copy-start(bf16[128,1024]{1,0:T(8,128)(2,1)} %copy-done.11) | copy-start | bytes 786436
  29.1 2.1 %collective-permute-start.10 = (bf16[64,1024]{1,0:T(8,128)(2,1)}, bf16[64,1024]{1,0:T(8,128)(2,1)}, u32[]{:S(2)}, u32[]{:S(2)}) collective-permute-start(bf16[64,1024]{1,0:T(8,128)(2,1)} %select_select_fusion.1), channel_id=1, source_target_pairs={{0,32},{32,0},{64,96},{96,64},{128,160},{160,128},{192,224},{224,1... | collective-permute-start | bytes 393224 | tf_op jit(solution)/shard_map/ppermute | solution.py:488
  30.6 11.8 %copy-start.7 = (bf16[4096,256]{1,0:T(8,128)(2,1)}, bf16[4096,256]{1,0:T(8,128)(2,1)S(1)}, u32[]{:S(2)}) copy-start(bf16[4096,256]{1,0:T(8,128)(2,1)S(1)} %constant_dynamic-update-slice_fusion.w_kv.refs_1_) | copy-start | bytes 6291460
  31.3 11.1 %copy-start.16 = (bf16[64,1024]{1,0:T(8,128)(2,1)}, bf16[64,1024]{1,0:T(8,128)(2,1)S(1)}, u32[]{:S(2)}) copy-start(bf16[64,1024]{1,0:T(8,128)(2,1)S(1)} %select_select_fusion.own) | copy-start | bytes 393220
  31.3 9.8 %collective-permute-start.13 = (bf16[64,1024]{1,0:T(8,128)(2,1)S(1)}, bf16[64,1024]{1,0:T(8,128)(2,1)S(1)}, u32[]{:S(2)}, u32[]{:S(2)}) collective-permute-start(bf16[64,1024]{1,0:T(8,128)(2,1)S(1)} %select_select_fusion.own), channel_id=1, source_target_pairs={{0,2},{1,3},{2,0},{3,1},{4,6},{5,7},{6,4},{7,5},{8,10},{9,11},{10,... | collective-permute-start | bytes 393224 | tf_op jit(solution)/shard_map/ppermute | solution.py:45
  33.4 9.0 %collective-permute-start.12 = (bf16[64,1024]{1,0:T(8,128)(2,1)S(1)}, bf16[64,1024]{1,0:T(8,128)(2,1)S(1)}, u32[]{:S(2)}, u32[]{:S(2)}) collective-permute-start(bf16[64,1024]{1,0:T(8,128)(2,1)S(1)} %select_select_fusion.own), channel_id=1, source_target_pairs={{0,3},{1,2},{2,1},{3,0},{4,7},{5,6},{6,5},{7,4},{8,11},{9,10},{10,... | collective-permute-start | bytes 393224 | tf_op jit(solution)/shard_map/ppermute | solution.py:45
  34.6 7.8 %collective-permute-start.11 = (bf16[64,1024]{1,0:T(8,128)(2,1)S(1)}, bf16[64,1024]{1,0:T(8,128)(2,1)S(1)}, u32[]{:S(2)}, u32[]{:S(2)}) collective-permute-start(bf16[64,1024]{1,0:T(8,128)(2,1)S(1)} %select_select_fusion.own), channel_id=1, source_target_pairs={{0,1},{1,0},{2,3},{3,2},{4,5},{5,4},{6,7},{7,6},{8,9},{9,8},{10,11... | collective-permute-start | bytes 393224 | tf_op jit(solution)/shard_map/ppermute | solution.py:45
  36.7 13.8 %copy-start.8 = (bf16[384,1024]{1,0:T(8,128)(2,1)}, bf16[384,1024]{1,0:T(8,128)(2,1)S(1)}, u32[]{:S(2)}) copy-start(bf16[384,1024]{1,0:T(8,128)(2,1)S(1)} %collective-permute-done.3.three_b) | copy-start | bytes 2359300
  36.7 17.0 %collective-permute-start.4 = (bf16[128,1024]{1,0:T(8,128)(2,1)S(1)}, bf16[128,1024]{1,0:T(8,128)(2,1)S(1)}, u32[]{:S(2)}, u32[]{:S(2)}) collective-permute-start(bf16[128,1024]{1,0:T(8,128)(2,1)S(1)} %copy-done.12), channel_id=1, source_target_pairs={{0,3},{1,2},{2,1},{3,0},{4,7},{5,6},{6,5},{7,4},{8,11},{9,10},{10,... | collective-permute-start | bytes 786440 | tf_op jit(solution)/shard_map/ppermute | solution.py:45
  38.6 15.1 %collective-permute-start.6 = (bf16[256,1024]{1,0:T(8,128)(2,1)S(1)}, bf16[256,1024]{1,0:T(8,128)(2,1)S(1)}, u32[]{:S(2)}, u32[]{:S(2)}) collective-permute-start(bf16[256,1024]{1,0:T(8,128)(2,1)S(1)} %slice.33), channel_id=1, source_target_pairs={{0,1},{1,0},{2,3},{3,2},{4,5},{5,4},{6,7},{7,6},{8,9},{9,8},{10,11... | collective-permute-start | bytes 1572872 | tf_op jit(solution)/shard_map/ppermute | solution.py:45
  41.1 1.3 copy-start.17
  41.1 12.6 %collective-permute-start.5 = (bf16[128,1024]{1,0:T(8,128)(2,1)S(1)}, bf16[128,1024]{1,0:T(8,128)(2,1)S(1)}, u32[]{:S(2)}, u32[]{:S(2)}) collective-permute-start(bf16[128,1024]{1,0:T(8,128)(2,1)S(1)} %slice.32), channel_id=1, source_target_pairs={{0,3},{1,2},{2,1},{3,0},{4,7},{5,6},{6,5},{7,4},{8,11},{9,10},{10,... | collective-permute-start | bytes 786440 | tf_op jit(solution)/shard_map/ppermute | solution.py:45
  42.4 0.6 copy-start.18
  42.4 0.7 copy-start.19
  50.5 12.6 %collective-permute-start.18 = (bf16[320,256]{1,0:T(8,128)(2,1)}, bf16[320,256]{1,0:T(8,128)(2,1)S(1)}, u32[]{:S(2)}, u32[]{:S(2)}) collective-permute-start(bf16[320,256]{1,0:T(8,128)(2,1)} %project_image.1.refs_4_.refs_2_), channel_id=1, source_target_pairs={{0,28},{4,0},{8,4},{12,8},{16,12},{20,16},{24,20},{28,24},{1,29},{... | collective-permute-start | bytes 491528 | tf_op jit(solution)/shard_map/ppermute | solution.py:41
  51.5 11.6 %collective-permute-start.14 = (bf16[320,256]{1,0:T(8,128)(2,1)}, bf16[320,256]{1,0:T(8,128)(2,1)S(1)}, u32[]{:S(2)}, u32[]{:S(2)}) collective-permute-start(bf16[320,256]{1,0:T(8,128)(2,1)} %project_image.1.refs_4_.refs_2_), channel_id=1, source_target_pairs={{0,4},{4,8},{8,12},{12,16},{16,20},{20,24},{24,28},{28,0},{1,5},{5... | collective-permute-start | bytes 491528 | tf_op jit(solution)/shard_map/ppermute | solution.py:41
  53.8 0.7 copy-start.14
  53.8 0.8 copy-start.15
  54.6 0.8 copy-start.13
  64.2 12.6 %collective-permute-start.19 = (bf16[832,256]{1,0:T(8,128)(2,1)S(1)}, bf16[832,256]{1,0:T(8,128)(2,1)S(1)}, u32[]{:S(2)}, u32[]{:S(2)}) collective-permute-start(bf16[832,256]{1,0:T(8,128)(2,1)S(1)} %get-tuple-element.21), channel_id=1, source_target_pairs={{0,28},{4,0},{8,4},{12,8},{16,12},{20,16},{24,20},{28,24},{1,29},{... | collective-permute-start | bytes 1277960 | tf_op jit(solution)/shard_map/ppermute | solution.py:41
  64.8 12.0 %collective-permute-start.15 = (bf16[832,256]{1,0:T(8,128)(2,1)S(1)}, bf16[832,256]{1,0:T(8,128)(2,1)S(1)}, u32[]{:S(2)}, u32[]{:S(2)}) collective-permute-start(bf16[832,256]{1,0:T(8,128)(2,1)S(1)} %get-tuple-element.22), channel_id=1, source_target_pairs={{0,4},{4,8},{8,12},{12,16},{16,20},{20,24},{24,28},{28,0},{1,5},{5... | collective-permute-start | bytes 1277960 | tf_op jit(solution)/shard_map/ppermute | solution.py:41
  76.8 11.6 %collective-permute-start.20 = (bf16[832,256]{1,0:T(8,128)(2,1)S(1)}, bf16[832,256]{1,0:T(8,128)(2,1)S(1)}, u32[]{:S(2)}, u32[]{:S(2)}) collective-permute-start(bf16[832,256]{1,0:T(8,128)(2,1)S(1)} %collective-permute-done.19.refs_9_), channel_id=1, source_target_pairs={{0,28},{4,0},{8,4},{12,8},{16,12},{20,16},{24,20},{28,24},{1,29},{... | collective-permute-start | bytes 1277960 | tf_op jit(solution)/shard_map/ppermute | solution.py:41
  76.8 11.7 %collective-permute-start.16 = (bf16[832,256]{1,0:T(8,128)(2,1)S(1)}, bf16[832,256]{1,0:T(8,128)(2,1)S(1)}, u32[]{:S(2)}, u32[]{:S(2)}) collective-permute-start(bf16[832,256]{1,0:T(8,128)(2,1)S(1)} %collective-permute-done.15.refs_5_), channel_id=1, source_target_pairs={{0,4},{4,8},{8,12},{12,16},{16,20},{20,24},{24,28},{28,0},{1,5},{5... | collective-permute-start | bytes 1277960 | tf_op jit(solution)/shard_map/ppermute | solution.py:41
  88.4 9.7 %collective-permute-start.21 = (bf16[672,256]{1,0:T(8,128)(2,1)S(1)}, bf16[672,256]{1,0:T(8,128)(2,1)S(1)}, u32[]{:S(2)}, u32[]{:S(2)}) collective-permute-start(bf16[672,256]{1,0:T(8,128)(2,1)S(1)} %slice.35), channel_id=1, source_target_pairs={{0,28},{4,0},{8,4},{12,8},{16,12},{20,16},{24,20},{28,24},{1,29},{... | collective-permute-start | bytes 1032200 | tf_op jit(solution)/shard_map/ppermute | solution.py:41
  88.5 13.0 %copy-start = (bf16[512,256]{1,0:T(8,128)(2,1)S(1)}, bf16[512,256]{1,0:T(8,128)(2,1)}, u32[]{:S(2)}) copy-start(bf16[512,256]{1,0:T(8,128)(2,1)} %get-tuple-element.13.refs_3_) | copy-start | bytes 786436
  88.5 13.0 %copy-start.1 = (bf16[320,256]{1,0:T(8,128)(2,1)S(1)}, bf16[320,256]{1,0:T(8,128)(2,1)}, u32[]{:S(2)}) copy-start(bf16[320,256]{1,0:T(8,128)(2,1)} %project_image.1.refs_4_.refs_2_) | copy-start | bytes 491524
  88.5 13.0 %copy-start.3 = (s32[3]{0:T(128)S(1)}, s32[3]{0:T(128)}, u32[]{:S(2)}) copy-start(s32[3]{0:T(128)} %pad_add_fusion.refs_2_.ids_ref) | copy-start | bytes 40
  88.6 13.0 %copy-start.5 = (bf16[512,512]{1,0:T(8,128)(2,1)S(1)}, bf16[512,512]{1,0:T(8,128)(2,1)}, u32[]{:S(2)}) copy-start(bf16[512,512]{1,0:T(8,128)(2,1)} %query.3.refs_1_) | copy-start | bytes 1572868
  88.6 9.7 %collective-permute-start.17 = (bf16[672,256]{1,0:T(8,128)(2,1)S(1)}, bf16[672,256]{1,0:T(8,128)(2,1)S(1)}, u32[]{:S(2)}, u32[]{:S(2)}) collective-permute-start(bf16[672,256]{1,0:T(8,128)(2,1)S(1)} %slice.34), channel_id=1, source_target_pairs={{0,4},{4,8},{8,12},{12,16},{16,20},{20,24},{24,28},{28,0},{1,5},{5... | collective-permute-start | bytes 1032200 | tf_op jit(solution)/shard_map/ppermute | solution.py:41
  98.1 35.9 %collective-permute-start.23 = (bf16[256,256]{1,0:T(8,128)(2,1)S(1)}, bf16[256,256]{1,0:T(8,128)(2,1)S(1)}, u32[]{:S(2)}, u32[]{:S(2)}) collective-permute-start(bf16[256,256]{1,0:T(8,128)(2,1)S(1)} %slice.37), channel_id=1, source_target_pairs={{0,28},{4,0},{8,4},{12,8},{16,12},{20,16},{24,20},{28,24},{1,29},{... | collective-permute-start | bytes 393224 | tf_op jit(solution)/shard_map/ppermute | solution.py:41
  98.3 35.8 %collective-permute-start.22 = (bf16[256,256]{1,0:T(8,128)(2,1)S(1)}, bf16[256,256]{1,0:T(8,128)(2,1)S(1)}, u32[]{:S(2)}, u32[]{:S(2)}) collective-permute-start(bf16[256,256]{1,0:T(8,128)(2,1)S(1)} %slice.36), channel_id=1, source_target_pairs={{0,4},{4,8},{8,12},{12,16},{16,20},{20,24},{24,28},{28,0},{1,5},{5... | collective-permute-start | bytes 393224 | tf_op jit(solution)/shard_map/ppermute | solution.py:41
  101.6 1.0 copy-start.6
